TPU v7x, 32 devices: a whole 2x2x4 slice. The times are simulated.
32 devices in a mesh: dp: 8 (over z, x), expert: 4 (over y, core).
Axes of the slice: x: 2, y: 2, z: 4, core: 2. Of those that a mesh axis runs over, the one named last changes fastest.
Arguments:
- tokens: bfloat16 [128, 4096], P(('dp', 'expert')), may hold values from -6 to 6
- expert_ids: int32 [128, 2], P(('dp', 'expert')), may hold values from 0 to 3, all different within a row; in each aligned block of 16 rows (0 to 15, 16 to 31, ...) at most 16 rows name the same one
- route_weights: bfloat16 [128, 2], P(('dp', 'expert')), may hold values from 0.099609375 to 1
- out_grad: bfloat16 [128, 4096], P(('dp', 'expert')), may hold values from -6 to 6
- gate_weight: bfloat16 [4, 1536, 4096], P('expert', 'dp'), may hold values from -0.09375 to 0.09375
- up_weight: bfloat16 [4, 1536, 4096], P('expert', 'dp'), may hold values from -0.09375 to 0.09375
- down_weight: bfloat16 [4, 1536, 4096], P('expert', 'dp'), may hold values from -0.15625 to 0.15625
Outputs:
- mixed: bfloat16 [128, 4096], P(('dp', 'expert'))
- input_grad: bfloat16 [128, 4096], P(('dp', 'expert'))
- gate_grad: bfloat16 [4, 1536, 4096], P('expert', 'dp')
- up_grad: bfloat16 [4, 1536, 4096], P('expert', 'dp')
- down_grad: bfloat16 [4, 1536, 4096], P('expert', 'dp')
Inputs may be any that keep to these rules, and one draw needn't show every extreme that they name: `expert_ids`: each row names 2 different experts. In each aligned block of 16 rows (the tokens of one index of dp) no expert is named by more than 16 rows, a bound that some block reaches.
All inputs are finite; a program needn't handle non-finite values.
Results may differ from a plain program's by a relative error of at most 0.024.
Values may be sent and summed in bfloat16 or wider, within the bound.
No kernel may reach another device: no remote copies, remote signals or barrier semaphores. Data moves between devices by JAX's collectives and lax.ppermute only.
A program may use at most 64 MiB of HBM per device.

v0:
```python
import jax
import jax.numpy as jnp
from jax import lax
from jax.sharding import PartitionSpec as P

ROW_CAP = 16


def contract_rows(left, right):
    return lax.dot_general(
        left, right, (((1,), (1,)), ((), ())), preferred_element_type=jnp.float32
    )


def contract_first(left, right):
    return lax.dot_general(
        left, right, (((0,), (0,)), ((), ())), preferred_element_type=jnp.float32
    )


def shards(tokens, expert_ids, route_weights, out_grad, gate_weight, up_weight, down_weight):
    expert = lax.axis_index("expert")
    width = tokens.shape[1]
    local_tokens = tokens.shape[0]
    group_x, group_dy, group_w = (
        lax.all_gather(tokens, "expert", axis=0, tiled=True),
        lax.all_gather(out_grad, "expert", axis=0, tiled=True),
        lax.all_gather(route_weights, "expert", axis=0, tiled=True),
    )
    group_ids = lax.all_gather(expert_ids, "expert", axis=0, tiled=True)
    matches = group_ids == expert
    routed = jnp.any(matches, axis=1)
    weight = jnp.sum(jnp.where(matches, group_w.astype(jnp.float32), 0.0), axis=1)
    slot_rank = jnp.cumsum(routed.astype(jnp.int32)) - 1
    slot_index = jnp.arange(ROW_CAP, dtype=jnp.int32)
    picker = ((slot_rank[None, :] == slot_index[:, None]) & routed[None, :]).astype(jnp.bfloat16)
    slot_x = jnp.dot(picker, group_x, preferred_element_type=jnp.float32).astype(jnp.bfloat16)
    scaled = (weight[:, None] * group_dy.astype(jnp.float32)).astype(jnp.bfloat16)
    slot_dy = jnp.dot(picker, scaled, preferred_element_type=jnp.float32).astype(jnp.bfloat16)
    w_gate = gate_weight[0]
    w_up = up_weight[0]
    w_down = down_weight[0]
    all_x = lax.all_gather(slot_x, "dp", axis=0, tiled=True)
    gate_pre = contract_rows(w_gate, all_x)
    up_pre = contract_rows(w_up, all_x)
    gate_sig = jax.nn.sigmoid(gate_pre)
    silu_gate = gate_pre * gate_sig
    hidden = (silu_gate * up_pre).astype(jnp.bfloat16)
    expert_out = lax.psum_scatter(
        contract_first(hidden, w_down).astype(jnp.bfloat16), "dp", scatter_dimension=0, tiled=True
    )
    all_dy = lax.all_gather(slot_dy, "dp", axis=0, tiled=True)
    hidden_grad = contract_rows(w_down, all_dy)
    silu_slope = gate_sig * (1.0 + gate_pre * (1.0 - gate_sig))
    gate_act = (hidden_grad * up_pre * silu_slope).astype(jnp.bfloat16)
    up_act = (hidden_grad * silu_gate).astype(jnp.bfloat16)
    grad_down = jnp.dot(hidden, all_dy, preferred_element_type=jnp.float32).astype(jnp.bfloat16)
    grad_gate = jnp.dot(gate_act, all_x, preferred_element_type=jnp.float32).astype(jnp.bfloat16)
    grad_up = jnp.dot(up_act, all_x, preferred_element_type=jnp.float32).astype(jnp.bfloat16)
    expert_in = lax.psum_scatter(
        (contract_first(gate_act, w_gate) + contract_first(up_act, w_up)).astype(jnp.bfloat16),
        "dp",
        scatter_dimension=0,
        tiled=True,
    )
    back_out = contract_first(picker, expert_out).astype(jnp.bfloat16)
    back_in = contract_first(picker, expert_in).astype(jnp.bfloat16)
    got_out, got_in = (
        lax.all_to_all(back_out, "expert", split_axis=0, concat_axis=0, tiled=True),
        lax.all_to_all(back_in, "expert", split_axis=0, concat_axis=0, tiled=True),
    )
    expert_count = lax.axis_size("expert")
    got_out = got_out.reshape(expert_count, local_tokens, width)
    got_in = got_in.reshape(expert_count, local_tokens, width)
    expert_range = jnp.arange(expert_count, dtype=jnp.int32)
    own_match = expert_ids[:, :, None] == expert_range[None, None, :]
    mix_weight = jnp.sum(
        jnp.where(own_match, route_weights.astype(jnp.float32)[:, :, None], 0.0), axis=1
    )
    mixed_out = jnp.sum(jnp.transpose(mix_weight)[:, :, None] * got_out.astype(jnp.float32), axis=0)
    input_total = jnp.sum(got_in.astype(jnp.float32), axis=0)
    return (
        mixed_out.astype(jnp.bfloat16),
        input_total.astype(jnp.bfloat16),
        grad_gate[None],
        grad_up[None],
        grad_down[None],
    )


def solution(mesh):
    return jax.shard_map(
        shards,
        mesh=mesh,
        in_specs=(
            P(("dp", "expert"), None),
            P(("dp", "expert"), None),
            P(("dp", "expert"), None),
            P(("dp", "expert"), None),
            P("expert", "dp", None),
            P("expert", "dp", None),
            P("expert", "dp", None),
        ),
        out_specs=(
            P(("dp", "expert"), None),
            P(("dp", "expert"), None),
            P("expert", "dp", None),
            P("expert", "dp", None),
            P("expert", "dp", None),
        ),
        check_vma=False,
    )
```

profile of v0, /device:TPU:0, one launch (start us, length us, event | category | flops | bytes accessed | tf_op | source)
XLA Modules:
  0.0 253.1 jit_solution(5729147935112396989)
XLA Ops:
  7.2 6.9 %all-gather.1 = bf16[4,4,4096]{2,1,0:T(4,128)(2,1)S(1)} all-gather(bf16[1,4,4096]{2,1,0:T(4,128)(2,1)} %bitcast.57), channel_id=1, replica_groups=mesh['dp'=8,'expert'=4] {'expert'}, dimensions={0}, use_global_device_ids=true | all-gather | bytes 163840 | tf_op jit(solution)/shard_map/all_gather | solution.py:26
  14.1 5.5 %all-gather = s32[4,4,2]{1,2,0:T(2,128)S(1)} all-gather(s32[1,4,2]{1,2,0:T(2,128)} %bitcast.60), channel_id=1, replica_groups=mesh['dp'=8,'expert'=4] {'expert'}, dimensions={0}, use_global_device_ids=true | all-gather | bytes 160 | tf_op jit(solution)/shard_map/all_gather | solution.py:30
  19.9 0.8 convolution_convert_fusion.7
  20.8 5.2 %all-gather.2 = bf16[4,4,2]{1,2,0:T(2,128)(2,1)S(1)} all-gather(bf16[1,4,2]{1,2,0:T(2,128)(2,1)} %bitcast.61), channel_id=1, replica_groups=mesh['dp'=8,'expert'=4] {'expert'}, dimensions={0}, use_global_device_ids=true | all-gather | bytes 80 | tf_op jit(solution)/shard_map/all_gather | solution.py:28
  26.0 5.6 %all-gather.3 = bf16[4,4,4096]{2,1,0:T(4,128)(2,1)S(1)} all-gather(bf16[1,4,4096]{2,1,0:T(4,128)(2,1)} %bitcast.58), channel_id=1, replica_groups=mesh['dp'=8,'expert'=4] {'expert'}, dimensions={0}, use_global_device_ids=true | all-gather | bytes 163840 | tf_op jit(solution)/shard_map/all_gather | solution.py:27
  31.8 0.9 convolution_convert_fusion.5
  32.7 29.8 %all-gather.7.cloned.1.call-done = bf16[128,4096]{1,0:T(8,128)(2,1)} async-done(((bf16[16,4096]{1,0:T(8,128)(2,1)}), bf16[128,4096]{1,0:T(8,128)(2,1)}) %all-gather.7.cloned.1.call-update) | async-done | bytes 1048592 | tf_op jit(solution)/shard_map/all_gather | solution.py:43
  62.6 2.4 fusion.14
  64.9 2.0 fusion.17
  66.9 37.3 %all-gather.9.cloned.1.call-done = bf16[128,4096]{1,0:T(8,128)(2,1)} async-done(((bf16[16,4096]{1,0:T(8,128)(2,1)}), bf16[128,4096]{1,0:T(8,128)(2,1)}) %all-gather.9.cloned.1.call-update) | async-done | bytes 1048592 | tf_op jit(solution)/shard_map/all_gather | solution.py:52
  104.2 1.8 multiply_convert_fusion.2
  106.0 1.4 convolution_convert_fusion.3
  107.5 2.0 fusion.10
  109.5 1.5 fusion
  111.3 1.7 fusion.1
  113.0 1.7 fusion.2
  114.7 1.7 fusion.3
  116.4 53.6 %reduce-scatter.3.cloned.1.call-done = bf16[16,4096]{1,0:T(8,128)(2,1)} async-done(((bf16[128,4096]{1,0:T(8,128)(2,1)}), bf16[16,4096]{1,0:T(8,128)(2,1)}) %reduce-scatter.3.cloned.1.call-update) | async-done | bytes 131088 | tf_op jit(solution)/shard_map/reduce_scatter | solution.py:49
  169.9 1.1 convolution_convert_fusion.6
  171.8 3.3 %all-to-all-start = ((bf16[4,4,4096]{2,1,0:T(4,128)(2,1)}), bf16[4,4,4096]{2,1,0:T(4,128)(2,1)S(1)}, u32[]{:S(2)}, u32[]{:S(2)}) async-start(bf16[4,4,4096]{2,1,0:T(4,128)(2,1)} %all_to_all.12), calls=%async_computation.1 | async-start | bytes 262144 | tf_op jit(solution)/shard_map/all_to_all | solution.py:69
  175.1 60.9 %reduce-scatter.5.cloned.1.call-done = bf16[16,4096]{1,0:T(8,128)(2,1)} async-done(((bf16[128,4096]{1,0:T(8,128)(2,1)}), bf16[16,4096]{1,0:T(8,128)(2,1)}) %reduce-scatter.5.cloned.1.call-update) | async-done | bytes 131088 | tf_op jit(solution)/shard_map/reduce_scatter | solution.py:60
  236.1 1.1 convolution_convert_fusion.4
  237.9 3.3 %all-to-all-start.1 = ((bf16[4,4,4096]{2,1,0:T(4,128)(2,1)}), bf16[4,4,4096]{2,1,0:T(4,128)(2,1)S(1)}, u32[]{:S(2)}, u32[]{:S(2)}) async-start(bf16[4,4,4096]{2,1,0:T(4,128)(2,1)} %all_to_all.14), calls=%async_computation.3 | async-start | bytes 262144 | tf_op jit(solution)/shard_map/all_to_all | solution.py:70
  242.0 3.8 %all-to-all-done.1 = bf16[4,4,4096]{2,1,0:T(4,128)(2,1)S(1)} async-done(((bf16[4,4,4096]{2,1,0:T(4,128)(2,1)}), bf16[4,4,4096]{2,1,0:T(4,128)(2,1)S(1)}, u32[]{:S(2)}, u32[]{:S(2)}) %all-to-all-start.1) | async-done | bytes 131104 | tf_op jit(solution)/shard_map/all_to_all | solution.py:70
  (38 shorter events, 3.8 us)
Async XLA Ops:
  7.2 97.0 %copy-start = (bf16[1,192,4096]{2,1,0:T(8,128)(2,1)S(1)}, bf16[1,192,4096]{2,1,0:T(8,128)(2,1)}, u32[]{:S(2)}) copy-start(bf16[1,192,4096]{2,1,0:T(8,128)(2,1)} %param.13) | copy-start | bytes 4718596
  7.2 55.4 %all-gather.7.cloned.1.call-start = ((), (), s32[]{:S(2)}) async-start(), calls=%async_computation.4 | async-start | bytes 1179648 | tf_op jit(solution)/shard_map/all_gather | solution.py:43
  20.8 83.4 %all-gather.9.cloned.1.call-start = ((), (), s32[]{:S(2)}) async-start(), calls=%async_computation.6 | async-start | bytes 1179648 | tf_op jit(solution)/shard_map/all_gather | solution.py:52
  32.7 137.3 %reduce-scatter.3.cloned.1.call-start = ((), (), s32[]{:S(2)}) async-start(), calls=%async_computation.5 | async-start | bytes 1179648 | tf_op jit(solution)/shard_map/reduce_scatter | solution.py:49
  62.5 2.4 copy-start.1
  107.5 128.6 %reduce-scatter.5.cloned.1.call-start = ((), (), s32[]{:S(2)}) async-start(), calls=%async_computation.7 | async-start | bytes 1179648 | tf_op jit(solution)/shard_map/reduce_scatter | solution.py:60
  107.5 2.0 copy-start.2
  109.5 1.6 copy-start.5
  109.5 1.6 copy-start.4
  113.0 1.7 copy-start.3
  171.8 66.1 %all-to-all-start = ((bf16[4,4,4096]{2,1,0:T(4,128)(2,1)}), bf16[4,4,4096]{2,1,0:T(4,128)(2,1)S(1)}, u32[]{:S(2)}, u32[]{:S(2)}) async-start(bf16[4,4,4096]{2,1,0:T(4,128)(2,1)} %all_to_all.12), calls=%async_computation.1 | async-start | bytes 262144 | tf_op jit(solution)/shard_map/all_to_all | solution.py:69
  237.9 7.9 %all-to-all-start.1 = ((bf16[4,4,4096]{2,1,0:T(4,128)(2,1)}), bf16[4,4,4096]{2,1,0:T(4,128)(2,1)S(1)}, u32[]{:S(2)}, u32[]{:S(2)}) async-start(bf16[4,4,4096]{2,1,0:T(4,128)(2,1)} %all_to_all.14), calls=%async_computation.3 | async-start | bytes 262144 | tf_op jit(solution)/shard_map/all_to_all | solution.py:70
Sparse Core Ops, SparseCore 0:
  20.9 41.5 all-gather.6
  65.2 38.9 all-gather.8
  107.6 62.2 reduce-scatter.2
  173.6 62.4 reduce-scatter.4
where the time goes:
time: 254 us; the launch traced here: 253 us
  waiting for transfers between devices  185 us (73%)
  blocking collectives  23.1 us (9%)
  matrix products  20.2 us (8%)
  between operations  13.9 us (5%)
  starting transfers between devices  6.81 us (3%)
    reduce_scatter x1, waiting for transfers between devices, shards(): lax.psum_scatter((contract_first(gate_act, w_gate) + contract_first(up_ac...  60.9 us
    reduce_scatter x1, waiting for transfers between devices, shards(): lax.psum_scatter(contract_first(hidden, w_down).astype(jnp.bfloat16), 'dp...  53.6 us
    all_gather x1, waiting for transfers between devices, shards(): all_dy = lax.all_gather(slot_dy, 'dp', axis=0, tiled=True)  37.3 us
    all_gather x1, waiting for transfers between devices, shards(): all_x = lax.all_gather(slot_x, 'dp', axis=0, tiled=True)  29.8 us
    dot_general x5, matrix products, contract_first(): lax.dot_general(left, right, (((0,), (0,)), ((), ())), preferred_element_...  7.18 us
    all_gather x1, blocking collectives, shards(): lax.all_gather(tokens, 'expert', axis=0, tiled=True)  6.85 us
    dot_general x3, matrix products, contract_rows(): lax.dot_general(left, right, (((1,), (1,)), ((), ())), preferred_element_...  6.15 us
    all_gather x1, blocking collectives, shards(): lax.all_gather(out_grad, 'expert', axis=0, tiled=True)  5.62 us
  transfers between devices with their start and end apart: 6, of which 5 were waited for; matrix products, arithmetic and copies ran while one was open for 7% of the time, Pallas kernels for 0%

commit v1 on v0

--- a/solution.py
+++ b/solution.py
@@ -4,6 +4,7 @@
 from jax.sharding import PartitionSpec as P
 
 ROW_CAP = 16
+AXES = ("dp", "expert")
 
 
 def contract_rows(left, right):
@@ -18,7 +19,7 @@
     )
 
 
-def shards(tokens, expert_ids, route_weights, out_grad, gate_weight, up_weight, down_weight):
+def slotted(tokens, expert_ids, route_weights, out_grad, gate_weight, up_weight, down_weight):
     expert = lax.axis_index("expert")
     width = tokens.shape[1]
     local_tokens = tokens.shape[0]
@@ -88,6 +89,81 @@
     )
 
 
+def bit_stages(devices):
+    bits = devices.bit_length() - 1
+    stages, high = [], bits - 1
+    while high > 0:
+        low = max(high - 1, 1)
+        stages.append(tuple(k << low for k in range(1, 1 << (high - low + 1))))
+        high = low - 1
+    stages.append((1,))
+    return stages
+
+
+def from_xor(value, mask, devices):
+    return lax.ppermute(value, AXES, [(i, i ^ mask) for i in range(devices)])
+
+
+def route_columns(expert_ids, route_weights, experts):
+    named = expert_ids[:, :, None] == jnp.arange(experts, dtype=jnp.int32)[None, None, :]
+    return jnp.sum(jnp.where(named, route_weights.astype(jnp.float32)[:, :, None], 0.0), axis=1)
+
+
+def dense(tokens, expert_ids, route_weights, out_grad, gate_weight, up_weight, down_weight):
+    experts = lax.axis_size("expert")
+    devices = lax.axis_size("dp") * experts
+    expert = lax.axis_index("expert")
+    rows, width = tokens.shape
+    w_gate, w_up, w_down = gate_weight[0], up_weight[0], down_weight[0]
+    stages = bit_stages(devices)
+
+    route = route_columns(expert_ids, route_weights, experts).astype(jnp.bfloat16)
+    route = jnp.pad(route, ((0, 0), (0, -experts % 128)))
+    have = jnp.concatenate([tokens, out_grad, route], axis=1)
+    for masks in stages:
+        have = jnp.concatenate([have] + [from_xor(have, m, devices) for m in masks], axis=0)
+    all_x, all_dy, all_route = have[:, :width], have[:, width : 2 * width], have[:, 2 * width :]
+    mine = jnp.arange(all_route.shape[1]) == expert
+    weight = jnp.sum(jnp.where(mine[None, :], all_route.astype(jnp.float32), 0.0), axis=1)[:, None]
+
+    gate_pre = contract_rows(all_x, w_gate)
+    up_pre = contract_rows(all_x, w_up)
+    hidden_grad = weight * contract_rows(all_dy, w_down)
+    gate_sig = jax.nn.sigmoid(gate_pre)
+    silu_gate = gate_pre * gate_sig
+    hidden = (weight * (silu_gate * up_pre)).astype(jnp.bfloat16)
+    silu_slope = gate_sig * (1.0 + gate_pre * (1.0 - gate_sig))
+    gate_act = (hidden_grad * up_pre * silu_slope).astype(jnp.bfloat16)
+    up_act = (hidden_grad * silu_gate).astype(jnp.bfloat16)
+
+    out = jnp.dot(hidden, w_down, preferred_element_type=jnp.float32)
+    into = jnp.dot(gate_act, w_gate, preferred_element_type=jnp.float32) + jnp.dot(
+        up_act, w_up, preferred_element_type=jnp.float32
+    )
+    total = jnp.concatenate([out.astype(jnp.bfloat16), into.astype(jnp.bfloat16)], axis=1)
+    for masks in reversed(stages):
+        part = total.shape[0] // (len(masks) + 1)
+        pieces = [total[k * part : (k + 1) * part] for k in range(len(masks) + 1)]
+        summed = pieces[0].astype(jnp.float32)
+        for m, piece in zip(masks, pieces[1:]):
+            summed = summed + from_xor(piece, m, devices).astype(jnp.float32)
+        total = summed.astype(jnp.bfloat16)
+
+    grad_down = contract_first(hidden, all_dy).astype(jnp.bfloat16)
+    grad_gate = contract_first(gate_act, all_x).astype(jnp.bfloat16)
+    grad_up = contract_first(up_act, all_x).astype(jnp.bfloat16)
+    return total[:, :width], total[:, width:], grad_gate[None], grad_up[None], grad_down[None]
+
+
+def shards(tokens, *others):
+    experts = lax.axis_size("expert")
+    devices = lax.axis_size("dp") * experts
+    whole_group = tokens.shape[0] * experts <= ROW_CAP
+    if whole_group and devices & (devices - 1) == 0:
+        return dense(tokens, *others)
+    return slotted(tokens, *others)
+
+
 def solution(mesh):
     return jax.shard_map(
         shards,

time: 254 us -> 92 us (0.36)
  waiting for transfers between devices: 185 us -> 32.4 us
  blocking collectives: 23.1 us -> 0 us
  local copies, waits for them, and re-layouts: 1.85 us -> 24.8 us
  between operations: 13.9 us -> 0.8 us
  starting transfers between devices: 6.81 us -> 17.4 us
  matrix products: 20.2 us -> 10.9 us
  other arithmetic: 1.73 us -> 4.83 us
    reduce_scatter x2 -> x0, waiting for transfers between devices: 115 us -> none  [the longest x1 60.9 us: shards(): lax.psum_scatter((contract_first(gate_act, w_gate) + contract_first(up_ac...]
    all_gather x2 -> x0, waiting for transfers between devices: 67.1 us -> none  [the longest x1 37.3 us: shards(): all_dy = lax.all_gather(slot_dy, 'dp', axis=0, tiled=True)]
    ppermute x0 -> x14, waiting for transfers between devices: none -> 32.4 us  [from_xor(): return lax.ppermute(value, AXES, [(i, i ^ mask) for i in range(devices)])]
    all_gather x4 -> x0, blocking collectives: 23.1 us -> none  [the longest x1 6.85 us: shards(): lax.all_gather(tokens, 'expert', axis=0, tiled=True)]
    concatenate x0 -> x2, local copies, waits for them, and re-layouts: none -> 23 us  [dense(): jnp.concatenate([have] + [from_xor(have, m, devices) for m in masks], axi...]
    ppermute x0 -> x14, starting transfers between devices: none -> 17.4 us  [from_xor(): return lax.ppermute(value, AXES, [(i, i ^ mask) for i in range(devices)])]
    all_to_all x2 -> x0, starting transfers between devices: 6.65 us -> none  [the longest x1 3.32 us: shards(): lax.all_to_all(back_in, 'expert', split_axis=0, concat_axis=0, tiled=True)]
    dot_general x5 -> x3, matrix products: 6.83 us -> 1.44 us  [the longest x1 0.49 us: dense(): jnp.dot(up_act, w_up, preferred_element_type=jnp.float32)]
  transfers between devices with their start and end apart: 6 -> 14, of which waited for: 5 -> 11; matrix products, arithmetic and copies ran while one was open for 7% -> 6% of each run, Pallas kernels for 0% -> 0%
where the time goes in v1:
time: 92 us; the launch traced here: 91.1 us
  waiting for transfers between devices  32.4 us (35%)
  local copies, waits for them, and re-layouts  24.8 us (27%)
  starting transfers between devices  17.4 us (19%)
  matrix products  10.9 us (12%)
  other arithmetic  4.83 us (5%)
    ppermute x14, waiting for transfers between devices, from_xor(): return lax.ppermute(value, AXES, [(i, i ^ mask) for i in range(devices)])  32.4 us
    concatenate x2, local copies, waits for them, and re-layouts, dense(): jnp.concatenate([have] + [from_xor(have, m, devices) for m in masks], axi...  23 us
    ppermute x14, starting transfers between devices, from_xor(): return lax.ppermute(value, AXES, [(i, i ^ mask) for i in range(devices)])  17.4 us
    dot_general x3, matrix products, contract_first(): lax.dot_general(left, right, (((0,), (0,)), ((), ())), preferred_element_...  5.09 us
    dot_general x3, matrix products, contract_rows(): lax.dot_general(left, right, (((1,), (1,)), ((), ())), preferred_element_...  4.37 us
  transfers between devices with their start and end apart: 14, of which 11 were waited for; matrix products, arithmetic and copies ran while one was open for 6% of the time, Pallas kernels for 0%

profile of v1, /device:TPU:0, one launch (start us, length us, event | category | flops | bytes accessed | tf_op | source)
XLA Modules:
  0.0 91.1 jit_solution(1832287430957160434)
XLA Ops:
  3.0 3.1 %collective-permute-start = (bf16[4,8320]{1,0:T(4,128)(2,1)S(1)}, bf16[4,8320]{1,0:T(4,128)(2,1)S(1)}, u32[]{:S(2)}, u32[]{:S(2)}) collective-permute-start(bf16[4,8320]{1,0:T(4,128)(2,1)S(1)} %pad_maximum_fusion.2), channel_id=1, source_target_pairs={{0,8},{1,9},{2,10},{3,11},{4,12},{5,13},{6,14},{7,15},{8,0},{9,1},... | collective-permute-start | bytes 199688 | tf_op jit(solution)/shard_map/ppermute | solution.py:104
  6.1 2.6 %collective-permute-start.1 = (bf16[4,8320]{1,0:T(4,128)(2,1)S(1)}, bf16[4,8320]{1,0:T(4,128)(2,1)S(1)}, u32[]{:S(2)}, u32[]{:S(2)}) collective-permute-start(bf16[4,8320]{1,0:T(4,128)(2,1)S(1)} %pad_maximum_fusion.2), channel_id=1, source_target_pairs={{0,16},{1,17},{2,18},{3,19},{4,20},{5,21},{6,22},{7,23},{8,24},{9,... | collective-permute-start | bytes 199688 | tf_op jit(solution)/shard_map/ppermute | solution.py:104
  8.7 4.7 %collective-permute-done.1 = bf16[4,8320]{1,0:T(4,128)(2,1)S(1)} collective-permute-done((bf16[4,8320]{1,0:T(4,128)(2,1)S(1)}, bf16[4,8320]{1,0:T(4,128)(2,1)S(1)}, u32[]{:S(2)}, u32[]{:S(2)}) %collective-permute-start.1) | collective-permute-done | bytes 66592 | tf_op jit(solution)/shard_map/ppermute | solution.py:104
  13.4 1.4 %collective-permute-done.2 = bf16[4,8320]{1,0:T(4,128)(2,1)S(1)} collective-permute-done((bf16[4,8320]{1,0:T(4,128)(2,1)S(1)}, bf16[4,8320]{1,0:T(4,128)(2,1)S(1)}, u32[]{:S(2)}, u32[]{:S(2)}) %collective-permute-start.2) | collective-permute-done | bytes 66592 | tf_op jit(solution)/shard_map/ppermute | solution.py:104
  15.8 1.6 %collective-permute-start.3 = (bf16[16,8320]{1,0:T(8,128)(2,1)S(1)}, bf16[16,8320]{1,0:T(8,128)(2,1)S(1)}, u32[]{:S(2)}, u32[]{:S(2)}) collective-permute-start(bf16[16,8320]{1,0:T(8,128)(2,1)S(1)} %pad_maximum_fusion.1), channel_id=1, source_target_pairs={{0,2},{1,3},{2,0},{3,1},{4,6},{5,7},{6,4},{7,5},{8,10},{9,11},{10,... | collective-permute-start | bytes 798728 | tf_op jit(solution)/shard_map/ppermute | solution.py:104
  17.4 1.5 %collective-permute-start.4 = (bf16[16,8320]{1,0:T(8,128)(2,1)S(1)}, bf16[16,8320]{1,0:T(8,128)(2,1)S(1)}, u32[]{:S(2)}, u32[]{:S(2)}) collective-permute-start(bf16[16,8320]{1,0:T(8,128)(2,1)S(1)} %pad_maximum_fusion.1), channel_id=1, source_target_pairs={{0,4},{1,5},{2,6},{3,7},{4,0},{5,1},{6,2},{7,3},{8,12},{9,13},{10,... | collective-permute-start | bytes 798728 | tf_op jit(solution)/shard_map/ppermute | solution.py:104
  19.4 4.9 %collective-permute-done.3 = bf16[16,8320]{1,0:T(8,128)(2,1)S(1)} collective-permute-done((bf16[16,8320]{1,0:T(8,128)(2,1)S(1)}, bf16[16,8320]{1,0:T(8,128)(2,1)S(1)}, u32[]{:S(2)}, u32[]{:S(2)}) %collective-permute-start.3) | collective-permute-done | bytes 266272 | tf_op jit(solution)/shard_map/ppermute | solution.py:104
  24.3 2.1 %collective-permute-done.4 = bf16[16,8320]{1,0:T(8,128)(2,1)S(1)} collective-permute-done((bf16[16,8320]{1,0:T(8,128)(2,1)S(1)}, bf16[16,8320]{1,0:T(8,128)(2,1)S(1)}, u32[]{:S(2)}, u32[]{:S(2)}) %collective-permute-start.4) | collective-permute-done | bytes 266272 | tf_op jit(solution)/shard_map/ppermute | solution.py:104
  26.4 2.8 %collective-permute-done.5 = bf16[16,8320]{1,0:T(8,128)(2,1)S(1)} collective-permute-done((bf16[16,8320]{1,0:T(8,128)(2,1)S(1)}, bf16[16,8320]{1,0:T(8,128)(2,1)S(1)}, u32[]{:S(2)}, u32[]{:S(2)}) %collective-permute-start.5) | collective-permute-done | bytes 266272 | tf_op jit(solution)/shard_map/ppermute | solution.py:104
  29.2 6.7 %concatenate.19 = bf16[64,8320]{1,0:T(8,128)(2,1)} concatenate(bf16[4,8320]{1,0:T(4,128)(2,1)S(1)} %pad_maximum_fusion.2, bf16[4,8320]{1,0:T(4,128)(2,1)S(1)} %collective-permute-done, bf16[4,8320]{1,0:T(4,128)(2,1)S(1)} %collective-permute-done.1, bf16[4,8320]{1,0:T(4,128)(2,1)S(1)} %collective-permute-done.2, bf16[16,8320]{1,0:T(8,128)(2,1)S(1)} %collective-permute-done.3, ...), dimensions={0} | concatenate | bytes 2129920 | tf_op jit(solution)/shard_map/concatenate | solution.py:124
  36.0 3.0 %collective-permute-done.6 = bf16[64,8320]{1,0:T(8,128)(2,1)} collective-permute-done((bf16[64,8320]{1,0:T(8,128)(2,1)}, bf16[64,8320]{1,0:T(8,128)(2,1)}, u32[]{:S(2)}, u32[]{:S(2)}) %collective-permute-start.6) | collective-permute-done | bytes 1064992 | tf_op jit(solution)/shard_map/ppermute | solution.py:104
  39.0 16.3 %concatenate.20 = bf16[128,8320]{1,0:T(8,128)(2,1)} concatenate(bf16[4,8320]{1,0:T(4,128)(2,1)S(1)} %pad_maximum_fusion.2, bf16[4,8320]{1,0:T(4,128)(2,1)S(1)} %collective-permute-done, bf16[4,8320]{1,0:T(4,128)(2,1)} %copy-done.6, bf16[4,8320]{1,0:T(4,128)(2,1)} %copy-done.7, bf16[16,8320]{1,0:T(8,128)(2,1)S(1)} %collective-permute-done.3, bf16[16,8320]{1,0:T(8,128)(2,1)} %copy-done.4, ...), dimensions={0} | concatenate | bytes 4259840 | tf_op jit(solution)/shard_map/concatenate | solution.py:124
  56.3 1.8 %fusion.12 = f32[128,192]{0,1:T(8,128)S(1)} fusion(bf16[1,192,4096]{2,1,0:T(8,128)(2,1)S(1)} %copy-done.2, bf16[128,8320]{1,0:T(8,128)(2,1)} %concatenate.20), kind=kOutput, calls=%fused_computation.20 | convolution fusion | flops 201326592 | bytes 2719744 | tf_op jit(solution)/shard_map/dot_general | solution.py:11
  58.1 2.0 %fusion.14 = f32[128,192]{0,1:T(8,128)S(1)} fusion(bf16[1,192,4096]{2,1,0:T(8,128)(2,1)} %param.13, bf16[128,8320]{1,0:T(8,128)(2,1)S(1)} %copy-done.1, f32[128]{0:T(128)S(1)} %select_reduce_fusion), kind=kOutput, calls=%fused_computation.22 | convolution fusion | flops 201351168 | bytes 2720256 | tf_op jit(solution)/shard_map/dot_general | solution.py:11
  63.3 2.6 %collective-permute-done.7 = bf16[64,8192]{1,0:T(8,128)(2,1)S(1)} collective-permute-done((bf16[64,8192]{1,0:T(8,128)(2,1)S(1)}, bf16[64,8192]{1,0:T(8,128)(2,1)S(1)}, u32[]{:S(2)}, u32[]{:S(2)}) %collective-permute-start.7) | collective-permute-done | bytes 1048608 | tf_op jit(solution)/shard_map/ppermute | solution.py:104
  66.2 2.6 %collective-permute-start.10 = (bf16[16,8192]{1,0:T(8,128)(2,1)S(1)}, bf16[16,8192]{1,0:T(8,128)(2,1)S(1)}, u32[]{:S(2)}, u32[]{:S(2)}) collective-permute-start(bf16[16,8192]{1,0:T(8,128)(2,1)S(1)} %get-tuple-element.6), channel_id=1, source_target_pairs={{0,6},{1,7},{2,4},{3,5},{4,2},{5,3},{6,0},{7,1},{8,14},{9,15},{10,... | collective-permute-start | bytes 786440 | tf_op jit(solution)/shard_map/ppermute | solution.py:104
  69.7 1.7 %fusion.1 = bf16[1,192,4096]{2,1,0:T(8,128)(2,1)} fusion(bf16[128,192]{0,1:T(8,128)(2,1)S(1)} %get-tuple-element.12, bf16[128,8320]{1,0:T(8,128)(2,1)S(1)} %copy-done.1), kind=kOutput, calls=%fused_computation.6 | convolution fusion | flops 202113024 | bytes 2670592 | tf_op jit(solution)/shard_map/dot_general | solution.py:17
  71.4 1.7 %fusion.2 = bf16[1,192,4096]{2,1,0:T(8,128)(2,1)} fusion(bf16[128,192]{0,1:T(8,128)(2,1)S(1)} %get-tuple-element.13, bf16[128,8320]{1,0:T(8,128)(2,1)S(1)} %copy-done.1), kind=kOutput, calls=%fused_computation.7 | convolution fusion | flops 202113024 | bytes 2670592 | tf_op jit(solution)/shard_map/dot_general | solution.py:17
  73.1 3.2 %collective-permute-done.10 = bf16[16,8192]{1,0:T(8,128)(2,1)S(1)} collective-permute-done((bf16[16,8192]{1,0:T(8,128)(2,1)S(1)}, bf16[16,8192]{1,0:T(8,128)(2,1)S(1)}, u32[]{:S(2)}, u32[]{:S(2)}) %collective-permute-start.10) | collective-permute-done | bytes 262176 | tf_op jit(solution)/shard_map/ppermute | solution.py:104
  76.3 4.8 %collective-permute-done.8 = bf16[16,8192]{1,0:T(8,128)(2,1)S(1)} collective-permute-done((bf16[16,8192]{1,0:T(8,128)(2,1)S(1)}, bf16[16,8192]{1,0:T(8,128)(2,1)S(1)}, u32[]{:S(2)}, u32[]{:S(2)}) %collective-permute-start.8) | collective-permute-done | bytes 262176 | tf_op jit(solution)/shard_map/ppermute | solution.py:104
  82.2 1.5 %collective-permute-start.12 = (bf16[4,8192]{1,0:T(4,128)(2,1)S(1)}, bf16[4,8192]{1,0:T(4,128)(2,1)S(1)}, u32[]{:S(2)}, u32[]{:S(2)}) collective-permute-start(bf16[4,8192]{1,0:T(4,128)(2,1)S(1)} %get-tuple-element.10), channel_id=1, source_target_pairs={{0,16},{1,17},{2,18},{3,19},{4,20},{5,21},{6,22},{7,23},{8,24},{9,... | collective-permute-start | bytes 196616 | tf_op jit(solution)/shard_map/ppermute | solution.py:104
  83.7 2.3 %collective-permute-start.13 = (bf16[4,8192]{1,0:T(4,128)(2,1)S(1)}, bf16[4,8192]{1,0:T(4,128)(2,1)S(1)}, u32[]{:S(2)}, u32[]{:S(2)}) collective-permute-start(bf16[4,8192]{1,0:T(4,128)(2,1)S(1)} %get-tuple-element.9), channel_id=1, source_target_pairs={{0,24},{1,25},{2,26},{3,27},{4,28},{5,29},{6,30},{7,31},{8,16},{9,... | collective-permute-start | bytes 196616 | tf_op jit(solution)/shard_map/ppermute | solution.py:104
  85.9 1.7 %fusion.3 = bf16[1,192,4096]{2,1,0:T(8,128)(2,1)} fusion(bf16[128,192]{0,1:T(8,128)(2,1)S(1)} %get-tuple-element.11, bf16[128,8320]{1,0:T(8,128)(2,1)S(1)} %copy-done.1), kind=kOutput, calls=%fused_computation.8 | convolution fusion | flops 202113024 | bytes 2670592 | tf_op jit(solution)/shard_map/dot_general | solution.py:17
  87.6 2.7 %collective-permute-done.12 = bf16[4,8192]{1,0:T(4,128)(2,1)S(1)} collective-permute-done((bf16[4,8192]{1,0:T(4,128)(2,1)S(1)}, bf16[4,8192]{1,0:T(4,128)(2,1)S(1)}, u32[]{:S(2)}, u32[]{:S(2)}) %collective-permute-start.12) | collective-permute-done | bytes 65568 | tf_op jit(solution)/shard_map/ppermute | solution.py:104
  (45 shorter events, 11.2 us)
Async XLA Ops:
  0.6 59.4 %copy-start = (bf16[1,192,4096]{2,1,0:T(8,128)(2,1)S(1)}, bf16[1,192,4096]{2,1,0:T(8,128)(2,1)}, u32[]{:S(2)}) copy-start(bf16[1,192,4096]{2,1,0:T(8,128)(2,1)} %param.12) | copy-start | bytes 4718596
  3.0 5.7 %collective-permute-start = (bf16[4,8320]{1,0:T(4,128)(2,1)S(1)}, bf16[4,8320]{1,0:T(4,128)(2,1)S(1)}, u32[]{:S(2)}, u32[]{:S(2)}) collective-permute-start(bf16[4,8320]{1,0:T(4,128)(2,1)S(1)} %pad_maximum_fusion.2), channel_id=1, source_target_pairs={{0,8},{1,9},{2,10},{3,11},{4,12},{5,13},{6,14},{7,15},{8,0},{9,1},... | collective-permute-start | bytes 199688 | tf_op jit(solution)/shard_map/ppermute | solution.py:104
  6.1 7.3 %collective-permute-start.1 = (bf16[4,8320]{1,0:T(4,128)(2,1)S(1)}, bf16[4,8320]{1,0:T(4,128)(2,1)S(1)}, u32[]{:S(2)}, u32[]{:S(2)}) collective-permute-start(bf16[4,8320]{1,0:T(4,128)(2,1)S(1)} %pad_maximum_fusion.2), channel_id=1, source_target_pairs={{0,16},{1,17},{2,18},{3,19},{4,20},{5,21},{6,22},{7,23},{8,24},{9,... | collective-permute-start | bytes 199688 | tf_op jit(solution)/shard_map/ppermute | solution.py:104
  8.7 6.2 %collective-permute-start.2 = (bf16[4,8320]{1,0:T(4,128)(2,1)S(1)}, bf16[4,8320]{1,0:T(4,128)(2,1)S(1)}, u32[]{:S(2)}, u32[]{:S(2)}) collective-permute-start(bf16[4,8320]{1,0:T(4,128)(2,1)S(1)} %pad_maximum_fusion.2), channel_id=1, source_target_pairs={{0,24},{1,25},{2,26},{3,27},{4,28},{5,29},{6,30},{7,31},{8,16},{9,... | collective-permute-start | bytes 199688 | tf_op jit(solution)/shard_map/ppermute | solution.py:104
  13.4 22.5 %copy-start.6 = (bf16[4,8320]{1,0:T(4,128)(2,1)}, bf16[4,8320]{1,0:T(4,128)(2,1)S(1)}, u32[]{:S(2)}) copy-start(bf16[4,8320]{1,0:T(4,128)(2,1)S(1)} %collective-permute-done.1) | copy-start | bytes 199684
  14.8 21.1 %copy-start.7 = (bf16[4,8320]{1,0:T(4,128)(2,1)}, bf16[4,8320]{1,0:T(4,128)(2,1)S(1)}, u32[]{:S(2)}) copy-start(bf16[4,8320]{1,0:T(4,128)(2,1)S(1)} %collective-permute-done.2) | copy-start | bytes 199684
  15.8 8.5 %collective-permute-start.3 = (bf16[16,8320]{1,0:T(8,128)(2,1)S(1)}, bf16[16,8320]{1,0:T(8,128)(2,1)S(1)}, u32[]{:S(2)}, u32[]{:S(2)}) collective-permute-start(bf16[16,8320]{1,0:T(8,128)(2,1)S(1)} %pad_maximum_fusion.1), channel_id=1, source_target_pairs={{0,2},{1,3},{2,0},{3,1},{4,6},{5,7},{6,4},{7,5},{8,10},{9,11},{10,... | collective-permute-start | bytes 798728 | tf_op jit(solution)/shard_map/ppermute | solution.py:104
  17.4 9.0 %collective-permute-start.4 = (bf16[16,8320]{1,0:T(8,128)(2,1)S(1)}, bf16[16,8320]{1,0:T(8,128)(2,1)S(1)}, u32[]{:S(2)}, u32[]{:S(2)}) collective-permute-start(bf16[16,8320]{1,0:T(8,128)(2,1)S(1)} %pad_maximum_fusion.1), channel_id=1, source_target_pairs={{0,4},{1,5},{2,6},{3,7},{4,0},{5,1},{6,2},{7,3},{8,12},{9,13},{10,... | collective-permute-start | bytes 798728 | tf_op jit(solution)/shard_map/ppermute | solution.py:104
  18.9 10.3 %collective-permute-start.5 = (bf16[16,8320]{1,0:T(8,128)(2,1)S(1)}, bf16[16,8320]{1,0:T(8,128)(2,1)S(1)}, u32[]{:S(2)}, u32[]{:S(2)}) collective-permute-start(bf16[16,8320]{1,0:T(8,128)(2,1)S(1)} %pad_maximum_fusion.1), channel_id=1, source_target_pairs={{0,6},{1,7},{2,4},{3,5},{4,2},{5,3},{6,0},{7,1},{8,14},{9,15},{10,... | collective-permute-start | bytes 798728 | tf_op jit(solution)/shard_map/ppermute | solution.py:104
  26.4 9.5 %copy-start.4 = (bf16[16,8320]{1,0:T(8,128)(2,1)}, bf16[16,8320]{1,0:T(8,128)(2,1)S(1)}, u32[]{:S(2)}) copy-start(bf16[16,8320]{1,0:T(8,128)(2,1)S(1)} %collective-permute-done.4) | copy-start | bytes 798724
  29.2 6.8 %copy-start.5 = (bf16[16,8320]{1,0:T(8,128)(2,1)}, bf16[16,8320]{1,0:T(8,128)(2,1)S(1)}, u32[]{:S(2)}) copy-start(bf16[16,8320]{1,0:T(8,128)(2,1)S(1)} %collective-permute-done.5) | copy-start | bytes 798724
  35.9 3.0 %collective-permute-start.6 = (bf16[64,8320]{1,0:T(8,128)(2,1)}, bf16[64,8320]{1,0:T(8,128)(2,1)}, u32[]{:S(2)}, u32[]{:S(2)}) collective-permute-start(bf16[64,8320]{1,0:T(8,128)(2,1)} %concatenate.19), channel_id=1, source_target_pairs={{0,1},{1,0},{2,3},{3,2},{4,5},{5,4},{6,7},{7,6},{8,9},{9,8},{10,11... | collective-permute-start | bytes 3194888 | tf_op jit(solution)/shard_map/ppermute | solution.py:104
  36.0 20.3 %copy-start.2 = (bf16[1,192,4096]{2,1,0:T(8,128)(2,1)S(1)}, bf16[1,192,4096]{2,1,0:T(8,128)(2,1)}, u32[]{:S(2)}) copy-start(bf16[1,192,4096]{2,1,0:T(8,128)(2,1)} %param.11) | copy-start | bytes 4718596
  55.2 2.8 %copy-start.1 = (bf16[128,8320]{1,0:T(8,128)(2,1)S(1)}, bf16[128,8320]{1,0:T(8,128)(2,1)}, u32[]{:S(2)}) copy-start(bf16[128,8320]{1,0:T(8,128)(2,1)} %concatenate.20) | copy-start | bytes 6389764
  60.7 1.4 %copy-start.3 = (bf16[1,192,4096]{2,1,0:T(8,128)(2,1)S(1)}, bf16[1,192,4096]{2,1,0:T(8,128)(2,1)}, u32[]{:S(2)}) copy-start(bf16[1,192,4096]{2,1,0:T(8,128)(2,1)} %param.13) | copy-start | bytes 4718596
  63.1 2.7 %collective-permute-start.7 = (bf16[64,8192]{1,0:T(8,128)(2,1)S(1)}, bf16[64,8192]{1,0:T(8,128)(2,1)S(1)}, u32[]{:S(2)}, u32[]{:S(2)}) collective-permute-start(bf16[64,8192]{1,0:T(8,128)(2,1)S(1)} %pad_maximum_fusion), channel_id=1, source_target_pairs={{0,1},{1,0},{2,3},{3,2},{4,5},{5,4},{6,7},{7,6},{8,9},{9,8},{10,11... | collective-permute-start | bytes 3145736 | tf_op jit(solution)/shard_map/ppermute | solution.py:104
  66.2 10.2 %collective-permute-start.10 = (bf16[16,8192]{1,0:T(8,128)(2,1)S(1)}, bf16[16,8192]{1,0:T(8,128)(2,1)S(1)}, u32[]{:S(2)}, u32[]{:S(2)}) collective-permute-start(bf16[16,8192]{1,0:T(8,128)(2,1)S(1)} %get-tuple-element.6), channel_id=1, source_target_pairs={{0,6},{1,7},{2,4},{3,5},{4,2},{5,3},{6,0},{7,1},{8,14},{9,15},{10,... | collective-permute-start | bytes 786440 | tf_op jit(solution)/shard_map/ppermute | solution.py:104
  68.7 12.4 %collective-permute-start.8 = (bf16[16,8192]{1,0:T(8,128)(2,1)S(1)}, bf16[16,8192]{1,0:T(8,128)(2,1)S(1)}, u32[]{:S(2)}, u32[]{:S(2)}) collective-permute-start(bf16[16,8192]{1,0:T(8,128)(2,1)S(1)} %get-tuple-element.5), channel_id=1, source_target_pairs={{0,2},{1,3},{2,0},{3,1},{4,6},{5,7},{6,4},{7,5},{8,10},{9,11},{10,... | collective-permute-start | bytes 786440 | tf_op jit(solution)/shard_map/ppermute | solution.py:104
  69.2 12.0 %collective-permute-start.9 = (bf16[16,8192]{1,0:T(8,128)(2,1)S(1)}, bf16[16,8192]{1,0:T(8,128)(2,1)S(1)}, u32[]{:S(2)}, u32[]{:S(2)}) collective-permute-start(bf16[16,8192]{1,0:T(8,128)(2,1)S(1)} %get-tuple-element.7), channel_id=1, source_target_pairs={{0,4},{1,5},{2,6},{3,7},{4,0},{5,1},{6,2},{7,3},{8,12},{9,13},{10,... | collective-permute-start | bytes 786440 | tf_op jit(solution)/shard_map/ppermute | solution.py:104
  81.5 6.2 %collective-permute-start.11 = (bf16[4,8192]{1,0:T(4,128)(2,1)S(1)}, bf16[4,8192]{1,0:T(4,128)(2,1)S(1)}, u32[]{:S(2)}, u32[]{:S(2)}) collective-permute-start(bf16[4,8192]{1,0:T(4,128)(2,1)S(1)} %get-tuple-element.8), channel_id=1, source_target_pairs={{0,8},{1,9},{2,10},{3,11},{4,12},{5,13},{6,14},{7,15},{8,0},{9,1},... | collective-permute-start | bytes 196616 | tf_op jit(solution)/shard_map/ppermute | solution.py:104
  82.2 8.1 %collective-permute-start.12 = (bf16[4,8192]{1,0:T(4,128)(2,1)S(1)}, bf16[4,8192]{1,0:T(4,128)(2,1)S(1)}, u32[]{:S(2)}, u32[]{:S(2)}) collective-permute-start(bf16[4,8192]{1,0:T(4,128)(2,1)S(1)} %get-tuple-element.10), channel_id=1, source_target_pairs={{0,16},{1,17},{2,18},{3,19},{4,20},{5,21},{6,22},{7,23},{8,24},{9,... | collective-permute-start | bytes 196616 | tf_op jit(solution)/shard_map/ppermute | solution.py:104
  83.7 6.7 %collective-permute-start.13 = (bf16[4,8192]{1,0:T(4,128)(2,1)S(1)}, bf16[4,8192]{1,0:T(4,128)(2,1)S(1)}, u32[]{:S(2)}, u32[]{:S(2)}) collective-permute-start(bf16[4,8192]{1,0:T(4,128)(2,1)S(1)} %get-tuple-element.9), channel_id=1, source_target_pairs={{0,24},{1,25},{2,26},{3,27},{4,28},{5,29},{6,30},{7,31},{8,16},{9,... | collective-permute-start | bytes 196616 | tf_op jit(solution)/shard_map/ppermute | solution.py:104

commit v2 on v0

--- a/solution.py
+++ b/solution.py
@@ -1,9 +1,14 @@
+import functools
+
 import jax
 import jax.numpy as jnp
 from jax import lax
+from jax.experimental import pallas as pl
+from jax.experimental.pallas import tpu as pltpu
 from jax.sharding import PartitionSpec as P
 
 ROW_CAP = 16
+AXES = ("dp", "expert")
 
 
 def contract_rows(left, right):
@@ -18,7 +23,7 @@
     )
 
 
-def shards(tokens, expert_ids, route_weights, out_grad, gate_weight, up_weight, down_weight):
+def slotted(tokens, expert_ids, route_weights, out_grad, gate_weight, up_weight, down_weight):
     expert = lax.axis_index("expert")
     width = tokens.shape[1]
     local_tokens = tokens.shape[0]
@@ -88,6 +93,213 @@
     )
 
 
+def split_masks(devices):
+    far = tuple(k << 1 for k in range(1, 4))
+    near = tuple(k << 3 for k in range(1, devices >> 3))
+    return near, far
+
+
+def from_xor(value, mask, devices):
+    return lax.ppermute(value, AXES, [(i, i ^ mask) for i in range(devices)])
+
+
+def kernel_call(body, out_shape, scratch, cost, *operands):
+    vmem, smem = pl.BlockSpec(memory_space=pltpu.VMEM), pl.BlockSpec(memory_space=pltpu.SMEM)
+    specs = [smem if o.ndim == 1 else vmem for o in operands]
+    return pl.pallas_call(
+        body,
+        out_shape=out_shape,
+        in_specs=specs,
+        out_specs=jax.tree.map(lambda _: vmem, out_shape),
+        scratch_shapes=scratch,
+        compiler_params=pltpu.CompilerParams(vmem_limit_bytes=24 << 20),
+        cost_estimate=pl.CostEstimate(flops=cost, bytes_accessed=4 << 20, transcendentals=0),
+    )(*operands)
+
+
+def pack_body(x_ref, dy_ref, ids_ref, w_ref, msg_ref):
+    rows, width = x_ref.shape
+    top = ids_ref.shape[0]
+    lanes = msg_ref.shape[1] - 2 * width
+    msg_ref[:, :width] = x_ref[...]
+    msg_ref[:, width : 2 * width] = dy_ref[...]
+    diagonal = lax.broadcasted_iota(jnp.int32, (rows, rows), 0) == lax.broadcasted_iota(
+        jnp.int32, (rows, rows), 1
+    )
+    expert = lax.broadcasted_iota(jnp.int32, (rows, lanes), 1)
+    route = jnp.zeros((rows, lanes), jnp.float32)
+    for k in range(top):
+        named = jnp.sum(jnp.where(diagonal, ids_ref[k : k + 1, :], 0), axis=1, keepdims=True)
+        weight = jnp.sum(jnp.where(diagonal, w_ref[k : k + 1, :], 0.0), axis=1, keepdims=True)
+        route = route + jnp.where(expert == named, weight, 0.0)
+    msg_ref[:, 2 * width :] = route.astype(jnp.bfloat16)
+
+
+def gathered(pieces, into):
+    rows = pieces[0].shape[0]
+    for i, piece in enumerate(pieces):
+        into[i * rows : (i + 1) * rows, :] = piece[...]
+
+
+def projections(x, dy, wg_ref, wu_ref, wd_ref):
+    return (
+        contract_rows(x, wg_ref[0]),
+        contract_rows(x, wu_ref[0]),
+        contract_rows(dy, wd_ref[0]),
+    )
+
+
+def pre_body(count, width, *refs):
+    pieces, (wg_ref, wu_ref, wd_ref, pre_ref, have) = refs[:count], refs[count:]
+    gathered(pieces, have)
+    ff = wg_ref.shape[1]
+    pre = projections(have[:, :width], have[:, width : 2 * width], wg_ref, wu_ref, wd_ref)
+    for i, value in enumerate(pre):
+        pre_ref[:, i * ff : (i + 1) * ff] = value
+
+
+def activations(pre, route, expert):
+    gate_pre, up_pre, hidden_grad = pre
+    lane = lax.broadcasted_iota(jnp.int32, route.shape, 1)
+    weight = jnp.sum(jnp.where(lane == expert, route.astype(jnp.float32), 0.0), axis=1, keepdims=True)
+    hidden_grad = weight * hidden_grad
+    gate_sig = 1.0 / (1.0 + jnp.exp(-gate_pre))
+    silu_gate = gate_pre * gate_sig
+    hidden = weight * (silu_gate * up_pre)
+    silu_slope = gate_sig * (1.0 + gate_pre * (1.0 - gate_sig))
+    gate_act = hidden_grad * up_pre * silu_slope
+    up_act = hidden_grad * silu_gate
+    return [v.astype(jnp.bfloat16) for v in (gate_act, up_act, hidden)]
+
+
+def outputs(acts, wg_ref, wu_ref, wd_ref):
+    gate_act, up_act, hidden = acts
+    out = jnp.dot(hidden, wd_ref[0], preferred_element_type=jnp.float32)
+    into = jnp.dot(gate_act, wg_ref[0], preferred_element_type=jnp.float32) + jnp.dot(
+        up_act, wu_ref[0], preferred_element_type=jnp.float32
+    )
+    return out, into
+
+
+def act_body(count, width, *refs):
+    own, other = refs[:count], refs[count : 2 * count]
+    pre_ref, wg_ref, wu_ref, wd_ref, expert_ref, acts_ref, msg_ref, have = refs[2 * count :]
+    half, ff, expert = have.shape[0], wg_ref.shape[1], expert_ref[0]
+    gathered(other, have)
+    pre = projections(have[:, :width], have[:, width : 2 * width], wg_ref, wu_ref, wd_ref)
+    acts = activations(pre, have[:, 2 * width :], expert)
+    for i, value in enumerate(acts):
+        acts_ref[half:, i * ff : (i + 1) * ff] = value
+    out, into = outputs(acts, wg_ref, wu_ref, wd_ref)
+    msg_ref[:, :width] = out.astype(jnp.bfloat16)
+    msg_ref[:, width:] = into.astype(jnp.bfloat16)
+    route = jnp.concatenate([piece[:, 2 * width :] for piece in own], axis=0)
+    pre = [pre_ref[:, i * ff : (i + 1) * ff] for i in range(3)]
+    for i, value in enumerate(activations(pre, route, expert)):
+        acts_ref[:half, i * ff : (i + 1) * ff] = value
+
+
+def own_body(acts_ref, wg_ref, wu_ref, wd_ref, own_ref):
+    half, ff = own_ref.shape[0], wg_ref.shape[1]
+    width = own_ref.shape[1] // 2
+    acts = [acts_ref[:half, i * ff : (i + 1) * ff] for i in range(3)]
+    out, into = outputs(acts, wg_ref, wu_ref, wd_ref)
+    own_ref[:, :width] = out
+    own_ref[:, width:] = into
+
+
+def grad_body(count, width, *refs):
+    pieces, (acts_ref, gg_ref, gu_ref, gd_ref, have) = refs[:count], refs[count:]
+    gathered(pieces, have)
+    ff = gg_ref.shape[1]
+    for i, (ref, side) in enumerate(((gg_ref, 0), (gu_ref, 0), (gd_ref, width))):
+        ref[0] = contract_first(
+            acts_ref[:, i * ff : (i + 1) * ff], have[:, side : side + width]
+        ).astype(jnp.bfloat16)
+
+
+def dense(tokens, expert_ids, route_weights, out_grad, gate_weight, up_weight, down_weight):
+    experts = lax.axis_size("expert")
+    devices = lax.axis_size("dp") * experts
+    expert = lax.axis_index("expert").astype(jnp.int32).reshape(1)
+    rows, width = tokens.shape
+    ff = gate_weight.shape[1]
+    near, far = split_masks(devices)
+    weights = (gate_weight, up_weight, down_weight)
+    shape = jax.ShapeDtypeStruct
+    bf16, f32 = jnp.bfloat16, jnp.float32
+    columns = 2 * width + experts + -experts % 128
+    half = rows * devices // 2
+
+    message = kernel_call(
+        pack_body,
+        shape((rows, columns), bf16),
+        [],
+        0,
+        tokens,
+        out_grad,
+        expert_ids.T,
+        route_weights.astype(f32).T,
+    )
+    block = jnp.concatenate([message] + [from_xor(message, m, devices) for m in near], axis=0)
+    own = [block] + [from_xor(block, m, devices) for m in far]
+    other = [from_xor(piece, 1, devices) for piece in own]
+    count = len(own)
+
+    held = pltpu.VMEM((half, columns), bf16)
+    pre = kernel_call(
+        functools.partial(pre_body, count, width),
+        shape((half, 3 * ff), f32),
+        [held],
+        6 * half * ff * width,
+        *own,
+        *weights,
+    )
+    acts, message = kernel_call(
+        functools.partial(act_body, count, width),
+        (shape((2 * half, 3 * ff), bf16), shape((half, 2 * width), bf16)),
+        [held],
+        12 * half * ff * width,
+        *own,
+        *other,
+        pre,
+        *weights,
+        expert,
+    )
+    passed = from_xor(message, 1, devices)
+    mine = kernel_call(
+        own_body, shape((half, 2 * width), f32), [], 6 * half * ff * width, acts, *weights
+    )
+    total = (mine + passed.astype(f32)).astype(bf16)
+    for masks in (far, near):
+        part = total.shape[0] // (len(masks) + 1)
+        pieces = [total[k * part : (k + 1) * part] for k in range(len(masks) + 1)]
+        summed = pieces[0].astype(f32)
+        for m, piece in zip(masks, pieces[1:]):
+            summed = summed + from_xor(piece, m, devices).astype(f32)
+        total = summed.astype(bf16)
+
+    grads = kernel_call(
+        functools.partial(grad_body, 2 * count, width),
+        (shape(gate_weight.shape, bf16),) * 3,
+        [pltpu.VMEM((2 * half, columns), bf16)],
+        12 * half * ff * width,
+        *own,
+        *other,
+        acts,
+    )
+    return total[:, :width], total[:, width:], *grads
+
+
+def shards(tokens, *others):
+    experts = lax.axis_size("expert")
+    devices = lax.axis_size("dp") * experts
+    whole_group = tokens.shape[0] * experts <= ROW_CAP
+    if whole_group and devices >= 16 and devices & (devices - 1) == 0:
+        return dense(tokens, *others)
+    return slotted(tokens, *others)
+
+
 def solution(mesh):
     return jax.shard_map(
         shards,

time: 254 us -> 66.9 us (0.26)
  waiting for transfers between devices: 185 us -> 31.4 us
  blocking collectives: 23.1 us -> 0 us
  matrix products: 20.2 us -> 0 us
  between operations: 13.9 us -> 0.79 us
  starting transfers between devices: 6.81 us -> 16.9 us
  Pallas kernels: 0 us -> 9.07 us
  local copies, waits for them, and re-layouts: 1.85 us -> 7.22 us
    reduce_scatter x2 -> x0, waiting for transfers between devices: 115 us -> none  [the longest x1 60.9 us: shards(): lax.psum_scatter((contract_first(gate_act, w_gate) + contract_first(up_ac...]
    all_gather x2 -> x0, waiting for transfers between devices: 67.1 us -> none  [the longest x1 37.3 us: shards(): all_dy = lax.all_gather(slot_dy, 'dp', axis=0, tiled=True)]
    ppermute x0 -> x17, waiting for transfers between devices: none -> 31.4 us  [from_xor(): return lax.ppermute(value, AXES, [(i, i ^ mask) for i in range(devices)])]
    all_gather x4 -> x0, blocking collectives: 23.1 us -> none  [the longest x1 6.85 us: shards(): lax.all_gather(tokens, 'expert', axis=0, tiled=True)]
    dot_general x13 -> x0, matrix products: 20.2 us -> none  [the longest x5 7.18 us: contract_first(): lax.dot_general(left, right, (((0,), (0,)), ((), ())), preferred_element_...]
    ppermute x0 -> x17, starting transfers between devices: none -> 16.9 us  [from_xor(): return lax.ppermute(value, AXES, [(i, i ^ mask) for i in range(devices)])]
    pallas_call x0 -> x5, Pallas kernels: none -> 9.07 us  [kernel_call(): pl.pallas_call(body, out_shape=out_shape, in_specs=specs, out_specs=jax.t...]
    all_to_all x2 -> x0, starting transfers between devices: 6.65 us -> none  [the longest x1 3.32 us: shards(): lax.all_to_all(back_in, 'expert', split_axis=0, concat_axis=0, tiled=True)]
  transfers between devices with their start and end apart: 6 -> 17, of which waited for: 5 -> 8; matrix products, arithmetic and copies ran while one was open for 7% -> 0% of each run, Pallas kernels for 0% -> 9%
where the time goes in v2:
time: 66.9 us; the launch traced here: 66.6 us
  waiting for transfers between devices  31.4 us (47%)
  starting transfers between devices  16.9 us (25%)
  Pallas kernels  9.07 us (14%)
  local copies, waits for them, and re-layouts  7.22 us (11%)
  other arithmetic  1.2 us (2%)
  between operations  0.79 us (1%)
    ppermute x17, waiting for transfers between devices, from_xor(): return lax.ppermute(value, AXES, [(i, i ^ mask) for i in range(devices)])  31.4 us
    ppermute x17, starting transfers between devices, from_xor(): return lax.ppermute(value, AXES, [(i, i ^ mask) for i in range(devices)])  16.9 us
    pallas_call x5, Pallas kernels, kernel_call(): pl.pallas_call(body, out_shape=out_shape, in_specs=specs, out_specs=jax.t...  9.07 us
    unnamed x18, local copies, waits for them, and re-layouts  6.43 us
  transfers between devices with their start and end apart: 17, of which 8 were waited for; matrix products, arithmetic and copies ran while one was open for 0% of the time, Pallas kernels for 9%

profile of v2, /device:TPU:0, one launch (start us, length us, event | category | flops | bytes accessed | tf_op | source)
XLA Modules:
  0.0 66.6 jit_solution(15086575706816027178)
XLA Ops:
  1.3 0.8 %copy-done.6 = bf16[4,4096]{1,0:T(4,128)(2,1)S(1)} copy-done((bf16[4,4096]{1,0:T(4,128)(2,1)S(1)}, bf16[4,4096]{1,0:T(4,128)(2,1)}, u32[]{:S(2)}) %copy-start.6) | copy-done | bytes 32792
  2.0 0.8 %copy-done.7 = bf16[4,4096]{1,0:T(4,128)(2,1)S(1)} copy-done((bf16[4,4096]{1,0:T(4,128)(2,1)S(1)}, bf16[4,4096]{1,0:T(4,128)(2,1)}, u32[]{:S(2)}) %copy-start.7) | copy-done | bytes 32792
  2.8 0.7 %copy-done.8 = s32[4,2]{0,1:T(2,128)S(1)} copy-done((s32[4,2]{0,1:T(2,128)S(1)}, s32[4,2]{0,1:T(2,128)}, u32[]{:S(2)}) %copy-start.8) | copy-done | bytes 56
  3.6 5.1 %collective-permute-start.2 = (bf16[4,8320]{1,0:T(4,128)(2,1)S(1)}, bf16[4,8320]{1,0:T(4,128)(2,1)S(1)}, u32[]{:S(2)}, u32[]{:S(2)}) collective-permute-start(bf16[4,8320]{1,0:T(4,128)(2,1)S(1)} %shard_map.110), channel_id=1, source_target_pairs={{0,24},{1,25},{2,26},{3,27},{4,28},{5,29},{6,30},{7,31},{8,16},{9,... | collective-permute-start | bytes 199688 | tf_op jit(solution)/shard_map/ppermute | solution.py:103
  9.3 2.0 %collective-permute-done.2 = bf16[4,8320]{1,0:T(4,128)(2,1)S(1)} collective-permute-done((bf16[4,8320]{1,0:T(4,128)(2,1)S(1)}, bf16[4,8320]{1,0:T(4,128)(2,1)S(1)}, u32[]{:S(2)}, u32[]{:S(2)}) %collective-permute-start.2) | collective-permute-done | bytes 66592 | tf_op jit(solution)/shard_map/ppermute | solution.py:103
  11.2 3.1 %collective-permute-done.1 = bf16[4,8320]{1,0:T(4,128)(2,1)S(1)} collective-permute-done((bf16[4,8320]{1,0:T(4,128)(2,1)S(1)}, bf16[4,8320]{1,0:T(4,128)(2,1)S(1)}, u32[]{:S(2)}, u32[]{:S(2)}) %collective-permute-start.1) | collective-permute-done | bytes 66592 | tf_op jit(solution)/shard_map/ppermute | solution.py:103
  14.5 2.5 %collective-permute-start.5 = (bf16[16,8320]{1,0:T(8,128)(2,1)S(1)}, bf16[16,8320]{1,0:T(8,128)(2,1)S(1)}, u32[]{:S(2)}, u32[]{:S(2)}) collective-permute-start(bf16[16,8320]{1,0:T(8,128)(2,1)S(1)} %pad_maximum_fusion.refs_0_), channel_id=1, source_target_pairs={{0,6},{1,7},{2,4},{3,5},{4,2},{5,3},{6,0},{7,1},{8,14},{9,15},{10,... | collective-permute-start | bytes 798728 | tf_op jit(solution)/shard_map/ppermute | solution.py:103
  18.0 6.8 %collective-permute-done.5.refs_3_ = bf16[16,8320]{1,0:T(8,128)(2,1)S(1)} collective-permute-done((bf16[16,8320]{1,0:T(8,128)(2,1)S(1)}, bf16[16,8320]{1,0:T(8,128)(2,1)S(1)}, u32[]{:S(2)}, u32[]{:S(2)}) %collective-permute-start.5) | collective-permute-done | bytes 266272 | tf_op jit(solution)/shard_map/ppermute | solution.py:103
  24.8 4.6 %collective-permute-done.4.refs_2_ = bf16[16,8320]{1,0:T(8,128)(2,1)S(1)} collective-permute-done((bf16[16,8320]{1,0:T(8,128)(2,1)S(1)}, bf16[16,8320]{1,0:T(8,128)(2,1)S(1)}, u32[]{:S(2)}, u32[]{:S(2)}) %collective-permute-start.4) | collective-permute-done | bytes 266272 | tf_op jit(solution)/shard_map/ppermute | solution.py:103
  29.9 1.4 %copy-done = bf16[1,192,4096]{2,1,0:T(8,128)(2,1)S(1)} copy-done((bf16[1,192,4096]{2,1,0:T(8,128)(2,1)S(1)}, bf16[1,192,4096]{2,1,0:T(8,128)(2,1)}, u32[]{:S(2)}) %copy-start) | copy-done | bytes 1572888
  31.3 1.4 %copy-done.2 = bf16[1,192,4096]{2,1,0:T(8,128)(2,1)S(1)} copy-done((bf16[1,192,4096]{2,1,0:T(8,128)(2,1)S(1)}, bf16[1,192,4096]{2,1,0:T(8,128)(2,1)}, u32[]{:S(2)}) %copy-start.2) | copy-done | bytes 1572888
  32.7 1.4 %copy-done.4 = bf16[1,192,4096]{2,1,0:T(8,128)(2,1)S(1)} copy-done((bf16[1,192,4096]{2,1,0:T(8,128)(2,1)S(1)}, bf16[1,192,4096]{2,1,0:T(8,128)(2,1)}, u32[]{:S(2)}) %copy-start.4) | copy-done | bytes 1572888
  34.2 1.7 %shard_map.111.refs_8_ = f32[64,576]{1,0:T(8,128)S(1)} custom-call(bf16[16,8320]{1,0:T(8,128)(2,1)S(1)} %pad_maximum_fusion.refs_0_, bf16[16,8320]{1,0:T(8,128)(2,1)S(1)} %collective-permute-done.3.refs_1_, bf16[16,8320]{1,0:T(8,128)(2,1)S(1)} %collective-permute-done.4.refs_2_, bf16[16,8320]{1,0:T(8,128)(2,1)S(1)} %collective-permute-done.5.refs_3_, ...), custom_call_target="tpu_custom_call" | custom-call | flops 301989888 | bytes 4194304 | tf_op jit(solution)/shard_map/pallas_call | solution.py:109
  35.9 3.0 %shard_map.112 = (bf16[128,576]{1,0:T(8,128)(2,1)S(1)}, bf16[64,8192]{1,0:T(8,128)(2,1)S(1)}) custom-call(bf16[16,8320]{1,0:T(8,128)(2,1)S(1)} %pad_maximum_fusion.refs_0_, bf16[16,8320]{1,0:T(8,128)(2,1)S(1)} %collective-permute-done.3.refs_1_, bf16[16,8320]{1,0:T(8,128)(2,1)S(1)} %collective-permute-done.4.refs_2_, ...), custom_call_target="tpu_custom_call" | custom-call | flops 603979776 | bytes 4194304 | tf_op jit(solution)/shard_map/pallas_call | solution.py:109
  39.0 1.0 %shard_map.113 = f32[64,8192]{1,0:T(8,128)S(1)} custom-call(bf16[128,576]{1,0:T(8,128)(2,1)S(1)} %get-tuple-element.10.acts_ref.refs_8_, bf16[1,192,4096]{2,1,0:T(8,128)(2,1)S(1)} %copy-done.1, bf16[1,192,4096]{2,1,0:T(8,128)(2,1)S(1)} %copy-done.3, bf16[1,192,4096]{2,1,0:T(8,128)(2,1)S(1)} %copy-done.5), custom_call_target="tpu_custom_call" | custom-call | flops 301989888 | bytes 4194304 | tf_op jit(solution)/shard_map/pallas_call | solution.py:109
  40.0 1.6 %collective-permute-done.10 = bf16[64,8192]{1,0:T(8,128)(2,1)S(1)} collective-permute-done((bf16[64,8192]{1,0:T(8,128)(2,1)S(1)}, bf16[64,8192]{1,0:T(8,128)(2,1)S(1)}, u32[]{:S(2)}, u32[]{:S(2)}) %collective-permute-start.10) | collective-permute-done | bytes 1048608 | tf_op jit(solution)/shard_map/ppermute | solution.py:103
  41.8 1.1 %collective-permute-start.11 = (bf16[16,8192]{1,0:T(8,128)(2,1)S(1)}, bf16[16,8192]{1,0:T(8,128)(2,1)S(1)}, u32[]{:S(2)}, u32[]{:S(2)}) collective-permute-start(bf16[16,8192]{1,0:T(8,128)(2,1)S(1)} %get-tuple-element.15), channel_id=1, source_target_pairs={{0,2},{1,3},{2,0},{3,1},{4,6},{5,7},{6,4},{7,5},{8,10},{9,11},{10,... | collective-permute-start | bytes 786440 | tf_op jit(solution)/shard_map/ppermute | solution.py:103
  43.0 1.9 %collective-permute-start.13 = (bf16[16,8192]{1,0:T(8,128)(2,1)S(1)}, bf16[16,8192]{1,0:T(8,128)(2,1)S(1)}, u32[]{:S(2)}, u32[]{:S(2)}) collective-permute-start(bf16[16,8192]{1,0:T(8,128)(2,1)S(1)} %get-tuple-element.16), channel_id=1, source_target_pairs={{0,6},{1,7},{2,4},{3,5},{4,2},{5,3},{6,0},{7,1},{8,14},{9,15},{10,... | collective-permute-start | bytes 786440 | tf_op jit(solution)/shard_map/ppermute | solution.py:103
  45.4 10.5 %collective-permute-done.11 = bf16[16,8192]{1,0:T(8,128)(2,1)S(1)} collective-permute-done((bf16[16,8192]{1,0:T(8,128)(2,1)S(1)}, bf16[16,8192]{1,0:T(8,128)(2,1)S(1)}, u32[]{:S(2)}, u32[]{:S(2)}) %collective-permute-start.11) | collective-permute-done | bytes 262176 | tf_op jit(solution)/shard_map/ppermute | solution.py:103
  55.9 1.2 %collective-permute-done.12 = bf16[16,8192]{1,0:T(8,128)(2,1)S(1)} collective-permute-done((bf16[16,8192]{1,0:T(8,128)(2,1)S(1)}, bf16[16,8192]{1,0:T(8,128)(2,1)S(1)}, u32[]{:S(2)}, u32[]{:S(2)}) %collective-permute-start.12) | collective-permute-done | bytes 262176 | tf_op jit(solution)/shard_map/ppermute | solution.py:103
  57.4 1.5 %collective-permute-start.16 = (bf16[4,8192]{1,0:T(4,128)(2,1)S(1)}, bf16[4,8192]{1,0:T(4,128)(2,1)S(1)}, u32[]{:S(2)}, u32[]{:S(2)}) collective-permute-start(bf16[4,8192]{1,0:T(4,128)(2,1)S(1)} %get-tuple-element.19), channel_id=1, source_target_pairs={{0,24},{1,25},{2,26},{3,27},{4,28},{5,29},{6,30},{7,31},{8,16},{9,... | collective-permute-start | bytes 196616 | tf_op jit(solution)/shard_map/ppermute | solution.py:103
  58.9 1.9 %collective-permute-start.15 = (bf16[4,8192]{1,0:T(4,128)(2,1)S(1)}, bf16[4,8192]{1,0:T(4,128)(2,1)S(1)}, u32[]{:S(2)}, u32[]{:S(2)}) collective-permute-start(bf16[4,8192]{1,0:T(4,128)(2,1)S(1)} %get-tuple-element.20), channel_id=1, source_target_pairs={{0,16},{1,17},{2,18},{3,19},{4,20},{5,21},{6,22},{7,23},{8,24},{9,... | collective-permute-start | bytes 196616 | tf_op jit(solution)/shard_map/ppermute | solution.py:103
  60.9 3.3 %shard_map.114 = (bf16[1,192,4096]{2,1,0:T(8,128)(2,1)}, bf16[1,192,4096]{2,1,0:T(8,128)(2,1)}, bf16[1,192,4096]{2,1,0:T(8,128)(2,1)}) custom-call(bf16[16,8320]{1,0:T(8,128)(2,1)S(1)} %pad_maximum_fusion.refs_0_, bf16[16,8320]{1,0:T(8,128)(2,1)S(1)} %collective-permute-done.3.refs_1_, bf16[16,8320]{1,0:T(8,128)(2,1)S(1)} %collective-permute-done.4.refs_2_, ...), custom_call_target="tpu_custom_call" | custom-call | flops 603979776 | bytes 4194304 | tf_op jit(solution)/shard_map/pallas_call | solution.py:109
  64.2 1.6 %collective-permute-done.15 = bf16[4,8192]{1,0:T(4,128)(2,1)S(1)} collective-permute-done((bf16[4,8192]{1,0:T(4,128)(2,1)S(1)}, bf16[4,8192]{1,0:T(4,128)(2,1)S(1)}, u32[]{:S(2)}, u32[]{:S(2)}) %collective-permute-start.15) | collective-permute-done | bytes 65568 | tf_op jit(solution)/shard_map/ppermute | solution.py:103
  (41 shorter events, 5.0 us)
Async XLA Ops:
  1.3 0.8 %copy-start.6 = (bf16[4,4096]{1,0:T(4,128)(2,1)S(1)}, bf16[4,4096]{1,0:T(4,128)(2,1)}, u32[]{:S(2)}) copy-start(bf16[4,4096]{1,0:T(4,128)(2,1)} %x_ref.1) | copy-start | bytes 98308
  3.6 7.6 %collective-permute-start.2 = (bf16[4,8320]{1,0:T(4,128)(2,1)S(1)}, bf16[4,8320]{1,0:T(4,128)(2,1)S(1)}, u32[]{:S(2)}, u32[]{:S(2)}) collective-permute-start(bf16[4,8320]{1,0:T(4,128)(2,1)S(1)} %shard_map.110), channel_id=1, source_target_pairs={{0,24},{1,25},{2,26},{3,27},{4,28},{5,29},{6,30},{7,31},{8,16},{9,... | collective-permute-start | bytes 199688 | tf_op jit(solution)/shard_map/ppermute | solution.py:103
  8.6 5.7 %collective-permute-start.1 = (bf16[4,8320]{1,0:T(4,128)(2,1)S(1)}, bf16[4,8320]{1,0:T(4,128)(2,1)S(1)}, u32[]{:S(2)}, u32[]{:S(2)}) collective-permute-start(bf16[4,8320]{1,0:T(4,128)(2,1)S(1)} %shard_map.110), channel_id=1, source_target_pairs={{0,16},{1,17},{2,18},{3,19},{4,20},{5,21},{6,22},{7,23},{8,24},{9,... | collective-permute-start | bytes 199688 | tf_op jit(solution)/shard_map/ppermute | solution.py:103
  8.6 5.7 %collective-permute-start = (bf16[4,8320]{1,0:T(4,128)(2,1)S(1)}, bf16[4,8320]{1,0:T(4,128)(2,1)S(1)}, u32[]{:S(2)}, u32[]{:S(2)}) collective-permute-start(bf16[4,8320]{1,0:T(4,128)(2,1)S(1)} %shard_map.110), channel_id=1, source_target_pairs={{0,8},{1,9},{2,10},{3,11},{4,12},{5,13},{6,14},{7,15},{8,0},{9,1},... | collective-permute-start | bytes 199688 | tf_op jit(solution)/shard_map/ppermute | solution.py:103
  14.5 10.3 %collective-permute-start.5 = (bf16[16,8320]{1,0:T(8,128)(2,1)S(1)}, bf16[16,8320]{1,0:T(8,128)(2,1)S(1)}, u32[]{:S(2)}, u32[]{:S(2)}) collective-permute-start(bf16[16,8320]{1,0:T(8,128)(2,1)S(1)} %pad_maximum_fusion.refs_0_), channel_id=1, source_target_pairs={{0,6},{1,7},{2,4},{3,5},{4,2},{5,3},{6,0},{7,1},{8,14},{9,15},{10,... | collective-permute-start | bytes 798728 | tf_op jit(solution)/shard_map/ppermute | solution.py:103
  17.0 12.4 %collective-permute-start.4 = (bf16[16,8320]{1,0:T(8,128)(2,1)S(1)}, bf16[16,8320]{1,0:T(8,128)(2,1)S(1)}, u32[]{:S(2)}, u32[]{:S(2)}) collective-permute-start(bf16[16,8320]{1,0:T(8,128)(2,1)S(1)} %pad_maximum_fusion.refs_0_), channel_id=1, source_target_pairs={{0,4},{1,5},{2,6},{3,7},{4,0},{5,1},{6,2},{7,3},{8,12},{9,13},{10,... | collective-permute-start | bytes 798728 | tf_op jit(solution)/shard_map/ppermute | solution.py:103
  17.5 11.9 %collective-permute-start.3 = (bf16[16,8320]{1,0:T(8,128)(2,1)S(1)}, bf16[16,8320]{1,0:T(8,128)(2,1)S(1)}, u32[]{:S(2)}, u32[]{:S(2)}) collective-permute-start(bf16[16,8320]{1,0:T(8,128)(2,1)S(1)} %pad_maximum_fusion.refs_0_), channel_id=1, source_target_pairs={{0,2},{1,3},{2,0},{3,1},{4,6},{5,7},{6,4},{7,5},{8,10},{9,11},{10,... | collective-permute-start | bytes 798728 | tf_op jit(solution)/shard_map/ppermute | solution.py:103
  18.0 17.8 %collective-permute-start.6 = (bf16[16,8320]{1,0:T(8,128)(2,1)S(1)}, bf16[16,8320]{1,0:T(8,128)(2,1)S(1)}, u32[]{:S(2)}, u32[]{:S(2)}) collective-permute-start(bf16[16,8320]{1,0:T(8,128)(2,1)S(1)} %pad_maximum_fusion.refs_0_), channel_id=1, source_target_pairs={{0,1},{1,0},{2,3},{3,2},{4,5},{5,4},{6,7},{7,6},{8,9},{9,8},{10,11... | collective-permute-start | bytes 798728 | tf_op jit(solution)/shard_map/ppermute | solution.py:103
  24.8 11.1 %collective-permute-start.9 = (bf16[16,8320]{1,0:T(8,128)(2,1)S(1)}, bf16[16,8320]{1,0:T(8,128)(2,1)S(1)}, u32[]{:S(2)}, u32[]{:S(2)}) collective-permute-start(bf16[16,8320]{1,0:T(8,128)(2,1)S(1)} %collective-permute-done.5.refs_3_), channel_id=1, source_target_pairs={{0,1},{1,0},{2,3},{3,2},{4,5},{5,4},{6,7},{7,6},{8,9},{9,8},{10,11... | collective-permute-start | bytes 798728 | tf_op jit(solution)/shard_map/ppermute | solution.py:103
  29.4 6.4 %collective-permute-start.8 = (bf16[16,8320]{1,0:T(8,128)(2,1)S(1)}, bf16[16,8320]{1,0:T(8,128)(2,1)S(1)}, u32[]{:S(2)}, u32[]{:S(2)}) collective-permute-start(bf16[16,8320]{1,0:T(8,128)(2,1)S(1)} %collective-permute-done.4.refs_2_), channel_id=1, source_target_pairs={{0,1},{1,0},{2,3},{3,2},{4,5},{5,4},{6,7},{7,6},{8,9},{9,8},{10,11... | collective-permute-start | bytes 798728 | tf_op jit(solution)/shard_map/ppermute | solution.py:103
  29.4 6.5 %collective-permute-start.7 = (bf16[16,8320]{1,0:T(8,128)(2,1)S(1)}, bf16[16,8320]{1,0:T(8,128)(2,1)S(1)}, u32[]{:S(2)}, u32[]{:S(2)}) collective-permute-start(bf16[16,8320]{1,0:T(8,128)(2,1)S(1)} %collective-permute-done.3.refs_1_), channel_id=1, source_target_pairs={{0,1},{1,0},{2,3},{3,2},{4,5},{5,4},{6,7},{7,6},{8,9},{9,8},{10,11... | collective-permute-start | bytes 798728 | tf_op jit(solution)/shard_map/ppermute | solution.py:103
  29.9 1.4 %copy-start = (bf16[1,192,4096]{2,1,0:T(8,128)(2,1)S(1)}, bf16[1,192,4096]{2,1,0:T(8,128)(2,1)}, u32[]{:S(2)}) copy-start(bf16[1,192,4096]{2,1,0:T(8,128)(2,1)} %wg_ref.1) | copy-start | bytes 4718596
  31.3 1.4 %copy-start.2 = (bf16[1,192,4096]{2,1,0:T(8,128)(2,1)S(1)}, bf16[1,192,4096]{2,1,0:T(8,128)(2,1)}, u32[]{:S(2)}) copy-start(bf16[1,192,4096]{2,1,0:T(8,128)(2,1)} %wu_ref.1) | copy-start | bytes 4718596
  32.7 1.4 %copy-start.4 = (bf16[1,192,4096]{2,1,0:T(8,128)(2,1)S(1)}, bf16[1,192,4096]{2,1,0:T(8,128)(2,1)}, u32[]{:S(2)}) copy-start(bf16[1,192,4096]{2,1,0:T(8,128)(2,1)} %wd_ref.1) | copy-start | bytes 4718596
  35.9 3.1 %copy-start.1 = (bf16[1,192,4096]{2,1,0:T(8,128)(2,1)S(1)}, bf16[1,192,4096]{2,1,0:T(8,128)(2,1)}, u32[]{:S(2)}) copy-start(bf16[1,192,4096]{2,1,0:T(8,128)(2,1)} %wg_ref.1) | copy-start | bytes 4718596
  35.9 3.1 %copy-start.3 = (bf16[1,192,4096]{2,1,0:T(8,128)(2,1)S(1)}, bf16[1,192,4096]{2,1,0:T(8,128)(2,1)}, u32[]{:S(2)}) copy-start(bf16[1,192,4096]{2,1,0:T(8,128)(2,1)} %wu_ref.1) | copy-start | bytes 4718596
  35.9 3.1 %copy-start.5 = (bf16[1,192,4096]{2,1,0:T(8,128)(2,1)S(1)}, bf16[1,192,4096]{2,1,0:T(8,128)(2,1)}, u32[]{:S(2)}) copy-start(bf16[1,192,4096]{2,1,0:T(8,128)(2,1)} %wd_ref.1) | copy-start | bytes 4718596
  38.9 2.7 %collective-permute-start.10 = (bf16[64,8192]{1,0:T(8,128)(2,1)S(1)}, bf16[64,8192]{1,0:T(8,128)(2,1)S(1)}, u32[]{:S(2)}, u32[]{:S(2)}) collective-permute-start(bf16[64,8192]{1,0:T(8,128)(2,1)S(1)} %get-tuple-element.11), channel_id=1, source_target_pairs={{0,1},{1,0},{2,3},{3,2},{4,5},{5,4},{6,7},{7,6},{8,9},{9,8},{10,11... | collective-permute-start | bytes 3145736 | tf_op jit(solution)/shard_map/ppermute | solution.py:103
  41.8 14.0 %collective-permute-start.11 = (bf16[16,8192]{1,0:T(8,128)(2,1)S(1)}, bf16[16,8192]{1,0:T(8,128)(2,1)S(1)}, u32[]{:S(2)}, u32[]{:S(2)}) collective-permute-start(bf16[16,8192]{1,0:T(8,128)(2,1)S(1)} %get-tuple-element.15), channel_id=1, source_target_pairs={{0,2},{1,3},{2,0},{3,1},{4,6},{5,7},{6,4},{7,5},{8,10},{9,11},{10,... | collective-permute-start | bytes 786440 | tf_op jit(solution)/shard_map/ppermute | solution.py:103
  43.0 12.9 %collective-permute-start.13 = (bf16[16,8192]{1,0:T(8,128)(2,1)S(1)}, bf16[16,8192]{1,0:T(8,128)(2,1)S(1)}, u32[]{:S(2)}, u32[]{:S(2)}) collective-permute-start(bf16[16,8192]{1,0:T(8,128)(2,1)S(1)} %get-tuple-element.16), channel_id=1, source_target_pairs={{0,6},{1,7},{2,4},{3,5},{4,2},{5,3},{6,0},{7,1},{8,14},{9,15},{10,... | collective-permute-start | bytes 786440 | tf_op jit(solution)/shard_map/ppermute | solution.py:103
  44.9 12.2 %collective-permute-start.12 = (bf16[16,8192]{1,0:T(8,128)(2,1)S(1)}, bf16[16,8192]{1,0:T(8,128)(2,1)S(1)}, u32[]{:S(2)}, u32[]{:S(2)}) collective-permute-start(bf16[16,8192]{1,0:T(8,128)(2,1)S(1)} %get-tuple-element.17), channel_id=1, source_target_pairs={{0,4},{1,5},{2,6},{3,7},{4,0},{5,1},{6,2},{7,3},{8,12},{9,13},{10,... | collective-permute-start | bytes 786440 | tf_op jit(solution)/shard_map/ppermute | solution.py:103
  57.3 6.9 %collective-permute-start.14 = (bf16[4,8192]{1,0:T(4,128)(2,1)S(1)}, bf16[4,8192]{1,0:T(4,128)(2,1)S(1)}, u32[]{:S(2)}, u32[]{:S(2)}) collective-permute-start(bf16[4,8192]{1,0:T(4,128)(2,1)S(1)} %get-tuple-element.18), channel_id=1, source_target_pairs={{0,8},{1,9},{2,10},{3,11},{4,12},{5,13},{6,14},{7,15},{8,0},{9,1},... | collective-permute-start | bytes 196616 | tf_op jit(solution)/shard_map/ppermute | solution.py:103
  57.4 6.8 %collective-permute-start.16 = (bf16[4,8192]{1,0:T(4,128)(2,1)S(1)}, bf16[4,8192]{1,0:T(4,128)(2,1)S(1)}, u32[]{:S(2)}, u32[]{:S(2)}) collective-permute-start(bf16[4,8192]{1,0:T(4,128)(2,1)S(1)} %get-tuple-element.19), channel_id=1, source_target_pairs={{0,24},{1,25},{2,26},{3,27},{4,28},{5,29},{6,30},{7,31},{8,16},{9,... | collective-permute-start | bytes 196616 | tf_op jit(solution)/shard_map/ppermute | solution.py:103
  58.9 6.9 %collective-permute-start.15 = (bf16[4,8192]{1,0:T(4,128)(2,1)S(1)}, bf16[4,8192]{1,0:T(4,128)(2,1)S(1)}, u32[]{:S(2)}, u32[]{:S(2)}) collective-permute-start(bf16[4,8192]{1,0:T(4,128)(2,1)S(1)} %get-tuple-element.20), channel_id=1, source_target_pairs={{0,16},{1,17},{2,18},{3,19},{4,20},{5,21},{6,22},{7,23},{8,24},{9,... | collective-permute-start | bytes 196616 | tf_op jit(solution)/shard_map/ppermute | solution.py:103
  (2 other events, 1.4 us)

commit v3 on v0

--- a/solution.py
+++ b/solution.py
@@ -1,9 +1,14 @@
+import functools
+
 import jax
 import jax.numpy as jnp
 from jax import lax
+from jax.experimental import pallas as pl
+from jax.experimental.pallas import tpu as pltpu
 from jax.sharding import PartitionSpec as P
 
 ROW_CAP = 16
+AXES = ("dp", "expert")
 
 
 def contract_rows(left, right):
@@ -18,7 +23,7 @@
     )
 
 
-def shards(tokens, expert_ids, route_weights, out_grad, gate_weight, up_weight, down_weight):
+def slotted(tokens, expert_ids, route_weights, out_grad, gate_weight, up_weight, down_weight):
     expert = lax.axis_index("expert")
     width = tokens.shape[1]
     local_tokens = tokens.shape[0]
@@ -88,6 +93,284 @@
     )
 
 
+def split_masks(devices):
+    far = tuple(k << 1 for k in range(1, 4))
+    near = tuple(k << 3 for k in range(1, devices >> 3))
+    return near, far
+
+
+def from_xor(value, mask, devices):
+    return lax.ppermute(value, AXES, [(i, i ^ mask) for i in range(devices)])
+
+
+def kernel_call(body, out_shape, cost, *operands, scratch=(), hbm=(), vmem_mib=24):
+    vmem, smem = pl.BlockSpec(memory_space=pltpu.VMEM), pl.BlockSpec(memory_space=pltpu.SMEM)
+    stay = pl.BlockSpec(memory_space=pltpu.HBM)
+    specs = [stay if i in hbm else smem if o.ndim == 1 else vmem for i, o in enumerate(operands)]
+    return pl.pallas_call(
+        body,
+        out_shape=out_shape,
+        in_specs=specs,
+        out_specs=jax.tree.map(lambda _: vmem, out_shape),
+        scratch_shapes=scratch,
+        compiler_params=pltpu.CompilerParams(vmem_limit_bytes=vmem_mib << 20),
+        cost_estimate=pl.CostEstimate(flops=cost, bytes_accessed=4 << 20, transcendentals=0),
+    )(*operands)
+
+
+def load_body(*refs):
+    count = len(refs) // 2
+    sems = refs[-1]
+    copies = [
+        pltpu.make_async_copy(refs[i], refs[count + i], sems.at[i]) for i in range(count)
+    ]
+    for copy in copies:
+        copy.start()
+    for copy in copies:
+        copy.wait()
+
+
+def pack_body(dy_ref, ids_ref, w_ref, msg_ref):
+    rows, width = dy_ref.shape
+    top = ids_ref.shape[0]
+    lanes = msg_ref.shape[1] - width
+    msg_ref[:, :width] = dy_ref[...]
+    diagonal = lax.broadcasted_iota(jnp.int32, (rows, rows), 0) == lax.broadcasted_iota(
+        jnp.int32, (rows, rows), 1
+    )
+    expert = lax.broadcasted_iota(jnp.int32, (rows, lanes), 1)
+    route = jnp.zeros((rows, lanes), jnp.float32)
+    for k in range(top):
+        named = jnp.sum(jnp.where(diagonal, ids_ref[k : k + 1, :], 0), axis=1, keepdims=True)
+        weight = jnp.sum(jnp.where(diagonal, w_ref[k : k + 1, :], 0.0), axis=1, keepdims=True)
+        route = route + jnp.where(expert == named, weight, 0.0)
+    msg_ref[:, width:] = route.astype(jnp.bfloat16)
+
+
+def gathered(pieces, into):
+    rows = pieces[0].shape[0]
+    for i, piece in enumerate(pieces):
+        into[i * rows : (i + 1) * rows, :] = piece[...]
+
+
+def forward_body(count, *refs):
+    pieces, (wg_ref, wu_ref, x_ref, hidden_ref, gate_ref, up_ref) = refs[:count], refs[count:]
+    gathered(pieces, x_ref)
+    x = x_ref[...]
+    gate_pre = contract_rows(x, wg_ref[0])
+    up_pre = contract_rows(x, wu_ref[0])
+    gate_sig = 1.0 / (1.0 + jnp.exp(-gate_pre))
+    silu_gate = gate_pre * gate_sig
+    hidden_ref[...] = silu_gate * up_pre
+    gate_ref[...] = up_pre * (gate_sig * (1.0 + gate_pre * (1.0 - gate_sig)))
+    up_ref[...] = silu_gate
+
+
+def back_body(count, *refs):
+    pieces, (wd_ref, dy_ref, grad_ref) = refs[:count], refs[count:]
+    gathered(pieces, dy_ref)
+    grad_ref[...] = contract_rows(dy_ref[:, : wd_ref.shape[2]], wd_ref[0])
+
+
+def out_body(count, *refs):
+    pieces, rest = refs[:count], refs[count:]
+    own_ref, hidden_ref, wd_ref, expert_ref, dy_ref, weight_ref, scaled_ref, msg_ref = rest
+    gathered(pieces, dy_ref)
+    half, width = msg_ref.shape
+    lane = lax.broadcasted_iota(jnp.int32, (half, dy_ref.shape[1] - width), 1)
+    for i, ref in enumerate((own_ref, dy_ref)):
+        route = jnp.where(lane == expert_ref[0], ref[:, width:].astype(jnp.float32), 0.0)
+        weight = jnp.sum(route, axis=1, keepdims=True)
+        here = slice(i * half, (i + 1) * half)
+        weight_ref[here, :] = jnp.broadcast_to(weight, (half, weight_ref.shape[1]))
+        scaled_ref[here, :] = (weight * hidden_ref[here, :]).astype(jnp.bfloat16)
+    msg_ref[...] = jnp.dot(
+        scaled_ref[half:, :], wd_ref[0], preferred_element_type=jnp.float32
+    ).astype(jnp.bfloat16)
+
+
+def into_sum(gate_act, up_act, wg_ref, wu_ref):
+    return jnp.dot(gate_act, wg_ref[0], preferred_element_type=jnp.float32) + jnp.dot(
+        up_act, wu_ref[0], preferred_element_type=jnp.float32
+    )
+
+
+def into_body(dy_ref, own_ref, weight_ref, gate_ref, up_ref, wg_ref, wu_ref, wd_ref, *outs):
+    gate_act_ref, up_act_ref, msg_ref = outs
+    half, width = msg_ref.shape
+    other = contract_rows(dy_ref[:, :width], wd_ref[0])
+    for i, grad in enumerate((own_ref[...], other)):
+        here = slice(i * half, (i + 1) * half)
+        grad = weight_ref[here, :1] * grad
+        gate_act_ref[here, :] = (grad * gate_ref[here, :]).astype(jnp.bfloat16)
+        up_act_ref[here, :] = (grad * up_ref[here, :]).astype(jnp.bfloat16)
+    msg_ref[...] = into_sum(gate_act_ref[half:, :], up_act_ref[half:, :], wg_ref, wu_ref).astype(
+        jnp.bfloat16
+    )
+
+
+def scattered(total, outs):
+    rows = outs[0].shape[0]
+    for i, ref in enumerate(outs):
+        ref[...] = total[i * rows : (i + 1) * rows, :].astype(ref.dtype)
+
+
+def own_out_body(scaled_ref, wd_ref, passed_ref, *outs):
+    half = passed_ref.shape[0]
+    total = jnp.dot(scaled_ref[:half, :], wd_ref[0], preferred_element_type=jnp.float32)
+    scattered(total + passed_ref[...].astype(jnp.float32), outs)
+
+
+def own_into_body(gate_act_ref, up_act_ref, wg_ref, wu_ref, passed_ref, *outs):
+    half = passed_ref.shape[0]
+    total = into_sum(gate_act_ref[:half, :], up_act_ref[:half, :], wg_ref, wu_ref)
+    scattered(total + passed_ref[...].astype(jnp.float32), outs)
+
+
+def pair_grad_body(gate_act_ref, up_act_ref, x_ref, gg_ref, gu_ref):
+    gg_ref[0] = contract_first(gate_act_ref[...], x_ref[...]).astype(jnp.bfloat16)
+    gu_ref[0] = contract_first(up_act_ref[...], x_ref[...]).astype(jnp.bfloat16)
+
+
+def down_grad_body(scaled_ref, own_ref, other_ref, gd_ref):
+    half, width = own_ref.shape[0], gd_ref.shape[2]
+    gd_ref[0] = (
+        contract_first(scaled_ref[:half, :], own_ref[:, :width])
+        + contract_first(scaled_ref[half:, :], other_ref[:, :width])
+    ).astype(jnp.bfloat16)
+
+
+def dense(tokens, expert_ids, route_weights, out_grad, gate_weight, up_weight, down_weight):
+    experts = lax.axis_size("expert")
+    devices = lax.axis_size("dp") * experts
+    expert = lax.axis_index("expert").astype(jnp.int32).reshape(1)
+    rows, width = tokens.shape
+    ff = gate_weight.shape[1]
+    near, far = split_masks(devices)
+    bf16, f32 = jnp.bfloat16, jnp.float32
+    lanes = experts + -experts % 128
+    half = rows * devices // 2
+    unit = 2 * half * ff * width
+
+    def shape(*dims, dtype=bf16):
+        return jax.ShapeDtypeStruct(dims, dtype)
+
+    def near_block(value):
+        return jnp.concatenate([value] + [from_xor(value, m, devices) for m in near], axis=0)
+
+    def far_pieces(block):
+        own = [block] + [from_xor(block, m, devices) for m in far]
+        return own, [from_xor(piece, 1, devices) for piece in own]
+
+    block_x = near_block(tokens)
+    message = kernel_call(
+        pack_body,
+        shape(rows, width + lanes),
+        0,
+        out_grad,
+        expert_ids.T,
+        route_weights.astype(f32).T,
+    )
+    w_gate, w_up, w_down = kernel_call(
+        load_body,
+        (shape(*gate_weight.shape),) * 3,
+        0,
+        gate_weight,
+        up_weight,
+        down_weight,
+        scratch=[pltpu.SemaphoreType.DMA((3,))],
+        hbm=(0, 1, 2),
+        vmem_mib=8,
+    )
+    block_x, w_gate, w_up, w_down = lax.optimization_barrier((block_x, w_gate, w_up, w_down))
+    own_x, other_x = far_pieces(block_x)
+    own_dy, other_dy = far_pieces(near_block(message))
+    count = len(own_x)
+
+    all_x, hidden, gate_part, up_part = kernel_call(
+        functools.partial(forward_body, 2 * count),
+        (shape(2 * half, width),) + (shape(2 * half, ff, dtype=f32),) * 3,
+        4 * unit,
+        *own_x,
+        *other_x,
+        w_gate,
+        w_up,
+    )
+    dy_own, grad_own = kernel_call(
+        functools.partial(back_body, count),
+        (shape(half, width + lanes), shape(half, ff, dtype=f32)),
+        unit,
+        *own_dy,
+        w_down,
+    )
+    dy_other, weight, scaled, message = kernel_call(
+        functools.partial(out_body, count),
+        (
+            shape(half, width + lanes),
+            shape(2 * half, lanes, dtype=f32),
+            shape(2 * half, ff),
+            shape(half, width),
+        ),
+        unit,
+        *other_dy,
+        dy_own,
+        hidden,
+        w_down,
+        expert,
+    )
+    passed_out = from_xor(message, 1, devices)
+    gate_act, up_act, message = kernel_call(
+        into_body,
+        (shape(2 * half, ff), shape(2 * half, ff), shape(half, width)),
+        3 * unit,
+        dy_other,
+        grad_own,
+        weight,
+        gate_part,
+        up_part,
+        w_gate,
+        w_up,
+        w_down,
+    )
+    passed_into = from_xor(message, 1, devices)
+
+    quarter = half // count
+    piece_shapes = (shape(quarter, width, dtype=f32),) + (shape(quarter, width),) * (count - 1)
+    out_pieces = kernel_call(own_out_body, piece_shapes, unit, scaled, w_down, passed_out)
+    into_pieces = kernel_call(
+        own_into_body, piece_shapes, 2 * unit, gate_act, up_act, w_gate, w_up, passed_into
+    )
+
+    def reduced(pieces):
+        total = pieces[0]
+        for m, piece in zip(far, pieces[1:]):
+            total = total + from_xor(piece, m, devices).astype(f32)
+        total = total.astype(bf16)
+        pieces = [total[k * rows : (k + 1) * rows] for k in range(len(near) + 1)]
+        total = pieces[0].astype(f32)
+        for m, piece in zip(near, pieces[1:]):
+            total = total + from_xor(piece, m, devices).astype(f32)
+        return total.astype(bf16)
+
+    mixed, input_grad = reduced(out_pieces), reduced(into_pieces)
+    grad_down = kernel_call(
+        down_grad_body, shape(*down_weight.shape), 2 * unit, scaled, dy_own, dy_other
+    )
+    grad_gate, grad_up = kernel_call(
+        pair_grad_body, (shape(*gate_weight.shape),) * 2, 4 * unit, gate_act, up_act, all_x
+    )
+    return mixed, input_grad, grad_gate, grad_up, grad_down
+
+
+def shards(tokens, *others):
+    experts = lax.axis_size("expert")
+    devices = lax.axis_size("dp") * experts
+    whole_group = tokens.shape[0] * experts <= ROW_CAP
+    if whole_group and devices >= 16 and devices & (devices - 1) == 0:
+        return dense(tokens, *others)
+    return slotted(tokens, *others)
+
+
 def solution(mesh):
     return jax.shard_map(
         shards,

time: 254 us -> 72.4 us (0.29)
  waiting for transfers between devices: 185 us -> 7.01 us
  starting transfers between devices: 6.81 us -> 37.3 us
  blocking collectives: 23.1 us -> 0 us
  matrix products: 20.2 us -> 0 us
  Pallas kernels: 0 us -> 13.5 us
  between operations: 13.9 us -> 0.88 us
  local copies, waits for them, and re-layouts: 1.85 us -> 11.1 us
    reduce_scatter x2 -> x0, waiting for transfers between devices: 115 us -> none  [the longest x1 60.9 us: shards(): lax.psum_scatter((contract_first(gate_act, w_gate) + contract_first(up_ac...]
    all_gather x2 -> x0, waiting for transfers between devices: 67.1 us -> none  [the longest x1 37.3 us: shards(): all_dy = lax.all_gather(slot_dy, 'dp', axis=0, tiled=True)]
    ppermute x0 -> x34, starting transfers between devices: none -> 37.3 us  [from_xor(): return lax.ppermute(value, AXES, [(i, i ^ mask) for i in range(devices)])]
    all_gather x4 -> x0, blocking collectives: 23.1 us -> none  [the longest x1 6.85 us: shards(): lax.all_gather(tokens, 'expert', axis=0, tiled=True)]
    dot_general x13 -> x0, matrix products: 20.2 us -> none  [the longest x5 7.18 us: contract_first(): lax.dot_general(left, right, (((0,), (0,)), ((), ())), preferred_element_...]
    pallas_call x0 -> x10, Pallas kernels: none -> 13.5 us  [kernel_call(): pl.pallas_call(body, out_shape=out_shape, in_specs=specs, out_specs=jax.t...]
    unnamed x13 -> x36, local copies, waits for them, and re-layouts: 0.07 us -> 11 us
    ppermute x0 -> x34, waiting for transfers between devices: none -> 7.01 us  [from_xor(): return lax.ppermute(value, AXES, [(i, i ^ mask) for i in range(devices)])]
  transfers between devices with their start and end apart: 6 -> 34, of which waited for: 5 -> 7; matrix products, arithmetic and copies ran while one was open for 7% -> 2% of each run, Pallas kernels for 0% -> 17%
where the time goes in v3:
time: 72.4 us; the launch traced here: 72.1 us
  starting transfers between devices  37.3 us (52%)
  Pallas kernels  13.5 us (19%)
  local copies, waits for them, and re-layouts  11.1 us (15%)
  waiting for transfers between devices  7.01 us (10%)
  other arithmetic  2.25 us (3%)
  between operations  0.88 us (1%)
    ppermute x34, starting transfers between devices, from_xor(): return lax.ppermute(value, AXES, [(i, i ^ mask) for i in range(devices)])  37.3 us
    pallas_call x10, Pallas kernels, kernel_call(): pl.pallas_call(body, out_shape=out_shape, in_specs=specs, out_specs=jax.t...  13.5 us
    unnamed x36, local copies, waits for them, and re-layouts  11 us
    ppermute x34, waiting for transfers between devices, from_xor(): return lax.ppermute(value, AXES, [(i, i ^ mask) for i in range(devices)])  7.01 us
  transfers between devices with their start and end apart: 34, of which 7 were waited for; matrix products, arithmetic and copies ran while one was open for 2% of the time, Pallas kernels for 17%

profile of v3, /device:TPU:0, one launch (start us, length us, event | category | flops | bytes accessed | tf_op | source)
XLA Modules:
  0.0 72.1 jit_solution(14607180318022940198)
XLA Ops:
  0.6 5.1 %collective-permute-start.12 = (bf16[4,4096]{1,0:T(4,128)(2,1)}, bf16[4,4096]{1,0:T(4,128)(2,1)S(1)}, u32[]{:S(2)}, u32[]{:S(2)}) collective-permute-start(bf16[4,4096]{1,0:T(4,128)(2,1)} %param.7), channel_id=1, source_target_pairs={{0,24},{1,25},{2,26},{3,27},{4,28},{5,29},{6,30},{7,31},{8,16},{9,... | collective-permute-start | bytes 98312 | tf_op jit(solution)/shard_map/ppermute | solution.py:103
  8.6 3.7 %collective-permute-start.2 = (bf16[4,4224]{1,0:T(4,128)(2,1)S(1)}, bf16[4,4224]{1,0:T(4,128)(2,1)S(1)}, u32[]{:S(2)}, u32[]{:S(2)}) collective-permute-start(bf16[4,4224]{1,0:T(4,128)(2,1)S(1)} %shard_map.110), channel_id=1, source_target_pairs={{0,24},{1,25},{2,26},{3,27},{4,28},{5,29},{6,30},{7,31},{8,16},{9,... | collective-permute-start | bytes 101384 | tf_op jit(solution)/shard_map/ppermute | solution.py:103
  12.3 1.4 %copy-done.2 = bf16[1,192,4096]{2,1,0:T(8,128)(2,1)S(1)} copy-done((bf16[1,192,4096]{2,1,0:T(8,128)(2,1)S(1)}, bf16[1,192,4096]{2,1,0:T(8,128)(2,1)}, u32[]{:S(2)}) %copy-start.2) | copy-done | bytes 1572888
  13.7 1.4 %copy-done.3 = bf16[1,192,4096]{2,1,0:T(8,128)(2,1)S(1)} copy-done((bf16[1,192,4096]{2,1,0:T(8,128)(2,1)S(1)}, bf16[1,192,4096]{2,1,0:T(8,128)(2,1)}, u32[]{:S(2)}) %copy-start.3) | copy-done | bytes 1572888
  15.1 1.4 %copy-done.4 = bf16[1,192,4096]{2,1,0:T(8,128)(2,1)S(1)} copy-done((bf16[1,192,4096]{2,1,0:T(8,128)(2,1)S(1)}, bf16[1,192,4096]{2,1,0:T(8,128)(2,1)}, u32[]{:S(2)}) %copy-start.4) | copy-done | bytes 1572888
  18.8 1.7 %collective-permute-start.13 = (bf16[16,4096]{1,0:T(8,128)(2,1)S(1)}, bf16[16,4096]{1,0:T(8,128)(2,1)S(1)}, u32[]{:S(2)}, u32[]{:S(2)}) collective-permute-start(bf16[16,4096]{1,0:T(8,128)(2,1)S(1)} %pad_maximum_fusion.1.refs_0_), channel_id=1, source_target_pairs={{0,2},{1,3},{2,0},{3,1},{4,6},{5,7},{6,4},{7,5},{8,10},{9,11},{10,... | collective-permute-start | bytes 393224 | tf_op jit(solution)/shard_map/ppermute | solution.py:103
  20.5 1.5 %collective-permute-start.14 = (bf16[16,4096]{1,0:T(8,128)(2,1)S(1)}, bf16[16,4096]{1,0:T(8,128)(2,1)S(1)}, u32[]{:S(2)}, u32[]{:S(2)}) collective-permute-start(bf16[16,4096]{1,0:T(8,128)(2,1)S(1)} %pad_maximum_fusion.1.refs_0_), channel_id=1, source_target_pairs={{0,4},{1,5},{2,6},{3,7},{4,0},{5,1},{6,2},{7,3},{8,12},{9,13},{10,... | collective-permute-start | bytes 393224 | tf_op jit(solution)/shard_map/ppermute | solution.py:103
  22.5 1.7 %collective-permute-start.4 = (bf16[16,4224]{1,0:T(8,128)(2,1)S(1)}, bf16[16,4224]{1,0:T(8,128)(2,1)S(1)}, u32[]{:S(2)}, u32[]{:S(2)}) collective-permute-start(bf16[16,4224]{1,0:T(8,128)(2,1)S(1)} %pad_maximum_fusion.refs_0_), channel_id=1, source_target_pairs={{0,2},{1,3},{2,0},{3,1},{4,6},{5,7},{6,4},{7,5},{8,10},{9,11},{10,... | collective-permute-start | bytes 405512 | tf_op jit(solution)/shard_map/ppermute | solution.py:103
  25.0 1.8 %collective-permute-start.6 = (bf16[16,4224]{1,0:T(8,128)(2,1)S(1)}, bf16[16,4224]{1,0:T(8,128)(2,1)}, u32[]{:S(2)}, u32[]{:S(2)}) collective-permute-start(bf16[16,4224]{1,0:T(8,128)(2,1)S(1)} %pad_maximum_fusion.refs_0_), channel_id=1, source_target_pairs={{0,4},{1,5},{2,6},{3,7},{4,0},{5,1},{6,2},{7,3},{8,12},{9,13},{10,... | collective-permute-start | bytes 405512 | tf_op jit(solution)/shard_map/ppermute | solution.py:103
  26.8 1.5 %collective-permute-start.8 = (bf16[16,4224]{1,0:T(8,128)(2,1)S(1)}, bf16[16,4224]{1,0:T(8,128)(2,1)}, u32[]{:S(2)}, u32[]{:S(2)}) collective-permute-start(bf16[16,4224]{1,0:T(8,128)(2,1)S(1)} %pad_maximum_fusion.refs_0_), channel_id=1, source_target_pairs={{0,6},{1,7},{2,4},{3,5},{4,2},{5,3},{6,0},{7,1},{8,14},{9,15},{10,... | collective-permute-start | bytes 405512 | tf_op jit(solution)/shard_map/ppermute | solution.py:103
  32.1 1.7 %collective-permute-done.8.refs_3_ = bf16[16,4224]{1,0:T(8,128)(2,1)} collective-permute-done((bf16[16,4224]{1,0:T(8,128)(2,1)S(1)}, bf16[16,4224]{1,0:T(8,128)(2,1)}, u32[]{:S(2)}, u32[]{:S(2)}) %collective-permute-start.8) | collective-permute-done | bytes 135200 | tf_op jit(solution)/shard_map/ppermute | solution.py:103
  35.6 1.7 %shard_map.112 = (bf16[64,4224]{1,0:T(8,128)(2,1)S(1)}, f32[64,192]{1,0:T(8,128)S(1)}) custom-call(bf16[16,4224]{1,0:T(8,128)(2,1)S(1)} %pad_maximum_fusion.refs_0_, bf16[16,4224]{1,0:T(8,128)(2,1)S(1)} %collective-permute-done.4.refs_1_, bf16[16,4224]{1,0:T(8,128)(2,1)} %collective-permute-done.6.refs_2_, bf16[16,4224]{1,0:T(8,128)(2,1)} %collective-permute-done.8.refs_3_, ...), custom_call_target="tpu_custom_call" | custom-call | flops 100663296 | bytes 4194304 | tf_op jit(solution)/shard_map/pallas_call | solution.py:110
  38.3 2.2 %shard_map.113 = (bf16[128,4096]{1,0:T(8,128)(2,1)S(1)}, f32[128,192]{1,0:T(8,128)S(1)}, f32[128,192]{1,0:T(8,128)S(1)}, f32[128,192]{1,0:T(8,128)S(1)}) custom-call(bf16[16,4096]{1,0:T(8,128)(2,1)S(1)} %pad_maximum_fusion.1.refs_0_, bf16[16,4096]{1,0:T(8,128)(2,1)S(1)} %copy-done.6, bf16[16,4096]{1,0:T(8,128)(2,1)S(1)} %copy-done.8, ...), custom_call_target="tpu_custom_call" | custom-call | flops 402653184 | bytes 4194304 | tf_op jit(solution)/shard_map/pallas_call | solution.py:110
  40.6 1.6 %shard_map.114 = (bf16[64,4224]{1,0:T(8,128)(2,1)S(1)}, f32[128,128]{1,0:T(8,128)S(1)}, bf16[128,192]{1,0:T(8,128)(2,1)S(1)}, bf16[64,4096]{1,0:T(8,128)(2,1)S(1)}) custom-call(bf16[16,4224]{1,0:T(8,128)(2,1)} %collective-permute-done.3.refs_0_, bf16[16,4224]{1,0:T(8,128)(2,1)} %collective-permute-done.5.refs_1_, ...), custom_call_target="tpu_custom_call" | custom-call | flops 100663296 | bytes 4194304 | tf_op jit(solution)/shard_map/pallas_call | solution.py:110
  42.8 1.9 %shard_map.116 = (bf16[128,192]{1,0:T(8,128)(2,1)S(1)}, bf16[128,192]{1,0:T(8,128)(2,1)S(1)}, bf16[64,4096]{1,0:T(8,128)(2,1)S(1)}) custom-call(bf16[64,4224]{1,0:T(8,128)(2,1)S(1)} %get-tuple-element.50.dy_ref.other_ref, f32[64,192]{1,0:T(8,128)S(1)} %get-tuple-element.51.own_ref, f32[128,128]{1,0:T(8,128)S(1)} %get-tuple-element.52.weight_ref, ...), custom_call_target="tpu_custom_call" | custom-call | flops 301989888 | bytes 4194304 | tf_op jit(solution)/shard_map/pallas_call | solution.py:110
  45.1 1.6 %collective-permute-start.23 = (bf16[16,4096]{1,0:T(8,128)(2,1)S(1)}, bf16[16,4096]{1,0:T(8,128)(2,1)S(1)}, u32[]{:S(2)}, u32[]{:S(2)}) collective-permute-start(bf16[16,4096]{1,0:T(8,128)(2,1)S(1)} %get-tuple-element.49), channel_id=1, source_target_pairs={{0,6},{1,7},{2,4},{3,5},{4,2},{5,3},{6,0},{7,1},{8,14},{9,15},{10,... | collective-permute-start | bytes 393224 | tf_op jit(solution)/shard_map/ppermute | solution.py:103
  47.2 1.5 %collective-permute-start.21 = (bf16[16,4096]{1,0:T(8,128)(2,1)S(1)}, bf16[16,4096]{1,0:T(8,128)(2,1)S(1)}, u32[]{:S(2)}, u32[]{:S(2)}) collective-permute-start(bf16[16,4096]{1,0:T(8,128)(2,1)S(1)} %get-tuple-element.47), channel_id=1, source_target_pairs={{0,2},{1,3},{2,0},{3,1},{4,6},{5,7},{6,4},{7,5},{8,10},{9,11},{10,... | collective-permute-start | bytes 393224 | tf_op jit(solution)/shard_map/ppermute | solution.py:103
  48.7 2.1 %shard_map.119 = bf16[1,192,4096]{2,1,0:T(8,128)(2,1)} custom-call(bf16[128,192]{1,0:T(8,128)(2,1)S(1)} %get-tuple-element.44.scaled_ref, bf16[64,4224]{1,0:T(8,128)(2,1)S(1)} %get-tuple-element.39.refs_4_.own_ref, bf16[64,4224]{1,0:T(8,128)(2,1)S(1)} %get-tuple-element.50.dy_ref.other_ref), custom_call_target="tpu_custom_call" | custom-call | flops 201326592 | bytes 4194304 | tf_op jit(solution)/shard_map/pallas_call | solution.py:110
  50.8 2.4 %shard_map.118 = (bf16[1,192,4096]{2,1,0:T(8,128)(2,1)}, bf16[1,192,4096]{2,1,0:T(8,128)(2,1)}) custom-call(bf16[128,192]{1,0:T(8,128)(2,1)S(1)} %get-tuple-element.55.gate_act_ref, bf16[128,192]{1,0:T(8,128)(2,1)S(1)} %get-tuple-element.56.up_act_ref, bf16[128,4096]{1,0:T(8,128)(2,1)S(1)} %get-tuple-element.62.x_ref), custom_call_target="tpu_custom_call" | custom-call | flops 402653184 | bytes 4194304 | tf_op jit(solution)/shard_map/pallas_call | solution.py:110
  54.0 1.6 %collective-permute-start.30 = (bf16[16,4096]{1,0:T(8,128)(2,1)S(1)}, bf16[16,4096]{1,0:T(8,128)(2,1)S(1)}, u32[]{:S(2)}, u32[]{:S(2)}) collective-permute-start(bf16[16,4096]{1,0:T(8,128)(2,1)S(1)} %get-tuple-element.61), channel_id=1, source_target_pairs={{0,6},{1,7},{2,4},{3,5},{4,2},{5,3},{6,0},{7,1},{8,14},{9,15},{10,... | collective-permute-start | bytes 393224 | tf_op jit(solution)/shard_map/ppermute | solution.py:103
  56.1 1.5 %collective-permute-start.28 = (bf16[16,4096]{1,0:T(8,128)(2,1)S(1)}, bf16[16,4096]{1,0:T(8,128)(2,1)S(1)}, u32[]{:S(2)}, u32[]{:S(2)}) collective-permute-start(bf16[16,4096]{1,0:T(8,128)(2,1)S(1)} %get-tuple-element.59), channel_id=1, source_target_pairs={{0,2},{1,3},{2,0},{3,1},{4,6},{5,7},{6,4},{7,5},{8,10},{9,11},{10,... | collective-permute-start | bytes 393224 | tf_op jit(solution)/shard_map/ppermute | solution.py:103
  57.7 3.6 %collective-permute-start.26 = (bf16[4,4096]{1,0:T(4,128)(2,1)S(1)}, bf16[4,4096]{1,0:T(4,128)(2,1)S(1)}, u32[]{:S(2)}, u32[]{:S(2)}) collective-permute-start(bf16[4,4096]{1,0:T(4,128)(2,1)S(1)} %get-tuple-element.69), channel_id=1, source_target_pairs={{0,24},{1,25},{2,26},{3,27},{4,28},{5,29},{6,30},{7,31},{8,16},{9,... | collective-permute-start | bytes 98312 | tf_op jit(solution)/shard_map/ppermute | solution.py:103
  62.9 3.6 %collective-permute-start.33 = (bf16[4,4096]{1,0:T(4,128)(2,1)S(1)}, bf16[4,4096]{1,0:T(4,128)(2,1)S(1)}, u32[]{:S(2)}, u32[]{:S(2)}) collective-permute-start(bf16[4,4096]{1,0:T(4,128)(2,1)S(1)} %get-tuple-element.66), channel_id=1, source_target_pairs={{0,24},{1,25},{2,26},{3,27},{4,28},{5,29},{6,30},{7,31},{8,16},{9,... | collective-permute-start | bytes 98312 | tf_op jit(solution)/shard_map/ppermute | solution.py:103
  68.8 2.6 %collective-permute-done.32 = bf16[4,4096]{1,0:T(4,128)(2,1)S(1)} collective-permute-done((bf16[4,4096]{1,0:T(4,128)(2,1)S(1)}, bf16[4,4096]{1,0:T(4,128)(2,1)S(1)}, u32[]{:S(2)}, u32[]{:S(2)}) %collective-permute-start.32) | collective-permute-done | bytes 32800 | tf_op jit(solution)/shard_map/ppermute | solution.py:103
  (99 shorter events, 20.2 us)
Async XLA Ops:
  0.6 17.4 %collective-permute-start.12 = (bf16[4,4096]{1,0:T(4,128)(2,1)}, bf16[4,4096]{1,0:T(4,128)(2,1)S(1)}, u32[]{:S(2)}, u32[]{:S(2)}) collective-permute-start(bf16[4,4096]{1,0:T(4,128)(2,1)} %param.7), channel_id=1, source_target_pairs={{0,24},{1,25},{2,26},{3,27},{4,28},{5,29},{6,30},{7,31},{8,16},{9,... | collective-permute-start | bytes 98312 | tf_op jit(solution)/shard_map/ppermute | solution.py:103
  5.7 13.0 %collective-permute-start.11 = (bf16[4,4096]{1,0:T(4,128)(2,1)}, bf16[4,4096]{1,0:T(4,128)(2,1)S(1)}, u32[]{:S(2)}, u32[]{:S(2)}) collective-permute-start(bf16[4,4096]{1,0:T(4,128)(2,1)} %param.7), channel_id=1, source_target_pairs={{0,16},{1,17},{2,18},{3,19},{4,20},{5,21},{6,22},{7,23},{8,24},{9,... | collective-permute-start | bytes 98312 | tf_op jit(solution)/shard_map/ppermute | solution.py:103
  5.7 13.0 %collective-permute-start.10 = (bf16[4,4096]{1,0:T(4,128)(2,1)}, bf16[4,4096]{1,0:T(4,128)(2,1)S(1)}, u32[]{:S(2)}, u32[]{:S(2)}) collective-permute-start(bf16[4,4096]{1,0:T(4,128)(2,1)} %param.7), channel_id=1, source_target_pairs={{0,8},{1,9},{2,10},{3,11},{4,12},{5,13},{6,14},{7,15},{8,0},{9,1},... | collective-permute-start | bytes 98312 | tf_op jit(solution)/shard_map/ppermute | solution.py:103
  8.6 13.4 %collective-permute-start.2 = (bf16[4,4224]{1,0:T(4,128)(2,1)S(1)}, bf16[4,4224]{1,0:T(4,128)(2,1)S(1)}, u32[]{:S(2)}, u32[]{:S(2)}) collective-permute-start(bf16[4,4224]{1,0:T(4,128)(2,1)S(1)} %shard_map.110), channel_id=1, source_target_pairs={{0,24},{1,25},{2,26},{3,27},{4,28},{5,29},{6,30},{7,31},{8,16},{9,... | collective-permute-start | bytes 101384 | tf_op jit(solution)/shard_map/ppermute | solution.py:103
  12.3 10.0 %collective-permute-start.1 = (bf16[4,4224]{1,0:T(4,128)(2,1)S(1)}, bf16[4,4224]{1,0:T(4,128)(2,1)S(1)}, u32[]{:S(2)}, u32[]{:S(2)}) collective-permute-start(bf16[4,4224]{1,0:T(4,128)(2,1)S(1)} %shard_map.110), channel_id=1, source_target_pairs={{0,16},{1,17},{2,18},{3,19},{4,20},{5,21},{6,22},{7,23},{8,24},{9,... | collective-permute-start | bytes 101384 | tf_op jit(solution)/shard_map/ppermute | solution.py:103
  18.8 6.2 %collective-permute-start.13 = (bf16[16,4096]{1,0:T(8,128)(2,1)S(1)}, bf16[16,4096]{1,0:T(8,128)(2,1)S(1)}, u32[]{:S(2)}, u32[]{:S(2)}) collective-permute-start(bf16[16,4096]{1,0:T(8,128)(2,1)S(1)} %pad_maximum_fusion.1.refs_0_), channel_id=1, source_target_pairs={{0,2},{1,3},{2,0},{3,1},{4,6},{5,7},{6,4},{7,5},{8,10},{9,11},{10,... | collective-permute-start | bytes 393224 | tf_op jit(solution)/shard_map/ppermute | solution.py:103
  20.5 6.3 %collective-permute-start.14 = (bf16[16,4096]{1,0:T(8,128)(2,1)S(1)}, bf16[16,4096]{1,0:T(8,128)(2,1)S(1)}, u32[]{:S(2)}, u32[]{:S(2)}) collective-permute-start(bf16[16,4096]{1,0:T(8,128)(2,1)S(1)} %pad_maximum_fusion.1.refs_0_), channel_id=1, source_target_pairs={{0,4},{1,5},{2,6},{3,7},{4,0},{5,1},{6,2},{7,3},{8,12},{9,13},{10,... | collective-permute-start | bytes 393224 | tf_op jit(solution)/shard_map/ppermute | solution.py:103
  22.0 7.1 %collective-permute-start.15 = (bf16[16,4096]{1,0:T(8,128)(2,1)S(1)}, bf16[16,4096]{1,0:T(8,128)(2,1)}, u32[]{:S(2)}, u32[]{:S(2)}) collective-permute-start(bf16[16,4096]{1,0:T(8,128)(2,1)S(1)} %pad_maximum_fusion.1.refs_0_), channel_id=1, source_target_pairs={{0,6},{1,7},{2,4},{3,5},{4,2},{5,3},{6,0},{7,1},{8,14},{9,15},{10,... | collective-permute-start | bytes 393224 | tf_op jit(solution)/shard_map/ppermute | solution.py:103
  22.4 7.4 %collective-permute-start.16 = (bf16[16,4096]{1,0:T(8,128)(2,1)S(1)}, bf16[16,4096]{1,0:T(8,128)(2,1)S(1)}, u32[]{:S(2)}, u32[]{:S(2)}) collective-permute-start(bf16[16,4096]{1,0:T(8,128)(2,1)S(1)} %pad_maximum_fusion.1.refs_0_), channel_id=1, source_target_pairs={{0,1},{1,0},{2,3},{3,2},{4,5},{5,4},{6,7},{7,6},{8,9},{9,8},{10,11... | collective-permute-start | bytes 393224 | tf_op jit(solution)/shard_map/ppermute | solution.py:103
  22.5 9.1 %collective-permute-start.4 = (bf16[16,4224]{1,0:T(8,128)(2,1)S(1)}, bf16[16,4224]{1,0:T(8,128)(2,1)S(1)}, u32[]{:S(2)}, u32[]{:S(2)}) collective-permute-start(bf16[16,4224]{1,0:T(8,128)(2,1)S(1)} %pad_maximum_fusion.refs_0_), channel_id=1, source_target_pairs={{0,2},{1,3},{2,0},{3,1},{4,6},{5,7},{6,4},{7,5},{8,10},{9,11},{10,... | collective-permute-start | bytes 405512 | tf_op jit(solution)/shard_map/ppermute | solution.py:103
  25.0 6.6 %collective-permute-start.6 = (bf16[16,4224]{1,0:T(8,128)(2,1)S(1)}, bf16[16,4224]{1,0:T(8,128)(2,1)}, u32[]{:S(2)}, u32[]{:S(2)}) collective-permute-start(bf16[16,4224]{1,0:T(8,128)(2,1)S(1)} %pad_maximum_fusion.refs_0_), channel_id=1, source_target_pairs={{0,4},{1,5},{2,6},{3,7},{4,0},{5,1},{6,2},{7,3},{8,12},{9,13},{10,... | collective-permute-start | bytes 405512 | tf_op jit(solution)/shard_map/ppermute | solution.py:103
  26.8 7.0 %collective-permute-start.8 = (bf16[16,4224]{1,0:T(8,128)(2,1)S(1)}, bf16[16,4224]{1,0:T(8,128)(2,1)}, u32[]{:S(2)}, u32[]{:S(2)}) collective-permute-start(bf16[16,4224]{1,0:T(8,128)(2,1)S(1)} %pad_maximum_fusion.refs_0_), channel_id=1, source_target_pairs={{0,6},{1,7},{2,4},{3,5},{4,2},{5,3},{6,0},{7,1},{8,14},{9,15},{10,... | collective-permute-start | bytes 405512 | tf_op jit(solution)/shard_map/ppermute | solution.py:103
  31.6 9.0 %collective-permute-start.3 = (bf16[16,4224]{1,0:T(8,128)(2,1)S(1)}, bf16[16,4224]{1,0:T(8,128)(2,1)}, u32[]{:S(2)}, u32[]{:S(2)}) collective-permute-start(bf16[16,4224]{1,0:T(8,128)(2,1)S(1)} %pad_maximum_fusion.refs_0_), channel_id=1, source_target_pairs={{0,1},{1,0},{2,3},{3,2},{4,5},{5,4},{6,7},{7,6},{8,9},{9,8},{10,11... | collective-permute-start | bytes 405512 | tf_op jit(solution)/shard_map/ppermute | solution.py:103
  33.8 6.7 %collective-permute-start.5 = (bf16[16,4224]{1,0:T(8,128)(2,1)S(1)}, bf16[16,4224]{1,0:T(8,128)(2,1)}, u32[]{:S(2)}, u32[]{:S(2)}) collective-permute-start(bf16[16,4224]{1,0:T(8,128)(2,1)S(1)} %collective-permute-done.4.refs_1_), channel_id=1, source_target_pairs={{0,1},{1,0},{2,3},{3,2},{4,5},{5,4},{6,7},{7,6},{8,9},{9,8},{10,11... | collective-permute-start | bytes 405512 | tf_op jit(solution)/shard_map/ppermute | solution.py:103
  34.4 6.1 %collective-permute-start.7 = (bf16[16,4224]{1,0:T(8,128)(2,1)}, bf16[16,4224]{1,0:T(8,128)(2,1)}, u32[]{:S(2)}, u32[]{:S(2)}) collective-permute-start(bf16[16,4224]{1,0:T(8,128)(2,1)} %collective-permute-done.6.refs_2_), channel_id=1, source_target_pairs={{0,1},{1,0},{2,3},{3,2},{4,5},{5,4},{6,7},{7,6},{8,9},{9,8},{10,11... | collective-permute-start | bytes 405512 | tf_op jit(solution)/shard_map/ppermute | solution.py:103
  44.6 8.7 %collective-permute-start.27 = (bf16[64,4096]{1,0:T(8,128)(2,1)S(1)}, bf16[64,4096]{1,0:T(8,128)(2,1)S(1)}, u32[]{:S(2)}, u32[]{:S(2)}) collective-permute-start(bf16[64,4096]{1,0:T(8,128)(2,1)S(1)} %get-tuple-element.57), channel_id=1, source_target_pairs={{0,1},{1,0},{2,3},{3,2},{4,5},{5,4},{6,7},{7,6},{8,9},{9,8},{10,11... | collective-permute-start | bytes 1572872 | tf_op jit(solution)/shard_map/ppermute | solution.py:103
  45.1 11.0 %collective-permute-start.23 = (bf16[16,4096]{1,0:T(8,128)(2,1)S(1)}, bf16[16,4096]{1,0:T(8,128)(2,1)S(1)}, u32[]{:S(2)}, u32[]{:S(2)}) collective-permute-start(bf16[16,4096]{1,0:T(8,128)(2,1)S(1)} %get-tuple-element.49), channel_id=1, source_target_pairs={{0,6},{1,7},{2,4},{3,5},{4,2},{5,3},{6,0},{7,1},{8,14},{9,15},{10,... | collective-permute-start | bytes 393224 | tf_op jit(solution)/shard_map/ppermute | solution.py:103
  46.7 10.8 %collective-permute-start.22 = (bf16[16,4096]{1,0:T(8,128)(2,1)S(1)}, bf16[16,4096]{1,0:T(8,128)(2,1)S(1)}, u32[]{:S(2)}, u32[]{:S(2)}) collective-permute-start(bf16[16,4096]{1,0:T(8,128)(2,1)S(1)} %get-tuple-element.48), channel_id=1, source_target_pairs={{0,4},{1,5},{2,6},{3,7},{4,0},{5,1},{6,2},{7,3},{8,12},{9,13},{10,... | collective-permute-start | bytes 393224 | tf_op jit(solution)/shard_map/ppermute | solution.py:103
  47.2 10.3 %collective-permute-start.21 = (bf16[16,4096]{1,0:T(8,128)(2,1)S(1)}, bf16[16,4096]{1,0:T(8,128)(2,1)S(1)}, u32[]{:S(2)}, u32[]{:S(2)}) collective-permute-start(bf16[16,4096]{1,0:T(8,128)(2,1)S(1)} %get-tuple-element.47), channel_id=1, source_target_pairs={{0,2},{1,3},{2,0},{3,1},{4,6},{5,7},{6,4},{7,5},{8,10},{9,11},{10,... | collective-permute-start | bytes 393224 | tf_op jit(solution)/shard_map/ppermute | solution.py:103
  54.0 7.4 %collective-permute-start.30 = (bf16[16,4096]{1,0:T(8,128)(2,1)S(1)}, bf16[16,4096]{1,0:T(8,128)(2,1)S(1)}, u32[]{:S(2)}, u32[]{:S(2)}) collective-permute-start(bf16[16,4096]{1,0:T(8,128)(2,1)S(1)} %get-tuple-element.61), channel_id=1, source_target_pairs={{0,6},{1,7},{2,4},{3,5},{4,2},{5,3},{6,0},{7,1},{8,14},{9,15},{10,... | collective-permute-start | bytes 393224 | tf_op jit(solution)/shard_map/ppermute | solution.py:103
  55.6 7.0 %collective-permute-start.29 = (bf16[16,4096]{1,0:T(8,128)(2,1)S(1)}, bf16[16,4096]{1,0:T(8,128)(2,1)S(1)}, u32[]{:S(2)}, u32[]{:S(2)}) collective-permute-start(bf16[16,4096]{1,0:T(8,128)(2,1)S(1)} %get-tuple-element.60), channel_id=1, source_target_pairs={{0,4},{1,5},{2,6},{3,7},{4,0},{5,1},{6,2},{7,3},{8,12},{9,13},{10,... | collective-permute-start | bytes 393224 | tf_op jit(solution)/shard_map/ppermute | solution.py:103
  56.1 6.7 %collective-permute-start.28 = (bf16[16,4096]{1,0:T(8,128)(2,1)S(1)}, bf16[16,4096]{1,0:T(8,128)(2,1)S(1)}, u32[]{:S(2)}, u32[]{:S(2)}) collective-permute-start(bf16[16,4096]{1,0:T(8,128)(2,1)S(1)} %get-tuple-element.59), channel_id=1, source_target_pairs={{0,2},{1,3},{2,0},{3,1},{4,6},{5,7},{6,4},{7,5},{8,10},{9,11},{10,... | collective-permute-start | bytes 393224 | tf_op jit(solution)/shard_map/ppermute | solution.py:103
  57.7 8.9 %collective-permute-start.26 = (bf16[4,4096]{1,0:T(4,128)(2,1)S(1)}, bf16[4,4096]{1,0:T(4,128)(2,1)S(1)}, u32[]{:S(2)}, u32[]{:S(2)}) collective-permute-start(bf16[4,4096]{1,0:T(4,128)(2,1)S(1)} %get-tuple-element.69), channel_id=1, source_target_pairs={{0,24},{1,25},{2,26},{3,27},{4,28},{5,29},{6,30},{7,31},{8,16},{9,... | collective-permute-start | bytes 98312 | tf_op jit(solution)/shard_map/ppermute | solution.py:103
  61.3 6.1 %collective-permute-start.25 = (bf16[4,4096]{1,0:T(4,128)(2,1)S(1)}, bf16[4,4096]{1,0:T(4,128)(2,1)S(1)}, u32[]{:S(2)}, u32[]{:S(2)}) collective-permute-start(bf16[4,4096]{1,0:T(4,128)(2,1)S(1)} %get-tuple-element.70), channel_id=1, source_target_pairs={{0,16},{1,17},{2,18},{3,19},{4,20},{5,21},{6,22},{7,23},{8,24},{9,... | collective-permute-start | bytes 98312 | tf_op jit(solution)/shard_map/ppermute | solution.py:103
  (28 other events, 78.5 us)

commit v4 on v0

--- a/solution.py
+++ b/solution.py
@@ -1,9 +1,14 @@
+import functools
+
 import jax
 import jax.numpy as jnp
 from jax import lax
+from jax.experimental import pallas as pl
+from jax.experimental.pallas import tpu as pltpu
 from jax.sharding import PartitionSpec as P
 
 ROW_CAP = 16
+AXES = ("dp", "expert")
 
 
 def contract_rows(left, right):
@@ -18,7 +23,7 @@
     )
 
 
-def shards(tokens, expert_ids, route_weights, out_grad, gate_weight, up_weight, down_weight):
+def slotted(tokens, expert_ids, route_weights, out_grad, gate_weight, up_weight, down_weight):
     expert = lax.axis_index("expert")
     width = tokens.shape[1]
     local_tokens = tokens.shape[0]
@@ -88,6 +93,275 @@
     )
 
 
+CORE, FIRST, SECOND = 1, 2, 4
+
+
+def from_xor(value, mask, devices):
+    return lax.ppermute(value, AXES, [(i, i ^ mask) for i in range(devices)])
+
+
+def kernel_call(body, out_shape, cost, *operands, scratch=(), hbm=()):
+    vmem, smem = pl.BlockSpec(memory_space=pltpu.VMEM), pl.BlockSpec(memory_space=pltpu.SMEM)
+    stay = pl.BlockSpec(memory_space=pltpu.HBM)
+    specs = [stay if i in hbm else smem if o.ndim == 1 else vmem for i, o in enumerate(operands)]
+    operands = [
+        pltpu.with_memory_space_constraint(o, pltpu.HBM) if i in hbm else o
+        for i, o in enumerate(operands)
+    ]
+    return pl.pallas_call(
+        body,
+        out_shape=out_shape,
+        in_specs=specs,
+        out_specs=jax.tree.map(lambda _: vmem, out_shape),
+        scratch_shapes=scratch,
+        compiler_params=pltpu.CompilerParams(vmem_limit_bytes=24 << 20),
+        cost_estimate=pl.CostEstimate(flops=cost, bytes_accessed=4 << 20, transcendentals=0),
+    )(*operands)
+
+
+def copy_all(pairs, sems):
+    copies = [pltpu.make_async_copy(src, dst, sems.at[i]) for i, (src, dst) in enumerate(pairs)]
+    for copy in copies:
+        copy.start()
+    for copy in copies:
+        copy.wait()
+
+
+def load_body(*refs):
+    count = len(refs) // 2
+    copy_all(list(zip(refs[:count], refs[count:-1])), refs[-1])
+
+
+def pack_body(x_ref, dy_ref, ids_ref, w_ref, msg_ref, x_buf, dy_buf, sems):
+    rows, width = x_ref.shape
+    top = ids_ref.shape[0]
+    lanes = msg_ref.shape[1] - 2 * width
+    copy_all([(x_ref, x_buf), (dy_ref, dy_buf)], sems)
+    msg_ref[:, :width] = x_buf[...]
+    msg_ref[:, width : 2 * width] = dy_buf[...]
+    diagonal = lax.broadcasted_iota(jnp.int32, (rows, rows), 0) == lax.broadcasted_iota(
+        jnp.int32, (rows, rows), 1
+    )
+    expert = lax.broadcasted_iota(jnp.int32, (rows, lanes), 1)
+    route = jnp.zeros((rows, lanes), jnp.float32)
+    for k in range(top):
+        named = jnp.sum(jnp.where(diagonal, ids_ref[k : k + 1, :], 0), axis=1, keepdims=True)
+        weight = jnp.sum(jnp.where(diagonal, w_ref[k : k + 1, :], 0.0), axis=1, keepdims=True)
+        route = route + jnp.where(expert == named, weight, 0.0)
+    msg_ref[:, 2 * width :] = route.astype(jnp.bfloat16)
+
+
+def passes(have, wg_ref, wu_ref, wd_ref, expert_ref, acts_ref):
+    width, ff = wg_ref.shape[2], wg_ref.shape[1]
+    x, dy, route = have[:, :width], have[:, width : 2 * width], have[:, 2 * width :]
+    lanes = route.shape[1]
+    mine = lax.broadcasted_iota(jnp.int32, (8, lanes), 1) == expert_ref[0]
+    weight = contract_rows(mine.astype(jnp.float32).astype(jnp.bfloat16), route)[:1, :]
+    gate_pre = contract_rows(wg_ref[0], x)
+    up_pre = contract_rows(wu_ref[0], x)
+    hidden_grad = weight * contract_rows(wd_ref[0], dy)
+    gate_sig = 1.0 / (1.0 + jnp.exp(-gate_pre))
+    silu_gate = gate_pre * gate_sig
+    silu_slope = gate_sig * (1.0 + gate_pre * (1.0 - gate_sig))
+    acts_ref[:ff, :] = (hidden_grad * up_pre * silu_slope).astype(jnp.bfloat16)
+    acts_ref[ff : 2 * ff, :] = (hidden_grad * silu_gate).astype(jnp.bfloat16)
+    acts_ref[2 * ff :, :] = (weight * (silu_gate * up_pre)).astype(jnp.bfloat16)
+    out = contract_first(acts_ref[2 * ff :, :], wd_ref[0])
+    into = contract_first(acts_ref[:ff, :], wg_ref[0]) + contract_first(
+        acts_ref[ff : 2 * ff, :], wu_ref[0]
+    )
+    return out, into
+
+
+def give(out, into, own_ref, msg_ref):
+    half, width = own_ref.shape[0], out.shape[1]
+    for i, value in enumerate((out, into)):
+        own_ref[:, i * width : (i + 1) * width] = value[:half, :]
+        msg_ref[:, i * width : (i + 1) * width] = value[half:, :].astype(jnp.bfloat16)
+
+
+def early_body(count, *refs):
+    pieces, rest = refs[:count], refs[count:]
+    wg_ref, wu_ref, wd_ref, expert_ref, have, acts_ref, own_ref, msg_ref = rest
+    rows = pieces[0].shape[0]
+    for i, piece in enumerate(pieces):
+        have[i * rows : (i + 1) * rows, :] = piece[...]
+    out, into = passes(have, wg_ref, wu_ref, wd_ref, expert_ref, acts_ref)
+    give(out, into, own_ref, msg_ref)
+
+
+def late_body(*refs):
+    pieces, rest = refs[:4], refs[4:]
+    wg_ref, wu_ref, wd_ref, expert_ref, have, acts_ref, own_ref, msg_ref = rest
+    rows, width = pieces[0].shape
+    for i in range(2):
+        have[i * rows : (i + 1) * rows, :width] = pieces[2 * i][...]
+        have[i * rows : (i + 1) * rows, width:] = pieces[2 * i + 1][...]
+    out, into = passes(have, wg_ref, wu_ref, wd_ref, expert_ref, acts_ref)
+    give(out, into, own_ref, msg_ref)
+
+
+def late_sum_body(own_ref, passed_ref, out_ref, into_ref):
+    width = out_ref.shape[1]
+    total = own_ref[...] + passed_ref[...].astype(jnp.float32)
+    out_ref[...] = total[:, :width].astype(jnp.bfloat16)
+    into_ref[...] = total[:, width:].astype(jnp.bfloat16)
+
+
+def early_sum_body(own_ref, passed_ref, into_ref, out_ref, here_ref, first_ref, second_ref):
+    rows, width = into_ref.shape
+
+    def total(i, side):
+        at = (slice(i * rows, (i + 1) * rows), slice(side * width, (side + 1) * width))
+        return own_ref[at] + passed_ref[at].astype(jnp.float32)
+
+    here_ref[:, :width], here_ref[:, width:] = total(0, 0), total(0, 1)
+    second_ref[:, :width] = total(1, 0).astype(jnp.bfloat16)
+    second_ref[:, width:] = (total(1, 1) + into_ref[...].astype(jnp.float32)).astype(jnp.bfloat16)
+    first_ref[:, :width] = (total(2, 0) + out_ref[...].astype(jnp.float32)).astype(jnp.bfloat16)
+    first_ref[:, width:] = total(2, 1).astype(jnp.bfloat16)
+
+
+def grad_body(early_ref, late_ref, early_acts_ref, late_acts_ref, *grads):
+    width = grads[0].shape[2]
+    ff = grads[0].shape[1]
+    for i, ref in enumerate(grads):
+        first = early_acts_ref.shape[0] // ff - len(grads) if len(grads) == 1 else 0
+        here = slice((first + i) * ff, (first + i + 1) * ff)
+        side = slice(width, 2 * width) if len(grads) == 1 else slice(0, width)
+        ref[0] = (
+            jnp.dot(early_acts_ref[here, :], early_ref[:, side], preferred_element_type=jnp.float32)
+            + jnp.dot(late_acts_ref[here, :], late_ref[:, side], preferred_element_type=jnp.float32)
+        ).astype(jnp.bfloat16)
+
+
+def dense(tokens, expert_ids, route_weights, out_grad, gate_weight, up_weight, down_weight):
+    experts = lax.axis_size("expert")
+    devices = lax.axis_size("dp") * experts
+    expert = lax.axis_index("expert").astype(jnp.int32).reshape(1)
+    rows, width = tokens.shape
+    ff = gate_weight.shape[1]
+    near = tuple(k << 3 for k in range(1, devices >> 3))
+    block_rows = rows * (len(near) + 1)
+    bf16, f32 = jnp.bfloat16, jnp.float32
+    columns = 2 * width + experts + -experts % 128
+    unit = 2 * block_rows * ff * width
+
+    def shape(*dims, dtype=bf16):
+        return jax.ShapeDtypeStruct(dims, dtype)
+
+    def passed(value, mask):
+        return from_xor(value, mask, devices)
+
+    message = kernel_call(
+        pack_body,
+        shape(rows, columns),
+        0,
+        tokens,
+        out_grad,
+        expert_ids.T,
+        route_weights.astype(f32).T,
+        scratch=[
+            pltpu.VMEM((rows, width), bf16),
+            pltpu.VMEM((rows, width), bf16),
+            pltpu.SemaphoreType.DMA((2,)),
+        ],
+        hbm=(0, 1),
+    )
+    weights = kernel_call(
+        load_body,
+        (shape(*gate_weight.shape),) * 3,
+        0,
+        gate_weight,
+        up_weight,
+        down_weight,
+        scratch=[pltpu.SemaphoreType.DMA((3,))],
+        hbm=(0, 1, 2),
+    )
+    block = jnp.concatenate([message] + [passed(message, m) for m in near], axis=0)
+    block, *weights = lax.optimization_barrier((block, *weights))
+
+    by_second, by_first = passed(block, SECOND), passed(block, FIRST)
+    corner_x = passed(by_second[:, :width], FIRST)
+    corner_dy = passed(by_first[:, width:], SECOND)
+    own = [block, by_second, by_first]
+    other = [passed(piece, CORE) for piece in own]
+    corner = [corner_x, corner_dy, passed(corner_x, CORE), passed(corner_dy, CORE)]
+
+    early_rows = len(own) * block_rows
+    early, early_acts, early_own, message = kernel_call(
+        functools.partial(early_body, 2 * len(own)),
+        (
+            shape(2 * early_rows, columns),
+            shape(3 * ff, 2 * early_rows),
+            shape(early_rows, 2 * width, dtype=f32),
+            shape(early_rows, 2 * width),
+        ),
+        36 * unit,
+        *own,
+        *other,
+        *weights,
+        expert,
+    )
+    early_passed = passed(message, CORE)
+    late, late_acts, late_own, message = kernel_call(
+        late_body,
+        (
+            shape(2 * block_rows, columns),
+            shape(3 * ff, 2 * block_rows),
+            shape(block_rows, 2 * width, dtype=f32),
+            shape(block_rows, 2 * width),
+        ),
+        12 * unit,
+        *corner,
+        *weights,
+        expert,
+    )
+    late_passed = passed(message, CORE)
+
+    corner_out, corner_into = kernel_call(
+        late_sum_body, (shape(block_rows, width),) * 2, 0, late_own, late_passed
+    )
+    turned_out, turned_into = passed(corner_out, SECOND), passed(corner_into, FIRST)
+    here, for_first, for_second = kernel_call(
+        early_sum_body,
+        (
+            shape(block_rows, 2 * width, dtype=f32),
+            shape(block_rows, 2 * width),
+            shape(block_rows, 2 * width),
+        ),
+        0,
+        early_own,
+        early_passed,
+        turned_into,
+        turned_out,
+    )
+    total = here + passed(for_second, SECOND).astype(f32) + passed(for_first, FIRST).astype(f32)
+    total = total.astype(bf16)
+    pieces = [total[k * rows : (k + 1) * rows] for k in range(len(near) + 1)]
+    total = pieces[0].astype(f32)
+    for m, piece in zip(near, pieces[1:]):
+        total = total + passed(piece, m).astype(f32)
+    total = total.astype(bf16)
+
+    (grad_down,) = kernel_call(
+        grad_body, (shape(*down_weight.shape),), 8 * unit, early, late, early_acts, late_acts
+    )
+    grad_gate, grad_up = kernel_call(
+        grad_body, (shape(*gate_weight.shape),) * 2, 16 * unit, early, late, early_acts, late_acts
+    )
+    return total[:, :width], total[:, width:], grad_gate, grad_up, grad_down
+
+
+def shards(tokens, *others):
+    experts = lax.axis_size("expert")
+    devices = lax.axis_size("dp") * experts
+    whole_group = tokens.shape[0] * experts <= ROW_CAP
+    if whole_group and devices >= 16 and devices & (devices - 1) == 0:
+        return dense(tokens, *others)
+    return slotted(tokens, *others)
+
+
 def solution(mesh):
     return jax.shard_map(
         shards,

time: 254 us -> 71.1 us (0.28)
  waiting for transfers between devices: 185 us -> 26.1 us
  blocking collectives: 23.1 us -> 0 us
  matrix products: 20.2 us -> 0 us
  Pallas kernels: 0 us -> 16.2 us
  starting transfers between devices: 6.81 us -> 20.9 us
  between operations: 13.9 us -> 0.73 us
  local copies, waits for them, and re-layouts: 1.85 us -> 5.79 us
    reduce_scatter x2 -> x0, waiting for transfers between devices: 115 us -> none  [the longest x1 60.9 us: shards(): lax.psum_scatter((contract_first(gate_act, w_gate) + contract_first(up_ac...]
    all_gather x2 -> x0, waiting for transfers between devices: 67.1 us -> none  [the longest x1 37.3 us: shards(): all_dy = lax.all_gather(slot_dy, 'dp', axis=0, tiled=True)]
    ppermute x0 -> x21, waiting for transfers between devices: none -> 26.1 us  [from_xor(): return lax.ppermute(value, AXES, [(i, i ^ mask) for i in range(devices)])]
    all_gather x4 -> x0, blocking collectives: 23.1 us -> none  [the longest x1 6.85 us: shards(): lax.all_gather(tokens, 'expert', axis=0, tiled=True)]
    ppermute x0 -> x21, starting transfers between devices: none -> 20.9 us  [from_xor(): return lax.ppermute(value, AXES, [(i, i ^ mask) for i in range(devices)])]
    dot_general x13 -> x0, matrix products: 20.2 us -> none  [the longest x5 7.18 us: contract_first(): lax.dot_general(left, right, (((0,), (0,)), ((), ())), preferred_element_...]
    pallas_call x0 -> x8, Pallas kernels: none -> 16.2 us  [kernel_call(): pl.pallas_call(body, out_shape=out_shape, in_specs=specs, out_specs=jax.t...]
    all_to_all x2 -> x0, starting transfers between devices: 6.65 us -> none  [the longest x1 3.32 us: shards(): lax.all_to_all(back_in, 'expert', split_axis=0, concat_axis=0, tiled=True)]
  transfers between devices with their start and end apart: 6 -> 21, of which waited for: 5 -> 13; matrix products, arithmetic and copies ran while one was open for 7% -> 3% of each run, Pallas kernels for 0% -> 15%
where the time goes in v4:
time: 71.1 us; the launch traced here: 70.8 us
  waiting for transfers between devices  26.1 us (37%)
  starting transfers between devices  20.9 us (29%)
  Pallas kernels  16.2 us (23%)
  local copies, waits for them, and re-layouts  5.79 us (8%)
  other arithmetic  0.97 us (1%)
  between operations  0.73 us (1%)
    ppermute x21, waiting for transfers between devices, from_xor(): return lax.ppermute(value, AXES, [(i, i ^ mask) for i in range(devices)])  26.1 us
    ppermute x21, starting transfers between devices, from_xor(): return lax.ppermute(value, AXES, [(i, i ^ mask) for i in range(devices)])  20.9 us
    pallas_call x8, Pallas kernels, kernel_call(): pl.pallas_call(body, out_shape=out_shape, in_specs=specs, out_specs=jax.t...  16.2 us
    unnamed x8, local copies, waits for them, and re-layouts  3.23 us
  transfers between devices with their start and end apart: 21, of which 13 were waited for; matrix products, arithmetic and copies ran while one was open for 3% of the time, Pallas kernels for 15%

profile of v4, /device:TPU:0, one launch (start us, length us, event | category | flops | bytes accessed | tf_op | source)
XLA Modules:
  0.0 70.8 jit_solution(10570365578835369358)
XLA Ops:
  2.9 5.1 %collective-permute-start.2 = (bf16[4,8320]{1,0:T(4,128)(2,1)S(1)}, bf16[4,8320]{1,0:T(4,128)(2,1)S(1)}, u32[]{:S(2)}, u32[]{:S(2)}) collective-permute-start(bf16[4,8320]{1,0:T(4,128)(2,1)S(1)} %shard_map.110), channel_id=1, source_target_pairs={{0,24},{1,25},{2,26},{3,27},{4,28},{5,29},{6,30},{7,31},{8,16},{9,... | collective-permute-start | bytes 199688 | tf_op jit(solution)/shard_map/ppermute | solution.py:100
  8.6 2.4 %shard_map.111 = (bf16[1,192,4096]{2,1,0:T(8,128)(2,1)S(1)}, bf16[1,192,4096]{2,1,0:T(8,128)(2,1)S(1)}, bf16[1,192,4096]{2,1,0:T(8,128)(2,1)S(1)}) custom-call(bf16[1,192,4096]{2,1,0:T(8,128)(2,1)} %refs_0_.1, bf16[1,192,4096]{2,1,0:T(8,128)(2,1)} %refs_1_.1, bf16[1,192,4096]{2,1,0:T(8,128)(2,1)} %refs_2_.1), custom_call_target="tpu_custom_call" | custom-call | bytes 4194304 | tf_op jit(solution)/shard_map/pallas_call | solution.py:111
  12.2 1.5 %collective-permute-done.1 = bf16[4,8320]{1,0:T(4,128)(2,1)S(1)} collective-permute-done((bf16[4,8320]{1,0:T(4,128)(2,1)S(1)}, bf16[4,8320]{1,0:T(4,128)(2,1)S(1)}, u32[]{:S(2)}, u32[]{:S(2)}) %collective-permute-start.1) | collective-permute-done | bytes 66592 | tf_op jit(solution)/shard_map/ppermute | solution.py:100
  13.8 1.6 %collective-permute-start.3 = (bf16[16,8320]{1,0:T(8,128)(2,1)S(1)}, bf16[16,8320]{1,0:T(8,128)(2,1)}, u32[]{:S(2)}, u32[]{:S(2)}) collective-permute-start(bf16[16,8320]{1,0:T(8,128)(2,1)S(1)} %pad_maximum_fusion.refs_0_), channel_id=1, source_target_pairs={{0,4},{1,5},{2,6},{3,7},{4,0},{5,1},{6,2},{7,3},{8,12},{9,13},{10,... | collective-permute-start | bytes 798728 | tf_op jit(solution)/shard_map/ppermute | solution.py:100
  15.4 1.5 %collective-permute-start.4 = (bf16[16,8320]{1,0:T(8,128)(2,1)S(1)}, bf16[16,8320]{1,0:T(8,128)(2,1)}, u32[]{:S(2)}, u32[]{:S(2)}) collective-permute-start(bf16[16,8320]{1,0:T(8,128)(2,1)S(1)} %pad_maximum_fusion.refs_0_), channel_id=1, source_target_pairs={{0,2},{1,3},{2,0},{3,1},{4,6},{5,7},{6,4},{7,5},{8,10},{9,11},{10,... | collective-permute-start | bytes 798728 | tf_op jit(solution)/shard_map/ppermute | solution.py:100
  16.9 5.0 %collective-permute-done.3.refs_1_ = bf16[16,8320]{1,0:T(8,128)(2,1)} collective-permute-done((bf16[16,8320]{1,0:T(8,128)(2,1)S(1)}, bf16[16,8320]{1,0:T(8,128)(2,1)}, u32[]{:S(2)}, u32[]{:S(2)}) %collective-permute-start.3) | collective-permute-done | bytes 266272 | tf_op jit(solution)/shard_map/ppermute | solution.py:100
  21.9 1.5 %collective-permute-done.4.refs_2_ = bf16[16,8320]{1,0:T(8,128)(2,1)} collective-permute-done((bf16[16,8320]{1,0:T(8,128)(2,1)S(1)}, bf16[16,8320]{1,0:T(8,128)(2,1)}, u32[]{:S(2)}, u32[]{:S(2)}) %collective-permute-start.4) | collective-permute-done | bytes 266272 | tf_op jit(solution)/shard_map/ppermute | solution.py:100
  23.8 1.5 %collective-permute-done.7.refs_5_ = bf16[16,8320]{1,0:T(8,128)(2,1)} collective-permute-done((bf16[16,8320]{1,0:T(8,128)(2,1)}, bf16[16,8320]{1,0:T(8,128)(2,1)}, u32[]{:S(2)}, u32[]{:S(2)}) %collective-permute-start.7) | collective-permute-done | bytes 266272 | tf_op jit(solution)/shard_map/ppermute | solution.py:100
  25.3 1.4 %copy-done.1 = bf16[1,192,4096]{2,1,0:T(8,128)(2,1)S(1)} copy-done((bf16[1,192,4096]{2,1,0:T(8,128)(2,1)S(1)}, bf16[1,192,4096]{2,1,0:T(8,128)(2,1)}, u32[]{:S(2)}) %copy-start.1) | copy-done | bytes 1572888
  26.7 4.4 %shard_map.112 = (bf16[96,8320]{1,0:T(8,128)(2,1)S(1)}, bf16[576,96]{1,0:T(8,128)(2,1)S(1)}, f32[48,8192]{1,0:T(8,128)S(1)}, bf16[48,8192]{1,0:T(8,128)(2,1)S(1)}) custom-call(bf16[16,8320]{1,0:T(8,128)(2,1)S(1)} %pad_maximum_fusion.refs_0_, bf16[16,8320]{1,0:T(8,128)(2,1)} %collective-permute-done.3.refs_1_, ...), custom_call_target="tpu_custom_call" | custom-call | flops 905969664 | bytes 4194304 | tf_op jit(solution)/shard_map/pallas_call | solution.py:111
  33.8 1.6 %collective-permute-start.9 = (bf16[16,4096]{1,0:T(8,128)(2,1)S(1)}, bf16[16,4096]{1,0:T(8,128)(2,1)S(1)}, u32[]{:S(2)}, u32[]{:S(2)}) collective-permute-start(bf16[16,4096]{1,0:T(8,128)(2,1)S(1)} %slice.32), channel_id=1, source_target_pairs={{0,2},{1,3},{2,0},{3,1},{4,6},{5,7},{6,4},{7,5},{8,10},{9,11},{10,... | collective-permute-start | bytes 393224 | tf_op jit(solution)/shard_map/ppermute | solution.py:100
  35.4 2.7 %collective-permute-done.10.refs_1_ = bf16[16,4224]{1,0:T(8,128)(2,1)S(1)} collective-permute-done((bf16[16,4224]{1,0:T(8,128)(2,1)S(1)}, bf16[16,4224]{1,0:T(8,128)(2,1)S(1)}, u32[]{:S(2)}, u32[]{:S(2)}) %collective-permute-start.10) | collective-permute-done | bytes 135200 | tf_op jit(solution)/shard_map/ppermute | solution.py:100
  39.4 1.3 %collective-permute-done.11.refs_2_ = bf16[16,4096]{1,0:T(8,128)(2,1)S(1)} collective-permute-done((bf16[16,4096]{1,0:T(8,128)(2,1)S(1)}, bf16[16,4096]{1,0:T(8,128)(2,1)S(1)}, u32[]{:S(2)}, u32[]{:S(2)}) %collective-permute-start.11) | collective-permute-done | bytes 131104 | tf_op jit(solution)/shard_map/ppermute | solution.py:100
  40.7 2.9 %shard_map.113 = (bf16[32,8320]{1,0:T(8,128)(2,1)S(1)}, bf16[576,32]{1,0:T(8,128)(2,1)S(1)}, f32[16,8192]{1,0:T(8,128)S(1)}, bf16[16,8192]{1,0:T(8,128)(2,1)S(1)}) custom-call(bf16[16,4096]{1,0:T(8,128)(2,1)S(1)} %collective-permute-done.9.refs_0_, bf16[16,4224]{1,0:T(8,128)(2,1)S(1)} %collective-permute-done.10.refs_1_, ...), custom_call_target="tpu_custom_call" | custom-call | flops 301989888 | bytes 4194304 | tf_op jit(solution)/shard_map/pallas_call | solution.py:111
  43.9 1.4 %collective-permute-done.13.passed_ref = bf16[16,8192]{1,0:T(8,128)(2,1)S(1)} collective-permute-done((bf16[16,8192]{1,0:T(8,128)(2,1)S(1)}, bf16[16,8192]{1,0:T(8,128)(2,1)S(1)}, u32[]{:S(2)}, u32[]{:S(2)}) %collective-permute-start.13) | collective-permute-done | bytes 262176 | tf_op jit(solution)/shard_map/ppermute | solution.py:100
  45.3 1.6 %collective-permute-start.14 = (bf16[16,4096]{1,0:T(8,128)(2,1)S(1)}, bf16[16,4096]{1,0:T(8,128)(2,1)S(1)}, u32[]{:S(2)}, u32[]{:S(2)}) collective-permute-start(bf16[16,4096]{1,0:T(8,128)(2,1)S(1)} %get-tuple-element.38), channel_id=1, source_target_pairs={{0,2},{1,3},{2,0},{3,1},{4,6},{5,7},{6,4},{7,5},{8,10},{9,11},{10,... | collective-permute-start | bytes 393224 | tf_op jit(solution)/shard_map/ppermute | solution.py:100
  46.9 1.4 %collective-permute-start.15 = (bf16[16,4096]{1,0:T(8,128)(2,1)S(1)}, bf16[16,4096]{1,0:T(8,128)(2,1)S(1)}, u32[]{:S(2)}, u32[]{:S(2)}) collective-permute-start(bf16[16,4096]{1,0:T(8,128)(2,1)S(1)} %get-tuple-element.39), channel_id=1, source_target_pairs={{0,4},{1,5},{2,6},{3,7},{4,0},{5,1},{6,2},{7,3},{8,12},{9,13},{10,... | collective-permute-start | bytes 393224 | tf_op jit(solution)/shard_map/ppermute | solution.py:100
  48.3 2.7 %collective-permute-done.14.into_ref = bf16[16,4096]{1,0:T(8,128)(2,1)S(1)} collective-permute-done((bf16[16,4096]{1,0:T(8,128)(2,1)S(1)}, bf16[16,4096]{1,0:T(8,128)(2,1)S(1)}, u32[]{:S(2)}, u32[]{:S(2)}) %collective-permute-start.14) | collective-permute-done | bytes 131104 | tf_op jit(solution)/shard_map/ppermute | solution.py:100
  52.9 1.4 %collective-permute-start.16 = (bf16[16,8192]{1,0:T(8,128)(2,1)S(1)}, bf16[16,8192]{1,0:T(8,128)(2,1)S(1)}, u32[]{:S(2)}, u32[]{:S(2)}) collective-permute-start(bf16[16,8192]{1,0:T(8,128)(2,1)S(1)} %get-tuple-element.41), channel_id=1, source_target_pairs={{0,4},{1,5},{2,6},{3,7},{4,0},{5,1},{6,2},{7,3},{8,12},{9,13},{10,... | collective-permute-start | bytes 786440 | tf_op jit(solution)/shard_map/ppermute | solution.py:100
  54.3 5.3 %collective-permute-done.17 = bf16[16,8192]{1,0:T(8,128)(2,1)S(1)} collective-permute-done((bf16[16,8192]{1,0:T(8,128)(2,1)S(1)}, bf16[16,8192]{1,0:T(8,128)(2,1)S(1)}, u32[]{:S(2)}, u32[]{:S(2)}) %collective-permute-start.17) | collective-permute-done | bytes 262176 | tf_op jit(solution)/shard_map/ppermute | solution.py:100
  60.1 1.4 %collective-permute-start.20 = (bf16[4,8192]{1,0:T(4,128)(2,1)S(1)}, bf16[4,8192]{1,0:T(4,128)(2,1)S(1)}, u32[]{:S(2)}, u32[]{:S(2)}) collective-permute-start(bf16[4,8192]{1,0:T(4,128)(2,1)S(1)} %get-tuple-element.50), channel_id=1, source_target_pairs={{0,24},{1,25},{2,26},{3,27},{4,28},{5,29},{6,30},{7,31},{8,16},{9,... | collective-permute-start | bytes 196616 | tf_op jit(solution)/shard_map/ppermute | solution.py:100
  61.6 3.0 %collective-permute-start.18 = (bf16[4,8192]{1,0:T(4,128)(2,1)S(1)}, bf16[4,8192]{1,0:T(4,128)(2,1)S(1)}, u32[]{:S(2)}, u32[]{:S(2)}) collective-permute-start(bf16[4,8192]{1,0:T(4,128)(2,1)S(1)} %get-tuple-element.49), channel_id=1, source_target_pairs={{0,8},{1,9},{2,10},{3,11},{4,12},{5,13},{6,14},{7,15},{8,0},{9,1},... | collective-permute-start | bytes 196616 | tf_op jit(solution)/shard_map/ppermute | solution.py:100
  64.6 2.1 %shard_map.117 = bf16[1,192,4096]{2,1,0:T(8,128)(2,1)} custom-call(bf16[96,8320]{1,0:T(8,128)(2,1)S(1)} %get-tuple-element.43.early_ref, bf16[32,8320]{1,0:T(8,128)(2,1)S(1)} %get-tuple-element.44.late_ref, bf16[576,96]{1,0:T(8,128)(2,1)S(1)} %get-tuple-element.45.early_acts_ref, bf16[576,32]{1,0:T(8,128)(2,1)S(1)} %get-tuple-element.46.late_acts_ref), custom_call_target="tpu_custom_call" | custom-call | flops 201326592 | bytes 4194304 | tf_op jit(solution)/shard_map/pallas_call | solution.py:111
  66.7 3.3 %shard_map.116 = (bf16[1,192,4096]{2,1,0:T(8,128)(2,1)}, bf16[1,192,4096]{2,1,0:T(8,128)(2,1)}) custom-call(bf16[96,8320]{1,0:T(8,128)(2,1)S(1)} %get-tuple-element.43.early_ref, bf16[32,8320]{1,0:T(8,128)(2,1)S(1)} %get-tuple-element.44.late_ref, bf16[576,96]{1,0:T(8,128)(2,1)S(1)} %get-tuple-element.45.early_acts_ref, ...), custom_call_target="tpu_custom_call" | custom-call | flops 402653184 | bytes 4194304 | tf_op jit(solution)/shard_map/pallas_call | solution.py:111
  (42 shorter events, 12.1 us)
Async XLA Ops:
  2.9 9.3 %collective-permute-start.2 = (bf16[4,8320]{1,0:T(4,128)(2,1)S(1)}, bf16[4,8320]{1,0:T(4,128)(2,1)S(1)}, u32[]{:S(2)}, u32[]{:S(2)}) collective-permute-start(bf16[4,8320]{1,0:T(4,128)(2,1)S(1)} %shard_map.110), channel_id=1, source_target_pairs={{0,24},{1,25},{2,26},{3,27},{4,28},{5,29},{6,30},{7,31},{8,16},{9,... | collective-permute-start | bytes 199688 | tf_op jit(solution)/shard_map/ppermute | solution.py:100
  8.0 5.7 %collective-permute-start.1 = (bf16[4,8320]{1,0:T(4,128)(2,1)S(1)}, bf16[4,8320]{1,0:T(4,128)(2,1)S(1)}, u32[]{:S(2)}, u32[]{:S(2)}) collective-permute-start(bf16[4,8320]{1,0:T(4,128)(2,1)S(1)} %shard_map.110), channel_id=1, source_target_pairs={{0,16},{1,17},{2,18},{3,19},{4,20},{5,21},{6,22},{7,23},{8,24},{9,... | collective-permute-start | bytes 199688 | tf_op jit(solution)/shard_map/ppermute | solution.py:100
  8.0 5.7 %collective-permute-start = (bf16[4,8320]{1,0:T(4,128)(2,1)S(1)}, bf16[4,8320]{1,0:T(4,128)(2,1)S(1)}, u32[]{:S(2)}, u32[]{:S(2)}) collective-permute-start(bf16[4,8320]{1,0:T(4,128)(2,1)S(1)} %shard_map.110), channel_id=1, source_target_pairs={{0,8},{1,9},{2,10},{3,11},{4,12},{5,13},{6,14},{7,15},{8,0},{9,1},... | collective-permute-start | bytes 199688 | tf_op jit(solution)/shard_map/ppermute | solution.py:100
  11.0 1.1 %copy-start = (bf16[1,192,4096]{2,1,0:T(8,128)(2,1)}, bf16[1,192,4096]{2,1,0:T(8,128)(2,1)S(1)}, u32[]{:S(2)}) copy-start(bf16[1,192,4096]{2,1,0:T(8,128)(2,1)S(1)} %get-tuple-element.33.refs_8_.refs_6_) | copy-start | bytes 4718596
  13.8 8.1 %collective-permute-start.3 = (bf16[16,8320]{1,0:T(8,128)(2,1)S(1)}, bf16[16,8320]{1,0:T(8,128)(2,1)}, u32[]{:S(2)}, u32[]{:S(2)}) collective-permute-start(bf16[16,8320]{1,0:T(8,128)(2,1)S(1)} %pad_maximum_fusion.refs_0_), channel_id=1, source_target_pairs={{0,4},{1,5},{2,6},{3,7},{4,0},{5,1},{6,2},{7,3},{8,12},{9,13},{10,... | collective-permute-start | bytes 798728 | tf_op jit(solution)/shard_map/ppermute | solution.py:100
  15.4 8.0 %collective-permute-start.4 = (bf16[16,8320]{1,0:T(8,128)(2,1)S(1)}, bf16[16,8320]{1,0:T(8,128)(2,1)}, u32[]{:S(2)}, u32[]{:S(2)}) collective-permute-start(bf16[16,8320]{1,0:T(8,128)(2,1)S(1)} %pad_maximum_fusion.refs_0_), channel_id=1, source_target_pairs={{0,2},{1,3},{2,0},{3,1},{4,6},{5,7},{6,4},{7,5},{8,10},{9,11},{10,... | collective-permute-start | bytes 798728 | tf_op jit(solution)/shard_map/ppermute | solution.py:100
  16.9 6.5 %collective-permute-start.5 = (bf16[16,8320]{1,0:T(8,128)(2,1)S(1)}, bf16[16,8320]{1,0:T(8,128)(2,1)}, u32[]{:S(2)}, u32[]{:S(2)}) collective-permute-start(bf16[16,8320]{1,0:T(8,128)(2,1)S(1)} %pad_maximum_fusion.refs_0_), channel_id=1, source_target_pairs={{0,1},{1,0},{2,3},{3,2},{4,5},{5,4},{6,7},{7,6},{8,9},{9,8},{10,11... | collective-permute-start | bytes 798728 | tf_op jit(solution)/shard_map/ppermute | solution.py:100
  21.9 1.9 %collective-permute-start.6 = (bf16[16,8320]{1,0:T(8,128)(2,1)}, bf16[16,8320]{1,0:T(8,128)(2,1)}, u32[]{:S(2)}, u32[]{:S(2)}) collective-permute-start(bf16[16,8320]{1,0:T(8,128)(2,1)} %collective-permute-done.3.refs_1_), channel_id=1, source_target_pairs={{0,1},{1,0},{2,3},{3,2},{4,5},{5,4},{6,7},{7,6},{8,9},{9,8},{10,11... | collective-permute-start | bytes 798728 | tf_op jit(solution)/shard_map/ppermute | solution.py:100
  23.4 1.9 %collective-permute-start.7 = (bf16[16,8320]{1,0:T(8,128)(2,1)}, bf16[16,8320]{1,0:T(8,128)(2,1)}, u32[]{:S(2)}, u32[]{:S(2)}) collective-permute-start(bf16[16,8320]{1,0:T(8,128)(2,1)} %collective-permute-done.4.refs_2_), channel_id=1, source_target_pairs={{0,1},{1,0},{2,3},{3,2},{4,5},{5,4},{6,7},{7,6},{8,9},{9,8},{10,11... | collective-permute-start | bytes 798728 | tf_op jit(solution)/shard_map/ppermute | solution.py:100
  25.3 1.4 %copy-start.1 = (bf16[1,192,4096]{2,1,0:T(8,128)(2,1)S(1)}, bf16[1,192,4096]{2,1,0:T(8,128)(2,1)}, u32[]{:S(2)}) copy-start(bf16[1,192,4096]{2,1,0:T(8,128)(2,1)} %copy-done) | copy-start | bytes 4718596
  26.7 14.1 %copy-start.2 = (bf16[1,192,4096]{2,1,0:T(8,128)(2,1)S(1)}, bf16[1,192,4096]{2,1,0:T(8,128)(2,1)}, u32[]{:S(2)}) copy-start(bf16[1,192,4096]{2,1,0:T(8,128)(2,1)} %copy-done) | copy-start | bytes 4718596
  31.1 21.1 %collective-permute-start.8 = (bf16[48,8192]{1,0:T(8,128)(2,1)S(1)}, bf16[48,8192]{1,0:T(8,128)(2,1)S(1)}, u32[]{:S(2)}, u32[]{:S(2)}) collective-permute-start(bf16[48,8192]{1,0:T(8,128)(2,1)S(1)} %get-tuple-element.35), channel_id=1, source_target_pairs={{0,1},{1,0},{2,3},{3,2},{4,5},{5,4},{6,7},{7,6},{8,9},{9,8},{10,11... | collective-permute-start | bytes 2359304 | tf_op jit(solution)/shard_map/ppermute | solution.py:100
  32.2 5.9 %collective-permute-start.10 = (bf16[16,4224]{1,0:T(8,128)(2,1)S(1)}, bf16[16,4224]{1,0:T(8,128)(2,1)S(1)}, u32[]{:S(2)}, u32[]{:S(2)}) collective-permute-start(bf16[16,4224]{1,0:T(8,128)(2,1)S(1)} %slice.33), channel_id=1, source_target_pairs={{0,4},{1,5},{2,6},{3,7},{4,0},{5,1},{6,2},{7,3},{8,12},{9,13},{10,... | collective-permute-start | bytes 405512 | tf_op jit(solution)/shard_map/ppermute | solution.py:100
  33.8 5.5 %collective-permute-start.9 = (bf16[16,4096]{1,0:T(8,128)(2,1)S(1)}, bf16[16,4096]{1,0:T(8,128)(2,1)S(1)}, u32[]{:S(2)}, u32[]{:S(2)}) collective-permute-start(bf16[16,4096]{1,0:T(8,128)(2,1)S(1)} %slice.32), channel_id=1, source_target_pairs={{0,2},{1,3},{2,0},{3,1},{4,6},{5,7},{6,4},{7,5},{8,10},{9,11},{10,... | collective-permute-start | bytes 393224 | tf_op jit(solution)/shard_map/ppermute | solution.py:100
  38.1 2.6 %collective-permute-start.12 = (bf16[16,4224]{1,0:T(8,128)(2,1)S(1)}, bf16[16,4224]{1,0:T(8,128)(2,1)S(1)}, u32[]{:S(2)}, u32[]{:S(2)}) collective-permute-start(bf16[16,4224]{1,0:T(8,128)(2,1)S(1)} %collective-permute-done.10.refs_1_), channel_id=1, source_target_pairs={{0,1},{1,0},{2,3},{3,2},{4,5},{5,4},{6,7},{7,6},{8,9},{9,8},{10,11... | collective-permute-start | bytes 405512 | tf_op jit(solution)/shard_map/ppermute | solution.py:100
  39.4 1.3 %collective-permute-start.11 = (bf16[16,4096]{1,0:T(8,128)(2,1)S(1)}, bf16[16,4096]{1,0:T(8,128)(2,1)S(1)}, u32[]{:S(2)}, u32[]{:S(2)}) collective-permute-start(bf16[16,4096]{1,0:T(8,128)(2,1)S(1)} %collective-permute-done.9.refs_0_), channel_id=1, source_target_pairs={{0,1},{1,0},{2,3},{3,2},{4,5},{5,4},{6,7},{7,6},{8,9},{9,8},{10,11... | collective-permute-start | bytes 393224 | tf_op jit(solution)/shard_map/ppermute | solution.py:100
  43.7 1.6 %collective-permute-start.13 = (bf16[16,8192]{1,0:T(8,128)(2,1)S(1)}, bf16[16,8192]{1,0:T(8,128)(2,1)S(1)}, u32[]{:S(2)}, u32[]{:S(2)}) collective-permute-start(bf16[16,8192]{1,0:T(8,128)(2,1)S(1)} %get-tuple-element.37), channel_id=1, source_target_pairs={{0,1},{1,0},{2,3},{3,2},{4,5},{5,4},{6,7},{7,6},{8,9},{9,8},{10,11... | collective-permute-start | bytes 786440 | tf_op jit(solution)/shard_map/ppermute | solution.py:100
  45.3 5.6 %collective-permute-start.14 = (bf16[16,4096]{1,0:T(8,128)(2,1)S(1)}, bf16[16,4096]{1,0:T(8,128)(2,1)S(1)}, u32[]{:S(2)}, u32[]{:S(2)}) collective-permute-start(bf16[16,4096]{1,0:T(8,128)(2,1)S(1)} %get-tuple-element.38), channel_id=1, source_target_pairs={{0,2},{1,3},{2,0},{3,1},{4,6},{5,7},{6,4},{7,5},{8,10},{9,11},{10,... | collective-permute-start | bytes 393224 | tf_op jit(solution)/shard_map/ppermute | solution.py:100
  46.9 5.3 %collective-permute-start.15 = (bf16[16,4096]{1,0:T(8,128)(2,1)S(1)}, bf16[16,4096]{1,0:T(8,128)(2,1)S(1)}, u32[]{:S(2)}, u32[]{:S(2)}) collective-permute-start(bf16[16,4096]{1,0:T(8,128)(2,1)S(1)} %get-tuple-element.39), channel_id=1, source_target_pairs={{0,4},{1,5},{2,6},{3,7},{4,0},{5,1},{6,2},{7,3},{8,12},{9,13},{10,... | collective-permute-start | bytes 393224 | tf_op jit(solution)/shard_map/ppermute | solution.py:100
  52.4 7.3 %collective-permute-start.17 = (bf16[16,8192]{1,0:T(8,128)(2,1)S(1)}, bf16[16,8192]{1,0:T(8,128)(2,1)S(1)}, u32[]{:S(2)}, u32[]{:S(2)}) collective-permute-start(bf16[16,8192]{1,0:T(8,128)(2,1)S(1)} %get-tuple-element.42), channel_id=1, source_target_pairs={{0,2},{1,3},{2,0},{3,1},{4,6},{5,7},{6,4},{7,5},{8,10},{9,11},{10,... | collective-permute-start | bytes 786440 | tf_op jit(solution)/shard_map/ppermute | solution.py:100
  52.9 7.0 %collective-permute-start.16 = (bf16[16,8192]{1,0:T(8,128)(2,1)S(1)}, bf16[16,8192]{1,0:T(8,128)(2,1)S(1)}, u32[]{:S(2)}, u32[]{:S(2)}) collective-permute-start(bf16[16,8192]{1,0:T(8,128)(2,1)S(1)} %get-tuple-element.41), channel_id=1, source_target_pairs={{0,4},{1,5},{2,6},{3,7},{4,0},{5,1},{6,2},{7,3},{8,12},{9,13},{10,... | collective-permute-start | bytes 786440 | tf_op jit(solution)/shard_map/ppermute | solution.py:100
  60.1 9.9 %collective-permute-start.20 = (bf16[4,8192]{1,0:T(4,128)(2,1)S(1)}, bf16[4,8192]{1,0:T(4,128)(2,1)S(1)}, u32[]{:S(2)}, u32[]{:S(2)}) collective-permute-start(bf16[4,8192]{1,0:T(4,128)(2,1)S(1)} %get-tuple-element.50), channel_id=1, source_target_pairs={{0,24},{1,25},{2,26},{3,27},{4,28},{5,29},{6,30},{7,31},{8,16},{9,... | collective-permute-start | bytes 196616 | tf_op jit(solution)/shard_map/ppermute | solution.py:100
  61.6 8.4 %collective-permute-start.19 = (bf16[4,8192]{1,0:T(4,128)(2,1)S(1)}, bf16[4,8192]{1,0:T(4,128)(2,1)S(1)}, u32[]{:S(2)}, u32[]{:S(2)}) collective-permute-start(bf16[4,8192]{1,0:T(4,128)(2,1)S(1)} %get-tuple-element.51), channel_id=1, source_target_pairs={{0,16},{1,17},{2,18},{3,19},{4,20},{5,21},{6,22},{7,23},{8,24},{9,... | collective-permute-start | bytes 196616 | tf_op jit(solution)/shard_map/ppermute | solution.py:100
  61.6 8.4 %collective-permute-start.18 = (bf16[4,8192]{1,0:T(4,128)(2,1)S(1)}, bf16[4,8192]{1,0:T(4,128)(2,1)S(1)}, u32[]{:S(2)}, u32[]{:S(2)}) collective-permute-start(bf16[4,8192]{1,0:T(4,128)(2,1)S(1)} %get-tuple-element.49), channel_id=1, source_target_pairs={{0,8},{1,9},{2,10},{3,11},{4,12},{5,13},{6,14},{7,15},{8,0},{9,1},... | collective-permute-start | bytes 196616 | tf_op jit(solution)/shard_map/ppermute | solution.py:100
  (1 other events, 0.7 us)

commit v5 on v4

--- a/solution.py
+++ b/solution.py
@@ -114,7 +114,7 @@
         in_specs=specs,
         out_specs=jax.tree.map(lambda _: vmem, out_shape),
         scratch_shapes=scratch,
-        compiler_params=pltpu.CompilerParams(vmem_limit_bytes=24 << 20),
+        compiler_params=pltpu.CompilerParams(vmem_limit_bytes=16 << 20),
         cost_estimate=pl.CostEstimate(flops=cost, bytes_accessed=4 << 20, transcendentals=0),
     )(*operands)
 
@@ -132,11 +132,12 @@
     copy_all(list(zip(refs[:count], refs[count:-1])), refs[-1])
 
 
-def pack_body(x_ref, dy_ref, ids_ref, w_ref, msg_ref, x_buf, dy_buf, sems):
+def pack_body(x_ref, dy_ref, ids_ref, w_ref, expert_ref, msg_ref, mine_ref, *scratch):
+    x_buf, dy_buf, ids_buf, w_buf, sems = scratch
     rows, width = x_ref.shape
     top = ids_ref.shape[0]
     lanes = msg_ref.shape[1] - 2 * width
-    copy_all([(x_ref, x_buf), (dy_ref, dy_buf)], sems)
+    copy_all([(x_ref, x_buf), (dy_ref, dy_buf), (ids_ref, ids_buf), (w_ref, w_buf)], sems)
     msg_ref[:, :width] = x_buf[...]
     msg_ref[:, width : 2 * width] = dy_buf[...]
     diagonal = lax.broadcasted_iota(jnp.int32, (rows, rows), 0) == lax.broadcasted_iota(
@@ -145,18 +146,22 @@
     expert = lax.broadcasted_iota(jnp.int32, (rows, lanes), 1)
     route = jnp.zeros((rows, lanes), jnp.float32)
     for k in range(top):
-        named = jnp.sum(jnp.where(diagonal, ids_ref[k : k + 1, :], 0), axis=1, keepdims=True)
-        weight = jnp.sum(jnp.where(diagonal, w_ref[k : k + 1, :], 0.0), axis=1, keepdims=True)
+        named = jnp.sum(jnp.where(diagonal, ids_buf[k : k + 1, :], 0), axis=1, keepdims=True)
+        weight = jnp.sum(jnp.where(diagonal, w_buf[k : k + 1, :], 0.0), axis=1, keepdims=True)
         route = route + jnp.where(expert == named, weight, 0.0)
     msg_ref[:, 2 * width :] = route.astype(jnp.bfloat16)
-
-
-def passes(have, wg_ref, wu_ref, wd_ref, expert_ref, acts_ref):
+    lane = lax.broadcasted_iota(jnp.int32, mine_ref.shape, 1)
+    mine_ref[...] = jnp.where(lane == expert_ref[0], 1.0, 0.0)
+
+
+def half_body(start, from_ref, to_ref):
+    to_ref[...] = from_ref[:, start : start + to_ref.shape[1]]
+
+
+def passes(have, wg_ref, wu_ref, wd_ref, mine_ref, acts_ref):
     width, ff = wg_ref.shape[2], wg_ref.shape[1]
     x, dy, route = have[:, :width], have[:, width : 2 * width], have[:, 2 * width :]
-    lanes = route.shape[1]
-    mine = lax.broadcasted_iota(jnp.int32, (8, lanes), 1) == expert_ref[0]
-    weight = contract_rows(mine.astype(jnp.float32).astype(jnp.bfloat16), route)[:1, :]
+    weight = contract_rows(mine_ref[...].astype(jnp.bfloat16), route)[:1, :]
     gate_pre = contract_rows(wg_ref[0], x)
     up_pre = contract_rows(wu_ref[0], x)
     hidden_grad = weight * contract_rows(wd_ref[0], dy)
@@ -182,22 +187,22 @@
 
 def early_body(count, *refs):
     pieces, rest = refs[:count], refs[count:]
-    wg_ref, wu_ref, wd_ref, expert_ref, have, acts_ref, own_ref, msg_ref = rest
+    wg_ref, wu_ref, wd_ref, mine_ref, have, acts_ref, own_ref, msg_ref = rest
     rows = pieces[0].shape[0]
     for i, piece in enumerate(pieces):
         have[i * rows : (i + 1) * rows, :] = piece[...]
-    out, into = passes(have, wg_ref, wu_ref, wd_ref, expert_ref, acts_ref)
+    out, into = passes(have, wg_ref, wu_ref, wd_ref, mine_ref, acts_ref)
     give(out, into, own_ref, msg_ref)
 
 
 def late_body(*refs):
     pieces, rest = refs[:4], refs[4:]
-    wg_ref, wu_ref, wd_ref, expert_ref, have, acts_ref, own_ref, msg_ref = rest
+    wg_ref, wu_ref, wd_ref, mine_ref, have, acts_ref, own_ref, msg_ref = rest
     rows, width = pieces[0].shape
     for i in range(2):
         have[i * rows : (i + 1) * rows, :width] = pieces[2 * i][...]
         have[i * rows : (i + 1) * rows, width:] = pieces[2 * i + 1][...]
-    out, into = passes(have, wg_ref, wu_ref, wd_ref, expert_ref, acts_ref)
+    out, into = passes(have, wg_ref, wu_ref, wd_ref, mine_ref, acts_ref)
     give(out, into, own_ref, msg_ref)
 
 
@@ -253,20 +258,23 @@
     def passed(value, mask):
         return from_xor(value, mask, devices)
 
-    message = kernel_call(
+    message, mine = kernel_call(
         pack_body,
-        shape(rows, columns),
+        (shape(rows, columns), shape(8, columns - 2 * width, dtype=f32)),
         0,
         tokens,
         out_grad,
         expert_ids.T,
         route_weights.astype(f32).T,
+        expert,
         scratch=[
             pltpu.VMEM((rows, width), bf16),
             pltpu.VMEM((rows, width), bf16),
-            pltpu.SemaphoreType.DMA((2,)),
+            pltpu.VMEM(expert_ids.shape[::-1], jnp.int32),
+            pltpu.VMEM(expert_ids.shape[::-1], f32),
+            pltpu.SemaphoreType.DMA((4,)),
         ],
-        hbm=(0, 1),
+        hbm=(0, 1, 2, 3),
     )
     weights = kernel_call(
         load_body,
@@ -282,11 +290,18 @@
     block, *weights = lax.optimization_barrier((block, *weights))
 
     by_second, by_first = passed(block, SECOND), passed(block, FIRST)
-    corner_x = passed(by_second[:, :width], FIRST)
-    corner_dy = passed(by_first[:, width:], SECOND)
+    half_x = kernel_call(
+        functools.partial(half_body, 0), shape(block_rows, width), 0, by_second
+    )
+    half_dy = kernel_call(
+        functools.partial(half_body, width), shape(block_rows, columns - width), 0, by_first
+    )
+    by_second, by_first, half_x, half_dy = lax.optimization_barrier(
+        (by_second, by_first, half_x, half_dy)
+    )
+    corner_x, corner_dy = passed(half_x, FIRST), passed(half_dy, SECOND)
     own = [block, by_second, by_first]
     other = [passed(piece, CORE) for piece in own]
-    corner = [corner_x, corner_dy, passed(corner_x, CORE), passed(corner_dy, CORE)]
 
     early_rows = len(own) * block_rows
     early, early_acts, early_own, message = kernel_call(
@@ -301,8 +316,10 @@
         *own,
         *other,
         *weights,
-        expert,
-    )
+        mine,
+    )
+    corner_x, corner_dy, message = lax.optimization_barrier((corner_x, corner_dy, message))
+    corner = [corner_x, corner_dy, passed(corner_x, CORE), passed(corner_dy, CORE)]
     early_passed = passed(message, CORE)
     late, late_acts, late_own, message = kernel_call(
         late_body,
@@ -315,7 +332,7 @@
         12 * unit,
         *corner,
         *weights,
-        expert,
+        mine,
     )
     late_passed = passed(message, CORE)
 
@@ -323,6 +340,15 @@
         late_sum_body, (shape(block_rows, width),) * 2, 0, late_own, late_passed
     )
     turned_out, turned_into = passed(corner_out, SECOND), passed(corner_into, FIRST)
+    (grad_down,) = kernel_call(
+        grad_body, (shape(*down_weight.shape),), 8 * unit, early, late, early_acts, late_acts
+    )
+    grad_gate, grad_up = kernel_call(
+        grad_body, (shape(*gate_weight.shape),) * 2, 16 * unit, early, late, early_acts, late_acts
+    )
+    turned_out, turned_into, grad_down = lax.optimization_barrier(
+        (turned_out, turned_into, grad_down)
+    )
     here, for_first, for_second = kernel_call(
         early_sum_body,
         (
@@ -336,7 +362,11 @@
         turned_into,
         turned_out,
     )
-    total = here + passed(for_second, SECOND).astype(f32) + passed(for_first, FIRST).astype(f32)
+    from_second, from_first = passed(for_second, SECOND), passed(for_first, FIRST)
+    from_second, from_first, grad_gate, grad_up = lax.optimization_barrier(
+        (from_second, from_first, grad_gate, grad_up)
+    )
+    total = here + from_second.astype(f32) + from_first.astype(f32)
     total = total.astype(bf16)
     pieces = [total[k * rows : (k + 1) * rows] for k in range(len(near) + 1)]
     total = pieces[0].astype(f32)
@@ -344,12 +374,6 @@
         total = total + passed(piece, m).astype(f32)
     total = total.astype(bf16)
 
-    (grad_down,) = kernel_call(
-        grad_body, (shape(*down_weight.shape),), 8 * unit, early, late, early_acts, late_acts
-    )
-    grad_gate, grad_up = kernel_call(
-        grad_body, (shape(*gate_weight.shape),) * 2, 16 * unit, early, late, early_acts, late_acts
-    )
     return total[:, :width], total[:, width:], grad_gate, grad_up, grad_down
 
 

time: 71.1 us -> 61.3 us (0.86)
  local copies, waits for them, and re-layouts: 5.79 us -> 0.73 us
  starting transfers between devices: 20.9 us -> 18.7 us
  waiting for transfers between devices: 26.1 us -> 24.5 us
  Pallas kernels: 16.2 us -> 14.9 us
    unnamed x8 -> x0, local copies, waits for them, and re-layouts: 3.23 us -> none
    ppermute x21, starting transfers between devices: 20.9 us -> 18.7 us  [from_xor(): return lax.ppermute(value, AXES, [(i, i ^ mask) for i in range(devices)])]
    slice x2 -> x0, local copies, waits for them, and re-layouts: 1.83 us -> none  [the longest x1 0.91 us: dense(): corner_dy = passed(by_first[:, width:], SECOND)]
    ppermute x21, waiting for transfers between devices: 26.1 us -> 24.5 us  [from_xor(): return lax.ppermute(value, AXES, [(i, i ^ mask) for i in range(devices)])]
    pallas_call x8 -> x10, Pallas kernels: 16.2 us -> 14.9 us  [kernel_call(): pl.pallas_call(body, out_shape=out_shape, in_specs=specs, out_specs=jax.t...]
  transfers between devices with their start and end apart: 21 -> 21, of which waited for: 13 -> 13; matrix products, arithmetic and copies ran while one was open for 3% -> 0% of each run, Pallas kernels for 15% -> 23%
where the time goes in v5:
time: 61.3 us; the launch traced here: 61.1 us
  waiting for transfers between devices  24.5 us (40%)
  starting transfers between devices  18.7 us (31%)
  Pallas kernels  14.9 us (24%)
  other arithmetic  1.55 us (3%)
  between operations  0.74 us (1%)
  local copies, waits for them, and re-layouts  0.73 us (1%)
    ppermute x21, waiting for transfers between devices, from_xor(): return lax.ppermute(value, AXES, [(i, i ^ mask) for i in range(devices)])  24.5 us
    ppermute x21, starting transfers between devices, from_xor(): return lax.ppermute(value, AXES, [(i, i ^ mask) for i in range(devices)])  18.7 us
    pallas_call x10, Pallas kernels, kernel_call(): pl.pallas_call(body, out_shape=out_shape, in_specs=specs, out_specs=jax.t...  14.9 us
  transfers between devices with their start and end apart: 21, of which 13 were waited for; matrix products, arithmetic and copies ran while one was open for 0% of the time, Pallas kernels for 23%

profile of v5, /device:TPU:0, one launch (start us, length us, event | category | flops | bytes accessed | tf_op | source)
XLA Modules:
  0.0 61.1 jit_solution(1035976004382376590)
XLA Ops:
  0.6 1.2 %convert_bitcast_fusion.w_ref = f32[2,4]{1,0:T(2,128)} fusion(bf16[4,2]{0,1:T(2,128)(2,1)} %param.9), kind=kLoop, calls=%fused_computation.3 | loop fusion | flops 8 | bytes 48 | tf_op jit(solution)/shard_map/transpose | solution.py:268
  2.8 5.1 %collective-permute-start.2 = (bf16[4,8320]{1,0:T(4,128)(2,1)S(1)}, bf16[4,8320]{1,0:T(4,128)(2,1)S(1)}, u32[]{:S(2)}, u32[]{:S(2)}) collective-permute-start(bf16[4,8320]{1,0:T(4,128)(2,1)S(1)} %get-tuple-element.43), channel_id=1, source_target_pairs={{0,24},{1,25},{2,26},{3,27},{4,28},{5,29},{6,30},{7,31},{8,16},{9,... | collective-permute-start | bytes 199688 | tf_op jit(solution)/shard_map/ppermute | solution.py:100
  8.5 2.4 %shard_map.111 = (bf16[1,192,4096]{2,1,0:T(8,128)(2,1)S(1)}, bf16[1,192,4096]{2,1,0:T(8,128)(2,1)S(1)}, bf16[1,192,4096]{2,1,0:T(8,128)(2,1)S(1)}) custom-call(bf16[1,192,4096]{2,1,0:T(8,128)(2,1)} %refs_0_.1, bf16[1,192,4096]{2,1,0:T(8,128)(2,1)} %refs_1_.1, bf16[1,192,4096]{2,1,0:T(8,128)(2,1)} %refs_2_.1), custom_call_target="tpu_custom_call" | custom-call | bytes 4194304 | tf_op jit(solution)/shard_map/pallas_call | solution.py:111
  10.9 2.6 %collective-permute-done.1 = bf16[4,8320]{1,0:T(4,128)(2,1)S(1)} collective-permute-done((bf16[4,8320]{1,0:T(4,128)(2,1)S(1)}, bf16[4,8320]{1,0:T(4,128)(2,1)S(1)}, u32[]{:S(2)}, u32[]{:S(2)}) %collective-permute-start.1) | collective-permute-done | bytes 66592 | tf_op jit(solution)/shard_map/ppermute | solution.py:100
  13.7 1.6 %collective-permute-start.4 = (bf16[16,8320]{1,0:T(8,128)(2,1)S(1)}, bf16[16,8320]{1,0:T(8,128)(2,1)S(1)}, u32[]{:S(2)}, u32[]{:S(2)}) collective-permute-start(bf16[16,8320]{1,0:T(8,128)(2,1)S(1)} %pad_maximum_fusion.refs_0_), channel_id=1, source_target_pairs={{0,2},{1,3},{2,0},{3,1},{4,6},{5,7},{6,4},{7,5},{8,10},{9,11},{10,... | collective-permute-start | bytes 798728 | tf_op jit(solution)/shard_map/ppermute | solution.py:100
  15.3 1.5 %collective-permute-start.3 = (bf16[16,8320]{1,0:T(8,128)(2,1)S(1)}, bf16[16,8320]{1,0:T(8,128)(2,1)S(1)}, u32[]{:S(2)}, u32[]{:S(2)}) collective-permute-start(bf16[16,8320]{1,0:T(8,128)(2,1)S(1)} %pad_maximum_fusion.refs_0_), channel_id=1, source_target_pairs={{0,4},{1,5},{2,6},{3,7},{4,0},{5,1},{6,2},{7,3},{8,12},{9,13},{10,... | collective-permute-start | bytes 798728 | tf_op jit(solution)/shard_map/ppermute | solution.py:100
  16.8 4.9 %collective-permute-done.4.from_ref.refs_2_ = bf16[16,8320]{1,0:T(8,128)(2,1)S(1)} collective-permute-done((bf16[16,8320]{1,0:T(8,128)(2,1)S(1)}, bf16[16,8320]{1,0:T(8,128)(2,1)S(1)}, u32[]{:S(2)}, u32[]{:S(2)}) %collective-permute-start.4) | collective-permute-done | bytes 266272 | tf_op jit(solution)/shard_map/ppermute | solution.py:100
  21.8 1.4 %collective-permute-done.3.from_ref.refs_1_ = bf16[16,8320]{1,0:T(8,128)(2,1)S(1)} collective-permute-done((bf16[16,8320]{1,0:T(8,128)(2,1)S(1)}, bf16[16,8320]{1,0:T(8,128)(2,1)S(1)}, u32[]{:S(2)}, u32[]{:S(2)}) %collective-permute-start.3) | collective-permute-done | bytes 266272 | tf_op jit(solution)/shard_map/ppermute | solution.py:100
  23.8 1.5 %collective-permute-start.9 = (bf16[16,4224]{1,0:T(8,128)(2,1)S(1)}, bf16[16,4224]{1,0:T(8,128)(2,1)S(1)}, u32[]{:S(2)}, u32[]{:S(2)}) collective-permute-start(bf16[16,4224]{1,0:T(8,128)(2,1)S(1)} %shard_map.113), channel_id=1, source_target_pairs={{0,4},{1,5},{2,6},{3,7},{4,0},{5,1},{6,2},{7,3},{8,12},{9,13},{10,... | collective-permute-start | bytes 405512 | tf_op jit(solution)/shard_map/ppermute | solution.py:100
  25.8 3.0 %shard_map.114 = (bf16[96,8320]{1,0:T(8,128)(2,1)S(1)}, bf16[576,96]{1,0:T(8,128)(2,1)S(1)}, f32[48,8192]{1,0:T(8,128)S(1)}, bf16[48,8192]{1,0:T(8,128)(2,1)S(1)}) custom-call(bf16[16,8320]{1,0:T(8,128)(2,1)S(1)} %pad_maximum_fusion.refs_0_, bf16[16,8320]{1,0:T(8,128)(2,1)S(1)} %collective-permute-done.3.from_ref.refs_1_, ...), custom_call_target="tpu_custom_call" | custom-call | flops 905969664 | bytes 4194304 | tf_op jit(solution)/shard_map/pallas_call | solution.py:111
  28.8 1.7 %collective-permute-done.8.refs_0_ = bf16[16,4096]{1,0:T(8,128)(2,1)S(1)} collective-permute-done((bf16[16,4096]{1,0:T(8,128)(2,1)S(1)}, bf16[16,4096]{1,0:T(8,128)(2,1)S(1)}, u32[]{:S(2)}, u32[]{:S(2)}) %collective-permute-start.8) | collective-permute-done | bytes 131104 | tf_op jit(solution)/shard_map/ppermute | solution.py:100
  31.0 2.2 %collective-permute-done.11.refs_2_ = bf16[16,4096]{1,0:T(8,128)(2,1)S(1)} collective-permute-done((bf16[16,4096]{1,0:T(8,128)(2,1)S(1)}, bf16[16,4096]{1,0:T(8,128)(2,1)S(1)}, u32[]{:S(2)}, u32[]{:S(2)}) %collective-permute-start.11) | collective-permute-done | bytes 131104 | tf_op jit(solution)/shard_map/ppermute | solution.py:100
  33.2 2.9 %shard_map.115 = (bf16[32,8320]{1,0:T(8,128)(2,1)S(1)}, bf16[576,32]{1,0:T(8,128)(2,1)S(1)}, f32[16,8192]{1,0:T(8,128)S(1)}, bf16[16,8192]{1,0:T(8,128)(2,1)S(1)}) custom-call(bf16[16,4096]{1,0:T(8,128)(2,1)S(1)} %collective-permute-done.8.refs_0_, bf16[16,4224]{1,0:T(8,128)(2,1)S(1)} %collective-permute-done.9.refs_1_, ...), custom_call_target="tpu_custom_call" | custom-call | flops 301989888 | bytes 4194304 | tf_op jit(solution)/shard_map/pallas_call | solution.py:111
  36.3 1.4 %collective-permute-done.13.passed_ref = bf16[16,8192]{1,0:T(8,128)(2,1)S(1)} collective-permute-done((bf16[16,8192]{1,0:T(8,128)(2,1)S(1)}, bf16[16,8192]{1,0:T(8,128)(2,1)S(1)}, u32[]{:S(2)}, u32[]{:S(2)}) %collective-permute-start.13) | collective-permute-done | bytes 262176 | tf_op jit(solution)/shard_map/ppermute | solution.py:100
  38.7 2.1 %shard_map.117 = bf16[1,192,4096]{2,1,0:T(8,128)(2,1)} custom-call(bf16[96,8320]{1,0:T(8,128)(2,1)S(1)} %get-tuple-element.65.early_ref, bf16[32,8320]{1,0:T(8,128)(2,1)S(1)} %get-tuple-element.66.late_ref, bf16[576,96]{1,0:T(8,128)(2,1)S(1)} %get-tuple-element.67.early_acts_ref, bf16[576,32]{1,0:T(8,128)(2,1)S(1)} %get-tuple-element.68.late_acts_ref), custom_call_target="tpu_custom_call" | custom-call | flops 201326592 | bytes 4194304 | tf_op jit(solution)/shard_map/pallas_call | solution.py:111
  40.8 2.5 %collective-permute-done.14.out_ref = bf16[16,4096]{1,0:T(8,128)(2,1)S(1)} collective-permute-done((bf16[16,4096]{1,0:T(8,128)(2,1)S(1)}, bf16[16,4096]{1,0:T(8,128)(2,1)S(1)}, u32[]{:S(2)}, u32[]{:S(2)}) %collective-permute-start.14) | collective-permute-done | bytes 131104 | tf_op jit(solution)/shard_map/ppermute | solution.py:100
  43.8 1.6 %collective-permute-start.16 = (bf16[16,8192]{1,0:T(8,128)(2,1)S(1)}, bf16[16,8192]{1,0:T(8,128)(2,1)S(1)}, u32[]{:S(2)}, u32[]{:S(2)}) collective-permute-start(bf16[16,8192]{1,0:T(8,128)(2,1)S(1)} %get-tuple-element.72), channel_id=1, source_target_pairs={{0,4},{1,5},{2,6},{3,7},{4,0},{5,1},{6,2},{7,3},{8,12},{9,13},{10,... | collective-permute-start | bytes 786440 | tf_op jit(solution)/shard_map/ppermute | solution.py:100
  45.9 3.3 %shard_map.119 = (bf16[1,192,4096]{2,1,0:T(8,128)(2,1)}, bf16[1,192,4096]{2,1,0:T(8,128)(2,1)}) custom-call(bf16[96,8320]{1,0:T(8,128)(2,1)S(1)} %get-tuple-element.65.early_ref, bf16[32,8320]{1,0:T(8,128)(2,1)S(1)} %get-tuple-element.66.late_ref, bf16[576,96]{1,0:T(8,128)(2,1)S(1)} %get-tuple-element.67.early_acts_ref, ...), custom_call_target="tpu_custom_call" | custom-call | flops 402653184 | bytes 4194304 | tf_op jit(solution)/shard_map/pallas_call | solution.py:111
  49.2 1.9 %collective-permute-done.16 = bf16[16,8192]{1,0:T(8,128)(2,1)S(1)} collective-permute-done((bf16[16,8192]{1,0:T(8,128)(2,1)S(1)}, bf16[16,8192]{1,0:T(8,128)(2,1)S(1)}, u32[]{:S(2)}, u32[]{:S(2)}) %collective-permute-start.16) | collective-permute-done | bytes 262176 | tf_op jit(solution)/shard_map/ppermute | solution.py:100
  52.5 1.5 %collective-permute-start.20 = (bf16[4,8192]{1,0:T(4,128)(2,1)S(1)}, bf16[4,8192]{1,0:T(4,128)(2,1)S(1)}, u32[]{:S(2)}, u32[]{:S(2)}) collective-permute-start(bf16[4,8192]{1,0:T(4,128)(2,1)S(1)} %get-tuple-element.82), channel_id=1, source_target_pairs={{0,24},{1,25},{2,26},{3,27},{4,28},{5,29},{6,30},{7,31},{8,16},{9,... | collective-permute-start | bytes 196616 | tf_op jit(solution)/shard_map/ppermute | solution.py:100
  54.1 2.0 %collective-permute-start.19 = (bf16[4,8192]{1,0:T(4,128)(2,1)S(1)}, bf16[4,8192]{1,0:T(4,128)(2,1)S(1)}, u32[]{:S(2)}, u32[]{:S(2)}) collective-permute-start(bf16[4,8192]{1,0:T(4,128)(2,1)S(1)} %get-tuple-element.83), channel_id=1, source_target_pairs={{0,16},{1,17},{2,18},{3,19},{4,20},{5,21},{6,22},{7,23},{8,24},{9,... | collective-permute-start | bytes 196616 | tf_op jit(solution)/shard_map/ppermute | solution.py:100
  56.0 1.2 %collective-permute-done.18 = bf16[4,8192]{1,0:T(4,128)(2,1)S(1)} collective-permute-done((bf16[4,8192]{1,0:T(4,128)(2,1)S(1)}, bf16[4,8192]{1,0:T(4,128)(2,1)S(1)}, u32[]{:S(2)}, u32[]{:S(2)}) %collective-permute-start.18) | collective-permute-done | bytes 65568 | tf_op jit(solution)/shard_map/ppermute | solution.py:100
  57.2 1.5 %collective-permute-done.20 = bf16[4,8192]{1,0:T(4,128)(2,1)S(1)} collective-permute-done((bf16[4,8192]{1,0:T(4,128)(2,1)S(1)}, bf16[4,8192]{1,0:T(4,128)(2,1)S(1)}, u32[]{:S(2)}, u32[]{:S(2)}) %collective-permute-start.20) | collective-permute-done | bytes 65568 | tf_op jit(solution)/shard_map/ppermute | solution.py:100
  58.8 1.6 %collective-permute-done.19 = bf16[4,8192]{1,0:T(4,128)(2,1)S(1)} collective-permute-done((bf16[4,8192]{1,0:T(4,128)(2,1)S(1)}, bf16[4,8192]{1,0:T(4,128)(2,1)S(1)}, u32[]{:S(2)}, u32[]{:S(2)}) %collective-permute-start.19) | collective-permute-done | bytes 65568 | tf_op jit(solution)/shard_map/ppermute | solution.py:100
  (34 shorter events, 7.6 us)
Async XLA Ops:
  2.8 8.1 %collective-permute-start.2 = (bf16[4,8320]{1,0:T(4,128)(2,1)S(1)}, bf16[4,8320]{1,0:T(4,128)(2,1)S(1)}, u32[]{:S(2)}, u32[]{:S(2)}) collective-permute-start(bf16[4,8320]{1,0:T(4,128)(2,1)S(1)} %get-tuple-element.43), channel_id=1, source_target_pairs={{0,24},{1,25},{2,26},{3,27},{4,28},{5,29},{6,30},{7,31},{8,16},{9,... | collective-permute-start | bytes 199688 | tf_op jit(solution)/shard_map/ppermute | solution.py:100
  7.9 5.7 %collective-permute-start.1 = (bf16[4,8320]{1,0:T(4,128)(2,1)S(1)}, bf16[4,8320]{1,0:T(4,128)(2,1)S(1)}, u32[]{:S(2)}, u32[]{:S(2)}) collective-permute-start(bf16[4,8320]{1,0:T(4,128)(2,1)S(1)} %get-tuple-element.43), channel_id=1, source_target_pairs={{0,16},{1,17},{2,18},{3,19},{4,20},{5,21},{6,22},{7,23},{8,24},{9,... | collective-permute-start | bytes 199688 | tf_op jit(solution)/shard_map/ppermute | solution.py:100
  7.9 5.7 %collective-permute-start = (bf16[4,8320]{1,0:T(4,128)(2,1)S(1)}, bf16[4,8320]{1,0:T(4,128)(2,1)S(1)}, u32[]{:S(2)}, u32[]{:S(2)}) collective-permute-start(bf16[4,8320]{1,0:T(4,128)(2,1)S(1)} %get-tuple-element.43), channel_id=1, source_target_pairs={{0,8},{1,9},{2,10},{3,11},{4,12},{5,13},{6,14},{7,15},{8,0},{9,1},... | collective-permute-start | bytes 199688 | tf_op jit(solution)/shard_map/ppermute | solution.py:100
  13.7 8.0 %collective-permute-start.4 = (bf16[16,8320]{1,0:T(8,128)(2,1)S(1)}, bf16[16,8320]{1,0:T(8,128)(2,1)S(1)}, u32[]{:S(2)}, u32[]{:S(2)}) collective-permute-start(bf16[16,8320]{1,0:T(8,128)(2,1)S(1)} %pad_maximum_fusion.refs_0_), channel_id=1, source_target_pairs={{0,2},{1,3},{2,0},{3,1},{4,6},{5,7},{6,4},{7,5},{8,10},{9,11},{10,... | collective-permute-start | bytes 798728 | tf_op jit(solution)/shard_map/ppermute | solution.py:100
  15.3 7.9 %collective-permute-start.3 = (bf16[16,8320]{1,0:T(8,128)(2,1)S(1)}, bf16[16,8320]{1,0:T(8,128)(2,1)S(1)}, u32[]{:S(2)}, u32[]{:S(2)}) collective-permute-start(bf16[16,8320]{1,0:T(8,128)(2,1)S(1)} %pad_maximum_fusion.refs_0_), channel_id=1, source_target_pairs={{0,4},{1,5},{2,6},{3,7},{4,0},{5,1},{6,2},{7,3},{8,12},{9,13},{10,... | collective-permute-start | bytes 798728 | tf_op jit(solution)/shard_map/ppermute | solution.py:100
  16.8 9.0 %collective-permute-start.5 = (bf16[16,8320]{1,0:T(8,128)(2,1)S(1)}, bf16[16,8320]{1,0:T(8,128)(2,1)S(1)}, u32[]{:S(2)}, u32[]{:S(2)}) collective-permute-start(bf16[16,8320]{1,0:T(8,128)(2,1)S(1)} %pad_maximum_fusion.refs_0_), channel_id=1, source_target_pairs={{0,1},{1,0},{2,3},{3,2},{4,5},{5,4},{6,7},{7,6},{8,9},{9,8},{10,11... | collective-permute-start | bytes 798728 | tf_op jit(solution)/shard_map/ppermute | solution.py:100
  23.2 2.6 %collective-permute-start.6 = (bf16[16,8320]{1,0:T(8,128)(2,1)S(1)}, bf16[16,8320]{1,0:T(8,128)(2,1)S(1)}, u32[]{:S(2)}, u32[]{:S(2)}) collective-permute-start(bf16[16,8320]{1,0:T(8,128)(2,1)S(1)} %collective-permute-done.3.from_ref.refs_1_), channel_id=1, source_target_pairs={{0,1},{1,0},{2,3},{3,2},{4,5},{5,4},{6,7},{7,6},{8,9},{9,8},{10,11... | collective-permute-start | bytes 798728 | tf_op jit(solution)/shard_map/ppermute | solution.py:100
  23.3 2.5 %collective-permute-start.7 = (bf16[16,8320]{1,0:T(8,128)(2,1)S(1)}, bf16[16,8320]{1,0:T(8,128)(2,1)S(1)}, u32[]{:S(2)}, u32[]{:S(2)}) collective-permute-start(bf16[16,8320]{1,0:T(8,128)(2,1)S(1)} %collective-permute-done.4.from_ref.refs_2_), channel_id=1, source_target_pairs={{0,1},{1,0},{2,3},{3,2},{4,5},{5,4},{6,7},{7,6},{8,9},{9,8},{10,11... | collective-permute-start | bytes 798728 | tf_op jit(solution)/shard_map/ppermute | solution.py:100
  23.8 6.7 %collective-permute-start.9 = (bf16[16,4224]{1,0:T(8,128)(2,1)S(1)}, bf16[16,4224]{1,0:T(8,128)(2,1)S(1)}, u32[]{:S(2)}, u32[]{:S(2)}) collective-permute-start(bf16[16,4224]{1,0:T(8,128)(2,1)S(1)} %shard_map.113), channel_id=1, source_target_pairs={{0,4},{1,5},{2,6},{3,7},{4,0},{5,1},{6,2},{7,3},{8,12},{9,13},{10,... | collective-permute-start | bytes 405512 | tf_op jit(solution)/shard_map/ppermute | solution.py:100
  25.3 5.2 %collective-permute-start.8 = (bf16[16,4096]{1,0:T(8,128)(2,1)S(1)}, bf16[16,4096]{1,0:T(8,128)(2,1)S(1)}, u32[]{:S(2)}, u32[]{:S(2)}) collective-permute-start(bf16[16,4096]{1,0:T(8,128)(2,1)S(1)} %shard_map.112), channel_id=1, source_target_pairs={{0,2},{1,3},{2,0},{3,1},{4,6},{5,7},{6,4},{7,5},{8,10},{9,11},{10,... | collective-permute-start | bytes 393224 | tf_op jit(solution)/shard_map/ppermute | solution.py:100
  30.5 13.1 %collective-permute-start.10 = (bf16[48,8192]{1,0:T(8,128)(2,1)S(1)}, bf16[48,8192]{1,0:T(8,128)(2,1)S(1)}, u32[]{:S(2)}, u32[]{:S(2)}) collective-permute-start(bf16[48,8192]{1,0:T(8,128)(2,1)S(1)} %get-tuple-element.58), channel_id=1, source_target_pairs={{0,1},{1,0},{2,3},{3,2},{4,5},{5,4},{6,7},{7,6},{8,9},{9,8},{10,11... | collective-permute-start | bytes 2359304 | tf_op jit(solution)/shard_map/ppermute | solution.py:100
  30.5 2.7 %collective-permute-start.12 = (bf16[16,4224]{1,0:T(8,128)(2,1)S(1)}, bf16[16,4224]{1,0:T(8,128)(2,1)S(1)}, u32[]{:S(2)}, u32[]{:S(2)}) collective-permute-start(bf16[16,4224]{1,0:T(8,128)(2,1)S(1)} %collective-permute-done.9.refs_1_), channel_id=1, source_target_pairs={{0,1},{1,0},{2,3},{3,2},{4,5},{5,4},{6,7},{7,6},{8,9},{9,8},{10,11... | collective-permute-start | bytes 405512 | tf_op jit(solution)/shard_map/ppermute | solution.py:100
  31.0 2.2 %collective-permute-start.11 = (bf16[16,4096]{1,0:T(8,128)(2,1)S(1)}, bf16[16,4096]{1,0:T(8,128)(2,1)S(1)}, u32[]{:S(2)}, u32[]{:S(2)}) collective-permute-start(bf16[16,4096]{1,0:T(8,128)(2,1)S(1)} %collective-permute-done.8.refs_0_), channel_id=1, source_target_pairs={{0,1},{1,0},{2,3},{3,2},{4,5},{5,4},{6,7},{7,6},{8,9},{9,8},{10,11... | collective-permute-start | bytes 393224 | tf_op jit(solution)/shard_map/ppermute | solution.py:100
  36.1 1.6 %collective-permute-start.13 = (bf16[16,8192]{1,0:T(8,128)(2,1)S(1)}, bf16[16,8192]{1,0:T(8,128)(2,1)S(1)}, u32[]{:S(2)}, u32[]{:S(2)}) collective-permute-start(bf16[16,8192]{1,0:T(8,128)(2,1)S(1)} %get-tuple-element.62), channel_id=1, source_target_pairs={{0,1},{1,0},{2,3},{3,2},{4,5},{5,4},{6,7},{7,6},{8,9},{9,8},{10,11... | collective-permute-start | bytes 786440 | tf_op jit(solution)/shard_map/ppermute | solution.py:100
  37.8 5.6 %collective-permute-start.14 = (bf16[16,4096]{1,0:T(8,128)(2,1)S(1)}, bf16[16,4096]{1,0:T(8,128)(2,1)S(1)}, u32[]{:S(2)}, u32[]{:S(2)}) collective-permute-start(bf16[16,4096]{1,0:T(8,128)(2,1)S(1)} %get-tuple-element.63), channel_id=1, source_target_pairs={{0,4},{1,5},{2,6},{3,7},{4,0},{5,1},{6,2},{7,3},{8,12},{9,13},{10,... | collective-permute-start | bytes 393224 | tf_op jit(solution)/shard_map/ppermute | solution.py:100
  38.4 5.3 %collective-permute-start.15 = (bf16[16,4096]{1,0:T(8,128)(2,1)S(1)}, bf16[16,4096]{1,0:T(8,128)(2,1)S(1)}, u32[]{:S(2)}, u32[]{:S(2)}) collective-permute-start(bf16[16,4096]{1,0:T(8,128)(2,1)S(1)} %get-tuple-element.64), channel_id=1, source_target_pairs={{0,2},{1,3},{2,0},{3,1},{4,6},{5,7},{6,4},{7,5},{8,10},{9,11},{10,... | collective-permute-start | bytes 393224 | tf_op jit(solution)/shard_map/ppermute | solution.py:100
  43.8 7.3 %collective-permute-start.16 = (bf16[16,8192]{1,0:T(8,128)(2,1)S(1)}, bf16[16,8192]{1,0:T(8,128)(2,1)S(1)}, u32[]{:S(2)}, u32[]{:S(2)}) collective-permute-start(bf16[16,8192]{1,0:T(8,128)(2,1)S(1)} %get-tuple-element.72), channel_id=1, source_target_pairs={{0,4},{1,5},{2,6},{3,7},{4,0},{5,1},{6,2},{7,3},{8,12},{9,13},{10,... | collective-permute-start | bytes 786440 | tf_op jit(solution)/shard_map/ppermute | solution.py:100
  45.4 6.9 %collective-permute-start.17 = (bf16[16,8192]{1,0:T(8,128)(2,1)S(1)}, bf16[16,8192]{1,0:T(8,128)(2,1)S(1)}, u32[]{:S(2)}, u32[]{:S(2)}) collective-permute-start(bf16[16,8192]{1,0:T(8,128)(2,1)S(1)} %get-tuple-element.73), channel_id=1, source_target_pairs={{0,2},{1,3},{2,0},{3,1},{4,6},{5,7},{6,4},{7,5},{8,10},{9,11},{10,... | collective-permute-start | bytes 786440 | tf_op jit(solution)/shard_map/ppermute | solution.py:100
  52.5 4.8 %collective-permute-start.18 = (bf16[4,8192]{1,0:T(4,128)(2,1)S(1)}, bf16[4,8192]{1,0:T(4,128)(2,1)S(1)}, u32[]{:S(2)}, u32[]{:S(2)}) collective-permute-start(bf16[4,8192]{1,0:T(4,128)(2,1)S(1)} %get-tuple-element.81), channel_id=1, source_target_pairs={{0,8},{1,9},{2,10},{3,11},{4,12},{5,13},{6,14},{7,15},{8,0},{9,1},... | collective-permute-start | bytes 196616 | tf_op jit(solution)/shard_map/ppermute | solution.py:100
  52.5 6.2 %collective-permute-start.20 = (bf16[4,8192]{1,0:T(4,128)(2,1)S(1)}, bf16[4,8192]{1,0:T(4,128)(2,1)S(1)}, u32[]{:S(2)}, u32[]{:S(2)}) collective-permute-start(bf16[4,8192]{1,0:T(4,128)(2,1)S(1)} %get-tuple-element.82), channel_id=1, source_target_pairs={{0,24},{1,25},{2,26},{3,27},{4,28},{5,29},{6,30},{7,31},{8,16},{9,... | collective-permute-start | bytes 196616 | tf_op jit(solution)/shard_map/ppermute | solution.py:100
  54.1 6.3 %collective-permute-start.19 = (bf16[4,8192]{1,0:T(4,128)(2,1)S(1)}, bf16[4,8192]{1,0:T(4,128)(2,1)S(1)}, u32[]{:S(2)}, u32[]{:S(2)}) collective-permute-start(bf16[4,8192]{1,0:T(4,128)(2,1)S(1)} %get-tuple-element.83), channel_id=1, source_target_pairs={{0,16},{1,17},{2,18},{3,19},{4,20},{5,21},{6,22},{7,23},{8,24},{9,... | collective-permute-start | bytes 196616 | tf_op jit(solution)/shard_map/ppermute | solution.py:100

commit v6 on v3

v6 whole, which is shorter than its diff:
```python
import functools

import jax
import jax.numpy as jnp
from jax import lax
from jax.experimental import pallas as pl
from jax.experimental.pallas import tpu as pltpu
from jax.sharding import PartitionSpec as P

ROW_CAP = 16
AXES = ("dp", "expert")


def contract_rows(left, right):
    return lax.dot_general(
        left, right, (((1,), (1,)), ((), ())), preferred_element_type=jnp.float32
    )


def contract_first(left, right):
    return lax.dot_general(
        left, right, (((0,), (0,)), ((), ())), preferred_element_type=jnp.float32
    )


def slotted(tokens, expert_ids, route_weights, out_grad, gate_weight, up_weight, down_weight):
    expert = lax.axis_index("expert")
    width = tokens.shape[1]
    local_tokens = tokens.shape[0]
    group_x, group_dy, group_w = (
        lax.all_gather(tokens, "expert", axis=0, tiled=True),
        lax.all_gather(out_grad, "expert", axis=0, tiled=True),
        lax.all_gather(route_weights, "expert", axis=0, tiled=True),
    )
    group_ids = lax.all_gather(expert_ids, "expert", axis=0, tiled=True)
    matches = group_ids == expert
    routed = jnp.any(matches, axis=1)
    weight = jnp.sum(jnp.where(matches, group_w.astype(jnp.float32), 0.0), axis=1)
    slot_rank = jnp.cumsum(routed.astype(jnp.int32)) - 1
    slot_index = jnp.arange(ROW_CAP, dtype=jnp.int32)
    picker = ((slot_rank[None, :] == slot_index[:, None]) & routed[None, :]).astype(jnp.bfloat16)
    slot_x = jnp.dot(picker, group_x, preferred_element_type=jnp.float32).astype(jnp.bfloat16)
    scaled = (weight[:, None] * group_dy.astype(jnp.float32)).astype(jnp.bfloat16)
    slot_dy = jnp.dot(picker, scaled, preferred_element_type=jnp.float32).astype(jnp.bfloat16)
    w_gate = gate_weight[0]
    w_up = up_weight[0]
    w_down = down_weight[0]
    all_x = lax.all_gather(slot_x, "dp", axis=0, tiled=True)
    gate_pre = contract_rows(w_gate, all_x)
    up_pre = contract_rows(w_up, all_x)
    gate_sig = jax.nn.sigmoid(gate_pre)
    silu_gate = gate_pre * gate_sig
    hidden = (silu_gate * up_pre).astype(jnp.bfloat16)
    expert_out = lax.psum_scatter(
        contract_first(hidden, w_down).astype(jnp.bfloat16), "dp", scatter_dimension=0, tiled=True
    )
    all_dy = lax.all_gather(slot_dy, "dp", axis=0, tiled=True)
    hidden_grad = contract_rows(w_down, all_dy)
    silu_slope = gate_sig * (1.0 + gate_pre * (1.0 - gate_sig))
    gate_act = (hidden_grad * up_pre * silu_slope).astype(jnp.bfloat16)
    up_act = (hidden_grad * silu_gate).astype(jnp.bfloat16)
    grad_down = jnp.dot(hidden, all_dy, preferred_element_type=jnp.float32).astype(jnp.bfloat16)
    grad_gate = jnp.dot(gate_act, all_x, preferred_element_type=jnp.float32).astype(jnp.bfloat16)
    grad_up = jnp.dot(up_act, all_x, preferred_element_type=jnp.float32).astype(jnp.bfloat16)
    expert_in = lax.psum_scatter(
        (contract_first(gate_act, w_gate) + contract_first(up_act, w_up)).astype(jnp.bfloat16),
        "dp",
        scatter_dimension=0,
        tiled=True,
    )
    back_out = contract_first(picker, expert_out).astype(jnp.bfloat16)
    back_in = contract_first(picker, expert_in).astype(jnp.bfloat16)
    got_out, got_in = (
        lax.all_to_all(back_out, "expert", split_axis=0, concat_axis=0, tiled=True),
        lax.all_to_all(back_in, "expert", split_axis=0, concat_axis=0, tiled=True),
    )
    expert_count = lax.axis_size("expert")
    got_out = got_out.reshape(expert_count, local_tokens, width)
    got_in = got_in.reshape(expert_count, local_tokens, width)
    expert_range = jnp.arange(expert_count, dtype=jnp.int32)
    own_match = expert_ids[:, :, None] == expert_range[None, None, :]
    mix_weight = jnp.sum(
        jnp.where(own_match, route_weights.astype(jnp.float32)[:, :, None], 0.0), axis=1
    )
    mixed_out = jnp.sum(jnp.transpose(mix_weight)[:, :, None] * got_out.astype(jnp.float32), axis=0)
    input_total = jnp.sum(got_in.astype(jnp.float32), axis=0)
    return (
        mixed_out.astype(jnp.bfloat16),
        input_total.astype(jnp.bfloat16),
        grad_gate[None],
        grad_up[None],
        grad_down[None],
    )


CORE, FAR = 1, (2, 4, 6)


def from_xor(value, mask, devices):
    return lax.ppermute(value, AXES, [(i, i ^ mask) for i in range(devices)])


def kernel_call(body, out_shape, cost, *operands, scratch=(), hbm=()):
    vmem, smem = pl.BlockSpec(memory_space=pltpu.VMEM), pl.BlockSpec(memory_space=pltpu.SMEM)
    stay = pl.BlockSpec(memory_space=pltpu.HBM)
    specs = [stay if i in hbm else smem if o.ndim == 1 else vmem for i, o in enumerate(operands)]
    operands = [
        pltpu.with_memory_space_constraint(o, pltpu.HBM) if i in hbm else o
        for i, o in enumerate(operands)
    ]
    return pl.pallas_call(
        body,
        out_shape=out_shape,
        in_specs=specs,
        out_specs=jax.tree.map(lambda _: vmem, out_shape),
        scratch_shapes=scratch,
        compiler_params=pltpu.CompilerParams(vmem_limit_bytes=16 << 20),
        cost_estimate=pl.CostEstimate(flops=cost, bytes_accessed=4 << 20, transcendentals=0),
    )(*operands)


def copy_all(pairs, sems):
    copies = [pltpu.make_async_copy(src, dst, sems.at[i]) for i, (src, dst) in enumerate(pairs)]
    for copy in copies:
        copy.start()
    for copy in copies:
        copy.wait()


def load_body(*refs):
    count = len(refs) // 2
    copy_all(list(zip(refs[:count], refs[count:-1])), refs[-1])


def pack_body(x_ref, dy_ref, ids_ref, w_ref, expert_ref, msg_ref, mine_ref, *scratch):
    x_buf, dy_buf, ids_buf, w_buf, sems = scratch
    rows, width = x_ref.shape
    top = ids_ref.shape[0]
    lanes = msg_ref.shape[1] - 2 * width
    copy_all([(x_ref, x_buf), (dy_ref, dy_buf), (ids_ref, ids_buf), (w_ref, w_buf)], sems)
    msg_ref[:, :width] = x_buf[...]
    msg_ref[:, width : 2 * width] = dy_buf[...]
    diagonal = lax.broadcasted_iota(jnp.int32, (rows, rows), 0) == lax.broadcasted_iota(
        jnp.int32, (rows, rows), 1
    )
    expert = lax.broadcasted_iota(jnp.int32, (rows, lanes), 1)
    top_weights = w_buf[...].astype(jnp.float32)
    route = jnp.zeros((rows, lanes), jnp.float32)
    for k in range(top):
        named = jnp.sum(jnp.where(diagonal, ids_buf[k : k + 1, :], 0), axis=1, keepdims=True)
        weight = jnp.sum(jnp.where(diagonal, top_weights[k : k + 1, :], 0.0), axis=1, keepdims=True)
        route = route + jnp.where(expert == named, weight, 0.0)
    msg_ref[:, 2 * width :] = route.astype(jnp.bfloat16)
    lane = lax.broadcasted_iota(jnp.int32, mine_ref.shape, 1)
    mine_ref[...] = jnp.where(lane == expert_ref[0], 1.0, 0.0)


def places(pieces):
    start = 0
    for piece in pieces:
        yield slice(start, start + piece.shape[0]), piece
        start += piece.shape[0]


def cotangent_places(pieces):
    rows = pieces[0].shape[0] // 2
    for i, piece in enumerate(pieces):
        for k in range(2):
            at = i // 2 * 4 + (2 * k if i % 2 == 0 else 2 * k + 1)
            yield slice(at * rows, (at + 1) * rows), piece, slice(k * rows, (k + 1) * rows)


def stack_body(*refs):
    for here, piece in places(refs[:-1]):
        refs[-1][here, :] = piece[...]


def forward_body(count, *refs):
    pieces, (wg_ref, wu_ref, x_ref, hidden_ref, gate_ref, up_ref) = refs[:count], refs[count:]
    for here, piece in places(pieces):
        x_ref[here, :] = piece[...]
    x = x_ref[...]
    gate_pre = contract_rows(x, wg_ref[0])
    up_pre = contract_rows(x, wu_ref[0])
    gate_sig = 1.0 / (1.0 + jnp.exp(-gate_pre))
    silu_gate = gate_pre * gate_sig
    hidden_ref[...] = silu_gate * up_pre
    gate_ref[...] = up_pre * (gate_sig * (1.0 + gate_pre * (1.0 - gate_sig)))
    up_ref[...] = silu_gate


def out_body(count, *refs):
    pieces, (hidden_ref, wd_ref, mine_ref, weight_ref, scaled_ref, msg_ref) = (
        refs[:count],
        refs[count:],
    )
    half, width = msg_ref.shape
    for here, piece, there in cotangent_places(pieces):
        route = piece[there, width:].astype(jnp.float32) * mine_ref[:1, :]
        weight = jnp.sum(route, axis=1, keepdims=True)
        weight_ref[here, :] = jnp.broadcast_to(weight, (route.shape[0], weight_ref.shape[1]))
        scaled_ref[here, :] = (weight * hidden_ref[here, :]).astype(jnp.bfloat16)
    msg_ref[...] = jnp.dot(
        scaled_ref[half:, :], wd_ref[0], preferred_element_type=jnp.float32
    ).astype(jnp.bfloat16)


def into_sum(gate_act, up_act, wg_ref, wu_ref):
    return jnp.dot(gate_act, wg_ref[0], preferred_element_type=jnp.float32) + jnp.dot(
        up_act, wu_ref[0], preferred_element_type=jnp.float32
    )


def into_body(count, *refs):
    pieces, rest = refs[:count], refs[count:]
    weight_ref, gate_ref, up_ref, wg_ref, wu_ref, wd_ref = rest[:6]
    dy_ref, gate_act_ref, up_act_ref, msg_ref = rest[6:]
    half, width = msg_ref.shape
    for here, piece, there in cotangent_places(pieces):
        dy_ref[here, :] = piece[there, :width]
    hidden_grad = weight_ref[:, :1] * contract_rows(dy_ref[...], wd_ref[0])
    gate_act_ref[...] = (hidden_grad * gate_ref[...]).astype(jnp.bfloat16)
    up_act_ref[...] = (hidden_grad * up_ref[...]).astype(jnp.bfloat16)
    msg_ref[...] = into_sum(gate_act_ref[half:, :], up_act_ref[half:, :], wg_ref, wu_ref).astype(
        jnp.bfloat16
    )


def scattered(total, outs):
    rows = outs[0].shape[0]
    for i, ref in enumerate(outs):
        ref[...] = total[i * rows : (i + 1) * rows, :].astype(ref.dtype)


def own_out_body(scaled_ref, wd_ref, passed_ref, *outs):
    half = passed_ref.shape[0]
    total = jnp.dot(scaled_ref[:half, :], wd_ref[0], preferred_element_type=jnp.float32)
    scattered(total + passed_ref[...].astype(jnp.float32), outs)


def own_into_body(gate_act_ref, up_act_ref, wg_ref, wu_ref, passed_ref, *outs):
    half = passed_ref.shape[0]
    total = into_sum(gate_act_ref[:half, :], up_act_ref[:half, :], wg_ref, wu_ref)
    scattered(total + passed_ref[...].astype(jnp.float32), outs)


def turn_body(here_ref, came_ref, to_ref):
    to_ref[...] = (here_ref[...] + came_ref[...].astype(jnp.float32)).astype(jnp.bfloat16)


def deal_body(*refs):
    parts, outs = refs[:6], refs[6:]
    width, rows = parts[0].shape[1], outs[0].shape[0]
    for side in range(2):
        at = slice(side * width, (side + 1) * width)
        here = parts[3 * side : 3 * side + 3]
        total = here[0][...]
        for part in here[1:]:
            total = total + part[...].astype(jnp.float32)
        for i, ref in enumerate(outs):
            ref[:, at] = total[i * rows : (i + 1) * rows, :].astype(ref.dtype)


def end_body(own_ref, *refs):
    parts, (out_ref, into_ref) = refs[:-2], refs[-2:]
    total = own_ref[...]
    for part in parts:
        total = total + part[...].astype(jnp.float32)
    width = out_ref.shape[1]
    out_ref[...] = total[:, :width].astype(jnp.bfloat16)
    into_ref[...] = total[:, width:].astype(jnp.bfloat16)


def grad_body(rows_ref, *refs):
    acts, grads = refs[: len(refs) // 2], refs[len(refs) // 2 :]
    for act_ref, ref in zip(acts, grads):
        ref[0] = contract_first(act_ref[...], rows_ref[...]).astype(jnp.bfloat16)


def dense(tokens, expert_ids, route_weights, out_grad, gate_weight, up_weight, down_weight):
    experts = lax.axis_size("expert")
    devices = lax.axis_size("dp") * experts
    expert = lax.axis_index("expert").astype(jnp.int32).reshape(1)
    rows, width = tokens.shape
    ff = gate_weight.shape[1]
    near = tuple(k << 3 for k in range(1, devices >> 3))
    block_rows = rows * (len(near) + 1)
    bf16, f32 = jnp.bfloat16, jnp.float32
    columns = 2 * width + experts + -experts % 128
    unit = 2 * block_rows * ff * width

    def shape(*dims, dtype=bf16):
        return jax.ShapeDtypeStruct(dims, dtype)

    def passed(value, mask):
        return from_xor(value, mask, devices)

    message, mine = kernel_call(
        pack_body,
        (shape(rows, columns), shape(8, columns - 2 * width, dtype=f32)),
        0,
        tokens,
        out_grad,
        expert_ids.T,
        route_weights.T,
        expert,
        scratch=[
            pltpu.VMEM((rows, width), bf16),
            pltpu.VMEM((rows, width), bf16),
            pltpu.VMEM(expert_ids.shape[::-1], jnp.int32),
            pltpu.VMEM(route_weights.shape[::-1], bf16),
            pltpu.SemaphoreType.DMA((4,)),
        ],
        hbm=(0, 1, 2, 3),
    )
    weights = kernel_call(
        load_body,
        (shape(*gate_weight.shape),) * 3,
        0,
        gate_weight,
        up_weight,
        down_weight,
        scratch=[pltpu.SemaphoreType.DMA((3,))],
        hbm=(0, 1, 2),
    )
    arrived = [message] + [passed(message, m) for m in near]
    block_x = jnp.concatenate([piece[:, :width] for piece in arrived], axis=0)
    block_dy = jnp.concatenate([piece[:, width:] for piece in arrived], axis=0)
    block_x, block_dy, *weights = lax.optimization_barrier((block_x, block_dy, *weights))
    w_gate, w_up, w_down = weights

    first, second, _ = FAR
    second_x, first_dy = passed(block_x, second), passed(block_dy, first)
    second_dy, first_x = passed(block_dy, second), passed(block_x, first)
    corner_x, corner_dy = passed(second_x, first), passed(first_dy, second)
    half = (len(FAR) + 1) * block_rows

    def both_cores(*pairs):
        own = [
            kernel_call(stack_body, shape(2 * block_rows, pair[0].shape[1]), 0, *pair)
            for pair in pairs
        ]
        return own + [passed(pair, CORE) for pair in own]

    x_pieces = both_cores((block_x, second_x), (first_x, corner_x))
    early_dy, late_dy, other_early, other_late = both_cores(
        (block_dy, first_dy), (second_dy, corner_dy)
    )
    dy_pieces = [early_dy, late_dy, other_early, other_late]
    all_x, hidden, gate_part, up_part = kernel_call(
        functools.partial(forward_body, len(x_pieces)),
        (shape(2 * half, width),) + (shape(2 * half, ff, dtype=f32),) * 3,
        16 * unit,
        *x_pieces,
        w_gate,
        w_up,
    )
    weight, scaled, message = kernel_call(
        functools.partial(out_body, len(dy_pieces)),
        (
            shape(2 * half, columns - 2 * width, dtype=f32),
            shape(2 * half, ff),
            shape(half, width),
        ),
        4 * unit,
        *dy_pieces,
        hidden,
        w_down,
        mine,
    )
    passed_out = passed(message, CORE)
    all_dy, gate_act, up_act, message = kernel_call(
        functools.partial(into_body, len(dy_pieces)),
        (shape(2 * half, width), shape(2 * half, ff), shape(2 * half, ff), shape(half, width)),
        16 * unit,
        *dy_pieces,
        weight,
        gate_part,
        up_part,
        *weights,
    )
    passed_into = passed(message, CORE)

    piece, full = shape(block_rows, width), shape(block_rows, width, dtype=f32)
    out_here, out_second, out_first, out_corner = kernel_call(
        own_out_body, (full, piece, full, piece), 4 * unit, scaled, w_down, passed_out
    )
    passed_into, out_here = lax.optimization_barrier((passed_into, out_here))
    into_here, into_second, into_first, into_corner = kernel_call(
        own_into_body, (full, full, piece, piece), 8 * unit, gate_act, up_act, w_gate, w_up, passed_into
    )
    out_first = kernel_call(turn_body, piece, 0, out_first, passed(out_corner, second))
    into_second = kernel_call(turn_body, piece, 0, into_second, passed(into_corner, first))
    out_back = [passed(out_second, second), passed(out_first, first)]
    into_back = [passed(into_first, first), passed(into_second, second)]
    into_here, scaled, gate_act, up_act = lax.optimization_barrier(
        (into_here, scaled, gate_act, up_act)
    )
    grad_down = kernel_call(grad_body, shape(*down_weight.shape), 8 * unit, all_dy, scaled)
    into_here, grad_down = lax.optimization_barrier((into_here, grad_down))
    mine_sum, *away = kernel_call(
        deal_body,
        (shape(rows, 2 * width, dtype=f32),) + (shape(rows, 2 * width),) * len(near),
        0,
        out_here,
        *out_back,
        into_here,
        *into_back,
    )
    mine_sum, gate_act, up_act = lax.optimization_barrier((mine_sum, gate_act, up_act))
    grad_gate, grad_up = kernel_call(
        grad_body, (shape(*gate_weight.shape),) * 2, 16 * unit, all_x, gate_act, up_act
    )
    mixed, input_grad = kernel_call(
        end_body,
        (shape(rows, width),) * 2,
        0,
        mine_sum,
        *[passed(piece, m) for m, piece in zip(near, away)],
    )
    return mixed, input_grad, grad_gate, grad_up, grad_down


def shards(tokens, *others):
    experts = lax.axis_size("expert")
    devices = lax.axis_size("dp") * experts
    whole_group = tokens.shape[0] * experts <= ROW_CAP
    if whole_group and devices >= 16 and devices & (devices - 1) == 0:
        return dense(tokens, *others)
    return slotted(tokens, *others)


def solution(mesh):
    return jax.shard_map(
        shards,
        mesh=mesh,
        in_specs=(
            P(("dp", "expert"), None),
            P(("dp", "expert"), None),
            P(("dp", "expert"), None),
            P(("dp", "expert"), None),
            P("expert", "dp", None),
            P("expert", "dp", None),
            P("expert", "dp", None),
        ),
        out_specs=(
            P(("dp", "expert"), None),
            P(("dp", "expert"), None),
            P("expert", "dp", None),
            P("expert", "dp", None),
            P("expert", "dp", None),
        ),
        check_vma=False,
    )
```

time: 72.4 us -> 56.2 us (0.78)
  starting transfers between devices: 37.3 us -> 25.3 us
  local copies, waits for them, and re-layouts: 11.1 us -> 0.11 us
  waiting for transfers between devices: 7.01 us -> 16.4 us
  other arithmetic: 2.25 us -> 0.17 us
    ppermute x34 -> x24, starting transfers between devices: 37.3 us -> 25.3 us  [from_xor(): return lax.ppermute(value, AXES, [(i, i ^ mask) for i in range(devices)])]
    unnamed x36 -> x0, local copies, waits for them, and re-layouts: 11 us -> none
    ppermute x34 -> x24, waiting for transfers between devices: 7.01 us -> 16.4 us  [from_xor(): return lax.ppermute(value, AXES, [(i, i ^ mask) for i in range(devices)])]
    convert_element_type x4 -> x0, other arithmetic: 1.43 us -> none  [the longest x2 1.31 us: reduced(): return total.astype(bf16)]
    pallas_call x10 -> x17, Pallas kernels: 13.5 us -> 13.1 us  [kernel_call(): pl.pallas_call(body, out_shape=out_shape, in_specs=specs, out_specs=jax.t...]
  transfers between devices with their start and end apart: 34 -> 24, of which waited for: 7 -> 11; matrix products, arithmetic and copies ran while one was open for 2% -> 0% of each run, Pallas kernels for 17% -> 18%
where the time goes in v6:
time: 56.2 us; the launch traced here: 56 us
  starting transfers between devices  25.3 us (45%)
  waiting for transfers between devices  16.4 us (29%)
  Pallas kernels  13.1 us (23%)
  between operations  0.87 us (2%)
    ppermute x24, starting transfers between devices, from_xor(): return lax.ppermute(value, AXES, [(i, i ^ mask) for i in range(devices)])  25.3 us
    ppermute x24, waiting for transfers between devices, from_xor(): return lax.ppermute(value, AXES, [(i, i ^ mask) for i in range(devices)])  16.4 us
    pallas_call x17, Pallas kernels, kernel_call(): pl.pallas_call(body, out_shape=out_shape, in_specs=specs, out_specs=jax.t...  13.1 us
  transfers between devices with their start and end apart: 24, of which 11 were waited for; matrix products, arithmetic and copies ran while one was open for 0% of the time, Pallas kernels for 18%

profile of v6, /device:TPU:0, one launch (start us, length us, event | category | flops | bytes accessed | tf_op | source)
XLA Modules:
  0.0 56.0 jit_solution(13317331756314158523)
XLA Ops:
  1.5 5.1 %collective-permute-start.2 = (bf16[4,8320]{1,0:T(4,128)(2,1)S(1)}, bf16[4,8320]{1,0:T(4,128)(2,1)S(1)}, u32[]{:S(2)}, u32[]{:S(2)}) collective-permute-start(bf16[4,8320]{1,0:T(4,128)(2,1)S(1)} %get-tuple-element.53), channel_id=1, source_target_pairs={{0,24},{1,25},{2,26},{3,27},{4,28},{5,29},{6,30},{7,31},{8,16},{9,... | collective-permute-start | bytes 199688 | tf_op jit(solution)/shard_map/ppermute | solution.py:100
  7.3 2.4 %shard_map.111 = (bf16[1,192,4096]{2,1,0:T(8,128)(2,1)S(1)}, bf16[1,192,4096]{2,1,0:T(8,128)(2,1)S(1)}, bf16[1,192,4096]{2,1,0:T(8,128)(2,1)S(1)}) custom-call(bf16[1,192,4096]{2,1,0:T(8,128)(2,1)} %refs_0_.1, bf16[1,192,4096]{2,1,0:T(8,128)(2,1)} %refs_1_.1, bf16[1,192,4096]{2,1,0:T(8,128)(2,1)} %refs_2_.1), custom_call_target="tpu_custom_call" | custom-call | bytes 4194304 | tf_op jit(solution)/shard_map/pallas_call | solution.py:111
  9.8 2.6 %collective-permute-done.1 = bf16[4,8320]{1,0:T(4,128)(2,1)S(1)} collective-permute-done((bf16[4,8320]{1,0:T(4,128)(2,1)S(1)}, bf16[4,8320]{1,0:T(4,128)(2,1)S(1)}, u32[]{:S(2)}, u32[]{:S(2)}) %collective-permute-start.1) | collective-permute-done | bytes 66592 | tf_op jit(solution)/shard_map/ppermute | solution.py:100
  12.6 1.6 %collective-permute-start.8 = (bf16[16,4096]{1,0:T(8,128)(2,1)S(1)}, bf16[16,4096]{1,0:T(8,128)(2,1)S(1)}, u32[]{:S(2)}, u32[]{:S(2)}) collective-permute-start(bf16[16,4096]{1,0:T(8,128)(2,1)S(1)} %pad_maximum_fusion.1.refs_0_), channel_id=1, source_target_pairs={{0,4},{1,5},{2,6},{3,7},{4,0},{5,1},{6,2},{7,3},{8,12},{9,13},{10,... | collective-permute-start | bytes 393224 | tf_op jit(solution)/shard_map/ppermute | solution.py:100
  14.2 1.5 %collective-permute-start.3 = (bf16[16,4224]{1,0:T(8,128)(2,1)S(1)}, bf16[16,4224]{1,0:T(8,128)(2,1)S(1)}, u32[]{:S(2)}, u32[]{:S(2)}) collective-permute-start(bf16[16,4224]{1,0:T(8,128)(2,1)S(1)} %pad_maximum_fusion.refs_0_), channel_id=1, source_target_pairs={{0,2},{1,3},{2,0},{3,1},{4,6},{5,7},{6,4},{7,5},{8,10},{9,11},{10,... | collective-permute-start | bytes 405512 | tf_op jit(solution)/shard_map/ppermute | solution.py:100
  16.2 1.5 %collective-permute-done.8.refs_1_ = bf16[16,4096]{1,0:T(8,128)(2,1)S(1)} collective-permute-done((bf16[16,4096]{1,0:T(8,128)(2,1)S(1)}, bf16[16,4096]{1,0:T(8,128)(2,1)S(1)}, u32[]{:S(2)}, u32[]{:S(2)}) %collective-permute-start.8) | collective-permute-done | bytes 131104 | tf_op jit(solution)/shard_map/ppermute | solution.py:100
  17.7 1.8 %collective-permute-start.10 = (bf16[16,4096]{1,0:T(8,128)(2,1)S(1)}, bf16[16,4096]{1,0:T(8,128)(2,1)S(1)}, u32[]{:S(2)}, u32[]{:S(2)}) collective-permute-start(bf16[16,4096]{1,0:T(8,128)(2,1)S(1)} %collective-permute-done.8.refs_1_), channel_id=1, source_target_pairs={{0,2},{1,3},{2,0},{3,1},{4,6},{5,7},{6,4},{7,5},{8,10},{9,11},{10,... | collective-permute-start | bytes 393224 | tf_op jit(solution)/shard_map/ppermute | solution.py:100
  19.5 1.5 %collective-permute-start.4 = (bf16[16,4224]{1,0:T(8,128)(2,1)S(1)}, bf16[16,4224]{1,0:T(8,128)(2,1)S(1)}, u32[]{:S(2)}, u32[]{:S(2)}) collective-permute-start(bf16[16,4224]{1,0:T(8,128)(2,1)S(1)} %pad_maximum_fusion.refs_0_), channel_id=1, source_target_pairs={{0,4},{1,5},{2,6},{3,7},{4,0},{5,1},{6,2},{7,3},{8,12},{9,13},{10,... | collective-permute-start | bytes 405512 | tf_op jit(solution)/shard_map/ppermute | solution.py:100
  21.6 1.9 %collective-permute-done.9.refs_0_ = bf16[16,4096]{1,0:T(8,128)(2,1)S(1)} collective-permute-done((bf16[16,4096]{1,0:T(8,128)(2,1)S(1)}, bf16[16,4096]{1,0:T(8,128)(2,1)S(1)}, u32[]{:S(2)}, u32[]{:S(2)}) %collective-permute-start.9) | collective-permute-done | bytes 131104 | tf_op jit(solution)/shard_map/ppermute | solution.py:100
  23.5 1.4 %collective-permute-done.10.refs_1_ = bf16[16,4096]{1,0:T(8,128)(2,1)S(1)} collective-permute-done((bf16[16,4096]{1,0:T(8,128)(2,1)S(1)}, bf16[16,4096]{1,0:T(8,128)(2,1)S(1)}, u32[]{:S(2)}, u32[]{:S(2)}) %collective-permute-start.10) | collective-permute-done | bytes 131104 | tf_op jit(solution)/shard_map/ppermute | solution.py:100
  25.6 1.0 %collective-permute-done.5.refs_1_ = bf16[16,4224]{1,0:T(8,128)(2,1)S(1)} collective-permute-done((bf16[16,4224]{1,0:T(8,128)(2,1)S(1)}, bf16[16,4224]{1,0:T(8,128)(2,1)S(1)}, u32[]{:S(2)}, u32[]{:S(2)}) %collective-permute-start.5) | collective-permute-done | bytes 135200 | tf_op jit(solution)/shard_map/ppermute | solution.py:100
  26.7 1.3 %shard_map.116 = (bf16[128,4096]{1,0:T(8,128)(2,1)S(1)}, f32[128,192]{1,0:T(8,128)S(1)}, f32[128,192]{1,0:T(8,128)S(1)}, f32[128,192]{1,0:T(8,128)S(1)}) custom-call(bf16[32,4096]{1,0:T(8,128)(2,1)S(1)} %shard_map.114.refs_0_, bf16[32,4096]{1,0:T(8,128)(2,1)S(1)} %shard_map.115.refs_1_, bf16[32,4096]{1,0:T(8,128)(2,1)S(1)} %collective-permute-done.11.refs_2_, ...), custom_call_target="tpu_custom_call" | custom-call | flops 402653184 | bytes 4194304 | tf_op jit(solution)/shard_map/pallas_call | solution.py:111
  29.1 1.9 %shard_map.118 = (bf16[128,4096]{1,0:T(8,128)(2,1)S(1)}, bf16[128,192]{1,0:T(8,128)(2,1)S(1)}, bf16[128,192]{1,0:T(8,128)(2,1)S(1)}, bf16[64,4096]{1,0:T(8,128)(2,1)S(1)}) custom-call(bf16[32,4224]{1,0:T(8,128)(2,1)S(1)} %shard_map.112.refs_0_, bf16[32,4224]{1,0:T(8,128)(2,1)S(1)} %shard_map.113.refs_1_, ...), custom_call_target="tpu_custom_call" | custom-call | flops 402653184 | bytes 4194304 | tf_op jit(solution)/shard_map/pallas_call | solution.py:111
  31.7 1.2 %collective-permute-done.13.passed_ref = bf16[64,4096]{1,0:T(8,128)(2,1)S(1)} collective-permute-done((bf16[64,4096]{1,0:T(8,128)(2,1)S(1)}, bf16[64,4096]{1,0:T(8,128)(2,1)S(1)}, u32[]{:S(2)}, u32[]{:S(2)}) %collective-permute-start.13) | collective-permute-done | bytes 524320 | tf_op jit(solution)/shard_map/ppermute | solution.py:100
  33.7 1.0 %collective-permute-start.19 = (bf16[16,4096]{1,0:T(8,128)(2,1)S(1)}, bf16[16,4096]{1,0:T(8,128)(2,1)S(1)}, u32[]{:S(2)}, u32[]{:S(2)}) collective-permute-start(bf16[16,4096]{1,0:T(8,128)(2,1)S(1)} %get-tuple-element.85), channel_id=1, source_target_pairs={{0,2},{1,3},{2,0},{3,1},{4,6},{5,7},{6,4},{7,5},{8,10},{9,11},{10,... | collective-permute-start | bytes 393224 | tf_op jit(solution)/shard_map/ppermute | solution.py:100
  35.7 1.5 %collective-permute-start.18 = (bf16[16,4096]{1,0:T(8,128)(2,1)S(1)}, bf16[16,4096]{1,0:T(8,128)(2,1)S(1)}, u32[]{:S(2)}, u32[]{:S(2)}) collective-permute-start(bf16[16,4096]{1,0:T(8,128)(2,1)S(1)} %get-tuple-element.83), channel_id=1, source_target_pairs={{0,2},{1,3},{2,0},{3,1},{4,6},{5,7},{6,4},{7,5},{8,10},{9,11},{10,... | collective-permute-start | bytes 393224 | tf_op jit(solution)/shard_map/ppermute | solution.py:100
  37.8 2.3 %collective-permute-done.19.came_ref = bf16[16,4096]{1,0:T(8,128)(2,1)S(1)} collective-permute-done((bf16[16,4096]{1,0:T(8,128)(2,1)S(1)}, bf16[16,4096]{1,0:T(8,128)(2,1)S(1)}, u32[]{:S(2)}, u32[]{:S(2)}) %collective-permute-start.19) | collective-permute-done | bytes 131104 | tf_op jit(solution)/shard_map/ppermute | solution.py:100
  40.1 1.6 %collective-permute-start.20 = (bf16[16,4096]{1,0:T(8,128)(2,1)S(1)}, bf16[16,4096]{1,0:T(8,128)(2,1)S(1)}, u32[]{:S(2)}, u32[]{:S(2)}) collective-permute-start(bf16[16,4096]{1,0:T(8,128)(2,1)S(1)} %shard_map.123), channel_id=1, source_target_pairs={{0,4},{1,5},{2,6},{3,7},{4,0},{5,1},{6,2},{7,3},{8,12},{9,13},{10,... | collective-permute-start | bytes 393224 | tf_op jit(solution)/shard_map/ppermute | solution.py:100
  42.3 1.7 %shard_map.122 = bf16[1,192,4096]{2,1,0:T(8,128)(2,1)} custom-call(bf16[128,4096]{1,0:T(8,128)(2,1)S(1)} %get-tuple-element.80.rows_ref, bf16[128,192]{1,0:T(8,128)(2,1)S(1)} %get-tuple-element.81.scaled_ref.refs_0_), custom_call_target="tpu_custom_call" | custom-call | flops 201326592 | bytes 4194304 | tf_op jit(solution)/shard_map/pallas_call | solution.py:111
  44.0 1.8 %collective-permute-done.20.refs_5_ = bf16[16,4096]{1,0:T(8,128)(2,1)S(1)} collective-permute-done((bf16[16,4096]{1,0:T(8,128)(2,1)S(1)}, bf16[16,4096]{1,0:T(8,128)(2,1)S(1)}, u32[]{:S(2)}, u32[]{:S(2)}) %collective-permute-start.20) | collective-permute-done | bytes 131104 | tf_op jit(solution)/shard_map/ppermute | solution.py:100
  47.0 2.3 %collective-permute-start.22 = (bf16[4,8192]{1,0:T(4,128)(2,1)S(1)}, bf16[4,8192]{1,0:T(4,128)(2,1)S(1)}, u32[]{:S(2)}, u32[]{:S(2)}) collective-permute-start(bf16[4,8192]{1,0:T(4,128)(2,1)S(1)} %get-tuple-element.91), channel_id=1, source_target_pairs={{0,16},{1,17},{2,18},{3,19},{4,20},{5,21},{6,22},{7,23},{8,24},{9,... | collective-permute-start | bytes 196616 | tf_op jit(solution)/shard_map/ppermute | solution.py:100
  49.2 2.0 %collective-permute-start.23 = (bf16[4,8192]{1,0:T(4,128)(2,1)S(1)}, bf16[4,8192]{1,0:T(4,128)(2,1)S(1)}, u32[]{:S(2)}, u32[]{:S(2)}) collective-permute-start(bf16[4,8192]{1,0:T(4,128)(2,1)S(1)} %get-tuple-element.92), channel_id=1, source_target_pairs={{0,24},{1,25},{2,26},{3,27},{4,28},{5,29},{6,30},{7,31},{8,16},{9,... | collective-permute-start | bytes 196616 | tf_op jit(solution)/shard_map/ppermute | solution.py:100
  51.3 2.4 %shard_map.126 = (bf16[1,192,4096]{2,1,0:T(8,128)(2,1)}, bf16[1,192,4096]{2,1,0:T(8,128)(2,1)}) custom-call(bf16[128,4096]{1,0:T(8,128)(2,1)S(1)} %get-tuple-element.95.rows_ref, bf16[128,192]{1,0:T(8,128)(2,1)S(1)} %get-tuple-element.96.gate_act_ref.refs_0_, bf16[128,192]{1,0:T(8,128)(2,1)S(1)} %get-tuple-element.97.up_act_ref.refs_1_), custom_call_target="tpu_custom_call" | custom-call | flops 402653184 | bytes 4194304 | tf_op jit(solution)/shard_map/pallas_call | solution.py:111
  53.7 1.6 %collective-permute-done.23.refs_2_ = bf16[4,8192]{1,0:T(4,128)(2,1)S(1)} collective-permute-done((bf16[4,8192]{1,0:T(4,128)(2,1)S(1)}, bf16[4,8192]{1,0:T(4,128)(2,1)S(1)}, u32[]{:S(2)}, u32[]{:S(2)}) %collective-permute-start.23) | collective-permute-done | bytes 65568 | tf_op jit(solution)/shard_map/ppermute | solution.py:100
  (51 shorter events, 10.3 us)
Async XLA Ops:
  1.5 8.2 %collective-permute-start.2 = (bf16[4,8320]{1,0:T(4,128)(2,1)S(1)}, bf16[4,8320]{1,0:T(4,128)(2,1)S(1)}, u32[]{:S(2)}, u32[]{:S(2)}) collective-permute-start(bf16[4,8320]{1,0:T(4,128)(2,1)S(1)} %get-tuple-element.53), channel_id=1, source_target_pairs={{0,24},{1,25},{2,26},{3,27},{4,28},{5,29},{6,30},{7,31},{8,16},{9,... | collective-permute-start | bytes 199688 | tf_op jit(solution)/shard_map/ppermute | solution.py:100
  6.7 5.7 %collective-permute-start.1 = (bf16[4,8320]{1,0:T(4,128)(2,1)S(1)}, bf16[4,8320]{1,0:T(4,128)(2,1)S(1)}, u32[]{:S(2)}, u32[]{:S(2)}) collective-permute-start(bf16[4,8320]{1,0:T(4,128)(2,1)S(1)} %get-tuple-element.53), channel_id=1, source_target_pairs={{0,16},{1,17},{2,18},{3,19},{4,20},{5,21},{6,22},{7,23},{8,24},{9,... | collective-permute-start | bytes 199688 | tf_op jit(solution)/shard_map/ppermute | solution.py:100
  6.7 5.7 %collective-permute-start = (bf16[4,8320]{1,0:T(4,128)(2,1)S(1)}, bf16[4,8320]{1,0:T(4,128)(2,1)S(1)}, u32[]{:S(2)}, u32[]{:S(2)}) collective-permute-start(bf16[4,8320]{1,0:T(4,128)(2,1)S(1)} %get-tuple-element.53), channel_id=1, source_target_pairs={{0,8},{1,9},{2,10},{3,11},{4,12},{5,13},{6,14},{7,15},{8,0},{9,1},... | collective-permute-start | bytes 199688 | tf_op jit(solution)/shard_map/ppermute | solution.py:100
  12.6 5.1 %collective-permute-start.8 = (bf16[16,4096]{1,0:T(8,128)(2,1)S(1)}, bf16[16,4096]{1,0:T(8,128)(2,1)S(1)}, u32[]{:S(2)}, u32[]{:S(2)}) collective-permute-start(bf16[16,4096]{1,0:T(8,128)(2,1)S(1)} %pad_maximum_fusion.1.refs_0_), channel_id=1, source_target_pairs={{0,4},{1,5},{2,6},{3,7},{4,0},{5,1},{6,2},{7,3},{8,12},{9,13},{10,... | collective-permute-start | bytes 393224 | tf_op jit(solution)/shard_map/ppermute | solution.py:100
  14.2 6.8 %collective-permute-start.3 = (bf16[16,4224]{1,0:T(8,128)(2,1)S(1)}, bf16[16,4224]{1,0:T(8,128)(2,1)S(1)}, u32[]{:S(2)}, u32[]{:S(2)}) collective-permute-start(bf16[16,4224]{1,0:T(8,128)(2,1)S(1)} %pad_maximum_fusion.refs_0_), channel_id=1, source_target_pairs={{0,2},{1,3},{2,0},{3,1},{4,6},{5,7},{6,4},{7,5},{8,10},{9,11},{10,... | collective-permute-start | bytes 405512 | tf_op jit(solution)/shard_map/ppermute | solution.py:100
  15.7 7.8 %collective-permute-start.9 = (bf16[16,4096]{1,0:T(8,128)(2,1)S(1)}, bf16[16,4096]{1,0:T(8,128)(2,1)S(1)}, u32[]{:S(2)}, u32[]{:S(2)}) collective-permute-start(bf16[16,4096]{1,0:T(8,128)(2,1)S(1)} %pad_maximum_fusion.1.refs_0_), channel_id=1, source_target_pairs={{0,2},{1,3},{2,0},{3,1},{4,6},{5,7},{6,4},{7,5},{8,10},{9,11},{10,... | collective-permute-start | bytes 393224 | tf_op jit(solution)/shard_map/ppermute | solution.py:100
  17.7 7.2 %collective-permute-start.10 = (bf16[16,4096]{1,0:T(8,128)(2,1)S(1)}, bf16[16,4096]{1,0:T(8,128)(2,1)S(1)}, u32[]{:S(2)}, u32[]{:S(2)}) collective-permute-start(bf16[16,4096]{1,0:T(8,128)(2,1)S(1)} %collective-permute-done.8.refs_1_), channel_id=1, source_target_pairs={{0,2},{1,3},{2,0},{3,1},{4,6},{5,7},{6,4},{7,5},{8,10},{9,11},{10,... | collective-permute-start | bytes 393224 | tf_op jit(solution)/shard_map/ppermute | solution.py:100
  19.5 6.1 %collective-permute-start.4 = (bf16[16,4224]{1,0:T(8,128)(2,1)S(1)}, bf16[16,4224]{1,0:T(8,128)(2,1)S(1)}, u32[]{:S(2)}, u32[]{:S(2)}) collective-permute-start(bf16[16,4224]{1,0:T(8,128)(2,1)S(1)} %pad_maximum_fusion.refs_0_), channel_id=1, source_target_pairs={{0,4},{1,5},{2,6},{3,7},{4,0},{5,1},{6,2},{7,3},{8,12},{9,13},{10,... | collective-permute-start | bytes 405512 | tf_op jit(solution)/shard_map/ppermute | solution.py:100
  21.0 5.6 %collective-permute-start.5 = (bf16[16,4224]{1,0:T(8,128)(2,1)S(1)}, bf16[16,4224]{1,0:T(8,128)(2,1)S(1)}, u32[]{:S(2)}, u32[]{:S(2)}) collective-permute-start(bf16[16,4224]{1,0:T(8,128)(2,1)S(1)} %collective-permute-done.3.refs_1_), channel_id=1, source_target_pairs={{0,4},{1,5},{2,6},{3,7},{4,0},{5,1},{6,2},{7,3},{8,12},{9,13},{10,... | collective-permute-start | bytes 405512 | tf_op jit(solution)/shard_map/ppermute | solution.py:100
  21.6 5.2 %collective-permute-start.11 = (bf16[32,4096]{1,0:T(8,128)(2,1)S(1)}, bf16[32,4096]{1,0:T(8,128)(2,1)S(1)}, u32[]{:S(2)}, u32[]{:S(2)}) collective-permute-start(bf16[32,4096]{1,0:T(8,128)(2,1)S(1)} %shard_map.114.refs_0_), channel_id=1, source_target_pairs={{0,1},{1,0},{2,3},{3,2},{4,5},{5,4},{6,7},{7,6},{8,9},{9,8},{10,11... | collective-permute-start | bytes 786440 | tf_op jit(solution)/shard_map/ppermute | solution.py:100
  24.9 1.8 %collective-permute-start.12 = (bf16[32,4096]{1,0:T(8,128)(2,1)S(1)}, bf16[32,4096]{1,0:T(8,128)(2,1)S(1)}, u32[]{:S(2)}, u32[]{:S(2)}) collective-permute-start(bf16[32,4096]{1,0:T(8,128)(2,1)S(1)} %shard_map.115.refs_1_), channel_id=1, source_target_pairs={{0,1},{1,0},{2,3},{3,2},{4,5},{5,4},{6,7},{7,6},{8,9},{9,8},{10,11... | collective-permute-start | bytes 786440 | tf_op jit(solution)/shard_map/ppermute | solution.py:100
  25.0 3.0 %collective-permute-start.6 = (bf16[32,4224]{1,0:T(8,128)(2,1)S(1)}, bf16[32,4224]{1,0:T(8,128)(2,1)S(1)}, u32[]{:S(2)}, u32[]{:S(2)}) collective-permute-start(bf16[32,4224]{1,0:T(8,128)(2,1)S(1)} %shard_map.112.refs_0_), channel_id=1, source_target_pairs={{0,1},{1,0},{2,3},{3,2},{4,5},{5,4},{6,7},{7,6},{8,9},{9,8},{10,11... | collective-permute-start | bytes 811016 | tf_op jit(solution)/shard_map/ppermute | solution.py:100
  26.6 1.6 %collective-permute-start.7 = (bf16[32,4224]{1,0:T(8,128)(2,1)S(1)}, bf16[32,4224]{1,0:T(8,128)(2,1)S(1)}, u32[]{:S(2)}, u32[]{:S(2)}) collective-permute-start(bf16[32,4224]{1,0:T(8,128)(2,1)S(1)} %shard_map.113.refs_1_), channel_id=1, source_target_pairs={{0,1},{1,0},{2,3},{3,2},{4,5},{5,4},{6,7},{7,6},{8,9},{9,8},{10,11... | collective-permute-start | bytes 811016 | tf_op jit(solution)/shard_map/ppermute | solution.py:100
  28.7 2.6 %collective-permute-start.14 = (bf16[64,4096]{1,0:T(8,128)(2,1)S(1)}, bf16[64,4096]{1,0:T(8,128)(2,1)S(1)}, u32[]{:S(2)}, u32[]{:S(2)}) collective-permute-start(bf16[64,4096]{1,0:T(8,128)(2,1)S(1)} %get-tuple-element.69), channel_id=1, source_target_pairs={{0,1},{1,0},{2,3},{3,2},{4,5},{5,4},{6,7},{7,6},{8,9},{9,8},{10,11... | collective-permute-start | bytes 1572872 | tf_op jit(solution)/shard_map/ppermute | solution.py:100
  31.0 2.0 %collective-permute-start.13 = (bf16[64,4096]{1,0:T(8,128)(2,1)S(1)}, bf16[64,4096]{1,0:T(8,128)(2,1)S(1)}, u32[]{:S(2)}, u32[]{:S(2)}) collective-permute-start(bf16[64,4096]{1,0:T(8,128)(2,1)S(1)} %get-tuple-element.67), channel_id=1, source_target_pairs={{0,1},{1,0},{2,3},{3,2},{4,5},{5,4},{6,7},{7,6},{8,9},{9,8},{10,11... | collective-permute-start | bytes 1572872 | tf_op jit(solution)/shard_map/ppermute | solution.py:100
  33.7 6.4 %collective-permute-start.19 = (bf16[16,4096]{1,0:T(8,128)(2,1)S(1)}, bf16[16,4096]{1,0:T(8,128)(2,1)S(1)}, u32[]{:S(2)}, u32[]{:S(2)}) collective-permute-start(bf16[16,4096]{1,0:T(8,128)(2,1)S(1)} %get-tuple-element.85), channel_id=1, source_target_pairs={{0,2},{1,3},{2,0},{3,1},{4,6},{5,7},{6,4},{7,5},{8,10},{9,11},{10,... | collective-permute-start | bytes 393224 | tf_op jit(solution)/shard_map/ppermute | solution.py:100
  34.7 6.9 %collective-permute-start.16 = (bf16[16,4096]{1,0:T(8,128)(2,1)S(1)}, bf16[16,4096]{1,0:T(8,128)(2,1)S(1)}, u32[]{:S(2)}, u32[]{:S(2)}) collective-permute-start(bf16[16,4096]{1,0:T(8,128)(2,1)S(1)} %get-tuple-element.74), channel_id=1, source_target_pairs={{0,4},{1,5},{2,6},{3,7},{4,0},{5,1},{6,2},{7,3},{8,12},{9,13},{10,... | collective-permute-start | bytes 393224 | tf_op jit(solution)/shard_map/ppermute | solution.py:100
  35.7 8.3 %collective-permute-start.18 = (bf16[16,4096]{1,0:T(8,128)(2,1)S(1)}, bf16[16,4096]{1,0:T(8,128)(2,1)S(1)}, u32[]{:S(2)}, u32[]{:S(2)}) collective-permute-start(bf16[16,4096]{1,0:T(8,128)(2,1)S(1)} %get-tuple-element.83), channel_id=1, source_target_pairs={{0,2},{1,3},{2,0},{3,1},{4,6},{5,7},{6,4},{7,5},{8,10},{9,11},{10,... | collective-permute-start | bytes 393224 | tf_op jit(solution)/shard_map/ppermute | solution.py:100
  37.2 6.8 %collective-permute-start.15 = (bf16[16,4096]{1,0:T(8,128)(2,1)S(1)}, bf16[16,4096]{1,0:T(8,128)(2,1)S(1)}, u32[]{:S(2)}, u32[]{:S(2)}) collective-permute-start(bf16[16,4096]{1,0:T(8,128)(2,1)S(1)} %get-tuple-element.72), channel_id=1, source_target_pairs={{0,4},{1,5},{2,6},{3,7},{4,0},{5,1},{6,2},{7,3},{8,12},{9,13},{10,... | collective-permute-start | bytes 393224 | tf_op jit(solution)/shard_map/ppermute | solution.py:100
  40.1 5.7 %collective-permute-start.20 = (bf16[16,4096]{1,0:T(8,128)(2,1)S(1)}, bf16[16,4096]{1,0:T(8,128)(2,1)S(1)}, u32[]{:S(2)}, u32[]{:S(2)}) collective-permute-start(bf16[16,4096]{1,0:T(8,128)(2,1)S(1)} %shard_map.123), channel_id=1, source_target_pairs={{0,4},{1,5},{2,6},{3,7},{4,0},{5,1},{6,2},{7,3},{8,12},{9,13},{10,... | collective-permute-start | bytes 393224 | tf_op jit(solution)/shard_map/ppermute | solution.py:100
  41.7 5.0 %collective-permute-start.17 = (bf16[16,4096]{1,0:T(8,128)(2,1)S(1)}, bf16[16,4096]{1,0:T(8,128)(2,1)S(1)}, u32[]{:S(2)}, u32[]{:S(2)}) collective-permute-start(bf16[16,4096]{1,0:T(8,128)(2,1)S(1)} %shard_map.120), channel_id=1, source_target_pairs={{0,2},{1,3},{2,0},{3,1},{4,6},{5,7},{6,4},{7,5},{8,10},{9,11},{10,... | collective-permute-start | bytes 393224 | tf_op jit(solution)/shard_map/ppermute | solution.py:100
  46.8 6.9 %collective-permute-start.21 = (bf16[4,8192]{1,0:T(4,128)(2,1)S(1)}, bf16[4,8192]{1,0:T(4,128)(2,1)S(1)}, u32[]{:S(2)}, u32[]{:S(2)}) collective-permute-start(bf16[4,8192]{1,0:T(4,128)(2,1)S(1)} %get-tuple-element.90), channel_id=1, source_target_pairs={{0,8},{1,9},{2,10},{3,11},{4,12},{5,13},{6,14},{7,15},{8,0},{9,1},... | collective-permute-start | bytes 196616 | tf_op jit(solution)/shard_map/ppermute | solution.py:100
  47.0 6.7 %collective-permute-start.22 = (bf16[4,8192]{1,0:T(4,128)(2,1)S(1)}, bf16[4,8192]{1,0:T(4,128)(2,1)S(1)}, u32[]{:S(2)}, u32[]{:S(2)}) collective-permute-start(bf16[4,8192]{1,0:T(4,128)(2,1)S(1)} %get-tuple-element.91), channel_id=1, source_target_pairs={{0,16},{1,17},{2,18},{3,19},{4,20},{5,21},{6,22},{7,23},{8,24},{9,... | collective-permute-start | bytes 196616 | tf_op jit(solution)/shard_map/ppermute | solution.py:100
  49.2 6.1 %collective-permute-start.23 = (bf16[4,8192]{1,0:T(4,128)(2,1)S(1)}, bf16[4,8192]{1,0:T(4,128)(2,1)S(1)}, u32[]{:S(2)}, u32[]{:S(2)}) collective-permute-start(bf16[4,8192]{1,0:T(4,128)(2,1)S(1)} %get-tuple-element.92), channel_id=1, source_target_pairs={{0,24},{1,25},{2,26},{3,27},{4,28},{5,29},{6,30},{7,31},{8,16},{9,... | collective-permute-start | bytes 196616 | tf_op jit(solution)/shard_map/ppermute | solution.py:100

commit v7 on v6

--- a/solution.py
+++ b/solution.py
@@ -189,59 +189,45 @@
     up_ref[...] = silu_gate
 
 
-def out_body(count, *refs):
-    pieces, (hidden_ref, wd_ref, mine_ref, weight_ref, scaled_ref, msg_ref) = (
-        refs[:count],
-        refs[count:],
-    )
-    half, width = msg_ref.shape
+def corner_body(own_ref, came_ref, out_ref, into_ref):
+    rows, width = out_ref.shape
+    for side, ref in enumerate((out_ref, into_ref)):
+        at = slice(side * width, (side + 1) * width)
+        ref[...] = (own_ref[-rows:, at] + came_ref[:, at].astype(jnp.float32)).astype(jnp.bfloat16)
+
+
+def most_body(own_ref, came_ref, *outs):
+    rows, width = outs[0].shape
+    for i, ref in enumerate(outs):
+        here = (slice(i % 3 * rows, (i % 3 + 1) * rows), slice(i // 3 * width, (i // 3 + 1) * width))
+        ref[...] = (own_ref[here] + came_ref[here].astype(jnp.float32)).astype(ref.dtype)
+
+
+def backward_body(count, *refs):
+    pieces, rest = refs[:count], refs[count:]
+    hidden_ref, gate_ref, up_ref, mine_ref, wg_ref, wu_ref, wd_ref = rest[:7]
+    dy_ref, scaled_ref, gate_act_ref, up_act_ref, own_ref, most_ref, corner_ref, weight_ref = rest[7:]
+    width = dy_ref.shape[1]
     for here, piece, there in cotangent_places(pieces):
+        dy_ref[here, :] = piece[there, :width]
         route = piece[there, width:].astype(jnp.float32) * mine_ref[:1, :]
         weight = jnp.sum(route, axis=1, keepdims=True)
         weight_ref[here, :] = jnp.broadcast_to(weight, (route.shape[0], weight_ref.shape[1]))
-        scaled_ref[here, :] = (weight * hidden_ref[here, :]).astype(jnp.bfloat16)
-    msg_ref[...] = jnp.dot(
-        scaled_ref[half:, :], wd_ref[0], preferred_element_type=jnp.float32
-    ).astype(jnp.bfloat16)
-
-
-def into_sum(gate_act, up_act, wg_ref, wu_ref):
-    return jnp.dot(gate_act, wg_ref[0], preferred_element_type=jnp.float32) + jnp.dot(
-        up_act, wu_ref[0], preferred_element_type=jnp.float32
-    )
-
-
-def into_body(count, *refs):
-    pieces, rest = refs[:count], refs[count:]
-    weight_ref, gate_ref, up_ref, wg_ref, wu_ref, wd_ref = rest[:6]
-    dy_ref, gate_act_ref, up_act_ref, msg_ref = rest[6:]
-    half, width = msg_ref.shape
-    for here, piece, there in cotangent_places(pieces):
-        dy_ref[here, :] = piece[there, :width]
-    hidden_grad = weight_ref[:, :1] * contract_rows(dy_ref[...], wd_ref[0])
+    weight = weight_ref[:, :1]
+    scaled_ref[...] = (weight * hidden_ref[...]).astype(jnp.bfloat16)
+    hidden_grad = weight * contract_rows(dy_ref[...], wd_ref[0])
     gate_act_ref[...] = (hidden_grad * gate_ref[...]).astype(jnp.bfloat16)
     up_act_ref[...] = (hidden_grad * up_ref[...]).astype(jnp.bfloat16)
-    msg_ref[...] = into_sum(gate_act_ref[half:, :], up_act_ref[half:, :], wg_ref, wu_ref).astype(
-        jnp.bfloat16
-    )
-
-
-def scattered(total, outs):
-    rows = outs[0].shape[0]
-    for i, ref in enumerate(outs):
-        ref[...] = total[i * rows : (i + 1) * rows, :].astype(ref.dtype)
-
-
-def own_out_body(scaled_ref, wd_ref, passed_ref, *outs):
-    half = passed_ref.shape[0]
-    total = jnp.dot(scaled_ref[:half, :], wd_ref[0], preferred_element_type=jnp.float32)
-    scattered(total + passed_ref[...].astype(jnp.float32), outs)
-
-
-def own_into_body(gate_act_ref, up_act_ref, wg_ref, wu_ref, passed_ref, *outs):
-    half = passed_ref.shape[0]
-    total = into_sum(gate_act_ref[:half, :], up_act_ref[:half, :], wg_ref, wu_ref)
-    scattered(total + passed_ref[...].astype(jnp.float32), outs)
+    out = jnp.dot(scaled_ref[...], wd_ref[0], preferred_element_type=jnp.float32)
+    into = jnp.dot(gate_act_ref[...], wg_ref[0], preferred_element_type=jnp.float32) + jnp.dot(
+        up_act_ref[...], wu_ref[0], preferred_element_type=jnp.float32
+    )
+    half, most = own_ref.shape[0], most_ref.shape[0]
+    for side, total in enumerate((out, into)):
+        at = slice(side * width, (side + 1) * width)
+        own_ref[:, at] = total[:half, :]
+        corner_ref[:, at] = total[half + most :, :].astype(jnp.bfloat16)
+        most_ref[:, at] = total[half : half + most, :].astype(jnp.bfloat16)
 
 
 def turn_body(here_ref, came_ref, to_ref):
@@ -355,44 +341,38 @@
         w_gate,
         w_up,
     )
-    weight, scaled, message = kernel_call(
-        functools.partial(out_body, len(dy_pieces)),
+    all_dy, scaled, gate_act, up_act, own, message, corner_message = kernel_call(
+        functools.partial(backward_body, len(dy_pieces)),
         (
-            shape(2 * half, columns - 2 * width, dtype=f32),
-            shape(2 * half, ff),
-            shape(half, width),
+            shape(2 * half, width),
+            *(shape(2 * half, ff),) * 3,
+            shape(half, 2 * width, dtype=f32),
+            shape(half - block_rows, 2 * width),
+            shape(block_rows, 2 * width),
         ),
-        4 * unit,
+        24 * unit,
         *dy_pieces,
         hidden,
-        w_down,
-        mine,
-    )
-    passed_out = passed(message, CORE)
-    all_dy, gate_act, up_act, message = kernel_call(
-        functools.partial(into_body, len(dy_pieces)),
-        (shape(2 * half, width), shape(2 * half, ff), shape(2 * half, ff), shape(half, width)),
-        16 * unit,
-        *dy_pieces,
-        weight,
         gate_part,
         up_part,
+        mine,
         *weights,
-    )
-    passed_into = passed(message, CORE)
+        scratch=[pltpu.VMEM((2 * half, columns - 2 * width), f32)],
+    )
+    corner_came = passed(corner_message, CORE)
+    corner_came, message = lax.optimization_barrier((corner_came, message))
+    most_came = passed(message, CORE)
 
     piece, full = shape(block_rows, width), shape(block_rows, width, dtype=f32)
-    out_here, out_second, out_first, out_corner = kernel_call(
-        own_out_body, (full, piece, full, piece), 4 * unit, scaled, w_down, passed_out
-    )
-    passed_into, out_here = lax.optimization_barrier((passed_into, out_here))
-    into_here, into_second, into_first, into_corner = kernel_call(
-        own_into_body, (full, full, piece, piece), 8 * unit, gate_act, up_act, w_gate, w_up, passed_into
-    )
-    out_first = kernel_call(turn_body, piece, 0, out_first, passed(out_corner, second))
-    into_second = kernel_call(turn_body, piece, 0, into_second, passed(into_corner, first))
-    out_back = [passed(out_second, second), passed(out_first, first)]
-    into_back = [passed(into_first, first), passed(into_second, second)]
+    out_corner, into_corner = kernel_call(corner_body, (piece, piece), 0, own, corner_came)
+    out_here, out_second, out_first, into_here, into_second, into_first = kernel_call(
+        most_body, (full, piece, full, full, full, piece), 0, own, most_came
+    )
+    out_turn, into_turn = passed(out_corner, second), passed(into_corner, first)
+    out_second, into_first = passed(out_second, second), passed(into_first, first)
+    scaled, out_second, into_first = lax.optimization_barrier((scaled, out_second, into_first))
+    out_first = passed(kernel_call(turn_body, piece, 0, out_first, out_turn), first)
+    into_second = passed(kernel_call(turn_body, piece, 0, into_second, into_turn), second)
     into_here, scaled, gate_act, up_act = lax.optimization_barrier(
         (into_here, scaled, gate_act, up_act)
     )
@@ -403,9 +383,11 @@
         (shape(rows, 2 * width, dtype=f32),) + (shape(rows, 2 * width),) * len(near),
         0,
         out_here,
-        *out_back,
+        out_second,
+        out_first,
         into_here,
-        *into_back,
+        into_first,
+        into_second,
     )
     mine_sum, gate_act, up_act = lax.optimization_barrier((mine_sum, gate_act, up_act))
     grad_gate, grad_up = kernel_call(
@@ -416,7 +398,7 @@
         (shape(rows, width),) * 2,
         0,
         mine_sum,
-        *[passed(piece, m) for m, piece in zip(near, away)],
+        *[passed(piece, m) for m, piece in reversed(list(zip(near, away)))],
     )
     return mixed, input_grad, grad_gate, grad_up, grad_down
 

time: 56.2 us -> 54.2 us (0.964)
  Pallas kernels: 13.1 us -> 11.7 us
    pallas_call x17 -> x16, Pallas kernels: 13.1 us -> 11.7 us  [kernel_call(): pl.pallas_call(body, out_shape=out_shape, in_specs=specs, out_specs=jax.t...]
  transfers between devices with their start and end apart: 24 -> 24, of which waited for: 11 -> 13; matrix products, arithmetic and copies ran while one was open for 0% -> 0% of each run, Pallas kernels for 18% -> 15%
where the time goes in v7:
time: 54.2 us; the launch traced here: 54 us
  starting transfers between devices  24.9 us (46%)
  waiting for transfers between devices  16.3 us (30%)
  Pallas kernels  11.7 us (22%)
  between operations  0.85 us (2%)
    ppermute x24, starting transfers between devices, from_xor(): return lax.ppermute(value, AXES, [(i, i ^ mask) for i in range(devices)])  24.9 us
    ppermute x24, waiting for transfers between devices, from_xor(): return lax.ppermute(value, AXES, [(i, i ^ mask) for i in range(devices)])  16.3 us
    pallas_call x16, Pallas kernels, kernel_call(): pl.pallas_call(body, out_shape=out_shape, in_specs=specs, out_specs=jax.t...  11.7 us
  transfers between devices with their start and end apart: 24, of which 13 were waited for; matrix products, arithmetic and copies ran while one was open for 0% of the time, Pallas kernels for 15%

profile of v7, /device:TPU:0, one launch (start us, length us, event | category | flops | bytes accessed | tf_op | source)
XLA Modules:
  0.0 54.0 jit_solution(11864221246435775189)
XLA Ops:
  1.5 5.1 %collective-permute-start.2 = (bf16[4,8320]{1,0:T(4,128)(2,1)S(1)}, bf16[4,8320]{1,0:T(4,128)(2,1)S(1)}, u32[]{:S(2)}, u32[]{:S(2)}) collective-permute-start(bf16[4,8320]{1,0:T(4,128)(2,1)S(1)} %get-tuple-element.56), channel_id=1, source_target_pairs={{0,24},{1,25},{2,26},{3,27},{4,28},{5,29},{6,30},{7,31},{8,16},{9,... | collective-permute-start | bytes 199688 | tf_op jit(solution)/shard_map/ppermute | solution.py:100
  7.3 2.4 %shard_map.111 = (bf16[1,192,4096]{2,1,0:T(8,128)(2,1)S(1)}, bf16[1,192,4096]{2,1,0:T(8,128)(2,1)S(1)}, bf16[1,192,4096]{2,1,0:T(8,128)(2,1)S(1)}) custom-call(bf16[1,192,4096]{2,1,0:T(8,128)(2,1)} %refs_0_.1, bf16[1,192,4096]{2,1,0:T(8,128)(2,1)} %refs_1_.1, bf16[1,192,4096]{2,1,0:T(8,128)(2,1)} %refs_2_.1), custom_call_target="tpu_custom_call" | custom-call | bytes 4194304 | tf_op jit(solution)/shard_map/pallas_call | solution.py:111
  9.8 2.6 %collective-permute-done.1 = bf16[4,8320]{1,0:T(4,128)(2,1)S(1)} collective-permute-done((bf16[4,8320]{1,0:T(4,128)(2,1)S(1)}, bf16[4,8320]{1,0:T(4,128)(2,1)S(1)}, u32[]{:S(2)}, u32[]{:S(2)}) %collective-permute-start.1) | collective-permute-done | bytes 66592 | tf_op jit(solution)/shard_map/ppermute | solution.py:100
  12.6 1.6 %collective-permute-start.8 = (bf16[16,4096]{1,0:T(8,128)(2,1)S(1)}, bf16[16,4096]{1,0:T(8,128)(2,1)S(1)}, u32[]{:S(2)}, u32[]{:S(2)}) collective-permute-start(bf16[16,4096]{1,0:T(8,128)(2,1)S(1)} %pad_maximum_fusion.1.refs_0_), channel_id=1, source_target_pairs={{0,4},{1,5},{2,6},{3,7},{4,0},{5,1},{6,2},{7,3},{8,12},{9,13},{10,... | collective-permute-start | bytes 393224 | tf_op jit(solution)/shard_map/ppermute | solution.py:100
  14.2 1.5 %collective-permute-start.3 = (bf16[16,4224]{1,0:T(8,128)(2,1)S(1)}, bf16[16,4224]{1,0:T(8,128)(2,1)S(1)}, u32[]{:S(2)}, u32[]{:S(2)}) collective-permute-start(bf16[16,4224]{1,0:T(8,128)(2,1)S(1)} %pad_maximum_fusion.refs_0_), channel_id=1, source_target_pairs={{0,2},{1,3},{2,0},{3,1},{4,6},{5,7},{6,4},{7,5},{8,10},{9,11},{10,... | collective-permute-start | bytes 405512 | tf_op jit(solution)/shard_map/ppermute | solution.py:100
  16.2 1.5 %collective-permute-done.8.refs_1_ = bf16[16,4096]{1,0:T(8,128)(2,1)S(1)} collective-permute-done((bf16[16,4096]{1,0:T(8,128)(2,1)S(1)}, bf16[16,4096]{1,0:T(8,128)(2,1)S(1)}, u32[]{:S(2)}, u32[]{:S(2)}) %collective-permute-start.8) | collective-permute-done | bytes 131104 | tf_op jit(solution)/shard_map/ppermute | solution.py:100
  17.7 1.8 %collective-permute-start.10 = (bf16[16,4096]{1,0:T(8,128)(2,1)S(1)}, bf16[16,4096]{1,0:T(8,128)(2,1)S(1)}, u32[]{:S(2)}, u32[]{:S(2)}) collective-permute-start(bf16[16,4096]{1,0:T(8,128)(2,1)S(1)} %collective-permute-done.8.refs_1_), channel_id=1, source_target_pairs={{0,2},{1,3},{2,0},{3,1},{4,6},{5,7},{6,4},{7,5},{8,10},{9,11},{10,... | collective-permute-start | bytes 393224 | tf_op jit(solution)/shard_map/ppermute | solution.py:100
  19.5 1.5 %collective-permute-start.4 = (bf16[16,4224]{1,0:T(8,128)(2,1)S(1)}, bf16[16,4224]{1,0:T(8,128)(2,1)S(1)}, u32[]{:S(2)}, u32[]{:S(2)}) collective-permute-start(bf16[16,4224]{1,0:T(8,128)(2,1)S(1)} %pad_maximum_fusion.refs_0_), channel_id=1, source_target_pairs={{0,4},{1,5},{2,6},{3,7},{4,0},{5,1},{6,2},{7,3},{8,12},{9,13},{10,... | collective-permute-start | bytes 405512 | tf_op jit(solution)/shard_map/ppermute | solution.py:100
  21.6 1.9 %collective-permute-done.9.refs_0_ = bf16[16,4096]{1,0:T(8,128)(2,1)S(1)} collective-permute-done((bf16[16,4096]{1,0:T(8,128)(2,1)S(1)}, bf16[16,4096]{1,0:T(8,128)(2,1)S(1)}, u32[]{:S(2)}, u32[]{:S(2)}) %collective-permute-start.9) | collective-permute-done | bytes 131104 | tf_op jit(solution)/shard_map/ppermute | solution.py:100
  23.5 1.4 %collective-permute-done.10.refs_1_ = bf16[16,4096]{1,0:T(8,128)(2,1)S(1)} collective-permute-done((bf16[16,4096]{1,0:T(8,128)(2,1)S(1)}, bf16[16,4096]{1,0:T(8,128)(2,1)S(1)}, u32[]{:S(2)}, u32[]{:S(2)}) %collective-permute-start.10) | collective-permute-done | bytes 131104 | tf_op jit(solution)/shard_map/ppermute | solution.py:100
  25.6 1.0 %collective-permute-done.5.refs_1_ = bf16[16,4224]{1,0:T(8,128)(2,1)S(1)} collective-permute-done((bf16[16,4224]{1,0:T(8,128)(2,1)S(1)}, bf16[16,4224]{1,0:T(8,128)(2,1)S(1)}, u32[]{:S(2)}, u32[]{:S(2)}) %collective-permute-start.5) | collective-permute-done | bytes 135200 | tf_op jit(solution)/shard_map/ppermute | solution.py:100
  26.7 1.2 %shard_map.116 = (bf16[128,4096]{1,0:T(8,128)(2,1)S(1)}, f32[128,192]{1,0:T(8,128)S(1)}, f32[128,192]{1,0:T(8,128)S(1)}, f32[128,192]{1,0:T(8,128)S(1)}) custom-call(bf16[32,4096]{1,0:T(8,128)(2,1)S(1)} %shard_map.114.refs_0_, bf16[32,4096]{1,0:T(8,128)(2,1)S(1)} %shard_map.115.refs_1_, bf16[32,4096]{1,0:T(8,128)(2,1)S(1)} %collective-permute-done.11.refs_2_, ...), custom_call_target="tpu_custom_call" | custom-call | flops 402653184 | bytes 4194304 | tf_op jit(solution)/shard_map/pallas_call | solution.py:111
  28.3 1.9 %shard_map.117 = (bf16[128,4096]{1,0:T(8,128)(2,1)S(1)}, bf16[128,192]{1,0:T(8,128)(2,1)S(1)}, bf16[128,192]{1,0:T(8,128)(2,1)S(1)}, bf16[128,192]{1,0:T(8,128)(...) custom-call(bf16[32,4224]{1,0:T(8,128)(2,1)S(1)} %shard_map.112.refs_0_, ...), custom_call_target="tpu_custom_call" | custom-call | flops 603979776 | bytes 4194304 | tf_op jit(solution)/shard_map/pallas_call | solution.py:111
  30.5 1.3 %collective-permute-done.13.came_ref = bf16[16,8192]{1,0:T(8,128)(2,1)S(1)} collective-permute-done((bf16[16,8192]{1,0:T(8,128)(2,1)S(1)}, bf16[16,8192]{1,0:T(8,128)(2,1)S(1)}, u32[]{:S(2)}, u32[]{:S(2)}) %collective-permute-start.13) | collective-permute-done | bytes 262176 | tf_op jit(solution)/shard_map/ppermute | solution.py:100
  32.1 1.6 %collective-permute-start.17 = (bf16[16,4096]{1,0:T(8,128)(2,1)S(1)}, bf16[16,4096]{1,0:T(8,128)(2,1)S(1)}, u32[]{:S(2)}, u32[]{:S(2)}) collective-permute-start(bf16[16,4096]{1,0:T(8,128)(2,1)S(1)} %get-tuple-element.80), channel_id=1, source_target_pairs={{0,4},{1,5},{2,6},{3,7},{4,0},{5,1},{6,2},{7,3},{8,12},{9,13},{10,... | collective-permute-start | bytes 393224 | tf_op jit(solution)/shard_map/ppermute | solution.py:100
  34.3 1.5 %collective-permute-start.15 = (bf16[16,4096]{1,0:T(8,128)(2,1)S(1)}, bf16[16,4096]{1,0:T(8,128)(2,1)S(1)}, u32[]{:S(2)}, u32[]{:S(2)}) collective-permute-start(bf16[16,4096]{1,0:T(8,128)(2,1)S(1)} %get-tuple-element.75), channel_id=1, source_target_pairs={{0,4},{1,5},{2,6},{3,7},{4,0},{5,1},{6,2},{7,3},{8,12},{9,13},{10,... | collective-permute-start | bytes 393224 | tf_op jit(solution)/shard_map/ppermute | solution.py:100
  36.4 2.0 %collective-permute-done.17.came_ref = bf16[16,4096]{1,0:T(8,128)(2,1)S(1)} collective-permute-done((bf16[16,4096]{1,0:T(8,128)(2,1)S(1)}, bf16[16,4096]{1,0:T(8,128)(2,1)S(1)}, u32[]{:S(2)}, u32[]{:S(2)}) %collective-permute-start.17) | collective-permute-done | bytes 131104 | tf_op jit(solution)/shard_map/ppermute | solution.py:100
  38.5 1.0 %collective-permute-start.18 = (bf16[16,4096]{1,0:T(8,128)(2,1)S(1)}, bf16[16,4096]{1,0:T(8,128)(2,1)S(1)}, u32[]{:S(2)}, u32[]{:S(2)}) collective-permute-start(bf16[16,4096]{1,0:T(8,128)(2,1)S(1)} %shard_map.120), channel_id=1, source_target_pairs={{0,2},{1,3},{2,0},{3,1},{4,6},{5,7},{6,4},{7,5},{8,10},{9,11},{10,... | collective-permute-start | bytes 393224 | tf_op jit(solution)/shard_map/ppermute | solution.py:100
  40.7 1.9 %collective-permute-done.16.refs_4_ = bf16[16,4096]{1,0:T(8,128)(2,1)S(1)} collective-permute-done((bf16[16,4096]{1,0:T(8,128)(2,1)S(1)}, bf16[16,4096]{1,0:T(8,128)(2,1)S(1)}, u32[]{:S(2)}, u32[]{:S(2)}) %collective-permute-start.16) | collective-permute-done | bytes 131104 | tf_op jit(solution)/shard_map/ppermute | solution.py:100
  42.6 1.7 %shard_map.121 = bf16[1,192,4096]{2,1,0:T(8,128)(2,1)} custom-call(bf16[128,4096]{1,0:T(8,128)(2,1)S(1)} %get-tuple-element.86.rows_ref, bf16[128,192]{1,0:T(8,128)(2,1)S(1)} %get-tuple-element.87.refs_0_), custom_call_target="tpu_custom_call" | custom-call | flops 201326592 | bytes 4194304 | tf_op jit(solution)/shard_map/pallas_call | solution.py:111
  44.9 2.2 %collective-permute-start.21 = (bf16[4,8192]{1,0:T(4,128)(2,1)S(1)}, bf16[4,8192]{1,0:T(4,128)(2,1)S(1)}, u32[]{:S(2)}, u32[]{:S(2)}) collective-permute-start(bf16[4,8192]{1,0:T(4,128)(2,1)S(1)} %get-tuple-element.96), channel_id=1, source_target_pairs={{0,24},{1,25},{2,26},{3,27},{4,28},{5,29},{6,30},{7,31},{8,16},{9,... | collective-permute-start | bytes 196616 | tf_op jit(solution)/shard_map/ppermute | solution.py:100
  47.2 2.2 %collective-permute-start.23 = (bf16[4,8192]{1,0:T(4,128)(2,1)S(1)}, bf16[4,8192]{1,0:T(4,128)(2,1)S(1)}, u32[]{:S(2)}, u32[]{:S(2)}) collective-permute-start(bf16[4,8192]{1,0:T(4,128)(2,1)S(1)} %get-tuple-element.98), channel_id=1, source_target_pairs={{0,8},{1,9},{2,10},{3,11},{4,12},{5,13},{6,14},{7,15},{8,0},{9,1},... | collective-permute-start | bytes 196616 | tf_op jit(solution)/shard_map/ppermute | solution.py:100
  49.4 2.5 %shard_map.125 = (bf16[1,192,4096]{2,1,0:T(8,128)(2,1)}, bf16[1,192,4096]{2,1,0:T(8,128)(2,1)}) custom-call(bf16[128,4096]{1,0:T(8,128)(2,1)S(1)} %get-tuple-element.101.rows_ref, bf16[128,192]{1,0:T(8,128)(2,1)S(1)} %get-tuple-element.102.refs_0_, bf16[128,192]{1,0:T(8,128)(2,1)S(1)} %get-tuple-element.103.refs_1_), custom_call_target="tpu_custom_call" | custom-call | flops 402653184 | bytes 4194304 | tf_op jit(solution)/shard_map/pallas_call | solution.py:111
  51.8 1.5 %collective-permute-done.22.refs_1_ = bf16[4,8192]{1,0:T(4,128)(2,1)S(1)} collective-permute-done((bf16[4,8192]{1,0:T(4,128)(2,1)S(1)}, bf16[4,8192]{1,0:T(4,128)(2,1)S(1)}, u32[]{:S(2)}, u32[]{:S(2)}) %collective-permute-start.22) | collective-permute-done | bytes 65568 | tf_op jit(solution)/shard_map/ppermute | solution.py:100
  (50 shorter events, 8.3 us)
Async XLA Ops:
  1.5 8.2 %collective-permute-start.2 = (bf16[4,8320]{1,0:T(4,128)(2,1)S(1)}, bf16[4,8320]{1,0:T(4,128)(2,1)S(1)}, u32[]{:S(2)}, u32[]{:S(2)}) collective-permute-start(bf16[4,8320]{1,0:T(4,128)(2,1)S(1)} %get-tuple-element.56), channel_id=1, source_target_pairs={{0,24},{1,25},{2,26},{3,27},{4,28},{5,29},{6,30},{7,31},{8,16},{9,... | collective-permute-start | bytes 199688 | tf_op jit(solution)/shard_map/ppermute | solution.py:100
  6.7 5.7 %collective-permute-start.1 = (bf16[4,8320]{1,0:T(4,128)(2,1)S(1)}, bf16[4,8320]{1,0:T(4,128)(2,1)S(1)}, u32[]{:S(2)}, u32[]{:S(2)}) collective-permute-start(bf16[4,8320]{1,0:T(4,128)(2,1)S(1)} %get-tuple-element.56), channel_id=1, source_target_pairs={{0,16},{1,17},{2,18},{3,19},{4,20},{5,21},{6,22},{7,23},{8,24},{9,... | collective-permute-start | bytes 199688 | tf_op jit(solution)/shard_map/ppermute | solution.py:100
  6.7 5.7 %collective-permute-start = (bf16[4,8320]{1,0:T(4,128)(2,1)S(1)}, bf16[4,8320]{1,0:T(4,128)(2,1)S(1)}, u32[]{:S(2)}, u32[]{:S(2)}) collective-permute-start(bf16[4,8320]{1,0:T(4,128)(2,1)S(1)} %get-tuple-element.56), channel_id=1, source_target_pairs={{0,8},{1,9},{2,10},{3,11},{4,12},{5,13},{6,14},{7,15},{8,0},{9,1},... | collective-permute-start | bytes 199688 | tf_op jit(solution)/shard_map/ppermute | solution.py:100
  12.6 5.1 %collective-permute-start.8 = (bf16[16,4096]{1,0:T(8,128)(2,1)S(1)}, bf16[16,4096]{1,0:T(8,128)(2,1)S(1)}, u32[]{:S(2)}, u32[]{:S(2)}) collective-permute-start(bf16[16,4096]{1,0:T(8,128)(2,1)S(1)} %pad_maximum_fusion.1.refs_0_), channel_id=1, source_target_pairs={{0,4},{1,5},{2,6},{3,7},{4,0},{5,1},{6,2},{7,3},{8,12},{9,13},{10,... | collective-permute-start | bytes 393224 | tf_op jit(solution)/shard_map/ppermute | solution.py:100
  14.2 6.8 %collective-permute-start.3 = (bf16[16,4224]{1,0:T(8,128)(2,1)S(1)}, bf16[16,4224]{1,0:T(8,128)(2,1)S(1)}, u32[]{:S(2)}, u32[]{:S(2)}) collective-permute-start(bf16[16,4224]{1,0:T(8,128)(2,1)S(1)} %pad_maximum_fusion.refs_0_), channel_id=1, source_target_pairs={{0,2},{1,3},{2,0},{3,1},{4,6},{5,7},{6,4},{7,5},{8,10},{9,11},{10,... | collective-permute-start | bytes 405512 | tf_op jit(solution)/shard_map/ppermute | solution.py:100
  15.7 7.8 %collective-permute-start.9 = (bf16[16,4096]{1,0:T(8,128)(2,1)S(1)}, bf16[16,4096]{1,0:T(8,128)(2,1)S(1)}, u32[]{:S(2)}, u32[]{:S(2)}) collective-permute-start(bf16[16,4096]{1,0:T(8,128)(2,1)S(1)} %pad_maximum_fusion.1.refs_0_), channel_id=1, source_target_pairs={{0,2},{1,3},{2,0},{3,1},{4,6},{5,7},{6,4},{7,5},{8,10},{9,11},{10,... | collective-permute-start | bytes 393224 | tf_op jit(solution)/shard_map/ppermute | solution.py:100
  17.7 7.2 %collective-permute-start.10 = (bf16[16,4096]{1,0:T(8,128)(2,1)S(1)}, bf16[16,4096]{1,0:T(8,128)(2,1)S(1)}, u32[]{:S(2)}, u32[]{:S(2)}) collective-permute-start(bf16[16,4096]{1,0:T(8,128)(2,1)S(1)} %collective-permute-done.8.refs_1_), channel_id=1, source_target_pairs={{0,2},{1,3},{2,0},{3,1},{4,6},{5,7},{6,4},{7,5},{8,10},{9,11},{10,... | collective-permute-start | bytes 393224 | tf_op jit(solution)/shard_map/ppermute | solution.py:100
  19.5 6.1 %collective-permute-start.4 = (bf16[16,4224]{1,0:T(8,128)(2,1)S(1)}, bf16[16,4224]{1,0:T(8,128)(2,1)S(1)}, u32[]{:S(2)}, u32[]{:S(2)}) collective-permute-start(bf16[16,4224]{1,0:T(8,128)(2,1)S(1)} %pad_maximum_fusion.refs_0_), channel_id=1, source_target_pairs={{0,4},{1,5},{2,6},{3,7},{4,0},{5,1},{6,2},{7,3},{8,12},{9,13},{10,... | collective-permute-start | bytes 405512 | tf_op jit(solution)/shard_map/ppermute | solution.py:100
  21.0 5.6 %collective-permute-start.5 = (bf16[16,4224]{1,0:T(8,128)(2,1)S(1)}, bf16[16,4224]{1,0:T(8,128)(2,1)S(1)}, u32[]{:S(2)}, u32[]{:S(2)}) collective-permute-start(bf16[16,4224]{1,0:T(8,128)(2,1)S(1)} %collective-permute-done.3.refs_1_), channel_id=1, source_target_pairs={{0,4},{1,5},{2,6},{3,7},{4,0},{5,1},{6,2},{7,3},{8,12},{9,13},{10,... | collective-permute-start | bytes 405512 | tf_op jit(solution)/shard_map/ppermute | solution.py:100
  21.6 5.2 %collective-permute-start.11 = (bf16[32,4096]{1,0:T(8,128)(2,1)S(1)}, bf16[32,4096]{1,0:T(8,128)(2,1)S(1)}, u32[]{:S(2)}, u32[]{:S(2)}) collective-permute-start(bf16[32,4096]{1,0:T(8,128)(2,1)S(1)} %shard_map.114.refs_0_), channel_id=1, source_target_pairs={{0,1},{1,0},{2,3},{3,2},{4,5},{5,4},{6,7},{7,6},{8,9},{9,8},{10,11... | collective-permute-start | bytes 786440 | tf_op jit(solution)/shard_map/ppermute | solution.py:100
  24.9 1.8 %collective-permute-start.12 = (bf16[32,4096]{1,0:T(8,128)(2,1)S(1)}, bf16[32,4096]{1,0:T(8,128)(2,1)S(1)}, u32[]{:S(2)}, u32[]{:S(2)}) collective-permute-start(bf16[32,4096]{1,0:T(8,128)(2,1)S(1)} %shard_map.115.refs_1_), channel_id=1, source_target_pairs={{0,1},{1,0},{2,3},{3,2},{4,5},{5,4},{6,7},{7,6},{8,9},{9,8},{10,11... | collective-permute-start | bytes 786440 | tf_op jit(solution)/shard_map/ppermute | solution.py:100
  25.0 2.9 %collective-permute-start.6 = (bf16[32,4224]{1,0:T(8,128)(2,1)S(1)}, bf16[32,4224]{1,0:T(8,128)(2,1)S(1)}, u32[]{:S(2)}, u32[]{:S(2)}) collective-permute-start(bf16[32,4224]{1,0:T(8,128)(2,1)S(1)} %shard_map.112.refs_0_), channel_id=1, source_target_pairs={{0,1},{1,0},{2,3},{3,2},{4,5},{5,4},{6,7},{7,6},{8,9},{9,8},{10,11... | collective-permute-start | bytes 811016 | tf_op jit(solution)/shard_map/ppermute | solution.py:100
  26.6 1.6 %collective-permute-start.7 = (bf16[32,4224]{1,0:T(8,128)(2,1)S(1)}, bf16[32,4224]{1,0:T(8,128)(2,1)S(1)}, u32[]{:S(2)}, u32[]{:S(2)}) collective-permute-start(bf16[32,4224]{1,0:T(8,128)(2,1)S(1)} %shard_map.113.refs_1_), channel_id=1, source_target_pairs={{0,1},{1,0},{2,3},{3,2},{4,5},{5,4},{6,7},{7,6},{8,9},{9,8},{10,11... | collective-permute-start | bytes 811016 | tf_op jit(solution)/shard_map/ppermute | solution.py:100
  30.2 1.6 %collective-permute-start.13 = (bf16[16,8192]{1,0:T(8,128)(2,1)S(1)}, bf16[16,8192]{1,0:T(8,128)(2,1)S(1)}, u32[]{:S(2)}, u32[]{:S(2)}) collective-permute-start(bf16[16,8192]{1,0:T(8,128)(2,1)S(1)} %get-tuple-element.70), channel_id=1, source_target_pairs={{0,1},{1,0},{2,3},{3,2},{4,5},{5,4},{6,7},{7,6},{8,9},{9,8},{10,11... | collective-permute-start | bytes 786440 | tf_op jit(solution)/shard_map/ppermute | solution.py:100
  31.8 2.3 %collective-permute-start.14 = (bf16[48,8192]{1,0:T(8,128)(2,1)S(1)}, bf16[48,8192]{1,0:T(8,128)(2,1)S(1)}, u32[]{:S(2)}, u32[]{:S(2)}) collective-permute-start(bf16[48,8192]{1,0:T(8,128)(2,1)S(1)} %get-tuple-element.72), channel_id=1, source_target_pairs={{0,1},{1,0},{2,3},{3,2},{4,5},{5,4},{6,7},{7,6},{8,9},{9,8},{10,11... | collective-permute-start | bytes 2359304 | tf_op jit(solution)/shard_map/ppermute | solution.py:100
  32.1 6.4 %collective-permute-start.17 = (bf16[16,4096]{1,0:T(8,128)(2,1)S(1)}, bf16[16,4096]{1,0:T(8,128)(2,1)S(1)}, u32[]{:S(2)}, u32[]{:S(2)}) collective-permute-start(bf16[16,4096]{1,0:T(8,128)(2,1)S(1)} %get-tuple-element.80), channel_id=1, source_target_pairs={{0,4},{1,5},{2,6},{3,7},{4,0},{5,1},{6,2},{7,3},{8,12},{9,13},{10,... | collective-permute-start | bytes 393224 | tf_op jit(solution)/shard_map/ppermute | solution.py:100
  33.6 6.1 %collective-permute-start.19 = (bf16[16,4096]{1,0:T(8,128)(2,1)S(1)}, bf16[16,4096]{1,0:T(8,128)(2,1)S(1)}, u32[]{:S(2)}, u32[]{:S(2)}) collective-permute-start(bf16[16,4096]{1,0:T(8,128)(2,1)S(1)} %get-tuple-element.91), channel_id=1, source_target_pairs={{0,2},{1,3},{2,0},{3,1},{4,6},{5,7},{6,4},{7,5},{8,10},{9,11},{10,... | collective-permute-start | bytes 393224 | tf_op jit(solution)/shard_map/ppermute | solution.py:100
  34.3 6.3 %collective-permute-start.15 = (bf16[16,4096]{1,0:T(8,128)(2,1)S(1)}, bf16[16,4096]{1,0:T(8,128)(2,1)S(1)}, u32[]{:S(2)}, u32[]{:S(2)}) collective-permute-start(bf16[16,4096]{1,0:T(8,128)(2,1)S(1)} %get-tuple-element.75), channel_id=1, source_target_pairs={{0,4},{1,5},{2,6},{3,7},{4,0},{5,1},{6,2},{7,3},{8,12},{9,13},{10,... | collective-permute-start | bytes 393224 | tf_op jit(solution)/shard_map/ppermute | solution.py:100
  35.8 6.7 %collective-permute-start.16 = (bf16[16,4096]{1,0:T(8,128)(2,1)S(1)}, bf16[16,4096]{1,0:T(8,128)(2,1)S(1)}, u32[]{:S(2)}, u32[]{:S(2)}) collective-permute-start(bf16[16,4096]{1,0:T(8,128)(2,1)S(1)} %get-tuple-element.76), channel_id=1, source_target_pairs={{0,2},{1,3},{2,0},{3,1},{4,6},{5,7},{6,4},{7,5},{8,10},{9,11},{10,... | collective-permute-start | bytes 393224 | tf_op jit(solution)/shard_map/ppermute | solution.py:100
  38.5 6.2 %collective-permute-start.18 = (bf16[16,4096]{1,0:T(8,128)(2,1)S(1)}, bf16[16,4096]{1,0:T(8,128)(2,1)S(1)}, u32[]{:S(2)}, u32[]{:S(2)}) collective-permute-start(bf16[16,4096]{1,0:T(8,128)(2,1)S(1)} %shard_map.120), channel_id=1, source_target_pairs={{0,2},{1,3},{2,0},{3,1},{4,6},{5,7},{6,4},{7,5},{8,10},{9,11},{10,... | collective-permute-start | bytes 393224 | tf_op jit(solution)/shard_map/ppermute | solution.py:100
  39.8 5.0 %collective-permute-start.20 = (bf16[16,4096]{1,0:T(8,128)(2,1)S(1)}, bf16[16,4096]{1,0:T(8,128)(2,1)S(1)}, u32[]{:S(2)}, u32[]{:S(2)}) collective-permute-start(bf16[16,4096]{1,0:T(8,128)(2,1)S(1)} %shard_map.122), channel_id=1, source_target_pairs={{0,4},{1,5},{2,6},{3,7},{4,0},{5,1},{6,2},{7,3},{8,12},{9,13},{10,... | collective-permute-start | bytes 393224 | tf_op jit(solution)/shard_map/ppermute | solution.py:100
  44.9 6.9 %collective-permute-start.21 = (bf16[4,8192]{1,0:T(4,128)(2,1)S(1)}, bf16[4,8192]{1,0:T(4,128)(2,1)S(1)}, u32[]{:S(2)}, u32[]{:S(2)}) collective-permute-start(bf16[4,8192]{1,0:T(4,128)(2,1)S(1)} %get-tuple-element.96), channel_id=1, source_target_pairs={{0,24},{1,25},{2,26},{3,27},{4,28},{5,29},{6,30},{7,31},{8,16},{9,... | collective-permute-start | bytes 196616 | tf_op jit(solution)/shard_map/ppermute | solution.py:100
  47.2 6.2 %collective-permute-start.22 = (bf16[4,8192]{1,0:T(4,128)(2,1)S(1)}, bf16[4,8192]{1,0:T(4,128)(2,1)S(1)}, u32[]{:S(2)}, u32[]{:S(2)}) collective-permute-start(bf16[4,8192]{1,0:T(4,128)(2,1)S(1)} %get-tuple-element.97), channel_id=1, source_target_pairs={{0,16},{1,17},{2,18},{3,19},{4,20},{5,21},{6,22},{7,23},{8,24},{9,... | collective-permute-start | bytes 196616 | tf_op jit(solution)/shard_map/ppermute | solution.py:100
  47.2 6.2 %collective-permute-start.23 = (bf16[4,8192]{1,0:T(4,128)(2,1)S(1)}, bf16[4,8192]{1,0:T(4,128)(2,1)S(1)}, u32[]{:S(2)}, u32[]{:S(2)}) collective-permute-start(bf16[4,8192]{1,0:T(4,128)(2,1)S(1)} %get-tuple-element.98), channel_id=1, source_target_pairs={{0,8},{1,9},{2,10},{3,11},{4,12},{5,13},{6,14},{7,15},{8,0},{9,1},... | collective-permute-start | bytes 196616 | tf_op jit(solution)/shard_map/ppermute | solution.py:100

commit v8 on v7

--- a/solution.py
+++ b/solution.py
@@ -328,10 +328,11 @@
         ]
         return own + [passed(pair, CORE) for pair in own]
 
-    x_pieces = both_cores((block_x, second_x), (first_x, corner_x))
+    x_pieces = both_cores((block_x, first_x), (second_x, corner_x))
     early_dy, late_dy, other_early, other_late = both_cores(
-        (block_dy, first_dy), (second_dy, corner_dy)
-    )
+        (block_dy, second_dy), (first_dy, corner_dy)
+    )
+    x_pieces[2], other_early = lax.optimization_barrier((x_pieces[2], other_early))
     dy_pieces = [early_dy, late_dy, other_early, other_late]
     all_x, hidden, gate_part, up_part = kernel_call(
         functools.partial(forward_body, len(x_pieces)),
@@ -365,8 +366,8 @@
 
     piece, full = shape(block_rows, width), shape(block_rows, width, dtype=f32)
     out_corner, into_corner = kernel_call(corner_body, (piece, piece), 0, own, corner_came)
-    out_here, out_second, out_first, into_here, into_second, into_first = kernel_call(
-        most_body, (full, piece, full, full, full, piece), 0, own, most_came
+    out_here, out_first, out_second, into_here, into_first, into_second = kernel_call(
+        most_body, (full, full, piece, full, piece, full), 0, own, most_came
     )
     out_turn, into_turn = passed(out_corner, second), passed(into_corner, first)
     out_second, into_first = passed(out_second, second), passed(into_first, first)

time: 54.2 us -> 53.2 us (0.982)
  waiting for transfers between devices: 16.3 us -> 14.6 us
  starting transfers between devices: 24.9 us -> 25.5 us
    ppermute x24, waiting for transfers between devices: 16.3 us -> 14.6 us  [from_xor(): return lax.ppermute(value, AXES, [(i, i ^ mask) for i in range(devices)])]
    ppermute x24, starting transfers between devices: 24.9 us -> 25.5 us  [from_xor(): return lax.ppermute(value, AXES, [(i, i ^ mask) for i in range(devices)])]
where the time goes in v8:
time: 53.2 us; the launch traced here: 53 us
  starting transfers between devices  25.5 us (48%)
  waiting for transfers between devices  14.6 us (27%)
  Pallas kernels  11.7 us (22%)
  between operations  0.86 us (2%)
    ppermute x24, starting transfers between devices, from_xor(): return lax.ppermute(value, AXES, [(i, i ^ mask) for i in range(devices)])  25.5 us
    ppermute x24, waiting for transfers between devices, from_xor(): return lax.ppermute(value, AXES, [(i, i ^ mask) for i in range(devices)])  14.6 us
    pallas_call x16, Pallas kernels, kernel_call(): pl.pallas_call(body, out_shape=out_shape, in_specs=specs, out_specs=jax.t...  11.7 us
  transfers between devices with their start and end apart: 24, of which 13 were waited for; matrix products, arithmetic and copies ran while one was open for 0% of the time, Pallas kernels for 15%

profile of v8, /device:TPU:0, one launch (start us, length us, event | category | flops | bytes accessed | tf_op | source)
XLA Modules:
  0.0 53.0 jit_solution(16232791598630071450)
XLA Ops:
  0.6 0.9 %shard_map.110 = (bf16[4,8320]{1,0:T(4,128)(2,1)S(1)}, f32[8,128]{1,0:T(8,128)S(1)}) custom-call(bf16[4,4096]{1,0:T(4,128)(2,1)} %x_ref.1, bf16[4,4096]{1,0:T(4,128)(2,1)} %dy_ref.1, s32[2,4]{1,0:T(2,128)} %bitcast.3, bf16[2,4]{1,0:T(2,128)(2,1)} %bitcast.4, s32[1]{0:T(128)} %bitcast.2.expert_ref), custom_call_target="tpu_custom_call" | custom-call | bytes 4194304 | tf_op jit(solution)/shard_map/pallas_call | solution.py:111
  1.5 5.1 %collective-permute-start.2 = (bf16[4,8320]{1,0:T(4,128)(2,1)S(1)}, bf16[4,8320]{1,0:T(4,128)(2,1)S(1)}, u32[]{:S(2)}, u32[]{:S(2)}) collective-permute-start(bf16[4,8320]{1,0:T(4,128)(2,1)S(1)} %get-tuple-element.58), channel_id=1, source_target_pairs={{0,24},{1,25},{2,26},{3,27},{4,28},{5,29},{6,30},{7,31},{8,16},{9,... | collective-permute-start | bytes 199688 | tf_op jit(solution)/shard_map/ppermute | solution.py:100
  7.3 2.4 %shard_map.111 = (bf16[1,192,4096]{2,1,0:T(8,128)(2,1)S(1)}, bf16[1,192,4096]{2,1,0:T(8,128)(2,1)S(1)}, bf16[1,192,4096]{2,1,0:T(8,128)(2,1)S(1)}) custom-call(bf16[1,192,4096]{2,1,0:T(8,128)(2,1)} %refs_0_.1, bf16[1,192,4096]{2,1,0:T(8,128)(2,1)} %refs_1_.1, bf16[1,192,4096]{2,1,0:T(8,128)(2,1)} %refs_2_.1), custom_call_target="tpu_custom_call" | custom-call | bytes 4194304 | tf_op jit(solution)/shard_map/pallas_call | solution.py:111
  9.8 2.6 %collective-permute-done.1 = bf16[4,8320]{1,0:T(4,128)(2,1)S(1)} collective-permute-done((bf16[4,8320]{1,0:T(4,128)(2,1)S(1)}, bf16[4,8320]{1,0:T(4,128)(2,1)S(1)}, u32[]{:S(2)}, u32[]{:S(2)}) %collective-permute-start.1) | collective-permute-done | bytes 66592 | tf_op jit(solution)/shard_map/ppermute | solution.py:100
  12.6 1.6 %collective-permute-start.10 = (bf16[16,4096]{1,0:T(8,128)(2,1)S(1)}, bf16[16,4096]{1,0:T(8,128)(2,1)S(1)}, u32[]{:S(2)}, u32[]{:S(2)}) collective-permute-start(bf16[16,4096]{1,0:T(8,128)(2,1)S(1)} %pad_maximum_fusion.1.refs_0_), channel_id=1, source_target_pairs={{0,4},{1,5},{2,6},{3,7},{4,0},{5,1},{6,2},{7,3},{8,12},{9,13},{10,... | collective-permute-start | bytes 393224 | tf_op jit(solution)/shard_map/ppermute | solution.py:100
  14.2 1.5 %collective-permute-start.4 = (bf16[16,4224]{1,0:T(8,128)(2,1)S(1)}, bf16[16,4224]{1,0:T(8,128)(2,1)S(1)}, u32[]{:S(2)}, u32[]{:S(2)}) collective-permute-start(bf16[16,4224]{1,0:T(8,128)(2,1)S(1)} %pad_maximum_fusion.refs_0_), channel_id=1, source_target_pairs={{0,2},{1,3},{2,0},{3,1},{4,6},{5,7},{6,4},{7,5},{8,10},{9,11},{10,... | collective-permute-start | bytes 405512 | tf_op jit(solution)/shard_map/ppermute | solution.py:100
  16.8 1.3 %collective-permute-done.10.refs_0_ = bf16[16,4096]{1,0:T(8,128)(2,1)S(1)} collective-permute-done((bf16[16,4096]{1,0:T(8,128)(2,1)S(1)}, bf16[16,4096]{1,0:T(8,128)(2,1)S(1)}, u32[]{:S(2)}, u32[]{:S(2)}) %collective-permute-start.10) | collective-permute-done | bytes 131104 | tf_op jit(solution)/shard_map/ppermute | solution.py:100
  18.1 2.5 %collective-permute-start.11 = (bf16[16,4096]{1,0:T(8,128)(2,1)S(1)}, bf16[16,4096]{1,0:T(8,128)(2,1)S(1)}, u32[]{:S(2)}, u32[]{:S(2)}) collective-permute-start(bf16[16,4096]{1,0:T(8,128)(2,1)S(1)} %collective-permute-done.10.refs_0_), channel_id=1, source_target_pairs={{0,2},{1,3},{2,0},{3,1},{4,6},{5,7},{6,4},{7,5},{8,10},{9,11},{10,... | collective-permute-start | bytes 393224 | tf_op jit(solution)/shard_map/ppermute | solution.py:100
  20.7 1.4 %collective-permute-start.5 = (bf16[16,4224]{1,0:T(8,128)(2,1)S(1)}, bf16[16,4224]{1,0:T(8,128)(2,1)S(1)}, u32[]{:S(2)}, u32[]{:S(2)}) collective-permute-start(bf16[16,4224]{1,0:T(8,128)(2,1)S(1)} %collective-permute-done.4.refs_0_), channel_id=1, source_target_pairs={{0,4},{1,5},{2,6},{3,7},{4,0},{5,1},{6,2},{7,3},{8,12},{9,13},{10,... | collective-permute-start | bytes 405512 | tf_op jit(solution)/shard_map/ppermute | solution.py:100
  22.2 1.3 %collective-permute-done.6.refs_1_ = bf16[16,4096]{1,0:T(8,128)(2,1)S(1)} collective-permute-done((bf16[16,4096]{1,0:T(8,128)(2,1)S(1)}, bf16[16,4096]{1,0:T(8,128)(2,1)S(1)}, u32[]{:S(2)}, u32[]{:S(2)}) %collective-permute-start.6) | collective-permute-done | bytes 131104 | tf_op jit(solution)/shard_map/ppermute | solution.py:100
  23.6 1.3 %collective-permute-done.11.refs_1_ = bf16[16,4096]{1,0:T(8,128)(2,1)S(1)} collective-permute-done((bf16[16,4096]{1,0:T(8,128)(2,1)S(1)}, bf16[16,4096]{1,0:T(8,128)(2,1)S(1)}, u32[]{:S(2)}, u32[]{:S(2)}) %collective-permute-start.11) | collective-permute-done | bytes 131104 | tf_op jit(solution)/shard_map/ppermute | solution.py:100
  26.5 1.2 %shard_map.116 = (bf16[128,4096]{1,0:T(8,128)(2,1)S(1)}, f32[128,192]{1,0:T(8,128)S(1)}, f32[128,192]{1,0:T(8,128)S(1)}, f32[128,192]{1,0:T(8,128)S(1)}) custom-call(bf16[32,4096]{1,0:T(8,128)(2,1)S(1)} %shard_map.114.refs_0_, bf16[32,4096]{1,0:T(8,128)(2,1)S(1)} %shard_map.115.refs_1_, bf16[32,4096]{1,0:T(8,128)(2,1)S(1)} %collective-permute-done.7.refs_2_, ...), custom_call_target="tpu_custom_call" | custom-call | flops 402653184 | bytes 4194304 | tf_op jit(solution)/shard_map/pallas_call | solution.py:111
  27.7 1.9 %shard_map.117 = (bf16[128,4096]{1,0:T(8,128)(2,1)S(1)}, bf16[128,192]{1,0:T(8,128)(2,1)S(1)}, bf16[128,192]{1,0:T(8,128)(2,1)S(1)}, bf16[128,192]{1,0:T(8,128)(...) custom-call(bf16[32,4224]{1,0:T(8,128)(2,1)S(1)} %shard_map.112.refs_0_, ...), custom_call_target="tpu_custom_call" | custom-call | flops 603979776 | bytes 4194304 | tf_op jit(solution)/shard_map/pallas_call | solution.py:111
  29.9 1.4 %collective-permute-done.13.came_ref = bf16[16,8192]{1,0:T(8,128)(2,1)S(1)} collective-permute-done((bf16[16,8192]{1,0:T(8,128)(2,1)S(1)}, bf16[16,8192]{1,0:T(8,128)(2,1)S(1)}, u32[]{:S(2)}, u32[]{:S(2)}) %collective-permute-start.13) | collective-permute-done | bytes 262176 | tf_op jit(solution)/shard_map/ppermute | solution.py:100
  31.5 1.2 %collective-permute-start.17 = (bf16[16,4096]{1,0:T(8,128)(2,1)S(1)}, bf16[16,4096]{1,0:T(8,128)(2,1)S(1)}, u32[]{:S(2)}, u32[]{:S(2)}) collective-permute-start(bf16[16,4096]{1,0:T(8,128)(2,1)S(1)} %get-tuple-element.84), channel_id=1, source_target_pairs={{0,4},{1,5},{2,6},{3,7},{4,0},{5,1},{6,2},{7,3},{8,12},{9,13},{10,... | collective-permute-start | bytes 393224 | tf_op jit(solution)/shard_map/ppermute | solution.py:100
  32.7 1.1 %collective-permute-start.19 = (bf16[16,4096]{1,0:T(8,128)(2,1)S(1)}, bf16[16,4096]{1,0:T(8,128)(2,1)S(1)}, u32[]{:S(2)}, u32[]{:S(2)}) collective-permute-start(bf16[16,4096]{1,0:T(8,128)(2,1)S(1)} %get-tuple-element.95), channel_id=1, source_target_pairs={{0,2},{1,3},{2,0},{3,1},{4,6},{5,7},{6,4},{7,5},{8,10},{9,11},{10,... | collective-permute-start | bytes 393224 | tf_op jit(solution)/shard_map/ppermute | solution.py:100
  33.9 1.4 %collective-permute-start.15 = (bf16[16,4096]{1,0:T(8,128)(2,1)S(1)}, bf16[16,4096]{1,0:T(8,128)(2,1)S(1)}, u32[]{:S(2)}, u32[]{:S(2)}) collective-permute-start(bf16[16,4096]{1,0:T(8,128)(2,1)S(1)} %get-tuple-element.79), channel_id=1, source_target_pairs={{0,4},{1,5},{2,6},{3,7},{4,0},{5,1},{6,2},{7,3},{8,12},{9,13},{10,... | collective-permute-start | bytes 393224 | tf_op jit(solution)/shard_map/ppermute | solution.py:100
  36.0 1.9 %collective-permute-done.17.came_ref = bf16[16,4096]{1,0:T(8,128)(2,1)S(1)} collective-permute-done((bf16[16,4096]{1,0:T(8,128)(2,1)S(1)}, bf16[16,4096]{1,0:T(8,128)(2,1)S(1)}, u32[]{:S(2)}, u32[]{:S(2)}) %collective-permute-start.17) | collective-permute-done | bytes 131104 | tf_op jit(solution)/shard_map/ppermute | solution.py:100
  37.9 1.6 %collective-permute-start.18 = (bf16[16,4096]{1,0:T(8,128)(2,1)S(1)}, bf16[16,4096]{1,0:T(8,128)(2,1)S(1)}, u32[]{:S(2)}, u32[]{:S(2)}) collective-permute-start(bf16[16,4096]{1,0:T(8,128)(2,1)S(1)} %shard_map.120), channel_id=1, source_target_pairs={{0,2},{1,3},{2,0},{3,1},{4,6},{5,7},{6,4},{7,5},{8,10},{9,11},{10,... | collective-permute-start | bytes 393224 | tf_op jit(solution)/shard_map/ppermute | solution.py:100
  40.3 1.5 %collective-permute-done.16.refs_4_ = bf16[16,4096]{1,0:T(8,128)(2,1)S(1)} collective-permute-done((bf16[16,4096]{1,0:T(8,128)(2,1)S(1)}, bf16[16,4096]{1,0:T(8,128)(2,1)S(1)}, u32[]{:S(2)}, u32[]{:S(2)}) %collective-permute-start.16) | collective-permute-done | bytes 131104 | tf_op jit(solution)/shard_map/ppermute | solution.py:100
  41.8 1.7 %shard_map.121 = bf16[1,192,4096]{2,1,0:T(8,128)(2,1)} custom-call(bf16[128,4096]{1,0:T(8,128)(2,1)S(1)} %get-tuple-element.90.rows_ref, bf16[128,192]{1,0:T(8,128)(2,1)S(1)} %get-tuple-element.91.refs_0_), custom_call_target="tpu_custom_call" | custom-call | flops 201326592 | bytes 4194304 | tf_op jit(solution)/shard_map/pallas_call | solution.py:111
  44.7 2.5 %collective-permute-start.21 = (bf16[4,8192]{1,0:T(4,128)(2,1)S(1)}, bf16[4,8192]{1,0:T(4,128)(2,1)S(1)}, u32[]{:S(2)}, u32[]{:S(2)}) collective-permute-start(bf16[4,8192]{1,0:T(4,128)(2,1)S(1)} %get-tuple-element.100), channel_id=1, source_target_pairs={{0,24},{1,25},{2,26},{3,27},{4,28},{5,29},{6,30},{7,31},{8,16},{9,... | collective-permute-start | bytes 196616 | tf_op jit(solution)/shard_map/ppermute | solution.py:100
  47.1 2.0 %collective-permute-start.23 = (bf16[4,8192]{1,0:T(4,128)(2,1)S(1)}, bf16[4,8192]{1,0:T(4,128)(2,1)S(1)}, u32[]{:S(2)}, u32[]{:S(2)}) collective-permute-start(bf16[4,8192]{1,0:T(4,128)(2,1)S(1)} %get-tuple-element.102), channel_id=1, source_target_pairs={{0,8},{1,9},{2,10},{3,11},{4,12},{5,13},{6,14},{7,15},{8,0},{9,1},... | collective-permute-start | bytes 196616 | tf_op jit(solution)/shard_map/ppermute | solution.py:100
  49.1 2.5 %shard_map.125 = (bf16[1,192,4096]{2,1,0:T(8,128)(2,1)}, bf16[1,192,4096]{2,1,0:T(8,128)(2,1)}) custom-call(bf16[128,4096]{1,0:T(8,128)(2,1)S(1)} %get-tuple-element.105.rows_ref, bf16[128,192]{1,0:T(8,128)(2,1)S(1)} %get-tuple-element.106.refs_0_, bf16[128,192]{1,0:T(8,128)(2,1)S(1)} %get-tuple-element.107.refs_1_), custom_call_target="tpu_custom_call" | custom-call | flops 402653184 | bytes 4194304 | tf_op jit(solution)/shard_map/pallas_call | solution.py:111
  (50 shorter events, 8.4 us)
Async XLA Ops:
  1.5 8.2 %collective-permute-start.2 = (bf16[4,8320]{1,0:T(4,128)(2,1)S(1)}, bf16[4,8320]{1,0:T(4,128)(2,1)S(1)}, u32[]{:S(2)}, u32[]{:S(2)}) collective-permute-start(bf16[4,8320]{1,0:T(4,128)(2,1)S(1)} %get-tuple-element.58), channel_id=1, source_target_pairs={{0,24},{1,25},{2,26},{3,27},{4,28},{5,29},{6,30},{7,31},{8,16},{9,... | collective-permute-start | bytes 199688 | tf_op jit(solution)/shard_map/ppermute | solution.py:100
  6.7 5.7 %collective-permute-start.1 = (bf16[4,8320]{1,0:T(4,128)(2,1)S(1)}, bf16[4,8320]{1,0:T(4,128)(2,1)S(1)}, u32[]{:S(2)}, u32[]{:S(2)}) collective-permute-start(bf16[4,8320]{1,0:T(4,128)(2,1)S(1)} %get-tuple-element.58), channel_id=1, source_target_pairs={{0,16},{1,17},{2,18},{3,19},{4,20},{5,21},{6,22},{7,23},{8,24},{9,... | collective-permute-start | bytes 199688 | tf_op jit(solution)/shard_map/ppermute | solution.py:100
  6.7 5.7 %collective-permute-start = (bf16[4,8320]{1,0:T(4,128)(2,1)S(1)}, bf16[4,8320]{1,0:T(4,128)(2,1)S(1)}, u32[]{:S(2)}, u32[]{:S(2)}) collective-permute-start(bf16[4,8320]{1,0:T(4,128)(2,1)S(1)} %get-tuple-element.58), channel_id=1, source_target_pairs={{0,8},{1,9},{2,10},{3,11},{4,12},{5,13},{6,14},{7,15},{8,0},{9,1},... | collective-permute-start | bytes 199688 | tf_op jit(solution)/shard_map/ppermute | solution.py:100
  12.6 5.5 %collective-permute-start.10 = (bf16[16,4096]{1,0:T(8,128)(2,1)S(1)}, bf16[16,4096]{1,0:T(8,128)(2,1)S(1)}, u32[]{:S(2)}, u32[]{:S(2)}) collective-permute-start(bf16[16,4096]{1,0:T(8,128)(2,1)S(1)} %pad_maximum_fusion.1.refs_0_), channel_id=1, source_target_pairs={{0,4},{1,5},{2,6},{3,7},{4,0},{5,1},{6,2},{7,3},{8,12},{9,13},{10,... | collective-permute-start | bytes 393224 | tf_op jit(solution)/shard_map/ppermute | solution.py:100
  14.2 6.5 %collective-permute-start.4 = (bf16[16,4224]{1,0:T(8,128)(2,1)S(1)}, bf16[16,4224]{1,0:T(8,128)(2,1)S(1)}, u32[]{:S(2)}, u32[]{:S(2)}) collective-permute-start(bf16[16,4224]{1,0:T(8,128)(2,1)S(1)} %pad_maximum_fusion.refs_0_), channel_id=1, source_target_pairs={{0,2},{1,3},{2,0},{3,1},{4,6},{5,7},{6,4},{7,5},{8,10},{9,11},{10,... | collective-permute-start | bytes 405512 | tf_op jit(solution)/shard_map/ppermute | solution.py:100
  15.7 6.4 %collective-permute-start.3 = (bf16[16,4224]{1,0:T(8,128)(2,1)S(1)}, bf16[16,4224]{1,0:T(8,128)(2,1)S(1)}, u32[]{:S(2)}, u32[]{:S(2)}) collective-permute-start(bf16[16,4224]{1,0:T(8,128)(2,1)S(1)} %pad_maximum_fusion.refs_0_), channel_id=1, source_target_pairs={{0,4},{1,5},{2,6},{3,7},{4,0},{5,1},{6,2},{7,3},{8,12},{9,13},{10,... | collective-permute-start | bytes 405512 | tf_op jit(solution)/shard_map/ppermute | solution.py:100
  16.3 7.2 %collective-permute-start.6 = (bf16[16,4096]{1,0:T(8,128)(2,1)S(1)}, bf16[16,4096]{1,0:T(8,128)(2,1)S(1)}, u32[]{:S(2)}, u32[]{:S(2)}) collective-permute-start(bf16[16,4096]{1,0:T(8,128)(2,1)S(1)} %pad_maximum_fusion.1.refs_0_), channel_id=1, source_target_pairs={{0,2},{1,3},{2,0},{3,1},{4,6},{5,7},{6,4},{7,5},{8,10},{9,11},{10,... | collective-permute-start | bytes 393224 | tf_op jit(solution)/shard_map/ppermute | solution.py:100
  18.1 6.8 %collective-permute-start.11 = (bf16[16,4096]{1,0:T(8,128)(2,1)S(1)}, bf16[16,4096]{1,0:T(8,128)(2,1)S(1)}, u32[]{:S(2)}, u32[]{:S(2)}) collective-permute-start(bf16[16,4096]{1,0:T(8,128)(2,1)S(1)} %collective-permute-done.10.refs_0_), channel_id=1, source_target_pairs={{0,2},{1,3},{2,0},{3,1},{4,6},{5,7},{6,4},{7,5},{8,10},{9,11},{10,... | collective-permute-start | bytes 393224 | tf_op jit(solution)/shard_map/ppermute | solution.py:100
  20.7 5.0 %collective-permute-start.5 = (bf16[16,4224]{1,0:T(8,128)(2,1)S(1)}, bf16[16,4224]{1,0:T(8,128)(2,1)S(1)}, u32[]{:S(2)}, u32[]{:S(2)}) collective-permute-start(bf16[16,4224]{1,0:T(8,128)(2,1)S(1)} %collective-permute-done.4.refs_0_), channel_id=1, source_target_pairs={{0,4},{1,5},{2,6},{3,7},{4,0},{5,1},{6,2},{7,3},{8,12},{9,13},{10,... | collective-permute-start | bytes 405512 | tf_op jit(solution)/shard_map/ppermute | solution.py:100
  22.1 3.7 %collective-permute-start.8 = (bf16[32,4224]{1,0:T(8,128)(2,1)S(1)}, bf16[32,4224]{1,0:T(8,128)(2,1)S(1)}, u32[]{:S(2)}, u32[]{:S(2)}) collective-permute-start(bf16[32,4224]{1,0:T(8,128)(2,1)S(1)} %shard_map.112.refs_0_), channel_id=1, source_target_pairs={{0,1},{1,0},{2,3},{3,2},{4,5},{5,4},{6,7},{7,6},{8,9},{9,8},{10,11... | collective-permute-start | bytes 811016 | tf_op jit(solution)/shard_map/ppermute | solution.py:100
  23.5 2.3 %collective-permute-start.7 = (bf16[32,4096]{1,0:T(8,128)(2,1)S(1)}, bf16[32,4096]{1,0:T(8,128)(2,1)S(1)}, u32[]{:S(2)}, u32[]{:S(2)}) collective-permute-start(bf16[32,4096]{1,0:T(8,128)(2,1)S(1)} %shard_map.114.refs_0_), channel_id=1, source_target_pairs={{0,1},{1,0},{2,3},{3,2},{4,5},{5,4},{6,7},{7,6},{8,9},{9,8},{10,11... | collective-permute-start | bytes 786440 | tf_op jit(solution)/shard_map/ppermute | solution.py:100
  24.9 1.6 %collective-permute-start.12 = (bf16[32,4096]{1,0:T(8,128)(2,1)S(1)}, bf16[32,4096]{1,0:T(8,128)(2,1)S(1)}, u32[]{:S(2)}, u32[]{:S(2)}) collective-permute-start(bf16[32,4096]{1,0:T(8,128)(2,1)S(1)} %shard_map.115.refs_1_), channel_id=1, source_target_pairs={{0,1},{1,0},{2,3},{3,2},{4,5},{5,4},{6,7},{7,6},{8,9},{9,8},{10,11... | collective-permute-start | bytes 786440 | tf_op jit(solution)/shard_map/ppermute | solution.py:100
  25.7 2.0 %collective-permute-start.9 = (bf16[32,4224]{1,0:T(8,128)(2,1)S(1)}, bf16[32,4224]{1,0:T(8,128)(2,1)S(1)}, u32[]{:S(2)}, u32[]{:S(2)}) collective-permute-start(bf16[32,4224]{1,0:T(8,128)(2,1)S(1)} %shard_map.113.refs_1_), channel_id=1, source_target_pairs={{0,1},{1,0},{2,3},{3,2},{4,5},{5,4},{6,7},{7,6},{8,9},{9,8},{10,11... | collective-permute-start | bytes 811016 | tf_op jit(solution)/shard_map/ppermute | solution.py:100
  29.7 1.6 %collective-permute-start.13 = (bf16[16,8192]{1,0:T(8,128)(2,1)S(1)}, bf16[16,8192]{1,0:T(8,128)(2,1)S(1)}, u32[]{:S(2)}, u32[]{:S(2)}) collective-permute-start(bf16[16,8192]{1,0:T(8,128)(2,1)S(1)} %get-tuple-element.74), channel_id=1, source_target_pairs={{0,1},{1,0},{2,3},{3,2},{4,5},{5,4},{6,7},{7,6},{8,9},{9,8},{10,11... | collective-permute-start | bytes 786440 | tf_op jit(solution)/shard_map/ppermute | solution.py:100
  31.3 2.5 %collective-permute-start.14 = (bf16[48,8192]{1,0:T(8,128)(2,1)S(1)}, bf16[48,8192]{1,0:T(8,128)(2,1)S(1)}, u32[]{:S(2)}, u32[]{:S(2)}) collective-permute-start(bf16[48,8192]{1,0:T(8,128)(2,1)S(1)} %get-tuple-element.76), channel_id=1, source_target_pairs={{0,1},{1,0},{2,3},{3,2},{4,5},{5,4},{6,7},{7,6},{8,9},{9,8},{10,11... | collective-permute-start | bytes 2359304 | tf_op jit(solution)/shard_map/ppermute | solution.py:100
  31.5 6.4 %collective-permute-start.17 = (bf16[16,4096]{1,0:T(8,128)(2,1)S(1)}, bf16[16,4096]{1,0:T(8,128)(2,1)S(1)}, u32[]{:S(2)}, u32[]{:S(2)}) collective-permute-start(bf16[16,4096]{1,0:T(8,128)(2,1)S(1)} %get-tuple-element.84), channel_id=1, source_target_pairs={{0,4},{1,5},{2,6},{3,7},{4,0},{5,1},{6,2},{7,3},{8,12},{9,13},{10,... | collective-permute-start | bytes 393224 | tf_op jit(solution)/shard_map/ppermute | solution.py:100
  32.7 6.9 %collective-permute-start.19 = (bf16[16,4096]{1,0:T(8,128)(2,1)S(1)}, bf16[16,4096]{1,0:T(8,128)(2,1)S(1)}, u32[]{:S(2)}, u32[]{:S(2)}) collective-permute-start(bf16[16,4096]{1,0:T(8,128)(2,1)S(1)} %get-tuple-element.95), channel_id=1, source_target_pairs={{0,2},{1,3},{2,0},{3,1},{4,6},{5,7},{6,4},{7,5},{8,10},{9,11},{10,... | collective-permute-start | bytes 393224 | tf_op jit(solution)/shard_map/ppermute | solution.py:100
  33.9 6.3 %collective-permute-start.15 = (bf16[16,4096]{1,0:T(8,128)(2,1)S(1)}, bf16[16,4096]{1,0:T(8,128)(2,1)S(1)}, u32[]{:S(2)}, u32[]{:S(2)}) collective-permute-start(bf16[16,4096]{1,0:T(8,128)(2,1)S(1)} %get-tuple-element.79), channel_id=1, source_target_pairs={{0,4},{1,5},{2,6},{3,7},{4,0},{5,1},{6,2},{7,3},{8,12},{9,13},{10,... | collective-permute-start | bytes 393224 | tf_op jit(solution)/shard_map/ppermute | solution.py:100
  35.4 6.4 %collective-permute-start.16 = (bf16[16,4096]{1,0:T(8,128)(2,1)S(1)}, bf16[16,4096]{1,0:T(8,128)(2,1)S(1)}, u32[]{:S(2)}, u32[]{:S(2)}) collective-permute-start(bf16[16,4096]{1,0:T(8,128)(2,1)S(1)} %get-tuple-element.80), channel_id=1, source_target_pairs={{0,2},{1,3},{2,0},{3,1},{4,6},{5,7},{6,4},{7,5},{8,10},{9,11},{10,... | collective-permute-start | bytes 393224 | tf_op jit(solution)/shard_map/ppermute | solution.py:100
  37.9 5.8 %collective-permute-start.18 = (bf16[16,4096]{1,0:T(8,128)(2,1)S(1)}, bf16[16,4096]{1,0:T(8,128)(2,1)S(1)}, u32[]{:S(2)}, u32[]{:S(2)}) collective-permute-start(bf16[16,4096]{1,0:T(8,128)(2,1)S(1)} %shard_map.120), channel_id=1, source_target_pairs={{0,2},{1,3},{2,0},{3,1},{4,6},{5,7},{6,4},{7,5},{8,10},{9,11},{10,... | collective-permute-start | bytes 393224 | tf_op jit(solution)/shard_map/ppermute | solution.py:100
  39.5 5.0 %collective-permute-start.20 = (bf16[16,4096]{1,0:T(8,128)(2,1)S(1)}, bf16[16,4096]{1,0:T(8,128)(2,1)S(1)}, u32[]{:S(2)}, u32[]{:S(2)}) collective-permute-start(bf16[16,4096]{1,0:T(8,128)(2,1)S(1)} %shard_map.122), channel_id=1, source_target_pairs={{0,4},{1,5},{2,6},{3,7},{4,0},{5,1},{6,2},{7,3},{8,12},{9,13},{10,... | collective-permute-start | bytes 393224 | tf_op jit(solution)/shard_map/ppermute | solution.py:100
  44.7 6.9 %collective-permute-start.21 = (bf16[4,8192]{1,0:T(4,128)(2,1)S(1)}, bf16[4,8192]{1,0:T(4,128)(2,1)S(1)}, u32[]{:S(2)}, u32[]{:S(2)}) collective-permute-start(bf16[4,8192]{1,0:T(4,128)(2,1)S(1)} %get-tuple-element.100), channel_id=1, source_target_pairs={{0,24},{1,25},{2,26},{3,27},{4,28},{5,29},{6,30},{7,31},{8,16},{9,... | collective-permute-start | bytes 196616 | tf_op jit(solution)/shard_map/ppermute | solution.py:100
  47.1 5.2 %collective-permute-start.22 = (bf16[4,8192]{1,0:T(4,128)(2,1)S(1)}, bf16[4,8192]{1,0:T(4,128)(2,1)S(1)}, u32[]{:S(2)}, u32[]{:S(2)}) collective-permute-start(bf16[4,8192]{1,0:T(4,128)(2,1)S(1)} %get-tuple-element.101), channel_id=1, source_target_pairs={{0,16},{1,17},{2,18},{3,19},{4,20},{5,21},{6,22},{7,23},{8,24},{9,... | collective-permute-start | bytes 196616 | tf_op jit(solution)/shard_map/ppermute | solution.py:100
  47.1 5.2 %collective-permute-start.23 = (bf16[4,8192]{1,0:T(4,128)(2,1)S(1)}, bf16[4,8192]{1,0:T(4,128)(2,1)S(1)}, u32[]{:S(2)}, u32[]{:S(2)}) collective-permute-start(bf16[4,8192]{1,0:T(4,128)(2,1)S(1)} %get-tuple-element.102), channel_id=1, source_target_pairs={{0,8},{1,9},{2,10},{3,11},{4,12},{5,13},{6,14},{7,15},{8,0},{9,1},... | collective-permute-start | bytes 196616 | tf_op jit(solution)/shard_map/ppermute | solution.py:100

commit v9 on v7

--- a/solution.py
+++ b/solution.py
@@ -93,11 +93,11 @@
     )
 
 
-CORE, FAR = 1, (2, 4, 6)
-
-
-def from_xor(value, mask, devices):
-    return lax.ppermute(value, AXES, [(i, i ^ mask) for i in range(devices)])
+CORE, ASIDE, ACROSS = (1, 1), (4, 2), (2, 4)
+
+
+def from_xor(value, masks, devices):
+    return lax.ppermute(value, AXES, [(i, i ^ masks[i % 2]) for i in range(devices)])
 
 
 def kernel_call(body, out_shape, cost, *operands, scratch=(), hbm=()):
@@ -162,11 +162,11 @@
         start += piece.shape[0]
 
 
-def cotangent_places(pieces):
+def block_places(pieces, order):
     rows = pieces[0].shape[0] // 2
     for i, piece in enumerate(pieces):
         for k in range(2):
-            at = i // 2 * 4 + (2 * k if i % 2 == 0 else 2 * k + 1)
+            at = i // 2 * 4 + order[i % 2 * 2 + k]
             yield slice(at * rows, (at + 1) * rows), piece, slice(k * rows, (k + 1) * rows)
 
 
@@ -177,8 +177,8 @@
 
 def forward_body(count, *refs):
     pieces, (wg_ref, wu_ref, x_ref, hidden_ref, gate_ref, up_ref) = refs[:count], refs[count:]
-    for here, piece in places(pieces):
-        x_ref[here, :] = piece[...]
+    for here, piece, there in block_places(pieces, (0, 1, 2, 3)):
+        x_ref[here, :] = piece[there, :]
     x = x_ref[...]
     gate_pre = contract_rows(x, wg_ref[0])
     up_pre = contract_rows(x, wu_ref[0])
@@ -196,11 +196,14 @@
         ref[...] = (own_ref[-rows:, at] + came_ref[:, at].astype(jnp.float32)).astype(jnp.bfloat16)
 
 
-def most_body(own_ref, came_ref, *outs):
-    rows, width = outs[0].shape
-    for i, ref in enumerate(outs):
-        here = (slice(i % 3 * rows, (i % 3 + 1) * rows), slice(i // 3 * width, (i // 3 + 1) * width))
-        ref[...] = (own_ref[here] + came_ref[here].astype(jnp.float32)).astype(ref.dtype)
+def most_body(own_ref, came_ref, here_ref, aside_ref, out_ref, into_ref):
+    rows, width = out_ref.shape
+    for at, ref in ((0, here_ref), (2, aside_ref)):
+        at = slice(at * rows, (at + 1) * rows)
+        ref[...] = (own_ref[at, :] + came_ref[at, :].astype(jnp.float32)).astype(ref.dtype)
+    for side, ref in enumerate((out_ref, into_ref)):
+        at = (slice(rows, 2 * rows), slice(side * width, (side + 1) * width))
+        ref[...] = own_ref[at] + came_ref[at].astype(jnp.float32)
 
 
 def backward_body(count, *refs):
@@ -208,7 +211,7 @@
     hidden_ref, gate_ref, up_ref, mine_ref, wg_ref, wu_ref, wd_ref = rest[:7]
     dy_ref, scaled_ref, gate_act_ref, up_act_ref, own_ref, most_ref, corner_ref, weight_ref = rest[7:]
     width = dy_ref.shape[1]
-    for here, piece, there in cotangent_places(pieces):
+    for here, piece, there in block_places(pieces, (0, 2, 1, 3)):
         dy_ref[here, :] = piece[there, :width]
         route = piece[there, width:].astype(jnp.float32) * mine_ref[:1, :]
         weight = jnp.sum(route, axis=1, keepdims=True)
@@ -234,15 +237,13 @@
     to_ref[...] = (here_ref[...] + came_ref[...].astype(jnp.float32)).astype(jnp.bfloat16)
 
 
-def deal_body(*refs):
-    parts, outs = refs[:6], refs[6:]
+def deal_body(here_ref, aside_ref, *refs):
+    parts, outs = refs[:2], refs[2:]
     width, rows = parts[0].shape[1], outs[0].shape[0]
-    for side in range(2):
+    for side, part in enumerate(parts):
         at = slice(side * width, (side + 1) * width)
-        here = parts[3 * side : 3 * side + 3]
-        total = here[0][...]
-        for part in here[1:]:
-            total = total + part[...].astype(jnp.float32)
+        total = here_ref[:, at] + aside_ref[:, at].astype(jnp.float32)
+        total = total + part[...].astype(jnp.float32)
         for i, ref in enumerate(outs):
             ref[:, at] = total[i * rows : (i + 1) * rows, :].astype(ref.dtype)
 
@@ -269,7 +270,7 @@
     expert = lax.axis_index("expert").astype(jnp.int32).reshape(1)
     rows, width = tokens.shape
     ff = gate_weight.shape[1]
-    near = tuple(k << 3 for k in range(1, devices >> 3))
+    near = tuple((k << 3, k << 3) for k in range(1, devices >> 3))
     block_rows = rows * (len(near) + 1)
     bf16, f32 = jnp.bfloat16, jnp.float32
     columns = 2 * width + experts + -experts % 128
@@ -278,8 +279,8 @@
     def shape(*dims, dtype=bf16):
         return jax.ShapeDtypeStruct(dims, dtype)
 
-    def passed(value, mask):
-        return from_xor(value, mask, devices)
+    def passed(value, masks):
+        return from_xor(value, masks, devices)
 
     message, mine = kernel_call(
         pack_body,
@@ -315,11 +316,10 @@
     block_x, block_dy, *weights = lax.optimization_barrier((block_x, block_dy, *weights))
     w_gate, w_up, w_down = weights
 
-    first, second, _ = FAR
-    second_x, first_dy = passed(block_x, second), passed(block_dy, first)
-    second_dy, first_x = passed(block_dy, second), passed(block_x, first)
-    corner_x, corner_dy = passed(second_x, first), passed(first_dy, second)
-    half = (len(FAR) + 1) * block_rows
+    aside_x, across_dy = passed(block_x, ASIDE), passed(block_dy, ACROSS)
+    aside_dy, across_x = passed(block_dy, ASIDE), passed(block_x, ACROSS)
+    corner_x, corner_dy = passed(aside_x, ACROSS), passed(across_dy, ASIDE)
+    half = 4 * block_rows
 
     def both_cores(*pairs):
         own = [
@@ -328,11 +328,9 @@
         ]
         return own + [passed(pair, CORE) for pair in own]
 
-    x_pieces = both_cores((block_x, second_x), (first_x, corner_x))
-    early_dy, late_dy, other_early, other_late = both_cores(
-        (block_dy, first_dy), (second_dy, corner_dy)
-    )
-    dy_pieces = [early_dy, late_dy, other_early, other_late]
+    x_pieces = both_cores((block_x, across_x), (aside_x, corner_x))
+    dy_pieces = both_cores((block_dy, aside_dy), (across_dy, corner_dy))
+    x_pieces[2], dy_pieces[2] = lax.optimization_barrier((x_pieces[2], dy_pieces[2]))
     all_x, hidden, gate_part, up_part = kernel_call(
         functools.partial(forward_body, len(x_pieces)),
         (shape(2 * half, width),) + (shape(2 * half, ff, dtype=f32),) * 3,
@@ -365,34 +363,33 @@
 
     piece, full = shape(block_rows, width), shape(block_rows, width, dtype=f32)
     out_corner, into_corner = kernel_call(corner_body, (piece, piece), 0, own, corner_came)
-    out_here, out_second, out_first, into_here, into_second, into_first = kernel_call(
-        most_body, (full, piece, full, full, full, piece), 0, own, most_came
-    )
-    out_turn, into_turn = passed(out_corner, second), passed(into_corner, first)
-    out_second, into_first = passed(out_second, second), passed(into_first, first)
-    scaled, out_second, into_first = lax.optimization_barrier((scaled, out_second, into_first))
-    out_first = passed(kernel_call(turn_body, piece, 0, out_first, out_turn), first)
-    into_second = passed(kernel_call(turn_body, piece, 0, into_second, into_turn), second)
-    into_here, scaled, gate_act, up_act = lax.optimization_barrier(
-        (into_here, scaled, gate_act, up_act)
-    )
-    grad_down = kernel_call(grad_body, shape(*down_weight.shape), 8 * unit, all_dy, scaled)
-    into_here, grad_down = lax.optimization_barrier((into_here, grad_down))
+    here, aside, out_across, into_across = kernel_call(
+        most_body,
+        (shape(block_rows, 2 * width, dtype=f32), shape(block_rows, 2 * width), full, full),
+        0,
+        own,
+        most_came,
+    )
+    out_turn, into_turn = passed(out_corner, ASIDE), passed(into_corner, ASIDE)
+    aside = passed(aside, ASIDE)
+    out_across = passed(kernel_call(turn_body, piece, 0, out_across, out_turn), ACROSS)
+    into_across = passed(kernel_call(turn_body, piece, 0, into_across, into_turn), ACROSS)
+    here, scaled, gate_act, up_act = lax.optimization_barrier((here, scaled, gate_act, up_act))
+    grad_gate, grad_up = kernel_call(
+        grad_body, (shape(*gate_weight.shape),) * 2, 16 * unit, all_x, gate_act, up_act
+    )
+    here, grad_gate, grad_up = lax.optimization_barrier((here, grad_gate, grad_up))
     mine_sum, *away = kernel_call(
         deal_body,
         (shape(rows, 2 * width, dtype=f32),) + (shape(rows, 2 * width),) * len(near),
         0,
-        out_here,
-        out_second,
-        out_first,
-        into_here,
-        into_first,
-        into_second,
-    )
-    mine_sum, gate_act, up_act = lax.optimization_barrier((mine_sum, gate_act, up_act))
-    grad_gate, grad_up = kernel_call(
-        grad_body, (shape(*gate_weight.shape),) * 2, 16 * unit, all_x, gate_act, up_act
-    )
+        here,
+        aside,
+        out_across,
+        into_across,
+    )
+    mine_sum, scaled = lax.optimization_barrier((mine_sum, scaled))
+    grad_down = kernel_call(grad_body, shape(*down_weight.shape), 8 * unit, all_dy, scaled)
     mixed, input_grad = kernel_call(
         end_body,
         (shape(rows, width),) * 2,

time: 54.2 us -> 53.1 us (0.980)
  starting transfers between devices: 24.9 us -> 23 us
  waiting for transfers between devices: 16.3 us -> 17 us
    ppermute x24 -> x23, starting transfers between devices: 24.9 us -> 23 us  [from_xor(): lax.ppermute(value, AXES, [(i, i ^ masks[i % 2]) for i in range(devices)])]
    ppermute x24 -> x23, waiting for transfers between devices: 16.3 us -> 17 us  [from_xor(): lax.ppermute(value, AXES, [(i, i ^ masks[i % 2]) for i in range(devices)])]
  transfers between devices with their start and end apart: 24 -> 23, of which waited for: 13 -> 14; matrix products, arithmetic and copies ran while one was open for 0% -> 0% of each run, Pallas kernels for 15% -> 15%
where the time goes in v9:
time: 53.1 us; the launch traced here: 52.9 us
  starting transfers between devices  23 us (43%)
  waiting for transfers between devices  17 us (32%)
  Pallas kernels  11.7 us (22%)
  between operations  0.86 us (2%)
    ppermute x23, starting transfers between devices, from_xor(): lax.ppermute(value, AXES, [(i, i ^ masks[i % 2]) for i in range(devices)])  23 us
    ppermute x23, waiting for transfers between devices, from_xor(): lax.ppermute(value, AXES, [(i, i ^ masks[i % 2]) for i in range(devices)])  17 us
    pallas_call x16, Pallas kernels, kernel_call(): pl.pallas_call(body, out_shape=out_shape, in_specs=specs, out_specs=jax.t...  11.7 us
  transfers between devices with their start and end apart: 23, of which 14 were waited for; matrix products, arithmetic and copies ran while one was open for 0% of the time, Pallas kernels for 15%

profile of v9, /device:TPU:0, one launch (start us, length us, event | category | flops | bytes accessed | tf_op | source)
XLA Modules:
  0.0 52.9 jit_solution(216323196677452736)
XLA Ops:
  0.6 0.9 %shard_map.110 = (bf16[4,8320]{1,0:T(4,128)(2,1)S(1)}, f32[8,128]{1,0:T(8,128)S(1)}) custom-call(bf16[4,4096]{1,0:T(4,128)(2,1)} %x_ref.1, bf16[4,4096]{1,0:T(4,128)(2,1)} %dy_ref.1, s32[2,4]{1,0:T(2,128)} %bitcast.3, bf16[2,4]{1,0:T(2,128)(2,1)} %bitcast.4, s32[1]{0:T(128)} %bitcast.2.expert_ref), custom_call_target="tpu_custom_call" | custom-call | bytes 4194304 | tf_op jit(solution)/shard_map/pallas_call | solution.py:111
  1.5 5.1 %collective-permute-start.2 = (bf16[4,8320]{1,0:T(4,128)(2,1)S(1)}, bf16[4,8320]{1,0:T(4,128)(2,1)S(1)}, u32[]{:S(2)}, u32[]{:S(2)}) collective-permute-start(bf16[4,8320]{1,0:T(4,128)(2,1)S(1)} %get-tuple-element.53), channel_id=1, source_target_pairs={{0,24},{1,25},{2,26},{3,27},{4,28},{5,29},{6,30},{7,31},{8,16},{9,... | collective-permute-start | bytes 199688 | tf_op jit(solution)/shard_map/ppermute | solution.py:100
  7.3 2.4 %shard_map.111 = (bf16[1,192,4096]{2,1,0:T(8,128)(2,1)S(1)}, bf16[1,192,4096]{2,1,0:T(8,128)(2,1)S(1)}, bf16[1,192,4096]{2,1,0:T(8,128)(2,1)S(1)}) custom-call(bf16[1,192,4096]{2,1,0:T(8,128)(2,1)} %refs_0_.1, bf16[1,192,4096]{2,1,0:T(8,128)(2,1)} %refs_1_.1, bf16[1,192,4096]{2,1,0:T(8,128)(2,1)} %refs_2_.1), custom_call_target="tpu_custom_call" | custom-call | bytes 4194304 | tf_op jit(solution)/shard_map/pallas_call | solution.py:111
  9.8 2.6 %collective-permute-done.1 = bf16[4,8320]{1,0:T(4,128)(2,1)S(1)} collective-permute-done((bf16[4,8320]{1,0:T(4,128)(2,1)S(1)}, bf16[4,8320]{1,0:T(4,128)(2,1)S(1)}, u32[]{:S(2)}, u32[]{:S(2)}) %collective-permute-start.1) | collective-permute-done | bytes 66592 | tf_op jit(solution)/shard_map/ppermute | solution.py:100
  12.6 1.6 %collective-permute-start.10 = (bf16[16,4096]{1,0:T(8,128)(2,1)S(1)}, bf16[16,4096]{1,0:T(8,128)(2,1)S(1)}, u32[]{:S(2)}, u32[]{:S(2)}) collective-permute-start(bf16[16,4096]{1,0:T(8,128)(2,1)S(1)} %pad_maximum_fusion.1.refs_0_), channel_id=1, source_target_pairs={{0,4},{1,3},{2,6},{3,1},{4,0},{5,7},{6,2},{7,5},{8,12},{9,11},{10,... | collective-permute-start | bytes 393224 | tf_op jit(solution)/shard_map/ppermute | solution.py:100
  14.2 1.5 %collective-permute-start.4 = (bf16[16,4224]{1,0:T(8,128)(2,1)S(1)}, bf16[16,4224]{1,0:T(8,128)(2,1)S(1)}, u32[]{:S(2)}, u32[]{:S(2)}) collective-permute-start(bf16[16,4224]{1,0:T(8,128)(2,1)S(1)} %pad_maximum_fusion.refs_0_), channel_id=1, source_target_pairs={{0,2},{1,5},{2,0},{3,7},{4,6},{5,1},{6,4},{7,3},{8,10},{9,13},{10,... | collective-permute-start | bytes 405512 | tf_op jit(solution)/shard_map/ppermute | solution.py:100
  16.8 2.2 %collective-permute-done.10.refs_0_ = bf16[16,4096]{1,0:T(8,128)(2,1)S(1)} collective-permute-done((bf16[16,4096]{1,0:T(8,128)(2,1)S(1)}, bf16[16,4096]{1,0:T(8,128)(2,1)S(1)}, u32[]{:S(2)}, u32[]{:S(2)}) %collective-permute-start.10) | collective-permute-done | bytes 131104 | tf_op jit(solution)/shard_map/ppermute | solution.py:100
  18.9 0.9 %collective-permute-start.11 = (bf16[16,4096]{1,0:T(8,128)(2,1)S(1)}, bf16[16,4096]{1,0:T(8,128)(2,1)S(1)}, u32[]{:S(2)}, u32[]{:S(2)}) collective-permute-start(bf16[16,4096]{1,0:T(8,128)(2,1)S(1)} %collective-permute-done.10.refs_0_), channel_id=1, source_target_pairs={{0,2},{1,5},{2,0},{3,7},{4,6},{5,1},{6,4},{7,3},{8,10},{9,13},{10,... | collective-permute-start | bytes 393224 | tf_op jit(solution)/shard_map/ppermute | solution.py:100
  20.5 1.5 %collective-permute-start.5 = (bf16[16,4224]{1,0:T(8,128)(2,1)S(1)}, bf16[16,4224]{1,0:T(8,128)(2,1)S(1)}, u32[]{:S(2)}, u32[]{:S(2)}) collective-permute-start(bf16[16,4224]{1,0:T(8,128)(2,1)S(1)} %collective-permute-done.4.refs_0_), channel_id=1, source_target_pairs={{0,4},{1,3},{2,6},{3,1},{4,0},{5,7},{6,2},{7,5},{8,12},{9,11},{10,... | collective-permute-start | bytes 405512 | tf_op jit(solution)/shard_map/ppermute | solution.py:100
  22.9 1.9 %collective-permute-done.11.refs_1_ = bf16[16,4096]{1,0:T(8,128)(2,1)S(1)} collective-permute-done((bf16[16,4096]{1,0:T(8,128)(2,1)S(1)}, bf16[16,4096]{1,0:T(8,128)(2,1)S(1)}, u32[]{:S(2)}, u32[]{:S(2)}) %collective-permute-start.11) | collective-permute-done | bytes 131104 | tf_op jit(solution)/shard_map/ppermute | solution.py:100
  26.4 1.2 %shard_map.116 = (bf16[128,4096]{1,0:T(8,128)(2,1)S(1)}, f32[128,192]{1,0:T(8,128)S(1)}, f32[128,192]{1,0:T(8,128)S(1)}, f32[128,192]{1,0:T(8,128)S(1)}) custom-call(bf16[32,4096]{1,0:T(8,128)(2,1)S(1)} %shard_map.114.refs_0_, bf16[32,4096]{1,0:T(8,128)(2,1)S(1)} %shard_map.115.refs_1_, bf16[32,4096]{1,0:T(8,128)(2,1)S(1)} %collective-permute-done.7.refs_2_, ...), custom_call_target="tpu_custom_call" | custom-call | flops 402653184 | bytes 4194304 | tf_op jit(solution)/shard_map/pallas_call | solution.py:111
  27.6 1.9 %shard_map.117 = (bf16[128,4096]{1,0:T(8,128)(2,1)S(1)}, bf16[128,192]{1,0:T(8,128)(2,1)S(1)}, bf16[128,192]{1,0:T(8,128)(2,1)S(1)}, bf16[128,192]{1,0:T(8,128)(...) custom-call(bf16[32,4224]{1,0:T(8,128)(2,1)S(1)} %shard_map.112.refs_0_, ...), custom_call_target="tpu_custom_call" | custom-call | flops 603979776 | bytes 4194304 | tf_op jit(solution)/shard_map/pallas_call | solution.py:111
  29.8 1.4 %collective-permute-done.13.came_ref = bf16[16,8192]{1,0:T(8,128)(2,1)S(1)} collective-permute-done((bf16[16,8192]{1,0:T(8,128)(2,1)S(1)}, bf16[16,8192]{1,0:T(8,128)(2,1)S(1)}, u32[]{:S(2)}, u32[]{:S(2)}) %collective-permute-start.13) | collective-permute-done | bytes 262176 | tf_op jit(solution)/shard_map/ppermute | solution.py:100
  31.4 1.6 %collective-permute-start.16 = (bf16[16,4096]{1,0:T(8,128)(2,1)S(1)}, bf16[16,4096]{1,0:T(8,128)(2,1)S(1)}, u32[]{:S(2)}, u32[]{:S(2)}) collective-permute-start(bf16[16,4096]{1,0:T(8,128)(2,1)S(1)} %get-tuple-element.86), channel_id=1, source_target_pairs={{0,4},{1,3},{2,6},{3,1},{4,0},{5,7},{6,2},{7,5},{8,12},{9,11},{10,... | collective-permute-start | bytes 393224 | tf_op jit(solution)/shard_map/ppermute | solution.py:100
  33.7 1.6 %collective-permute-start.15 = (bf16[16,8192]{1,0:T(8,128)(2,1)S(1)}, bf16[16,8192]{1,0:T(8,128)(2,1)S(1)}, u32[]{:S(2)}, u32[]{:S(2)}) collective-permute-start(bf16[16,8192]{1,0:T(8,128)(2,1)S(1)} %get-tuple-element.83), channel_id=1, source_target_pairs={{0,4},{1,3},{2,6},{3,1},{4,0},{5,7},{6,2},{7,5},{8,12},{9,11},{10,... | collective-permute-start | bytes 786440 | tf_op jit(solution)/shard_map/ppermute | solution.py:100
  35.3 1.1 %collective-permute-done.16.came_ref = bf16[16,4096]{1,0:T(8,128)(2,1)S(1)} collective-permute-done((bf16[16,4096]{1,0:T(8,128)(2,1)S(1)}, bf16[16,4096]{1,0:T(8,128)(2,1)S(1)}, u32[]{:S(2)}, u32[]{:S(2)}) %collective-permute-start.16) | collective-permute-done | bytes 131104 | tf_op jit(solution)/shard_map/ppermute | solution.py:100
  37.0 1.0 %collective-permute-done.18.came_ref = bf16[16,4096]{1,0:T(8,128)(2,1)S(1)} collective-permute-done((bf16[16,4096]{1,0:T(8,128)(2,1)S(1)}, bf16[16,4096]{1,0:T(8,128)(2,1)S(1)}, u32[]{:S(2)}, u32[]{:S(2)}) %collective-permute-start.18) | collective-permute-done | bytes 131104 | tf_op jit(solution)/shard_map/ppermute | solution.py:100
  38.0 0.8 %collective-permute-start.19 = (bf16[16,4096]{1,0:T(8,128)(2,1)S(1)}, bf16[16,4096]{1,0:T(8,128)(2,1)S(1)}, u32[]{:S(2)}, u32[]{:S(2)}) collective-permute-start(bf16[16,4096]{1,0:T(8,128)(2,1)S(1)} %shard_map.122), channel_id=1, source_target_pairs={{0,2},{1,5},{2,0},{3,7},{4,6},{5,1},{6,4},{7,3},{8,10},{9,13},{10,... | collective-permute-start | bytes 393224 | tf_op jit(solution)/shard_map/ppermute | solution.py:100
  38.8 2.5 %shard_map.119 = (bf16[1,192,4096]{2,1,0:T(8,128)(2,1)}, bf16[1,192,4096]{2,1,0:T(8,128)(2,1)}) custom-call(bf16[128,4096]{1,0:T(8,128)(2,1)S(1)} %get-tuple-element.77.rows_ref, bf16[128,192]{1,0:T(8,128)(2,1)S(1)} %get-tuple-element.78.refs_0_, bf16[128,192]{1,0:T(8,128)(2,1)S(1)} %get-tuple-element.79.refs_1_), custom_call_target="tpu_custom_call" | custom-call | flops 402653184 | bytes 4194304 | tf_op jit(solution)/shard_map/pallas_call | solution.py:111
  41.5 1.6 %collective-permute-done.19.refs_1_ = bf16[16,4096]{1,0:T(8,128)(2,1)S(1)} collective-permute-done((bf16[16,4096]{1,0:T(8,128)(2,1)S(1)}, bf16[16,4096]{1,0:T(8,128)(2,1)S(1)}, u32[]{:S(2)}, u32[]{:S(2)}) %collective-permute-start.19) | collective-permute-done | bytes 131104 | tf_op jit(solution)/shard_map/ppermute | solution.py:100
  43.2 2.4 %collective-permute-start.20 = (bf16[4,8192]{1,0:T(4,128)(2,1)S(1)}, bf16[4,8192]{1,0:T(4,128)(2,1)S(1)}, u32[]{:S(2)}, u32[]{:S(2)}) collective-permute-start(bf16[4,8192]{1,0:T(4,128)(2,1)S(1)} %get-tuple-element.92), channel_id=1, source_target_pairs={{0,24},{1,25},{2,26},{3,27},{4,28},{5,29},{6,30},{7,31},{8,16},{9,... | collective-permute-start | bytes 196616 | tf_op jit(solution)/shard_map/ppermute | solution.py:100
  45.5 2.1 %collective-permute-start.22 = (bf16[4,8192]{1,0:T(4,128)(2,1)S(1)}, bf16[4,8192]{1,0:T(4,128)(2,1)S(1)}, u32[]{:S(2)}, u32[]{:S(2)}) collective-permute-start(bf16[4,8192]{1,0:T(4,128)(2,1)S(1)} %get-tuple-element.94), channel_id=1, source_target_pairs={{0,8},{1,9},{2,10},{3,11},{4,12},{5,13},{6,14},{7,15},{8,0},{9,1},... | collective-permute-start | bytes 196616 | tf_op jit(solution)/shard_map/ppermute | solution.py:100
  47.6 1.7 %shard_map.125 = bf16[1,192,4096]{2,1,0:T(8,128)(2,1)} custom-call(bf16[128,4096]{1,0:T(8,128)(2,1)S(1)} %get-tuple-element.99.rows_ref, bf16[128,192]{1,0:T(8,128)(2,1)S(1)} %get-tuple-element.100.refs_0_), custom_call_target="tpu_custom_call" | custom-call | flops 201326592 | bytes 4194304 | tf_op jit(solution)/shard_map/pallas_call | solution.py:111
  50.1 2.2 %collective-permute-done.21.refs_1_ = bf16[4,8192]{1,0:T(4,128)(2,1)S(1)} collective-permute-done((bf16[4,8192]{1,0:T(4,128)(2,1)S(1)}, bf16[4,8192]{1,0:T(4,128)(2,1)S(1)}, u32[]{:S(2)}, u32[]{:S(2)}) %collective-permute-start.21) | collective-permute-done | bytes 65568 | tf_op jit(solution)/shard_map/ppermute | solution.py:100
  (48 shorter events, 8.5 us)
Async XLA Ops:
  1.5 8.2 %collective-permute-start.2 = (bf16[4,8320]{1,0:T(4,128)(2,1)S(1)}, bf16[4,8320]{1,0:T(4,128)(2,1)S(1)}, u32[]{:S(2)}, u32[]{:S(2)}) collective-permute-start(bf16[4,8320]{1,0:T(4,128)(2,1)S(1)} %get-tuple-element.53), channel_id=1, source_target_pairs={{0,24},{1,25},{2,26},{3,27},{4,28},{5,29},{6,30},{7,31},{8,16},{9,... | collective-permute-start | bytes 199688 | tf_op jit(solution)/shard_map/ppermute | solution.py:100
  6.7 5.7 %collective-permute-start.1 = (bf16[4,8320]{1,0:T(4,128)(2,1)S(1)}, bf16[4,8320]{1,0:T(4,128)(2,1)S(1)}, u32[]{:S(2)}, u32[]{:S(2)}) collective-permute-start(bf16[4,8320]{1,0:T(4,128)(2,1)S(1)} %get-tuple-element.53), channel_id=1, source_target_pairs={{0,16},{1,17},{2,18},{3,19},{4,20},{5,21},{6,22},{7,23},{8,24},{9,... | collective-permute-start | bytes 199688 | tf_op jit(solution)/shard_map/ppermute | solution.py:100
  6.7 5.7 %collective-permute-start = (bf16[4,8320]{1,0:T(4,128)(2,1)S(1)}, bf16[4,8320]{1,0:T(4,128)(2,1)S(1)}, u32[]{:S(2)}, u32[]{:S(2)}) collective-permute-start(bf16[4,8320]{1,0:T(4,128)(2,1)S(1)} %get-tuple-element.53), channel_id=1, source_target_pairs={{0,8},{1,9},{2,10},{3,11},{4,12},{5,13},{6,14},{7,15},{8,0},{9,1},... | collective-permute-start | bytes 199688 | tf_op jit(solution)/shard_map/ppermute | solution.py:100
  12.6 6.3 %collective-permute-start.10 = (bf16[16,4096]{1,0:T(8,128)(2,1)S(1)}, bf16[16,4096]{1,0:T(8,128)(2,1)S(1)}, u32[]{:S(2)}, u32[]{:S(2)}) collective-permute-start(bf16[16,4096]{1,0:T(8,128)(2,1)S(1)} %pad_maximum_fusion.1.refs_0_), channel_id=1, source_target_pairs={{0,4},{1,3},{2,6},{3,1},{4,0},{5,7},{6,2},{7,5},{8,12},{9,11},{10,... | collective-permute-start | bytes 393224 | tf_op jit(solution)/shard_map/ppermute | solution.py:100
  14.2 6.3 %collective-permute-start.4 = (bf16[16,4224]{1,0:T(8,128)(2,1)S(1)}, bf16[16,4224]{1,0:T(8,128)(2,1)S(1)}, u32[]{:S(2)}, u32[]{:S(2)}) collective-permute-start(bf16[16,4224]{1,0:T(8,128)(2,1)S(1)} %pad_maximum_fusion.refs_0_), channel_id=1, source_target_pairs={{0,2},{1,5},{2,0},{3,7},{4,6},{5,1},{6,4},{7,3},{8,10},{9,13},{10,... | collective-permute-start | bytes 405512 | tf_op jit(solution)/shard_map/ppermute | solution.py:100
  15.7 6.5 %collective-permute-start.3 = (bf16[16,4224]{1,0:T(8,128)(2,1)S(1)}, bf16[16,4224]{1,0:T(8,128)(2,1)S(1)}, u32[]{:S(2)}, u32[]{:S(2)}) collective-permute-start(bf16[16,4224]{1,0:T(8,128)(2,1)S(1)} %pad_maximum_fusion.refs_0_), channel_id=1, source_target_pairs={{0,4},{1,3},{2,6},{3,1},{4,0},{5,7},{6,2},{7,5},{8,12},{9,11},{10,... | collective-permute-start | bytes 405512 | tf_op jit(solution)/shard_map/ppermute | solution.py:100
  16.3 6.1 %collective-permute-start.6 = (bf16[16,4096]{1,0:T(8,128)(2,1)S(1)}, bf16[16,4096]{1,0:T(8,128)(2,1)S(1)}, u32[]{:S(2)}, u32[]{:S(2)}) collective-permute-start(bf16[16,4096]{1,0:T(8,128)(2,1)S(1)} %pad_maximum_fusion.1.refs_0_), channel_id=1, source_target_pairs={{0,2},{1,5},{2,0},{3,7},{4,6},{5,1},{6,4},{7,3},{8,10},{9,13},{10,... | collective-permute-start | bytes 393224 | tf_op jit(solution)/shard_map/ppermute | solution.py:100
  18.9 5.8 %collective-permute-start.11 = (bf16[16,4096]{1,0:T(8,128)(2,1)S(1)}, bf16[16,4096]{1,0:T(8,128)(2,1)S(1)}, u32[]{:S(2)}, u32[]{:S(2)}) collective-permute-start(bf16[16,4096]{1,0:T(8,128)(2,1)S(1)} %collective-permute-done.10.refs_0_), channel_id=1, source_target_pairs={{0,2},{1,5},{2,0},{3,7},{4,6},{5,1},{6,4},{7,3},{8,10},{9,13},{10,... | collective-permute-start | bytes 393224 | tf_op jit(solution)/shard_map/ppermute | solution.py:100
  20.5 5.0 %collective-permute-start.5 = (bf16[16,4224]{1,0:T(8,128)(2,1)S(1)}, bf16[16,4224]{1,0:T(8,128)(2,1)S(1)}, u32[]{:S(2)}, u32[]{:S(2)}) collective-permute-start(bf16[16,4224]{1,0:T(8,128)(2,1)S(1)} %collective-permute-done.4.refs_0_), channel_id=1, source_target_pairs={{0,4},{1,3},{2,6},{3,1},{4,0},{5,7},{6,2},{7,5},{8,12},{9,11},{10,... | collective-permute-start | bytes 405512 | tf_op jit(solution)/shard_map/ppermute | solution.py:100
  22.3 3.4 %collective-permute-start.8 = (bf16[32,4224]{1,0:T(8,128)(2,1)S(1)}, bf16[32,4224]{1,0:T(8,128)(2,1)S(1)}, u32[]{:S(2)}, u32[]{:S(2)}) collective-permute-start(bf16[32,4224]{1,0:T(8,128)(2,1)S(1)} %shard_map.112.refs_0_), channel_id=1, source_target_pairs={{0,1},{1,0},{2,3},{3,2},{4,5},{5,4},{6,7},{7,6},{8,9},{9,8},{10,11... | collective-permute-start | bytes 811016 | tf_op jit(solution)/shard_map/ppermute | solution.py:100
  22.4 3.3 %collective-permute-start.7 = (bf16[32,4096]{1,0:T(8,128)(2,1)S(1)}, bf16[32,4096]{1,0:T(8,128)(2,1)S(1)}, u32[]{:S(2)}, u32[]{:S(2)}) collective-permute-start(bf16[32,4096]{1,0:T(8,128)(2,1)S(1)} %shard_map.114.refs_0_), channel_id=1, source_target_pairs={{0,1},{1,0},{2,3},{3,2},{4,5},{5,4},{6,7},{7,6},{8,9},{9,8},{10,11... | collective-permute-start | bytes 786440 | tf_op jit(solution)/shard_map/ppermute | solution.py:100
  24.8 1.6 %collective-permute-start.12 = (bf16[32,4096]{1,0:T(8,128)(2,1)S(1)}, bf16[32,4096]{1,0:T(8,128)(2,1)S(1)}, u32[]{:S(2)}, u32[]{:S(2)}) collective-permute-start(bf16[32,4096]{1,0:T(8,128)(2,1)S(1)} %shard_map.115.refs_1_), channel_id=1, source_target_pairs={{0,1},{1,0},{2,3},{3,2},{4,5},{5,4},{6,7},{7,6},{8,9},{9,8},{10,11... | collective-permute-start | bytes 786440 | tf_op jit(solution)/shard_map/ppermute | solution.py:100
  25.6 2.1 %collective-permute-start.9 = (bf16[32,4224]{1,0:T(8,128)(2,1)S(1)}, bf16[32,4224]{1,0:T(8,128)(2,1)S(1)}, u32[]{:S(2)}, u32[]{:S(2)}) collective-permute-start(bf16[32,4224]{1,0:T(8,128)(2,1)S(1)} %shard_map.113.refs_1_), channel_id=1, source_target_pairs={{0,1},{1,0},{2,3},{3,2},{4,5},{5,4},{6,7},{7,6},{8,9},{9,8},{10,11... | collective-permute-start | bytes 811016 | tf_op jit(solution)/shard_map/ppermute | solution.py:100
  29.6 1.6 %collective-permute-start.13 = (bf16[16,8192]{1,0:T(8,128)(2,1)S(1)}, bf16[16,8192]{1,0:T(8,128)(2,1)S(1)}, u32[]{:S(2)}, u32[]{:S(2)}) collective-permute-start(bf16[16,8192]{1,0:T(8,128)(2,1)S(1)} %get-tuple-element.69), channel_id=1, source_target_pairs={{0,1},{1,0},{2,3},{3,2},{4,5},{5,4},{6,7},{7,6},{8,9},{9,8},{10,11... | collective-permute-start | bytes 786440 | tf_op jit(solution)/shard_map/ppermute | solution.py:100
  31.2 2.3 %collective-permute-start.14 = (bf16[48,8192]{1,0:T(8,128)(2,1)S(1)}, bf16[48,8192]{1,0:T(8,128)(2,1)S(1)}, u32[]{:S(2)}, u32[]{:S(2)}) collective-permute-start(bf16[48,8192]{1,0:T(8,128)(2,1)S(1)} %get-tuple-element.71), channel_id=1, source_target_pairs={{0,1},{1,0},{2,3},{3,2},{4,5},{5,4},{6,7},{7,6},{8,9},{9,8},{10,11... | collective-permute-start | bytes 2359304 | tf_op jit(solution)/shard_map/ppermute | solution.py:100
  31.4 5.0 %collective-permute-start.16 = (bf16[16,4096]{1,0:T(8,128)(2,1)S(1)}, bf16[16,4096]{1,0:T(8,128)(2,1)S(1)}, u32[]{:S(2)}, u32[]{:S(2)}) collective-permute-start(bf16[16,4096]{1,0:T(8,128)(2,1)S(1)} %get-tuple-element.86), channel_id=1, source_target_pairs={{0,4},{1,3},{2,6},{3,1},{4,0},{5,7},{6,2},{7,5},{8,12},{9,11},{10,... | collective-permute-start | bytes 393224 | tf_op jit(solution)/shard_map/ppermute | solution.py:100
  33.0 5.0 %collective-permute-start.18 = (bf16[16,4096]{1,0:T(8,128)(2,1)S(1)}, bf16[16,4096]{1,0:T(8,128)(2,1)S(1)}, u32[]{:S(2)}, u32[]{:S(2)}) collective-permute-start(bf16[16,4096]{1,0:T(8,128)(2,1)S(1)} %get-tuple-element.88), channel_id=1, source_target_pairs={{0,4},{1,3},{2,6},{3,1},{4,0},{5,7},{6,2},{7,5},{8,12},{9,11},{10,... | collective-permute-start | bytes 393224 | tf_op jit(solution)/shard_map/ppermute | solution.py:100
  33.7 9.4 %collective-permute-start.15 = (bf16[16,8192]{1,0:T(8,128)(2,1)S(1)}, bf16[16,8192]{1,0:T(8,128)(2,1)S(1)}, u32[]{:S(2)}, u32[]{:S(2)}) collective-permute-start(bf16[16,8192]{1,0:T(8,128)(2,1)S(1)} %get-tuple-element.83), channel_id=1, source_target_pairs={{0,4},{1,3},{2,6},{3,1},{4,0},{5,7},{6,2},{7,5},{8,12},{9,11},{10,... | collective-permute-start | bytes 786440 | tf_op jit(solution)/shard_map/ppermute | solution.py:100
  36.5 5.0 %collective-permute-start.17 = (bf16[16,4096]{1,0:T(8,128)(2,1)S(1)}, bf16[16,4096]{1,0:T(8,128)(2,1)S(1)}, u32[]{:S(2)}, u32[]{:S(2)}) collective-permute-start(bf16[16,4096]{1,0:T(8,128)(2,1)S(1)} %shard_map.121), channel_id=1, source_target_pairs={{0,2},{1,5},{2,0},{3,7},{4,6},{5,1},{6,4},{7,3},{8,10},{9,13},{10,... | collective-permute-start | bytes 393224 | tf_op jit(solution)/shard_map/ppermute | solution.py:100
  38.0 5.0 %collective-permute-start.19 = (bf16[16,4096]{1,0:T(8,128)(2,1)S(1)}, bf16[16,4096]{1,0:T(8,128)(2,1)S(1)}, u32[]{:S(2)}, u32[]{:S(2)}) collective-permute-start(bf16[16,4096]{1,0:T(8,128)(2,1)S(1)} %shard_map.122), channel_id=1, source_target_pairs={{0,2},{1,5},{2,0},{3,7},{4,6},{5,1},{6,4},{7,3},{8,10},{9,13},{10,... | collective-permute-start | bytes 393224 | tf_op jit(solution)/shard_map/ppermute | solution.py:100
  43.2 6.9 %collective-permute-start.20 = (bf16[4,8192]{1,0:T(4,128)(2,1)S(1)}, bf16[4,8192]{1,0:T(4,128)(2,1)S(1)}, u32[]{:S(2)}, u32[]{:S(2)}) collective-permute-start(bf16[4,8192]{1,0:T(4,128)(2,1)S(1)} %get-tuple-element.92), channel_id=1, source_target_pairs={{0,24},{1,25},{2,26},{3,27},{4,28},{5,29},{6,30},{7,31},{8,16},{9,... | collective-permute-start | bytes 196616 | tf_op jit(solution)/shard_map/ppermute | solution.py:100
  45.5 6.7 %collective-permute-start.21 = (bf16[4,8192]{1,0:T(4,128)(2,1)S(1)}, bf16[4,8192]{1,0:T(4,128)(2,1)S(1)}, u32[]{:S(2)}, u32[]{:S(2)}) collective-permute-start(bf16[4,8192]{1,0:T(4,128)(2,1)S(1)} %get-tuple-element.93), channel_id=1, source_target_pairs={{0,16},{1,17},{2,18},{3,19},{4,20},{5,21},{6,22},{7,23},{8,24},{9,... | collective-permute-start | bytes 196616 | tf_op jit(solution)/shard_map/ppermute | solution.py:100
  45.5 6.7 %collective-permute-start.22 = (bf16[4,8192]{1,0:T(4,128)(2,1)S(1)}, bf16[4,8192]{1,0:T(4,128)(2,1)S(1)}, u32[]{:S(2)}, u32[]{:S(2)}) collective-permute-start(bf16[4,8192]{1,0:T(4,128)(2,1)S(1)} %get-tuple-element.94), channel_id=1, source_target_pairs={{0,8},{1,9},{2,10},{3,11},{4,12},{5,13},{6,14},{7,15},{8,0},{9,1},... | collective-permute-start | bytes 196616 | tf_op jit(solution)/shard_map/ppermute | solution.py:100

commit v10 on v9

--- a/solution.py
+++ b/solution.py
@@ -100,7 +100,7 @@
     return lax.ppermute(value, AXES, [(i, i ^ masks[i % 2]) for i in range(devices)])
 
 
-def kernel_call(body, out_shape, cost, *operands, scratch=(), hbm=()):
+def kernel_call(body, out_shape, cost, *operands, scratch=(), hbm=(), blocks=False):
     vmem, smem = pl.BlockSpec(memory_space=pltpu.VMEM), pl.BlockSpec(memory_space=pltpu.SMEM)
     stay = pl.BlockSpec(memory_space=pltpu.HBM)
     specs = [stay if i in hbm else smem if o.ndim == 1 else vmem for i, o in enumerate(operands)]
@@ -108,6 +108,16 @@
         pltpu.with_memory_space_constraint(o, pltpu.HBM) if i in hbm else o
         for i, o in enumerate(operands)
     ]
+    more = {}
+    if blocks:
+        specs = [
+            smem if o.ndim == 1 else pl.BlockSpec(o.shape, lambda i: (0, 0)) for o in operands
+        ]
+        operands = [
+            o if o.ndim == 1 else pltpu.with_memory_space_constraint(o, pltpu.HBM)
+            for o in operands
+        ]
+        more = {"grid": (1,)}
     return pl.pallas_call(
         body,
         out_shape=out_shape,
@@ -116,6 +126,7 @@
         scratch_shapes=scratch,
         compiler_params=pltpu.CompilerParams(vmem_limit_bytes=16 << 20),
         cost_estimate=pl.CostEstimate(flops=cost, bytes_accessed=4 << 20, transcendentals=0),
+        **more,
     )(*operands)
 
 
@@ -132,22 +143,20 @@
     copy_all(list(zip(refs[:count], refs[count:-1])), refs[-1])
 
 
-def pack_body(x_ref, dy_ref, ids_ref, w_ref, expert_ref, msg_ref, mine_ref, *scratch):
-    x_buf, dy_buf, ids_buf, w_buf, sems = scratch
+def pack_body(x_ref, dy_ref, ids_ref, w_ref, expert_ref, msg_ref, mine_ref):
     rows, width = x_ref.shape
     top = ids_ref.shape[0]
     lanes = msg_ref.shape[1] - 2 * width
-    copy_all([(x_ref, x_buf), (dy_ref, dy_buf), (ids_ref, ids_buf), (w_ref, w_buf)], sems)
-    msg_ref[:, :width] = x_buf[...]
-    msg_ref[:, width : 2 * width] = dy_buf[...]
+    msg_ref[:, :width] = x_ref[...]
+    msg_ref[:, width : 2 * width] = dy_ref[...]
     diagonal = lax.broadcasted_iota(jnp.int32, (rows, rows), 0) == lax.broadcasted_iota(
         jnp.int32, (rows, rows), 1
     )
     expert = lax.broadcasted_iota(jnp.int32, (rows, lanes), 1)
-    top_weights = w_buf[...].astype(jnp.float32)
+    top_weights = w_ref[...].astype(jnp.float32)
     route = jnp.zeros((rows, lanes), jnp.float32)
     for k in range(top):
-        named = jnp.sum(jnp.where(diagonal, ids_buf[k : k + 1, :], 0), axis=1, keepdims=True)
+        named = jnp.sum(jnp.where(diagonal, ids_ref[k : k + 1, :], 0), axis=1, keepdims=True)
         weight = jnp.sum(jnp.where(diagonal, top_weights[k : k + 1, :], 0.0), axis=1, keepdims=True)
         route = route + jnp.where(expert == named, weight, 0.0)
     msg_ref[:, 2 * width :] = route.astype(jnp.bfloat16)
@@ -291,14 +300,7 @@
         expert_ids.T,
         route_weights.T,
         expert,
-        scratch=[
-            pltpu.VMEM((rows, width), bf16),
-            pltpu.VMEM((rows, width), bf16),
-            pltpu.VMEM(expert_ids.shape[::-1], jnp.int32),
-            pltpu.VMEM(route_weights.shape[::-1], bf16),
-            pltpu.SemaphoreType.DMA((4,)),
-        ],
-        hbm=(0, 1, 2, 3),
+        blocks=True,
     )
     weights = kernel_call(
         load_body,

time: 53.1 us -> 53 us (level)
  no operation moved by 1% of the time
where the time goes in v10:
time: 53 us; the launch traced here: 52.8 us
  starting transfers between devices  22.9 us (43%)
  waiting for transfers between devices  17.1 us (32%)
  Pallas kernels  11.7 us (22%)
  between operations  0.85 us (2%)
    ppermute x23, starting transfers between devices, from_xor(): lax.ppermute(value, AXES, [(i, i ^ masks[i % 2]) for i in range(devices)])  22.9 us
    ppermute x23, waiting for transfers between devices, from_xor(): lax.ppermute(value, AXES, [(i, i ^ masks[i % 2]) for i in range(devices)])  17.1 us
    pallas_call x16, Pallas kernels, kernel_call(): pl.pallas_call(body, out_shape=out_shape, in_specs=specs, out_specs=jax.t...  11.7 us
  transfers between devices with their start and end apart: 23, of which 14 were waited for; matrix products, arithmetic and copies ran while one was open for 0% of the time, Pallas kernels for 15%

profile of v10, /device:TPU:0, one launch (start us, length us, event | category | flops | bytes accessed | tf_op | source)
XLA Modules:
  0.0 52.8 jit_solution(7582588485932800778)
XLA Ops:
  0.6 0.9 %shard_map.110 = (bf16[4,8320]{1,0:T(4,128)(2,1)S(1)}, f32[8,128]{1,0:T(8,128)S(1)}) custom-call(bf16[4,4096]{1,0:T(4,128)(2,1)} %x_ref.1, bf16[4,4096]{1,0:T(4,128)(2,1)} %dy_ref.1, s32[2,4]{1,0:T(2,128)} %bitcast.3, bf16[2,4]{1,0:T(2,128)(2,1)} %bitcast.4, s32[1]{0:T(128)} %bitcast.2.expert_ref), custom_call_target="tpu_custom_call" | custom-call | bytes 4194304 | tf_op jit(solution)/shard_map/pallas_call | solution.py:121
  1.5 5.1 %collective-permute-start.2 = (bf16[4,8320]{1,0:T(4,128)(2,1)S(1)}, bf16[4,8320]{1,0:T(4,128)(2,1)S(1)}, u32[]{:S(2)}, u32[]{:S(2)}) collective-permute-start(bf16[4,8320]{1,0:T(4,128)(2,1)S(1)} %get-tuple-element.53), channel_id=1, source_target_pairs={{0,24},{1,25},{2,26},{3,27},{4,28},{5,29},{6,30},{7,31},{8,16},{9,... | collective-permute-start | bytes 199688 | tf_op jit(solution)/shard_map/ppermute | solution.py:100
  7.3 2.4 %shard_map.111 = (bf16[1,192,4096]{2,1,0:T(8,128)(2,1)S(1)}, bf16[1,192,4096]{2,1,0:T(8,128)(2,1)S(1)}, bf16[1,192,4096]{2,1,0:T(8,128)(2,1)S(1)}) custom-call(bf16[1,192,4096]{2,1,0:T(8,128)(2,1)} %refs_0_.1, bf16[1,192,4096]{2,1,0:T(8,128)(2,1)} %refs_1_.1, bf16[1,192,4096]{2,1,0:T(8,128)(2,1)} %refs_2_.1), custom_call_target="tpu_custom_call" | custom-call | bytes 4194304 | tf_op jit(solution)/shard_map/pallas_call | solution.py:121
  9.7 2.6 %collective-permute-done.1 = bf16[4,8320]{1,0:T(4,128)(2,1)S(1)} collective-permute-done((bf16[4,8320]{1,0:T(4,128)(2,1)S(1)}, bf16[4,8320]{1,0:T(4,128)(2,1)S(1)}, u32[]{:S(2)}, u32[]{:S(2)}) %collective-permute-start.1) | collective-permute-done | bytes 66592 | tf_op jit(solution)/shard_map/ppermute | solution.py:100
  12.6 1.6 %collective-permute-start.10 = (bf16[16,4096]{1,0:T(8,128)(2,1)S(1)}, bf16[16,4096]{1,0:T(8,128)(2,1)S(1)}, u32[]{:S(2)}, u32[]{:S(2)}) collective-permute-start(bf16[16,4096]{1,0:T(8,128)(2,1)S(1)} %pad_maximum_fusion.1.refs_0_), channel_id=1, source_target_pairs={{0,4},{1,3},{2,6},{3,1},{4,0},{5,7},{6,2},{7,5},{8,12},{9,11},{10,... | collective-permute-start | bytes 393224 | tf_op jit(solution)/shard_map/ppermute | solution.py:100
  14.1 1.5 %collective-permute-start.4 = (bf16[16,4224]{1,0:T(8,128)(2,1)S(1)}, bf16[16,4224]{1,0:T(8,128)(2,1)S(1)}, u32[]{:S(2)}, u32[]{:S(2)}) collective-permute-start(bf16[16,4224]{1,0:T(8,128)(2,1)S(1)} %pad_maximum_fusion.refs_0_), channel_id=1, source_target_pairs={{0,2},{1,5},{2,0},{3,7},{4,6},{5,1},{6,4},{7,3},{8,10},{9,13},{10,... | collective-permute-start | bytes 405512 | tf_op jit(solution)/shard_map/ppermute | solution.py:100
  16.7 2.2 %collective-permute-done.10.refs_0_ = bf16[16,4096]{1,0:T(8,128)(2,1)S(1)} collective-permute-done((bf16[16,4096]{1,0:T(8,128)(2,1)S(1)}, bf16[16,4096]{1,0:T(8,128)(2,1)S(1)}, u32[]{:S(2)}, u32[]{:S(2)}) %collective-permute-start.10) | collective-permute-done | bytes 131104 | tf_op jit(solution)/shard_map/ppermute | solution.py:100
  18.9 0.9 %collective-permute-start.11 = (bf16[16,4096]{1,0:T(8,128)(2,1)S(1)}, bf16[16,4096]{1,0:T(8,128)(2,1)S(1)}, u32[]{:S(2)}, u32[]{:S(2)}) collective-permute-start(bf16[16,4096]{1,0:T(8,128)(2,1)S(1)} %collective-permute-done.10.refs_0_), channel_id=1, source_target_pairs={{0,2},{1,5},{2,0},{3,7},{4,6},{5,1},{6,4},{7,3},{8,10},{9,13},{10,... | collective-permute-start | bytes 393224 | tf_op jit(solution)/shard_map/ppermute | solution.py:100
  20.4 1.5 %collective-permute-start.5 = (bf16[16,4224]{1,0:T(8,128)(2,1)S(1)}, bf16[16,4224]{1,0:T(8,128)(2,1)S(1)}, u32[]{:S(2)}, u32[]{:S(2)}) collective-permute-start(bf16[16,4224]{1,0:T(8,128)(2,1)S(1)} %collective-permute-done.4.refs_0_), channel_id=1, source_target_pairs={{0,4},{1,3},{2,6},{3,1},{4,0},{5,7},{6,2},{7,5},{8,12},{9,11},{10,... | collective-permute-start | bytes 405512 | tf_op jit(solution)/shard_map/ppermute | solution.py:100
  22.8 1.9 %collective-permute-done.11.refs_1_ = bf16[16,4096]{1,0:T(8,128)(2,1)S(1)} collective-permute-done((bf16[16,4096]{1,0:T(8,128)(2,1)S(1)}, bf16[16,4096]{1,0:T(8,128)(2,1)S(1)}, u32[]{:S(2)}, u32[]{:S(2)}) %collective-permute-start.11) | collective-permute-done | bytes 131104 | tf_op jit(solution)/shard_map/ppermute | solution.py:100
  25.6 0.7 %collective-permute-done.12.refs_3_ = bf16[32,4096]{1,0:T(8,128)(2,1)S(1)} collective-permute-done((bf16[32,4096]{1,0:T(8,128)(2,1)S(1)}, bf16[32,4096]{1,0:T(8,128)(2,1)S(1)}, u32[]{:S(2)}, u32[]{:S(2)}) %collective-permute-start.12) | collective-permute-done | bytes 262176 | tf_op jit(solution)/shard_map/ppermute | solution.py:100
  26.3 1.2 %shard_map.116 = (bf16[128,4096]{1,0:T(8,128)(2,1)S(1)}, f32[128,192]{1,0:T(8,128)S(1)}, f32[128,192]{1,0:T(8,128)S(1)}, f32[128,192]{1,0:T(8,128)S(1)}) custom-call(bf16[32,4096]{1,0:T(8,128)(2,1)S(1)} %shard_map.114.refs_0_, bf16[32,4096]{1,0:T(8,128)(2,1)S(1)} %shard_map.115.refs_1_, bf16[32,4096]{1,0:T(8,128)(2,1)S(1)} %collective-permute-done.7.refs_2_, ...), custom_call_target="tpu_custom_call" | custom-call | flops 402653184 | bytes 4194304 | tf_op jit(solution)/shard_map/pallas_call | solution.py:121
  27.5 1.9 %shard_map.117 = (bf16[128,4096]{1,0:T(8,128)(2,1)S(1)}, bf16[128,192]{1,0:T(8,128)(2,1)S(1)}, bf16[128,192]{1,0:T(8,128)(2,1)S(1)}, bf16[128,192]{1,0:T(8,128)(...) custom-call(bf16[32,4224]{1,0:T(8,128)(2,1)S(1)} %shard_map.112.refs_0_, ...), custom_call_target="tpu_custom_call" | custom-call | flops 603979776 | bytes 4194304 | tf_op jit(solution)/shard_map/pallas_call | solution.py:121
  29.7 1.4 %collective-permute-done.13.came_ref = bf16[16,8192]{1,0:T(8,128)(2,1)S(1)} collective-permute-done((bf16[16,8192]{1,0:T(8,128)(2,1)S(1)}, bf16[16,8192]{1,0:T(8,128)(2,1)S(1)}, u32[]{:S(2)}, u32[]{:S(2)}) %collective-permute-start.13) | collective-permute-done | bytes 262176 | tf_op jit(solution)/shard_map/ppermute | solution.py:100
  31.3 1.7 %collective-permute-start.16 = (bf16[16,4096]{1,0:T(8,128)(2,1)S(1)}, bf16[16,4096]{1,0:T(8,128)(2,1)S(1)}, u32[]{:S(2)}, u32[]{:S(2)}) collective-permute-start(bf16[16,4096]{1,0:T(8,128)(2,1)S(1)} %get-tuple-element.86), channel_id=1, source_target_pairs={{0,4},{1,3},{2,6},{3,1},{4,0},{5,7},{6,2},{7,5},{8,12},{9,11},{10,... | collective-permute-start | bytes 393224 | tf_op jit(solution)/shard_map/ppermute | solution.py:100
  33.6 1.7 %collective-permute-start.15 = (bf16[16,8192]{1,0:T(8,128)(2,1)S(1)}, bf16[16,8192]{1,0:T(8,128)(2,1)S(1)}, u32[]{:S(2)}, u32[]{:S(2)}) collective-permute-start(bf16[16,8192]{1,0:T(8,128)(2,1)S(1)} %get-tuple-element.83), channel_id=1, source_target_pairs={{0,4},{1,3},{2,6},{3,1},{4,0},{5,7},{6,2},{7,5},{8,12},{9,11},{10,... | collective-permute-start | bytes 786440 | tf_op jit(solution)/shard_map/ppermute | solution.py:100
  35.2 1.1 %collective-permute-done.16.came_ref = bf16[16,4096]{1,0:T(8,128)(2,1)S(1)} collective-permute-done((bf16[16,4096]{1,0:T(8,128)(2,1)S(1)}, bf16[16,4096]{1,0:T(8,128)(2,1)S(1)}, u32[]{:S(2)}, u32[]{:S(2)}) %collective-permute-start.16) | collective-permute-done | bytes 131104 | tf_op jit(solution)/shard_map/ppermute | solution.py:100
  36.9 1.0 %collective-permute-done.18.came_ref = bf16[16,4096]{1,0:T(8,128)(2,1)S(1)} collective-permute-done((bf16[16,4096]{1,0:T(8,128)(2,1)S(1)}, bf16[16,4096]{1,0:T(8,128)(2,1)S(1)}, u32[]{:S(2)}, u32[]{:S(2)}) %collective-permute-start.18) | collective-permute-done | bytes 131104 | tf_op jit(solution)/shard_map/ppermute | solution.py:100
  38.7 2.5 %shard_map.119 = (bf16[1,192,4096]{2,1,0:T(8,128)(2,1)}, bf16[1,192,4096]{2,1,0:T(8,128)(2,1)}) custom-call(bf16[128,4096]{1,0:T(8,128)(2,1)S(1)} %get-tuple-element.77.rows_ref, bf16[128,192]{1,0:T(8,128)(2,1)S(1)} %get-tuple-element.78.refs_0_, bf16[128,192]{1,0:T(8,128)(2,1)S(1)} %get-tuple-element.79.refs_1_), custom_call_target="tpu_custom_call" | custom-call | flops 402653184 | bytes 4194304 | tf_op jit(solution)/shard_map/pallas_call | solution.py:121
  41.4 1.6 %collective-permute-done.19.refs_1_ = bf16[16,4096]{1,0:T(8,128)(2,1)S(1)} collective-permute-done((bf16[16,4096]{1,0:T(8,128)(2,1)S(1)}, bf16[16,4096]{1,0:T(8,128)(2,1)S(1)}, u32[]{:S(2)}, u32[]{:S(2)}) %collective-permute-start.19) | collective-permute-done | bytes 131104 | tf_op jit(solution)/shard_map/ppermute | solution.py:100
  43.1 2.3 %collective-permute-start.20 = (bf16[4,8192]{1,0:T(4,128)(2,1)S(1)}, bf16[4,8192]{1,0:T(4,128)(2,1)S(1)}, u32[]{:S(2)}, u32[]{:S(2)}) collective-permute-start(bf16[4,8192]{1,0:T(4,128)(2,1)S(1)} %get-tuple-element.92), channel_id=1, source_target_pairs={{0,24},{1,25},{2,26},{3,27},{4,28},{5,29},{6,30},{7,31},{8,16},{9,... | collective-permute-start | bytes 196616 | tf_op jit(solution)/shard_map/ppermute | solution.py:100
  45.4 2.1 %collective-permute-start.22 = (bf16[4,8192]{1,0:T(4,128)(2,1)S(1)}, bf16[4,8192]{1,0:T(4,128)(2,1)S(1)}, u32[]{:S(2)}, u32[]{:S(2)}) collective-permute-start(bf16[4,8192]{1,0:T(4,128)(2,1)S(1)} %get-tuple-element.94), channel_id=1, source_target_pairs={{0,8},{1,9},{2,10},{3,11},{4,12},{5,13},{6,14},{7,15},{8,0},{9,1},... | collective-permute-start | bytes 196616 | tf_op jit(solution)/shard_map/ppermute | solution.py:100
  47.6 1.7 %shard_map.125 = bf16[1,192,4096]{2,1,0:T(8,128)(2,1)} custom-call(bf16[128,4096]{1,0:T(8,128)(2,1)S(1)} %get-tuple-element.99.rows_ref, bf16[128,192]{1,0:T(8,128)(2,1)S(1)} %get-tuple-element.100.refs_0_), custom_call_target="tpu_custom_call" | custom-call | flops 201326592 | bytes 4194304 | tf_op jit(solution)/shard_map/pallas_call | solution.py:121
  50.0 2.2 %collective-permute-done.21.refs_1_ = bf16[4,8192]{1,0:T(4,128)(2,1)S(1)} collective-permute-done((bf16[4,8192]{1,0:T(4,128)(2,1)S(1)}, bf16[4,8192]{1,0:T(4,128)(2,1)S(1)}, u32[]{:S(2)}, u32[]{:S(2)}) %collective-permute-start.21) | collective-permute-done | bytes 65568 | tf_op jit(solution)/shard_map/ppermute | solution.py:100
  (48 shorter events, 8.4 us)
Async XLA Ops:
  1.5 8.2 %collective-permute-start.2 = (bf16[4,8320]{1,0:T(4,128)(2,1)S(1)}, bf16[4,8320]{1,0:T(4,128)(2,1)S(1)}, u32[]{:S(2)}, u32[]{:S(2)}) collective-permute-start(bf16[4,8320]{1,0:T(4,128)(2,1)S(1)} %get-tuple-element.53), channel_id=1, source_target_pairs={{0,24},{1,25},{2,26},{3,27},{4,28},{5,29},{6,30},{7,31},{8,16},{9,... | collective-permute-start | bytes 199688 | tf_op jit(solution)/shard_map/ppermute | solution.py:100
  6.6 5.7 %collective-permute-start.1 = (bf16[4,8320]{1,0:T(4,128)(2,1)S(1)}, bf16[4,8320]{1,0:T(4,128)(2,1)S(1)}, u32[]{:S(2)}, u32[]{:S(2)}) collective-permute-start(bf16[4,8320]{1,0:T(4,128)(2,1)S(1)} %get-tuple-element.53), channel_id=1, source_target_pairs={{0,16},{1,17},{2,18},{3,19},{4,20},{5,21},{6,22},{7,23},{8,24},{9,... | collective-permute-start | bytes 199688 | tf_op jit(solution)/shard_map/ppermute | solution.py:100
  6.6 5.7 %collective-permute-start = (bf16[4,8320]{1,0:T(4,128)(2,1)S(1)}, bf16[4,8320]{1,0:T(4,128)(2,1)S(1)}, u32[]{:S(2)}, u32[]{:S(2)}) collective-permute-start(bf16[4,8320]{1,0:T(4,128)(2,1)S(1)} %get-tuple-element.53), channel_id=1, source_target_pairs={{0,8},{1,9},{2,10},{3,11},{4,12},{5,13},{6,14},{7,15},{8,0},{9,1},... | collective-permute-start | bytes 199688 | tf_op jit(solution)/shard_map/ppermute | solution.py:100
  12.6 6.3 %collective-permute-start.10 = (bf16[16,4096]{1,0:T(8,128)(2,1)S(1)}, bf16[16,4096]{1,0:T(8,128)(2,1)S(1)}, u32[]{:S(2)}, u32[]{:S(2)}) collective-permute-start(bf16[16,4096]{1,0:T(8,128)(2,1)S(1)} %pad_maximum_fusion.1.refs_0_), channel_id=1, source_target_pairs={{0,4},{1,3},{2,6},{3,1},{4,0},{5,7},{6,2},{7,5},{8,12},{9,11},{10,... | collective-permute-start | bytes 393224 | tf_op jit(solution)/shard_map/ppermute | solution.py:100
  14.1 6.3 %collective-permute-start.4 = (bf16[16,4224]{1,0:T(8,128)(2,1)S(1)}, bf16[16,4224]{1,0:T(8,128)(2,1)S(1)}, u32[]{:S(2)}, u32[]{:S(2)}) collective-permute-start(bf16[16,4224]{1,0:T(8,128)(2,1)S(1)} %pad_maximum_fusion.refs_0_), channel_id=1, source_target_pairs={{0,2},{1,5},{2,0},{3,7},{4,6},{5,1},{6,4},{7,3},{8,10},{9,13},{10,... | collective-permute-start | bytes 405512 | tf_op jit(solution)/shard_map/ppermute | solution.py:100
  15.6 6.5 %collective-permute-start.3 = (bf16[16,4224]{1,0:T(8,128)(2,1)S(1)}, bf16[16,4224]{1,0:T(8,128)(2,1)S(1)}, u32[]{:S(2)}, u32[]{:S(2)}) collective-permute-start(bf16[16,4224]{1,0:T(8,128)(2,1)S(1)} %pad_maximum_fusion.refs_0_), channel_id=1, source_target_pairs={{0,4},{1,3},{2,6},{3,1},{4,0},{5,7},{6,2},{7,5},{8,12},{9,11},{10,... | collective-permute-start | bytes 405512 | tf_op jit(solution)/shard_map/ppermute | solution.py:100
  16.2 6.1 %collective-permute-start.6 = (bf16[16,4096]{1,0:T(8,128)(2,1)S(1)}, bf16[16,4096]{1,0:T(8,128)(2,1)S(1)}, u32[]{:S(2)}, u32[]{:S(2)}) collective-permute-start(bf16[16,4096]{1,0:T(8,128)(2,1)S(1)} %pad_maximum_fusion.1.refs_0_), channel_id=1, source_target_pairs={{0,2},{1,5},{2,0},{3,7},{4,6},{5,1},{6,4},{7,3},{8,10},{9,13},{10,... | collective-permute-start | bytes 393224 | tf_op jit(solution)/shard_map/ppermute | solution.py:100
  18.9 5.8 %collective-permute-start.11 = (bf16[16,4096]{1,0:T(8,128)(2,1)S(1)}, bf16[16,4096]{1,0:T(8,128)(2,1)S(1)}, u32[]{:S(2)}, u32[]{:S(2)}) collective-permute-start(bf16[16,4096]{1,0:T(8,128)(2,1)S(1)} %collective-permute-done.10.refs_0_), channel_id=1, source_target_pairs={{0,2},{1,5},{2,0},{3,7},{4,6},{5,1},{6,4},{7,3},{8,10},{9,13},{10,... | collective-permute-start | bytes 393224 | tf_op jit(solution)/shard_map/ppermute | solution.py:100
  20.4 5.0 %collective-permute-start.5 = (bf16[16,4224]{1,0:T(8,128)(2,1)S(1)}, bf16[16,4224]{1,0:T(8,128)(2,1)S(1)}, u32[]{:S(2)}, u32[]{:S(2)}) collective-permute-start(bf16[16,4224]{1,0:T(8,128)(2,1)S(1)} %collective-permute-done.4.refs_0_), channel_id=1, source_target_pairs={{0,4},{1,3},{2,6},{3,1},{4,0},{5,7},{6,2},{7,5},{8,12},{9,11},{10,... | collective-permute-start | bytes 405512 | tf_op jit(solution)/shard_map/ppermute | solution.py:100
  22.2 3.4 %collective-permute-start.8 = (bf16[32,4224]{1,0:T(8,128)(2,1)S(1)}, bf16[32,4224]{1,0:T(8,128)(2,1)S(1)}, u32[]{:S(2)}, u32[]{:S(2)}) collective-permute-start(bf16[32,4224]{1,0:T(8,128)(2,1)S(1)} %shard_map.112.refs_0_), channel_id=1, source_target_pairs={{0,1},{1,0},{2,3},{3,2},{4,5},{5,4},{6,7},{7,6},{8,9},{9,8},{10,11... | collective-permute-start | bytes 811016 | tf_op jit(solution)/shard_map/ppermute | solution.py:100
  22.3 3.3 %collective-permute-start.7 = (bf16[32,4096]{1,0:T(8,128)(2,1)S(1)}, bf16[32,4096]{1,0:T(8,128)(2,1)S(1)}, u32[]{:S(2)}, u32[]{:S(2)}) collective-permute-start(bf16[32,4096]{1,0:T(8,128)(2,1)S(1)} %shard_map.114.refs_0_), channel_id=1, source_target_pairs={{0,1},{1,0},{2,3},{3,2},{4,5},{5,4},{6,7},{7,6},{8,9},{9,8},{10,11... | collective-permute-start | bytes 786440 | tf_op jit(solution)/shard_map/ppermute | solution.py:100
  24.7 1.6 %collective-permute-start.12 = (bf16[32,4096]{1,0:T(8,128)(2,1)S(1)}, bf16[32,4096]{1,0:T(8,128)(2,1)S(1)}, u32[]{:S(2)}, u32[]{:S(2)}) collective-permute-start(bf16[32,4096]{1,0:T(8,128)(2,1)S(1)} %shard_map.115.refs_1_), channel_id=1, source_target_pairs={{0,1},{1,0},{2,3},{3,2},{4,5},{5,4},{6,7},{7,6},{8,9},{9,8},{10,11... | collective-permute-start | bytes 786440 | tf_op jit(solution)/shard_map/ppermute | solution.py:100
  25.5 2.0 %collective-permute-start.9 = (bf16[32,4224]{1,0:T(8,128)(2,1)S(1)}, bf16[32,4224]{1,0:T(8,128)(2,1)S(1)}, u32[]{:S(2)}, u32[]{:S(2)}) collective-permute-start(bf16[32,4224]{1,0:T(8,128)(2,1)S(1)} %shard_map.113.refs_1_), channel_id=1, source_target_pairs={{0,1},{1,0},{2,3},{3,2},{4,5},{5,4},{6,7},{7,6},{8,9},{9,8},{10,11... | collective-permute-start | bytes 811016 | tf_op jit(solution)/shard_map/ppermute | solution.py:100
  29.5 1.6 %collective-permute-start.13 = (bf16[16,8192]{1,0:T(8,128)(2,1)S(1)}, bf16[16,8192]{1,0:T(8,128)(2,1)S(1)}, u32[]{:S(2)}, u32[]{:S(2)}) collective-permute-start(bf16[16,8192]{1,0:T(8,128)(2,1)S(1)} %get-tuple-element.69), channel_id=1, source_target_pairs={{0,1},{1,0},{2,3},{3,2},{4,5},{5,4},{6,7},{7,6},{8,9},{9,8},{10,11... | collective-permute-start | bytes 786440 | tf_op jit(solution)/shard_map/ppermute | solution.py:100
  31.1 2.3 %collective-permute-start.14 = (bf16[48,8192]{1,0:T(8,128)(2,1)S(1)}, bf16[48,8192]{1,0:T(8,128)(2,1)S(1)}, u32[]{:S(2)}, u32[]{:S(2)}) collective-permute-start(bf16[48,8192]{1,0:T(8,128)(2,1)S(1)} %get-tuple-element.71), channel_id=1, source_target_pairs={{0,1},{1,0},{2,3},{3,2},{4,5},{5,4},{6,7},{7,6},{8,9},{9,8},{10,11... | collective-permute-start | bytes 2359304 | tf_op jit(solution)/shard_map/ppermute | solution.py:100
  31.3 5.0 %collective-permute-start.16 = (bf16[16,4096]{1,0:T(8,128)(2,1)S(1)}, bf16[16,4096]{1,0:T(8,128)(2,1)S(1)}, u32[]{:S(2)}, u32[]{:S(2)}) collective-permute-start(bf16[16,4096]{1,0:T(8,128)(2,1)S(1)} %get-tuple-element.86), channel_id=1, source_target_pairs={{0,4},{1,3},{2,6},{3,1},{4,0},{5,7},{6,2},{7,5},{8,12},{9,11},{10,... | collective-permute-start | bytes 393224 | tf_op jit(solution)/shard_map/ppermute | solution.py:100
  33.0 5.0 %collective-permute-start.18 = (bf16[16,4096]{1,0:T(8,128)(2,1)S(1)}, bf16[16,4096]{1,0:T(8,128)(2,1)S(1)}, u32[]{:S(2)}, u32[]{:S(2)}) collective-permute-start(bf16[16,4096]{1,0:T(8,128)(2,1)S(1)} %get-tuple-element.88), channel_id=1, source_target_pairs={{0,4},{1,3},{2,6},{3,1},{4,0},{5,7},{6,2},{7,5},{8,12},{9,11},{10,... | collective-permute-start | bytes 393224 | tf_op jit(solution)/shard_map/ppermute | solution.py:100
  33.6 9.5 %collective-permute-start.15 = (bf16[16,8192]{1,0:T(8,128)(2,1)S(1)}, bf16[16,8192]{1,0:T(8,128)(2,1)S(1)}, u32[]{:S(2)}, u32[]{:S(2)}) collective-permute-start(bf16[16,8192]{1,0:T(8,128)(2,1)S(1)} %get-tuple-element.83), channel_id=1, source_target_pairs={{0,4},{1,3},{2,6},{3,1},{4,0},{5,7},{6,2},{7,5},{8,12},{9,11},{10,... | collective-permute-start | bytes 786440 | tf_op jit(solution)/shard_map/ppermute | solution.py:100
  36.4 5.0 %collective-permute-start.17 = (bf16[16,4096]{1,0:T(8,128)(2,1)S(1)}, bf16[16,4096]{1,0:T(8,128)(2,1)S(1)}, u32[]{:S(2)}, u32[]{:S(2)}) collective-permute-start(bf16[16,4096]{1,0:T(8,128)(2,1)S(1)} %shard_map.121), channel_id=1, source_target_pairs={{0,2},{1,5},{2,0},{3,7},{4,6},{5,1},{6,4},{7,3},{8,10},{9,13},{10,... | collective-permute-start | bytes 393224 | tf_op jit(solution)/shard_map/ppermute | solution.py:100
  38.0 5.0 %collective-permute-start.19 = (bf16[16,4096]{1,0:T(8,128)(2,1)S(1)}, bf16[16,4096]{1,0:T(8,128)(2,1)S(1)}, u32[]{:S(2)}, u32[]{:S(2)}) collective-permute-start(bf16[16,4096]{1,0:T(8,128)(2,1)S(1)} %shard_map.122), channel_id=1, source_target_pairs={{0,2},{1,5},{2,0},{3,7},{4,6},{5,1},{6,4},{7,3},{8,10},{9,13},{10,... | collective-permute-start | bytes 393224 | tf_op jit(solution)/shard_map/ppermute | solution.py:100
  43.1 6.9 %collective-permute-start.20 = (bf16[4,8192]{1,0:T(4,128)(2,1)S(1)}, bf16[4,8192]{1,0:T(4,128)(2,1)S(1)}, u32[]{:S(2)}, u32[]{:S(2)}) collective-permute-start(bf16[4,8192]{1,0:T(4,128)(2,1)S(1)} %get-tuple-element.92), channel_id=1, source_target_pairs={{0,24},{1,25},{2,26},{3,27},{4,28},{5,29},{6,30},{7,31},{8,16},{9,... | collective-permute-start | bytes 196616 | tf_op jit(solution)/shard_map/ppermute | solution.py:100
  45.4 6.7 %collective-permute-start.21 = (bf16[4,8192]{1,0:T(4,128)(2,1)S(1)}, bf16[4,8192]{1,0:T(4,128)(2,1)S(1)}, u32[]{:S(2)}, u32[]{:S(2)}) collective-permute-start(bf16[4,8192]{1,0:T(4,128)(2,1)S(1)} %get-tuple-element.93), channel_id=1, source_target_pairs={{0,16},{1,17},{2,18},{3,19},{4,20},{5,21},{6,22},{7,23},{8,24},{9,... | collective-permute-start | bytes 196616 | tf_op jit(solution)/shard_map/ppermute | solution.py:100
  45.4 6.7 %collective-permute-start.22 = (bf16[4,8192]{1,0:T(4,128)(2,1)S(1)}, bf16[4,8192]{1,0:T(4,128)(2,1)S(1)}, u32[]{:S(2)}, u32[]{:S(2)}) collective-permute-start(bf16[4,8192]{1,0:T(4,128)(2,1)S(1)} %get-tuple-element.94), channel_id=1, source_target_pairs={{0,8},{1,9},{2,10},{3,11},{4,12},{5,13},{6,14},{7,15},{8,0},{9,1},... | collective-permute-start | bytes 196616 | tf_op jit(solution)/shard_map/ppermute | solution.py:100

commit v11 on v10

--- a/solution.py
+++ b/solution.py
@@ -138,9 +138,16 @@
         copy.wait()
 
 
-def load_body(*refs):
-    count = len(refs) // 2
-    copy_all(list(zip(refs[:count], refs[count:-1])), refs[-1])
+def load_body(gate_ref, up_ref, down_ref, pair_ref, down_out_ref, sems):
+    ff = gate_ref.shape[1]
+    copy_all(
+        [
+            (gate_ref.at[0], pair_ref.at[pl.ds(0, ff)]),
+            (up_ref.at[0], pair_ref.at[pl.ds(ff, ff)]),
+            (down_ref.at[0], down_out_ref),
+        ],
+        sems,
+    )
 
 
 def pack_body(x_ref, dy_ref, ids_ref, w_ref, expert_ref, msg_ref, mine_ref):
@@ -185,12 +192,13 @@
 
 
 def forward_body(count, *refs):
-    pieces, (wg_ref, wu_ref, x_ref, hidden_ref, gate_ref, up_ref) = refs[:count], refs[count:]
+    pieces, (pair_ref, x_ref, hidden_ref, gate_ref, up_ref) = refs[:count], refs[count:]
     for here, piece, there in block_places(pieces, (0, 1, 2, 3)):
         x_ref[here, :] = piece[there, :]
     x = x_ref[...]
-    gate_pre = contract_rows(x, wg_ref[0])
-    up_pre = contract_rows(x, wu_ref[0])
+    ff = gate_ref.shape[1]
+    gate_pre = contract_rows(x, pair_ref[:ff, :])
+    up_pre = contract_rows(x, pair_ref[ff:, :])
     gate_sig = 1.0 / (1.0 + jnp.exp(-gate_pre))
     silu_gate = gate_pre * gate_sig
     hidden_ref[...] = silu_gate * up_pre
@@ -217,8 +225,9 @@
 
 def backward_body(count, *refs):
     pieces, rest = refs[:count], refs[count:]
-    hidden_ref, gate_ref, up_ref, mine_ref, wg_ref, wu_ref, wd_ref = rest[:7]
-    dy_ref, scaled_ref, gate_act_ref, up_act_ref, own_ref, most_ref, corner_ref, weight_ref = rest[7:]
+    hidden_ref, gate_ref, up_ref, mine_ref, pair_ref, wd_ref = rest[:6]
+    dy_ref, scaled_ref, acts_ref, own_ref, most_ref, corner_ref, weight_ref = rest[6:]
+    ff = wd_ref.shape[0]
     width = dy_ref.shape[1]
     for here, piece, there in block_places(pieces, (0, 2, 1, 3)):
         dy_ref[here, :] = piece[there, :width]
@@ -227,13 +236,11 @@
         weight_ref[here, :] = jnp.broadcast_to(weight, (route.shape[0], weight_ref.shape[1]))
     weight = weight_ref[:, :1]
     scaled_ref[...] = (weight * hidden_ref[...]).astype(jnp.bfloat16)
-    hidden_grad = weight * contract_rows(dy_ref[...], wd_ref[0])
-    gate_act_ref[...] = (hidden_grad * gate_ref[...]).astype(jnp.bfloat16)
-    up_act_ref[...] = (hidden_grad * up_ref[...]).astype(jnp.bfloat16)
-    out = jnp.dot(scaled_ref[...], wd_ref[0], preferred_element_type=jnp.float32)
-    into = jnp.dot(gate_act_ref[...], wg_ref[0], preferred_element_type=jnp.float32) + jnp.dot(
-        up_act_ref[...], wu_ref[0], preferred_element_type=jnp.float32
-    )
+    hidden_grad = weight * contract_rows(dy_ref[...], wd_ref[...])
+    acts_ref[:, :ff] = (hidden_grad * gate_ref[...]).astype(jnp.bfloat16)
+    acts_ref[:, ff:] = (hidden_grad * up_ref[...]).astype(jnp.bfloat16)
+    out = jnp.dot(scaled_ref[...], wd_ref[...], preferred_element_type=jnp.float32)
+    into = jnp.dot(acts_ref[...], pair_ref[...], preferred_element_type=jnp.float32)
     half, most = own_ref.shape[0], most_ref.shape[0]
     for side, total in enumerate((out, into)):
         at = slice(side * width, (side + 1) * width)
@@ -267,10 +274,11 @@
     into_ref[...] = total[:, width:].astype(jnp.bfloat16)
 
 
-def grad_body(rows_ref, *refs):
-    acts, grads = refs[: len(refs) // 2], refs[len(refs) // 2 :]
-    for act_ref, ref in zip(acts, grads):
-        ref[0] = contract_first(act_ref[...], rows_ref[...]).astype(jnp.bfloat16)
+def grad_body(rows_ref, acts_ref, *grads):
+    ff = grads[0].shape[1]
+    for i, ref in enumerate(grads):
+        acts = acts_ref[:, i * ff : (i + 1) * ff]
+        ref[0] = contract_first(acts, rows_ref[...]).astype(jnp.bfloat16)
 
 
 def dense(tokens, expert_ids, route_weights, out_grad, gate_weight, up_weight, down_weight):
@@ -304,7 +312,7 @@
     )
     weights = kernel_call(
         load_body,
-        (shape(*gate_weight.shape),) * 3,
+        (shape(2 * ff, width), shape(ff, width)),
         0,
         gate_weight,
         up_weight,
@@ -315,8 +323,7 @@
     arrived = [message] + [passed(message, m) for m in near]
     block_x = jnp.concatenate([piece[:, :width] for piece in arrived], axis=0)
     block_dy = jnp.concatenate([piece[:, width:] for piece in arrived], axis=0)
-    block_x, block_dy, *weights = lax.optimization_barrier((block_x, block_dy, *weights))
-    w_gate, w_up, w_down = weights
+    block_dy, *weights = lax.optimization_barrier((block_dy, *weights))
 
     aside_x, across_dy = passed(block_x, ASIDE), passed(block_dy, ACROSS)
     aside_dy, across_x = passed(block_dy, ASIDE), passed(block_x, ACROSS)
@@ -338,14 +345,14 @@
         (shape(2 * half, width),) + (shape(2 * half, ff, dtype=f32),) * 3,
         16 * unit,
         *x_pieces,
-        w_gate,
-        w_up,
-    )
-    all_dy, scaled, gate_act, up_act, own, message, corner_message = kernel_call(
+        weights[0],
+    )
+    all_dy, scaled, acts, own, message, corner_message = kernel_call(
         functools.partial(backward_body, len(dy_pieces)),
         (
             shape(2 * half, width),
-            *(shape(2 * half, ff),) * 3,
+            shape(2 * half, ff),
+            shape(2 * half, 2 * ff),
             shape(half, 2 * width, dtype=f32),
             shape(half - block_rows, 2 * width),
             shape(block_rows, 2 * width),
@@ -376,9 +383,9 @@
     aside = passed(aside, ASIDE)
     out_across = passed(kernel_call(turn_body, piece, 0, out_across, out_turn), ACROSS)
     into_across = passed(kernel_call(turn_body, piece, 0, into_across, into_turn), ACROSS)
-    here, scaled, gate_act, up_act = lax.optimization_barrier((here, scaled, gate_act, up_act))
+    here, scaled, acts = lax.optimization_barrier((here, scaled, acts))
     grad_gate, grad_up = kernel_call(
-        grad_body, (shape(*gate_weight.shape),) * 2, 16 * unit, all_x, gate_act, up_act
+        grad_body, (shape(*gate_weight.shape),) * 2, 16 * unit, all_x, acts
     )
     here, grad_gate, grad_up = lax.optimization_barrier((here, grad_gate, grad_up))
     mine_sum, *away = kernel_call(

time: 53 us -> 53 us (level)
  no operation moved by 1% of the time
where the time goes in v11:
time: 53 us; the launch traced here: 52.8 us
  starting transfers between devices  22.7 us (43%)
  waiting for transfers between devices  17.2 us (32%)
  Pallas kernels  11.7 us (22%)
  between operations  0.85 us (2%)
    ppermute x23, starting transfers between devices, from_xor(): lax.ppermute(value, AXES, [(i, i ^ masks[i % 2]) for i in range(devices)])  22.7 us
    ppermute x23, waiting for transfers between devices, from_xor(): lax.ppermute(value, AXES, [(i, i ^ masks[i % 2]) for i in range(devices)])  17.2 us
    pallas_call x16, Pallas kernels, kernel_call(): pl.pallas_call(body, out_shape=out_shape, in_specs=specs, out_specs=jax.t...  11.7 us
  transfers between devices with their start and end apart: 23, of which 14 were waited for; matrix products, arithmetic and copies ran while one was open for 0% of the time, Pallas kernels for 15%

profile of v11, /device:TPU:0, one launch (start us, length us, event | category | flops | bytes accessed | tf_op | source)
XLA Modules:
  0.0 52.8 jit_solution(11106790400464764336)
XLA Ops:
  0.6 0.9 %shard_map.110 = (bf16[4,8320]{1,0:T(4,128)(2,1)S(1)}, f32[8,128]{1,0:T(8,128)S(1)}) custom-call(bf16[4,4096]{1,0:T(4,128)(2,1)} %x_ref.1, bf16[4,4096]{1,0:T(4,128)(2,1)} %dy_ref.1, s32[2,4]{1,0:T(2,128)} %bitcast.3, bf16[2,4]{1,0:T(2,128)(2,1)} %bitcast.4, s32[1]{0:T(128)} %bitcast.2.expert_ref), custom_call_target="tpu_custom_call" | custom-call | bytes 4194304 | tf_op jit(solution)/shard_map/pallas_call | solution.py:121
  1.5 5.1 %collective-permute-start.2 = (bf16[4,8320]{1,0:T(4,128)(2,1)S(1)}, bf16[4,8320]{1,0:T(4,128)(2,1)S(1)}, u32[]{:S(2)}, u32[]{:S(2)}) collective-permute-start(bf16[4,8320]{1,0:T(4,128)(2,1)S(1)} %get-tuple-element.48), channel_id=1, source_target_pairs={{0,24},{1,25},{2,26},{3,27},{4,28},{5,29},{6,30},{7,31},{8,16},{9,... | collective-permute-start | bytes 199688 | tf_op jit(solution)/shard_map/ppermute | solution.py:100
  7.3 2.4 %shard_map.111 = (bf16[384,4096]{1,0:T(8,128)(2,1)S(1)}, bf16[192,4096]{1,0:T(8,128)(2,1)S(1)}) custom-call(bf16[1,192,4096]{2,1,0:T(8,128)(2,1)} %gate_ref.1, bf16[1,192,4096]{2,1,0:T(8,128)(2,1)} %up_ref.1, bf16[1,192,4096]{2,1,0:T(8,128)(2,1)} %down_ref.1), custom_call_target="tpu_custom_call" | custom-call | bytes 4194304 | tf_op jit(solution)/shard_map/pallas_call | solution.py:121
  9.7 2.6 %collective-permute-done.1 = bf16[4,8320]{1,0:T(4,128)(2,1)S(1)} collective-permute-done((bf16[4,8320]{1,0:T(4,128)(2,1)S(1)}, bf16[4,8320]{1,0:T(4,128)(2,1)S(1)}, u32[]{:S(2)}, u32[]{:S(2)}) %collective-permute-start.1) | collective-permute-done | bytes 66592 | tf_op jit(solution)/shard_map/ppermute | solution.py:100
  12.4 1.6 %collective-permute-start.10 = (bf16[16,4096]{1,0:T(8,128)(2,1)S(1)}, bf16[16,4096]{1,0:T(8,128)(2,1)S(1)}, u32[]{:S(2)}, u32[]{:S(2)}) collective-permute-start(bf16[16,4096]{1,0:T(8,128)(2,1)S(1)} %pad_maximum_fusion.1.refs_0_), channel_id=1, source_target_pairs={{0,4},{1,3},{2,6},{3,1},{4,0},{5,7},{6,2},{7,5},{8,12},{9,11},{10,... | collective-permute-start | bytes 393224 | tf_op jit(solution)/shard_map/ppermute | solution.py:100
  14.1 1.6 %collective-permute-start.4 = (bf16[16,4224]{1,0:T(8,128)(2,1)S(1)}, bf16[16,4224]{1,0:T(8,128)(2,1)S(1)}, u32[]{:S(2)}, u32[]{:S(2)}) collective-permute-start(bf16[16,4224]{1,0:T(8,128)(2,1)S(1)} %pad_maximum_fusion.refs_0_), channel_id=1, source_target_pairs={{0,2},{1,5},{2,0},{3,7},{4,6},{5,1},{6,4},{7,3},{8,10},{9,13},{10,... | collective-permute-start | bytes 405512 | tf_op jit(solution)/shard_map/ppermute | solution.py:100
  16.7 1.8 %collective-permute-done.10.refs_0_ = bf16[16,4096]{1,0:T(8,128)(2,1)S(1)} collective-permute-done((bf16[16,4096]{1,0:T(8,128)(2,1)S(1)}, bf16[16,4096]{1,0:T(8,128)(2,1)S(1)}, u32[]{:S(2)}, u32[]{:S(2)}) %collective-permute-start.10) | collective-permute-done | bytes 131104 | tf_op jit(solution)/shard_map/ppermute | solution.py:100
  18.6 1.1 %collective-permute-start.11 = (bf16[16,4096]{1,0:T(8,128)(2,1)S(1)}, bf16[16,4096]{1,0:T(8,128)(2,1)S(1)}, u32[]{:S(2)}, u32[]{:S(2)}) collective-permute-start(bf16[16,4096]{1,0:T(8,128)(2,1)S(1)} %collective-permute-done.10.refs_0_), channel_id=1, source_target_pairs={{0,2},{1,5},{2,0},{3,7},{4,6},{5,1},{6,4},{7,3},{8,10},{9,13},{10,... | collective-permute-start | bytes 393224 | tf_op jit(solution)/shard_map/ppermute | solution.py:100
  19.7 0.8 %collective-permute-done.4.refs_0_ = bf16[16,4224]{1,0:T(8,128)(2,1)S(1)} collective-permute-done((bf16[16,4224]{1,0:T(8,128)(2,1)S(1)}, bf16[16,4224]{1,0:T(8,128)(2,1)S(1)}, u32[]{:S(2)}, u32[]{:S(2)}) %collective-permute-start.4) | collective-permute-done | bytes 135200 | tf_op jit(solution)/shard_map/ppermute | solution.py:100
  20.5 1.3 %collective-permute-start.5 = (bf16[16,4224]{1,0:T(8,128)(2,1)S(1)}, bf16[16,4224]{1,0:T(8,128)(2,1)S(1)}, u32[]{:S(2)}, u32[]{:S(2)}) collective-permute-start(bf16[16,4224]{1,0:T(8,128)(2,1)S(1)} %collective-permute-done.4.refs_0_), channel_id=1, source_target_pairs={{0,4},{1,3},{2,6},{3,1},{4,0},{5,7},{6,2},{7,5},{8,12},{9,11},{10,... | collective-permute-start | bytes 405512 | tf_op jit(solution)/shard_map/ppermute | solution.py:100
  22.9 1.9 %collective-permute-done.11.refs_1_ = bf16[16,4096]{1,0:T(8,128)(2,1)S(1)} collective-permute-done((bf16[16,4096]{1,0:T(8,128)(2,1)S(1)}, bf16[16,4096]{1,0:T(8,128)(2,1)S(1)}, u32[]{:S(2)}, u32[]{:S(2)}) %collective-permute-start.11) | collective-permute-done | bytes 131104 | tf_op jit(solution)/shard_map/ppermute | solution.py:100
  26.4 1.2 %shard_map.116 = (bf16[128,4096]{1,0:T(8,128)(2,1)S(1)}, f32[128,192]{1,0:T(8,128)S(1)}, f32[128,192]{1,0:T(8,128)S(1)}, f32[128,192]{1,0:T(8,128)S(1)}) custom-call(bf16[32,4096]{1,0:T(8,128)(2,1)S(1)} %shard_map.114.refs_0_, bf16[32,4096]{1,0:T(8,128)(2,1)S(1)} %shard_map.115.refs_1_, bf16[32,4096]{1,0:T(8,128)(2,1)S(1)} %collective-permute-done.7.refs_2_, ...), custom_call_target="tpu_custom_call" | custom-call | flops 402653184 | bytes 4194304 | tf_op jit(solution)/shard_map/pallas_call | solution.py:121
  27.6 1.9 %shard_map.117 = (bf16[128,4096]{1,0:T(8,128)(2,1)S(1)}, bf16[128,192]{1,0:T(8,128)(2,1)S(1)}, bf16[128,384]{1,0:T(8,128)(2,1)S(1)}, f32[64,8192]{1,0:T(8,128)S(...) custom-call(bf16[32,4224]{1,0:T(8,128)(2,1)S(1)} %shard_map.112.refs_0_, ...), custom_call_target="tpu_custom_call" | custom-call | flops 603979776 | bytes 4194304 | tf_op jit(solution)/shard_map/pallas_call | solution.py:121
  29.8 1.4 %collective-permute-done.13.came_ref = bf16[16,8192]{1,0:T(8,128)(2,1)S(1)} collective-permute-done((bf16[16,8192]{1,0:T(8,128)(2,1)S(1)}, bf16[16,8192]{1,0:T(8,128)(2,1)S(1)}, u32[]{:S(2)}, u32[]{:S(2)}) %collective-permute-start.13) | collective-permute-done | bytes 262176 | tf_op jit(solution)/shard_map/ppermute | solution.py:100
  31.4 1.6 %collective-permute-start.16 = (bf16[16,4096]{1,0:T(8,128)(2,1)S(1)}, bf16[16,4096]{1,0:T(8,128)(2,1)S(1)}, u32[]{:S(2)}, u32[]{:S(2)}) collective-permute-start(bf16[16,4096]{1,0:T(8,128)(2,1)S(1)} %get-tuple-element.76), channel_id=1, source_target_pairs={{0,4},{1,3},{2,6},{3,1},{4,0},{5,7},{6,2},{7,5},{8,12},{9,11},{10,... | collective-permute-start | bytes 393224 | tf_op jit(solution)/shard_map/ppermute | solution.py:100
  33.7 1.6 %collective-permute-start.15 = (bf16[16,8192]{1,0:T(8,128)(2,1)S(1)}, bf16[16,8192]{1,0:T(8,128)(2,1)S(1)}, u32[]{:S(2)}, u32[]{:S(2)}) collective-permute-start(bf16[16,8192]{1,0:T(8,128)(2,1)S(1)} %get-tuple-element.73), channel_id=1, source_target_pairs={{0,4},{1,3},{2,6},{3,1},{4,0},{5,7},{6,2},{7,5},{8,12},{9,11},{10,... | collective-permute-start | bytes 786440 | tf_op jit(solution)/shard_map/ppermute | solution.py:100
  35.2 1.2 %collective-permute-done.16.came_ref = bf16[16,4096]{1,0:T(8,128)(2,1)S(1)} collective-permute-done((bf16[16,4096]{1,0:T(8,128)(2,1)S(1)}, bf16[16,4096]{1,0:T(8,128)(2,1)S(1)}, u32[]{:S(2)}, u32[]{:S(2)}) %collective-permute-start.16) | collective-permute-done | bytes 131104 | tf_op jit(solution)/shard_map/ppermute | solution.py:100
  37.0 0.9 %collective-permute-done.18.came_ref = bf16[16,4096]{1,0:T(8,128)(2,1)S(1)} collective-permute-done((bf16[16,4096]{1,0:T(8,128)(2,1)S(1)}, bf16[16,4096]{1,0:T(8,128)(2,1)S(1)}, u32[]{:S(2)}, u32[]{:S(2)}) %collective-permute-start.18) | collective-permute-done | bytes 131104 | tf_op jit(solution)/shard_map/ppermute | solution.py:100
  38.6 2.5 %shard_map.119 = (bf16[1,192,4096]{2,1,0:T(8,128)(2,1)}, bf16[1,192,4096]{2,1,0:T(8,128)(2,1)}) custom-call(bf16[128,4096]{1,0:T(8,128)(2,1)S(1)} %get-tuple-element.68.rows_ref, bf16[128,384]{1,0:T(8,128)(2,1)S(1)} %get-tuple-element.69.acts_ref), custom_call_target="tpu_custom_call" | custom-call | flops 402653184 | bytes 4194304 | tf_op jit(solution)/shard_map/pallas_call | solution.py:121
  41.5 1.5 %collective-permute-done.19.refs_1_ = bf16[16,4096]{1,0:T(8,128)(2,1)S(1)} collective-permute-done((bf16[16,4096]{1,0:T(8,128)(2,1)S(1)}, bf16[16,4096]{1,0:T(8,128)(2,1)S(1)}, u32[]{:S(2)}, u32[]{:S(2)}) %collective-permute-start.19) | collective-permute-done | bytes 131104 | tf_op jit(solution)/shard_map/ppermute | solution.py:100
  43.1 2.2 %collective-permute-start.20 = (bf16[4,8192]{1,0:T(4,128)(2,1)S(1)}, bf16[4,8192]{1,0:T(4,128)(2,1)S(1)}, u32[]{:S(2)}, u32[]{:S(2)}) collective-permute-start(bf16[4,8192]{1,0:T(4,128)(2,1)S(1)} %get-tuple-element.82), channel_id=1, source_target_pairs={{0,24},{1,25},{2,26},{3,27},{4,28},{5,29},{6,30},{7,31},{8,16},{9,... | collective-permute-start | bytes 196616 | tf_op jit(solution)/shard_map/ppermute | solution.py:100
  45.3 2.2 %collective-permute-start.22 = (bf16[4,8192]{1,0:T(4,128)(2,1)S(1)}, bf16[4,8192]{1,0:T(4,128)(2,1)S(1)}, u32[]{:S(2)}, u32[]{:S(2)}) collective-permute-start(bf16[4,8192]{1,0:T(4,128)(2,1)S(1)} %get-tuple-element.84), channel_id=1, source_target_pairs={{0,8},{1,9},{2,10},{3,11},{4,12},{5,13},{6,14},{7,15},{8,0},{9,1},... | collective-permute-start | bytes 196616 | tf_op jit(solution)/shard_map/ppermute | solution.py:100
  47.6 1.7 %shard_map.125 = bf16[1,192,4096]{2,1,0:T(8,128)(2,1)} custom-call(bf16[128,4096]{1,0:T(8,128)(2,1)S(1)} %get-tuple-element.89.rows_ref, bf16[128,192]{1,0:T(8,128)(2,1)S(1)} %get-tuple-element.90.acts_ref), custom_call_target="tpu_custom_call" | custom-call | flops 201326592 | bytes 4194304 | tf_op jit(solution)/shard_map/pallas_call | solution.py:121
  50.0 2.2 %collective-permute-done.21.refs_1_ = bf16[4,8192]{1,0:T(4,128)(2,1)S(1)} collective-permute-done((bf16[4,8192]{1,0:T(4,128)(2,1)S(1)}, bf16[4,8192]{1,0:T(4,128)(2,1)S(1)}, u32[]{:S(2)}, u32[]{:S(2)}) %collective-permute-start.21) | collective-permute-done | bytes 65568 | tf_op jit(solution)/shard_map/ppermute | solution.py:100
  (48 shorter events, 8.8 us)
Async XLA Ops:
  1.5 8.2 %collective-permute-start.2 = (bf16[4,8320]{1,0:T(4,128)(2,1)S(1)}, bf16[4,8320]{1,0:T(4,128)(2,1)S(1)}, u32[]{:S(2)}, u32[]{:S(2)}) collective-permute-start(bf16[4,8320]{1,0:T(4,128)(2,1)S(1)} %get-tuple-element.48), channel_id=1, source_target_pairs={{0,24},{1,25},{2,26},{3,27},{4,28},{5,29},{6,30},{7,31},{8,16},{9,... | collective-permute-start | bytes 199688 | tf_op jit(solution)/shard_map/ppermute | solution.py:100
  6.6 5.7 %collective-permute-start.1 = (bf16[4,8320]{1,0:T(4,128)(2,1)S(1)}, bf16[4,8320]{1,0:T(4,128)(2,1)S(1)}, u32[]{:S(2)}, u32[]{:S(2)}) collective-permute-start(bf16[4,8320]{1,0:T(4,128)(2,1)S(1)} %get-tuple-element.48), channel_id=1, source_target_pairs={{0,16},{1,17},{2,18},{3,19},{4,20},{5,21},{6,22},{7,23},{8,24},{9,... | collective-permute-start | bytes 199688 | tf_op jit(solution)/shard_map/ppermute | solution.py:100
  6.6 5.7 %collective-permute-start = (bf16[4,8320]{1,0:T(4,128)(2,1)S(1)}, bf16[4,8320]{1,0:T(4,128)(2,1)S(1)}, u32[]{:S(2)}, u32[]{:S(2)}) collective-permute-start(bf16[4,8320]{1,0:T(4,128)(2,1)S(1)} %get-tuple-element.48), channel_id=1, source_target_pairs={{0,8},{1,9},{2,10},{3,11},{4,12},{5,13},{6,14},{7,15},{8,0},{9,1},... | collective-permute-start | bytes 199688 | tf_op jit(solution)/shard_map/ppermute | solution.py:100
  12.4 6.2 %collective-permute-start.10 = (bf16[16,4096]{1,0:T(8,128)(2,1)S(1)}, bf16[16,4096]{1,0:T(8,128)(2,1)S(1)}, u32[]{:S(2)}, u32[]{:S(2)}) collective-permute-start(bf16[16,4096]{1,0:T(8,128)(2,1)S(1)} %pad_maximum_fusion.1.refs_0_), channel_id=1, source_target_pairs={{0,4},{1,3},{2,6},{3,1},{4,0},{5,7},{6,2},{7,5},{8,12},{9,11},{10,... | collective-permute-start | bytes 393224 | tf_op jit(solution)/shard_map/ppermute | solution.py:100
  14.1 6.4 %collective-permute-start.4 = (bf16[16,4224]{1,0:T(8,128)(2,1)S(1)}, bf16[16,4224]{1,0:T(8,128)(2,1)S(1)}, u32[]{:S(2)}, u32[]{:S(2)}) collective-permute-start(bf16[16,4224]{1,0:T(8,128)(2,1)S(1)} %pad_maximum_fusion.refs_0_), channel_id=1, source_target_pairs={{0,2},{1,5},{2,0},{3,7},{4,6},{5,1},{6,4},{7,3},{8,10},{9,13},{10,... | collective-permute-start | bytes 405512 | tf_op jit(solution)/shard_map/ppermute | solution.py:100
  15.7 6.5 %collective-permute-start.3 = (bf16[16,4224]{1,0:T(8,128)(2,1)S(1)}, bf16[16,4224]{1,0:T(8,128)(2,1)S(1)}, u32[]{:S(2)}, u32[]{:S(2)}) collective-permute-start(bf16[16,4224]{1,0:T(8,128)(2,1)S(1)} %pad_maximum_fusion.refs_0_), channel_id=1, source_target_pairs={{0,4},{1,3},{2,6},{3,1},{4,0},{5,7},{6,2},{7,5},{8,12},{9,11},{10,... | collective-permute-start | bytes 405512 | tf_op jit(solution)/shard_map/ppermute | solution.py:100
  16.2 6.1 %collective-permute-start.6 = (bf16[16,4096]{1,0:T(8,128)(2,1)S(1)}, bf16[16,4096]{1,0:T(8,128)(2,1)S(1)}, u32[]{:S(2)}, u32[]{:S(2)}) collective-permute-start(bf16[16,4096]{1,0:T(8,128)(2,1)S(1)} %pad_maximum_fusion.1.refs_0_), channel_id=1, source_target_pairs={{0,2},{1,5},{2,0},{3,7},{4,6},{5,1},{6,4},{7,3},{8,10},{9,13},{10,... | collective-permute-start | bytes 393224 | tf_op jit(solution)/shard_map/ppermute | solution.py:100
  18.6 6.2 %collective-permute-start.11 = (bf16[16,4096]{1,0:T(8,128)(2,1)S(1)}, bf16[16,4096]{1,0:T(8,128)(2,1)S(1)}, u32[]{:S(2)}, u32[]{:S(2)}) collective-permute-start(bf16[16,4096]{1,0:T(8,128)(2,1)S(1)} %collective-permute-done.10.refs_0_), channel_id=1, source_target_pairs={{0,2},{1,5},{2,0},{3,7},{4,6},{5,1},{6,4},{7,3},{8,10},{9,13},{10,... | collective-permute-start | bytes 393224 | tf_op jit(solution)/shard_map/ppermute | solution.py:100
  20.5 5.0 %collective-permute-start.5 = (bf16[16,4224]{1,0:T(8,128)(2,1)S(1)}, bf16[16,4224]{1,0:T(8,128)(2,1)S(1)}, u32[]{:S(2)}, u32[]{:S(2)}) collective-permute-start(bf16[16,4224]{1,0:T(8,128)(2,1)S(1)} %collective-permute-done.4.refs_0_), channel_id=1, source_target_pairs={{0,4},{1,3},{2,6},{3,1},{4,0},{5,7},{6,2},{7,5},{8,12},{9,11},{10,... | collective-permute-start | bytes 405512 | tf_op jit(solution)/shard_map/ppermute | solution.py:100
  22.2 3.4 %collective-permute-start.8 = (bf16[32,4224]{1,0:T(8,128)(2,1)S(1)}, bf16[32,4224]{1,0:T(8,128)(2,1)S(1)}, u32[]{:S(2)}, u32[]{:S(2)}) collective-permute-start(bf16[32,4224]{1,0:T(8,128)(2,1)S(1)} %shard_map.112.refs_0_), channel_id=1, source_target_pairs={{0,1},{1,0},{2,3},{3,2},{4,5},{5,4},{6,7},{7,6},{8,9},{9,8},{10,11... | collective-permute-start | bytes 811016 | tf_op jit(solution)/shard_map/ppermute | solution.py:100
  22.4 3.3 %collective-permute-start.7 = (bf16[32,4096]{1,0:T(8,128)(2,1)S(1)}, bf16[32,4096]{1,0:T(8,128)(2,1)S(1)}, u32[]{:S(2)}, u32[]{:S(2)}) collective-permute-start(bf16[32,4096]{1,0:T(8,128)(2,1)S(1)} %shard_map.114.refs_0_), channel_id=1, source_target_pairs={{0,1},{1,0},{2,3},{3,2},{4,5},{5,4},{6,7},{7,6},{8,9},{9,8},{10,11... | collective-permute-start | bytes 786440 | tf_op jit(solution)/shard_map/ppermute | solution.py:100
  24.8 1.6 %collective-permute-start.12 = (bf16[32,4096]{1,0:T(8,128)(2,1)S(1)}, bf16[32,4096]{1,0:T(8,128)(2,1)S(1)}, u32[]{:S(2)}, u32[]{:S(2)}) collective-permute-start(bf16[32,4096]{1,0:T(8,128)(2,1)S(1)} %shard_map.115.refs_1_), channel_id=1, source_target_pairs={{0,1},{1,0},{2,3},{3,2},{4,5},{5,4},{6,7},{7,6},{8,9},{9,8},{10,11... | collective-permute-start | bytes 786440 | tf_op jit(solution)/shard_map/ppermute | solution.py:100
  25.5 2.1 %collective-permute-start.9 = (bf16[32,4224]{1,0:T(8,128)(2,1)S(1)}, bf16[32,4224]{1,0:T(8,128)(2,1)S(1)}, u32[]{:S(2)}, u32[]{:S(2)}) collective-permute-start(bf16[32,4224]{1,0:T(8,128)(2,1)S(1)} %shard_map.113.refs_1_), channel_id=1, source_target_pairs={{0,1},{1,0},{2,3},{3,2},{4,5},{5,4},{6,7},{7,6},{8,9},{9,8},{10,11... | collective-permute-start | bytes 811016 | tf_op jit(solution)/shard_map/ppermute | solution.py:100
  29.6 1.6 %collective-permute-start.13 = (bf16[16,8192]{1,0:T(8,128)(2,1)S(1)}, bf16[16,8192]{1,0:T(8,128)(2,1)S(1)}, u32[]{:S(2)}, u32[]{:S(2)}) collective-permute-start(bf16[16,8192]{1,0:T(8,128)(2,1)S(1)} %get-tuple-element.61), channel_id=1, source_target_pairs={{0,1},{1,0},{2,3},{3,2},{4,5},{5,4},{6,7},{7,6},{8,9},{9,8},{10,11... | collective-permute-start | bytes 786440 | tf_op jit(solution)/shard_map/ppermute | solution.py:100
  31.2 2.3 %collective-permute-start.14 = (bf16[48,8192]{1,0:T(8,128)(2,1)S(1)}, bf16[48,8192]{1,0:T(8,128)(2,1)S(1)}, u32[]{:S(2)}, u32[]{:S(2)}) collective-permute-start(bf16[48,8192]{1,0:T(8,128)(2,1)S(1)} %get-tuple-element.63), channel_id=1, source_target_pairs={{0,1},{1,0},{2,3},{3,2},{4,5},{5,4},{6,7},{7,6},{8,9},{9,8},{10,11... | collective-permute-start | bytes 2359304 | tf_op jit(solution)/shard_map/ppermute | solution.py:100
  31.4 5.0 %collective-permute-start.16 = (bf16[16,4096]{1,0:T(8,128)(2,1)S(1)}, bf16[16,4096]{1,0:T(8,128)(2,1)S(1)}, u32[]{:S(2)}, u32[]{:S(2)}) collective-permute-start(bf16[16,4096]{1,0:T(8,128)(2,1)S(1)} %get-tuple-element.76), channel_id=1, source_target_pairs={{0,4},{1,3},{2,6},{3,1},{4,0},{5,7},{6,2},{7,5},{8,12},{9,11},{10,... | collective-permute-start | bytes 393224 | tf_op jit(solution)/shard_map/ppermute | solution.py:100
  32.9 5.0 %collective-permute-start.18 = (bf16[16,4096]{1,0:T(8,128)(2,1)S(1)}, bf16[16,4096]{1,0:T(8,128)(2,1)S(1)}, u32[]{:S(2)}, u32[]{:S(2)}) collective-permute-start(bf16[16,4096]{1,0:T(8,128)(2,1)S(1)} %get-tuple-element.78), channel_id=1, source_target_pairs={{0,4},{1,3},{2,6},{3,1},{4,0},{5,7},{6,2},{7,5},{8,12},{9,11},{10,... | collective-permute-start | bytes 393224 | tf_op jit(solution)/shard_map/ppermute | solution.py:100
  33.7 9.3 %collective-permute-start.15 = (bf16[16,8192]{1,0:T(8,128)(2,1)S(1)}, bf16[16,8192]{1,0:T(8,128)(2,1)S(1)}, u32[]{:S(2)}, u32[]{:S(2)}) collective-permute-start(bf16[16,8192]{1,0:T(8,128)(2,1)S(1)} %get-tuple-element.73), channel_id=1, source_target_pairs={{0,4},{1,3},{2,6},{3,1},{4,0},{5,7},{6,2},{7,5},{8,12},{9,11},{10,... | collective-permute-start | bytes 786440 | tf_op jit(solution)/shard_map/ppermute | solution.py:100
  36.5 5.0 %collective-permute-start.17 = (bf16[16,4096]{1,0:T(8,128)(2,1)S(1)}, bf16[16,4096]{1,0:T(8,128)(2,1)S(1)}, u32[]{:S(2)}, u32[]{:S(2)}) collective-permute-start(bf16[16,4096]{1,0:T(8,128)(2,1)S(1)} %shard_map.121), channel_id=1, source_target_pairs={{0,2},{1,5},{2,0},{3,7},{4,6},{5,1},{6,4},{7,3},{8,10},{9,13},{10,... | collective-permute-start | bytes 393224 | tf_op jit(solution)/shard_map/ppermute | solution.py:100
  37.9 5.0 %collective-permute-start.19 = (bf16[16,4096]{1,0:T(8,128)(2,1)S(1)}, bf16[16,4096]{1,0:T(8,128)(2,1)S(1)}, u32[]{:S(2)}, u32[]{:S(2)}) collective-permute-start(bf16[16,4096]{1,0:T(8,128)(2,1)S(1)} %shard_map.122), channel_id=1, source_target_pairs={{0,2},{1,5},{2,0},{3,7},{4,6},{5,1},{6,4},{7,3},{8,10},{9,13},{10,... | collective-permute-start | bytes 393224 | tf_op jit(solution)/shard_map/ppermute | solution.py:100
  43.1 6.9 %collective-permute-start.20 = (bf16[4,8192]{1,0:T(4,128)(2,1)S(1)}, bf16[4,8192]{1,0:T(4,128)(2,1)S(1)}, u32[]{:S(2)}, u32[]{:S(2)}) collective-permute-start(bf16[4,8192]{1,0:T(4,128)(2,1)S(1)} %get-tuple-element.82), channel_id=1, source_target_pairs={{0,24},{1,25},{2,26},{3,27},{4,28},{5,29},{6,30},{7,31},{8,16},{9,... | collective-permute-start | bytes 196616 | tf_op jit(solution)/shard_map/ppermute | solution.py:100
  45.3 6.8 %collective-permute-start.21 = (bf16[4,8192]{1,0:T(4,128)(2,1)S(1)}, bf16[4,8192]{1,0:T(4,128)(2,1)S(1)}, u32[]{:S(2)}, u32[]{:S(2)}) collective-permute-start(bf16[4,8192]{1,0:T(4,128)(2,1)S(1)} %get-tuple-element.83), channel_id=1, source_target_pairs={{0,16},{1,17},{2,18},{3,19},{4,20},{5,21},{6,22},{7,23},{8,24},{9,... | collective-permute-start | bytes 196616 | tf_op jit(solution)/shard_map/ppermute | solution.py:100
  45.3 6.8 %collective-permute-start.22 = (bf16[4,8192]{1,0:T(4,128)(2,1)S(1)}, bf16[4,8192]{1,0:T(4,128)(2,1)S(1)}, u32[]{:S(2)}, u32[]{:S(2)}) collective-permute-start(bf16[4,8192]{1,0:T(4,128)(2,1)S(1)} %get-tuple-element.84), channel_id=1, source_target_pairs={{0,8},{1,9},{2,10},{3,11},{4,12},{5,13},{6,14},{7,15},{8,0},{9,1},... | collective-permute-start | bytes 196616 | tf_op jit(solution)/shard_map/ppermute | solution.py:100

commit v12 on v11

--- a/solution.py
+++ b/solution.py
@@ -210,17 +210,17 @@
     rows, width = out_ref.shape
     for side, ref in enumerate((out_ref, into_ref)):
         at = slice(side * width, (side + 1) * width)
-        ref[...] = (own_ref[-rows:, at] + came_ref[:, at].astype(jnp.float32)).astype(jnp.bfloat16)
+        ref[...] = (own_ref[-rows:, at].astype(jnp.float32) + came_ref[:, at].astype(jnp.float32)).astype(jnp.bfloat16)
 
 
 def most_body(own_ref, came_ref, here_ref, aside_ref, out_ref, into_ref):
     rows, width = out_ref.shape
     for at, ref in ((0, here_ref), (2, aside_ref)):
         at = slice(at * rows, (at + 1) * rows)
-        ref[...] = (own_ref[at, :] + came_ref[at, :].astype(jnp.float32)).astype(ref.dtype)
+        ref[...] = (own_ref[at, :].astype(jnp.float32) + came_ref[at, :].astype(jnp.float32)).astype(ref.dtype)
     for side, ref in enumerate((out_ref, into_ref)):
         at = (slice(rows, 2 * rows), slice(side * width, (side + 1) * width))
-        ref[...] = own_ref[at] + came_ref[at].astype(jnp.float32)
+        ref[...] = own_ref[at].astype(jnp.float32) + came_ref[at].astype(jnp.float32)
 
 
 def backward_body(count, *refs):
@@ -244,7 +244,7 @@
     half, most = own_ref.shape[0], most_ref.shape[0]
     for side, total in enumerate((out, into)):
         at = slice(side * width, (side + 1) * width)
-        own_ref[:, at] = total[:half, :]
+        own_ref[:, at] = total[:half, :].astype(jnp.bfloat16)
         corner_ref[:, at] = total[half + most :, :].astype(jnp.bfloat16)
         most_ref[:, at] = total[half : half + most, :].astype(jnp.bfloat16)
 
@@ -353,7 +353,7 @@
             shape(2 * half, width),
             shape(2 * half, ff),
             shape(2 * half, 2 * ff),
-            shape(half, 2 * width, dtype=f32),
+            shape(half, 2 * width),
             shape(half - block_rows, 2 * width),
             shape(block_rows, 2 * width),
         ),

time: 53 us -> 53 us (level)
  no operation moved by 1% of the time
where the time goes in v12:
time: 53 us; the launch traced here: 52.8 us
  starting transfers between devices  22.7 us (43%)
  waiting for transfers between devices  17.2 us (32%)
  Pallas kernels  11.7 us (22%)
  between operations  0.85 us (2%)
    ppermute x23, starting transfers between devices, from_xor(): lax.ppermute(value, AXES, [(i, i ^ masks[i % 2]) for i in range(devices)])  22.7 us
    ppermute x23, waiting for transfers between devices, from_xor(): lax.ppermute(value, AXES, [(i, i ^ masks[i % 2]) for i in range(devices)])  17.2 us
    pallas_call x16, Pallas kernels, kernel_call(): pl.pallas_call(body, out_shape=out_shape, in_specs=specs, out_specs=jax.t...  11.7 us
  transfers between devices with their start and end apart: 23, of which 14 were waited for; matrix products, arithmetic and copies ran while one was open for 0% of the time, Pallas kernels for 15%

profile of v12, /device:TPU:0, one launch (start us, length us, event | category | flops | bytes accessed | tf_op | source)
XLA Modules:
  0.0 52.8 jit_solution(11635676533303378453)
XLA Ops:
  0.6 0.9 %shard_map.110 = (bf16[4,8320]{1,0:T(4,128)(2,1)S(1)}, f32[8,128]{1,0:T(8,128)S(1)}) custom-call(bf16[4,4096]{1,0:T(4,128)(2,1)} %x_ref.1, bf16[4,4096]{1,0:T(4,128)(2,1)} %dy_ref.1, s32[2,4]{1,0:T(2,128)} %bitcast.3, bf16[2,4]{1,0:T(2,128)(2,1)} %bitcast.4, s32[1]{0:T(128)} %bitcast.2.expert_ref), custom_call_target="tpu_custom_call" | custom-call | bytes 4194304 | tf_op jit(solution)/shard_map/pallas_call | solution.py:121
  1.5 5.1 %collective-permute-start.2 = (bf16[4,8320]{1,0:T(4,128)(2,1)S(1)}, bf16[4,8320]{1,0:T(4,128)(2,1)S(1)}, u32[]{:S(2)}, u32[]{:S(2)}) collective-permute-start(bf16[4,8320]{1,0:T(4,128)(2,1)S(1)} %get-tuple-element.48), channel_id=1, source_target_pairs={{0,24},{1,25},{2,26},{3,27},{4,28},{5,29},{6,30},{7,31},{8,16},{9,... | collective-permute-start | bytes 199688 | tf_op jit(solution)/shard_map/ppermute | solution.py:100
  7.3 2.4 %shard_map.111 = (bf16[384,4096]{1,0:T(8,128)(2,1)S(1)}, bf16[192,4096]{1,0:T(8,128)(2,1)S(1)}) custom-call(bf16[1,192,4096]{2,1,0:T(8,128)(2,1)} %gate_ref.1, bf16[1,192,4096]{2,1,0:T(8,128)(2,1)} %up_ref.1, bf16[1,192,4096]{2,1,0:T(8,128)(2,1)} %down_ref.1), custom_call_target="tpu_custom_call" | custom-call | bytes 4194304 | tf_op jit(solution)/shard_map/pallas_call | solution.py:121
  9.7 2.6 %collective-permute-done.1 = bf16[4,8320]{1,0:T(4,128)(2,1)S(1)} collective-permute-done((bf16[4,8320]{1,0:T(4,128)(2,1)S(1)}, bf16[4,8320]{1,0:T(4,128)(2,1)S(1)}, u32[]{:S(2)}, u32[]{:S(2)}) %collective-permute-start.1) | collective-permute-done | bytes 66592 | tf_op jit(solution)/shard_map/ppermute | solution.py:100
  12.4 1.6 %collective-permute-start.10 = (bf16[16,4096]{1,0:T(8,128)(2,1)S(1)}, bf16[16,4096]{1,0:T(8,128)(2,1)S(1)}, u32[]{:S(2)}, u32[]{:S(2)}) collective-permute-start(bf16[16,4096]{1,0:T(8,128)(2,1)S(1)} %pad_maximum_fusion.1.refs_0_), channel_id=1, source_target_pairs={{0,4},{1,3},{2,6},{3,1},{4,0},{5,7},{6,2},{7,5},{8,12},{9,11},{10,... | collective-permute-start | bytes 393224 | tf_op jit(solution)/shard_map/ppermute | solution.py:100
  14.1 1.6 %collective-permute-start.4 = (bf16[16,4224]{1,0:T(8,128)(2,1)S(1)}, bf16[16,4224]{1,0:T(8,128)(2,1)S(1)}, u32[]{:S(2)}, u32[]{:S(2)}) collective-permute-start(bf16[16,4224]{1,0:T(8,128)(2,1)S(1)} %pad_maximum_fusion.refs_0_), channel_id=1, source_target_pairs={{0,2},{1,5},{2,0},{3,7},{4,6},{5,1},{6,4},{7,3},{8,10},{9,13},{10,... | collective-permute-start | bytes 405512 | tf_op jit(solution)/shard_map/ppermute | solution.py:100
  16.7 1.8 %collective-permute-done.10.refs_0_ = bf16[16,4096]{1,0:T(8,128)(2,1)S(1)} collective-permute-done((bf16[16,4096]{1,0:T(8,128)(2,1)S(1)}, bf16[16,4096]{1,0:T(8,128)(2,1)S(1)}, u32[]{:S(2)}, u32[]{:S(2)}) %collective-permute-start.10) | collective-permute-done | bytes 131104 | tf_op jit(solution)/shard_map/ppermute | solution.py:100
  18.6 1.1 %collective-permute-start.11 = (bf16[16,4096]{1,0:T(8,128)(2,1)S(1)}, bf16[16,4096]{1,0:T(8,128)(2,1)S(1)}, u32[]{:S(2)}, u32[]{:S(2)}) collective-permute-start(bf16[16,4096]{1,0:T(8,128)(2,1)S(1)} %collective-permute-done.10.refs_0_), channel_id=1, source_target_pairs={{0,2},{1,5},{2,0},{3,7},{4,6},{5,1},{6,4},{7,3},{8,10},{9,13},{10,... | collective-permute-start | bytes 393224 | tf_op jit(solution)/shard_map/ppermute | solution.py:100
  19.7 0.8 %collective-permute-done.4.refs_0_ = bf16[16,4224]{1,0:T(8,128)(2,1)S(1)} collective-permute-done((bf16[16,4224]{1,0:T(8,128)(2,1)S(1)}, bf16[16,4224]{1,0:T(8,128)(2,1)S(1)}, u32[]{:S(2)}, u32[]{:S(2)}) %collective-permute-start.4) | collective-permute-done | bytes 135200 | tf_op jit(solution)/shard_map/ppermute | solution.py:100
  20.5 1.3 %collective-permute-start.5 = (bf16[16,4224]{1,0:T(8,128)(2,1)S(1)}, bf16[16,4224]{1,0:T(8,128)(2,1)S(1)}, u32[]{:S(2)}, u32[]{:S(2)}) collective-permute-start(bf16[16,4224]{1,0:T(8,128)(2,1)S(1)} %collective-permute-done.4.refs_0_), channel_id=1, source_target_pairs={{0,4},{1,3},{2,6},{3,1},{4,0},{5,7},{6,2},{7,5},{8,12},{9,11},{10,... | collective-permute-start | bytes 405512 | tf_op jit(solution)/shard_map/ppermute | solution.py:100
  22.9 1.9 %collective-permute-done.11.refs_1_ = bf16[16,4096]{1,0:T(8,128)(2,1)S(1)} collective-permute-done((bf16[16,4096]{1,0:T(8,128)(2,1)S(1)}, bf16[16,4096]{1,0:T(8,128)(2,1)S(1)}, u32[]{:S(2)}, u32[]{:S(2)}) %collective-permute-start.11) | collective-permute-done | bytes 131104 | tf_op jit(solution)/shard_map/ppermute | solution.py:100
  26.4 1.2 %shard_map.116 = (bf16[128,4096]{1,0:T(8,128)(2,1)S(1)}, f32[128,192]{1,0:T(8,128)S(1)}, f32[128,192]{1,0:T(8,128)S(1)}, f32[128,192]{1,0:T(8,128)S(1)}) custom-call(bf16[32,4096]{1,0:T(8,128)(2,1)S(1)} %shard_map.114.refs_0_, bf16[32,4096]{1,0:T(8,128)(2,1)S(1)} %shard_map.115.refs_1_, bf16[32,4096]{1,0:T(8,128)(2,1)S(1)} %collective-permute-done.7.refs_2_, ...), custom_call_target="tpu_custom_call" | custom-call | flops 402653184 | bytes 4194304 | tf_op jit(solution)/shard_map/pallas_call | solution.py:121
  27.6 2.0 %shard_map.117 = (bf16[128,4096]{1,0:T(8,128)(2,1)S(1)}, bf16[128,192]{1,0:T(8,128)(2,1)S(1)}, bf16[128,384]{1,0:T(8,128)(2,1)S(1)}, bf16[64,8192]{1,0:T(8,128)(...) custom-call(bf16[32,4224]{1,0:T(8,128)(2,1)S(1)} %shard_map.112.refs_0_, ...), custom_call_target="tpu_custom_call" | custom-call | flops 603979776 | bytes 4194304 | tf_op jit(solution)/shard_map/pallas_call | solution.py:121
  29.8 1.4 %collective-permute-done.13.came_ref = bf16[16,8192]{1,0:T(8,128)(2,1)S(1)} collective-permute-done((bf16[16,8192]{1,0:T(8,128)(2,1)S(1)}, bf16[16,8192]{1,0:T(8,128)(2,1)S(1)}, u32[]{:S(2)}, u32[]{:S(2)}) %collective-permute-start.13) | collective-permute-done | bytes 262176 | tf_op jit(solution)/shard_map/ppermute | solution.py:100
  31.4 1.6 %collective-permute-start.16 = (bf16[16,4096]{1,0:T(8,128)(2,1)S(1)}, bf16[16,4096]{1,0:T(8,128)(2,1)S(1)}, u32[]{:S(2)}, u32[]{:S(2)}) collective-permute-start(bf16[16,4096]{1,0:T(8,128)(2,1)S(1)} %get-tuple-element.76), channel_id=1, source_target_pairs={{0,4},{1,3},{2,6},{3,1},{4,0},{5,7},{6,2},{7,5},{8,12},{9,11},{10,... | collective-permute-start | bytes 393224 | tf_op jit(solution)/shard_map/ppermute | solution.py:100
  33.7 1.6 %collective-permute-start.15 = (bf16[16,8192]{1,0:T(8,128)(2,1)S(1)}, bf16[16,8192]{1,0:T(8,128)(2,1)S(1)}, u32[]{:S(2)}, u32[]{:S(2)}) collective-permute-start(bf16[16,8192]{1,0:T(8,128)(2,1)S(1)} %get-tuple-element.73), channel_id=1, source_target_pairs={{0,4},{1,3},{2,6},{3,1},{4,0},{5,7},{6,2},{7,5},{8,12},{9,11},{10,... | collective-permute-start | bytes 786440 | tf_op jit(solution)/shard_map/ppermute | solution.py:100
  35.2 1.2 %collective-permute-done.16.came_ref = bf16[16,4096]{1,0:T(8,128)(2,1)S(1)} collective-permute-done((bf16[16,4096]{1,0:T(8,128)(2,1)S(1)}, bf16[16,4096]{1,0:T(8,128)(2,1)S(1)}, u32[]{:S(2)}, u32[]{:S(2)}) %collective-permute-start.16) | collective-permute-done | bytes 131104 | tf_op jit(solution)/shard_map/ppermute | solution.py:100
  37.0 0.9 %collective-permute-done.18.came_ref = bf16[16,4096]{1,0:T(8,128)(2,1)S(1)} collective-permute-done((bf16[16,4096]{1,0:T(8,128)(2,1)S(1)}, bf16[16,4096]{1,0:T(8,128)(2,1)S(1)}, u32[]{:S(2)}, u32[]{:S(2)}) %collective-permute-start.18) | collective-permute-done | bytes 131104 | tf_op jit(solution)/shard_map/ppermute | solution.py:100
  38.7 2.4 %shard_map.119 = (bf16[1,192,4096]{2,1,0:T(8,128)(2,1)}, bf16[1,192,4096]{2,1,0:T(8,128)(2,1)}) custom-call(bf16[128,4096]{1,0:T(8,128)(2,1)S(1)} %get-tuple-element.68.rows_ref, bf16[128,384]{1,0:T(8,128)(2,1)S(1)} %get-tuple-element.69.acts_ref), custom_call_target="tpu_custom_call" | custom-call | flops 402653184 | bytes 4194304 | tf_op jit(solution)/shard_map/pallas_call | solution.py:121
  41.5 1.5 %collective-permute-done.19.refs_1_ = bf16[16,4096]{1,0:T(8,128)(2,1)S(1)} collective-permute-done((bf16[16,4096]{1,0:T(8,128)(2,1)S(1)}, bf16[16,4096]{1,0:T(8,128)(2,1)S(1)}, u32[]{:S(2)}, u32[]{:S(2)}) %collective-permute-start.19) | collective-permute-done | bytes 131104 | tf_op jit(solution)/shard_map/ppermute | solution.py:100
  43.1 2.2 %collective-permute-start.20 = (bf16[4,8192]{1,0:T(4,128)(2,1)S(1)}, bf16[4,8192]{1,0:T(4,128)(2,1)S(1)}, u32[]{:S(2)}, u32[]{:S(2)}) collective-permute-start(bf16[4,8192]{1,0:T(4,128)(2,1)S(1)} %get-tuple-element.82), channel_id=1, source_target_pairs={{0,24},{1,25},{2,26},{3,27},{4,28},{5,29},{6,30},{7,31},{8,16},{9,... | collective-permute-start | bytes 196616 | tf_op jit(solution)/shard_map/ppermute | solution.py:100
  45.3 2.2 %collective-permute-start.22 = (bf16[4,8192]{1,0:T(4,128)(2,1)S(1)}, bf16[4,8192]{1,0:T(4,128)(2,1)S(1)}, u32[]{:S(2)}, u32[]{:S(2)}) collective-permute-start(bf16[4,8192]{1,0:T(4,128)(2,1)S(1)} %get-tuple-element.84), channel_id=1, source_target_pairs={{0,8},{1,9},{2,10},{3,11},{4,12},{5,13},{6,14},{7,15},{8,0},{9,1},... | collective-permute-start | bytes 196616 | tf_op jit(solution)/shard_map/ppermute | solution.py:100
  47.6 1.7 %shard_map.125 = bf16[1,192,4096]{2,1,0:T(8,128)(2,1)} custom-call(bf16[128,4096]{1,0:T(8,128)(2,1)S(1)} %get-tuple-element.89.rows_ref, bf16[128,192]{1,0:T(8,128)(2,1)S(1)} %get-tuple-element.90.acts_ref), custom_call_target="tpu_custom_call" | custom-call | flops 201326592 | bytes 4194304 | tf_op jit(solution)/shard_map/pallas_call | solution.py:121
  50.0 2.2 %collective-permute-done.21.refs_1_ = bf16[4,8192]{1,0:T(4,128)(2,1)S(1)} collective-permute-done((bf16[4,8192]{1,0:T(4,128)(2,1)S(1)}, bf16[4,8192]{1,0:T(4,128)(2,1)S(1)}, u32[]{:S(2)}, u32[]{:S(2)}) %collective-permute-start.21) | collective-permute-done | bytes 65568 | tf_op jit(solution)/shard_map/ppermute | solution.py:100
  (48 shorter events, 8.9 us)
Async XLA Ops:
  1.5 8.2 %collective-permute-start.2 = (bf16[4,8320]{1,0:T(4,128)(2,1)S(1)}, bf16[4,8320]{1,0:T(4,128)(2,1)S(1)}, u32[]{:S(2)}, u32[]{:S(2)}) collective-permute-start(bf16[4,8320]{1,0:T(4,128)(2,1)S(1)} %get-tuple-element.48), channel_id=1, source_target_pairs={{0,24},{1,25},{2,26},{3,27},{4,28},{5,29},{6,30},{7,31},{8,16},{9,... | collective-permute-start | bytes 199688 | tf_op jit(solution)/shard_map/ppermute | solution.py:100
  6.6 5.7 %collective-permute-start.1 = (bf16[4,8320]{1,0:T(4,128)(2,1)S(1)}, bf16[4,8320]{1,0:T(4,128)(2,1)S(1)}, u32[]{:S(2)}, u32[]{:S(2)}) collective-permute-start(bf16[4,8320]{1,0:T(4,128)(2,1)S(1)} %get-tuple-element.48), channel_id=1, source_target_pairs={{0,16},{1,17},{2,18},{3,19},{4,20},{5,21},{6,22},{7,23},{8,24},{9,... | collective-permute-start | bytes 199688 | tf_op jit(solution)/shard_map/ppermute | solution.py:100
  6.6 5.7 %collective-permute-start = (bf16[4,8320]{1,0:T(4,128)(2,1)S(1)}, bf16[4,8320]{1,0:T(4,128)(2,1)S(1)}, u32[]{:S(2)}, u32[]{:S(2)}) collective-permute-start(bf16[4,8320]{1,0:T(4,128)(2,1)S(1)} %get-tuple-element.48), channel_id=1, source_target_pairs={{0,8},{1,9},{2,10},{3,11},{4,12},{5,13},{6,14},{7,15},{8,0},{9,1},... | collective-permute-start | bytes 199688 | tf_op jit(solution)/shard_map/ppermute | solution.py:100
  12.4 6.2 %collective-permute-start.10 = (bf16[16,4096]{1,0:T(8,128)(2,1)S(1)}, bf16[16,4096]{1,0:T(8,128)(2,1)S(1)}, u32[]{:S(2)}, u32[]{:S(2)}) collective-permute-start(bf16[16,4096]{1,0:T(8,128)(2,1)S(1)} %pad_maximum_fusion.1.refs_0_), channel_id=1, source_target_pairs={{0,4},{1,3},{2,6},{3,1},{4,0},{5,7},{6,2},{7,5},{8,12},{9,11},{10,... | collective-permute-start | bytes 393224 | tf_op jit(solution)/shard_map/ppermute | solution.py:100
  14.1 6.4 %collective-permute-start.4 = (bf16[16,4224]{1,0:T(8,128)(2,1)S(1)}, bf16[16,4224]{1,0:T(8,128)(2,1)S(1)}, u32[]{:S(2)}, u32[]{:S(2)}) collective-permute-start(bf16[16,4224]{1,0:T(8,128)(2,1)S(1)} %pad_maximum_fusion.refs_0_), channel_id=1, source_target_pairs={{0,2},{1,5},{2,0},{3,7},{4,6},{5,1},{6,4},{7,3},{8,10},{9,13},{10,... | collective-permute-start | bytes 405512 | tf_op jit(solution)/shard_map/ppermute | solution.py:100
  15.7 6.5 %collective-permute-start.3 = (bf16[16,4224]{1,0:T(8,128)(2,1)S(1)}, bf16[16,4224]{1,0:T(8,128)(2,1)S(1)}, u32[]{:S(2)}, u32[]{:S(2)}) collective-permute-start(bf16[16,4224]{1,0:T(8,128)(2,1)S(1)} %pad_maximum_fusion.refs_0_), channel_id=1, source_target_pairs={{0,4},{1,3},{2,6},{3,1},{4,0},{5,7},{6,2},{7,5},{8,12},{9,11},{10,... | collective-permute-start | bytes 405512 | tf_op jit(solution)/shard_map/ppermute | solution.py:100
  16.2 6.1 %collective-permute-start.6 = (bf16[16,4096]{1,0:T(8,128)(2,1)S(1)}, bf16[16,4096]{1,0:T(8,128)(2,1)S(1)}, u32[]{:S(2)}, u32[]{:S(2)}) collective-permute-start(bf16[16,4096]{1,0:T(8,128)(2,1)S(1)} %pad_maximum_fusion.1.refs_0_), channel_id=1, source_target_pairs={{0,2},{1,5},{2,0},{3,7},{4,6},{5,1},{6,4},{7,3},{8,10},{9,13},{10,... | collective-permute-start | bytes 393224 | tf_op jit(solution)/shard_map/ppermute | solution.py:100
  18.6 6.2 %collective-permute-start.11 = (bf16[16,4096]{1,0:T(8,128)(2,1)S(1)}, bf16[16,4096]{1,0:T(8,128)(2,1)S(1)}, u32[]{:S(2)}, u32[]{:S(2)}) collective-permute-start(bf16[16,4096]{1,0:T(8,128)(2,1)S(1)} %collective-permute-done.10.refs_0_), channel_id=1, source_target_pairs={{0,2},{1,5},{2,0},{3,7},{4,6},{5,1},{6,4},{7,3},{8,10},{9,13},{10,... | collective-permute-start | bytes 393224 | tf_op jit(solution)/shard_map/ppermute | solution.py:100
  20.5 5.0 %collective-permute-start.5 = (bf16[16,4224]{1,0:T(8,128)(2,1)S(1)}, bf16[16,4224]{1,0:T(8,128)(2,1)S(1)}, u32[]{:S(2)}, u32[]{:S(2)}) collective-permute-start(bf16[16,4224]{1,0:T(8,128)(2,1)S(1)} %collective-permute-done.4.refs_0_), channel_id=1, source_target_pairs={{0,4},{1,3},{2,6},{3,1},{4,0},{5,7},{6,2},{7,5},{8,12},{9,11},{10,... | collective-permute-start | bytes 405512 | tf_op jit(solution)/shard_map/ppermute | solution.py:100
  22.2 3.4 %collective-permute-start.8 = (bf16[32,4224]{1,0:T(8,128)(2,1)S(1)}, bf16[32,4224]{1,0:T(8,128)(2,1)S(1)}, u32[]{:S(2)}, u32[]{:S(2)}) collective-permute-start(bf16[32,4224]{1,0:T(8,128)(2,1)S(1)} %shard_map.112.refs_0_), channel_id=1, source_target_pairs={{0,1},{1,0},{2,3},{3,2},{4,5},{5,4},{6,7},{7,6},{8,9},{9,8},{10,11... | collective-permute-start | bytes 811016 | tf_op jit(solution)/shard_map/ppermute | solution.py:100
  22.4 3.3 %collective-permute-start.7 = (bf16[32,4096]{1,0:T(8,128)(2,1)S(1)}, bf16[32,4096]{1,0:T(8,128)(2,1)S(1)}, u32[]{:S(2)}, u32[]{:S(2)}) collective-permute-start(bf16[32,4096]{1,0:T(8,128)(2,1)S(1)} %shard_map.114.refs_0_), channel_id=1, source_target_pairs={{0,1},{1,0},{2,3},{3,2},{4,5},{5,4},{6,7},{7,6},{8,9},{9,8},{10,11... | collective-permute-start | bytes 786440 | tf_op jit(solution)/shard_map/ppermute | solution.py:100
  24.8 1.6 %collective-permute-start.12 = (bf16[32,4096]{1,0:T(8,128)(2,1)S(1)}, bf16[32,4096]{1,0:T(8,128)(2,1)S(1)}, u32[]{:S(2)}, u32[]{:S(2)}) collective-permute-start(bf16[32,4096]{1,0:T(8,128)(2,1)S(1)} %shard_map.115.refs_1_), channel_id=1, source_target_pairs={{0,1},{1,0},{2,3},{3,2},{4,5},{5,4},{6,7},{7,6},{8,9},{9,8},{10,11... | collective-permute-start | bytes 786440 | tf_op jit(solution)/shard_map/ppermute | solution.py:100
  25.5 2.1 %collective-permute-start.9 = (bf16[32,4224]{1,0:T(8,128)(2,1)S(1)}, bf16[32,4224]{1,0:T(8,128)(2,1)S(1)}, u32[]{:S(2)}, u32[]{:S(2)}) collective-permute-start(bf16[32,4224]{1,0:T(8,128)(2,1)S(1)} %shard_map.113.refs_1_), channel_id=1, source_target_pairs={{0,1},{1,0},{2,3},{3,2},{4,5},{5,4},{6,7},{7,6},{8,9},{9,8},{10,11... | collective-permute-start | bytes 811016 | tf_op jit(solution)/shard_map/ppermute | solution.py:100
  29.6 1.6 %collective-permute-start.13 = (bf16[16,8192]{1,0:T(8,128)(2,1)S(1)}, bf16[16,8192]{1,0:T(8,128)(2,1)S(1)}, u32[]{:S(2)}, u32[]{:S(2)}) collective-permute-start(bf16[16,8192]{1,0:T(8,128)(2,1)S(1)} %get-tuple-element.61), channel_id=1, source_target_pairs={{0,1},{1,0},{2,3},{3,2},{4,5},{5,4},{6,7},{7,6},{8,9},{9,8},{10,11... | collective-permute-start | bytes 786440 | tf_op jit(solution)/shard_map/ppermute | solution.py:100
  31.2 2.3 %collective-permute-start.14 = (bf16[48,8192]{1,0:T(8,128)(2,1)S(1)}, bf16[48,8192]{1,0:T(8,128)(2,1)S(1)}, u32[]{:S(2)}, u32[]{:S(2)}) collective-permute-start(bf16[48,8192]{1,0:T(8,128)(2,1)S(1)} %get-tuple-element.63), channel_id=1, source_target_pairs={{0,1},{1,0},{2,3},{3,2},{4,5},{5,4},{6,7},{7,6},{8,9},{9,8},{10,11... | collective-permute-start | bytes 2359304 | tf_op jit(solution)/shard_map/ppermute | solution.py:100
  31.4 5.0 %collective-permute-start.16 = (bf16[16,4096]{1,0:T(8,128)(2,1)S(1)}, bf16[16,4096]{1,0:T(8,128)(2,1)S(1)}, u32[]{:S(2)}, u32[]{:S(2)}) collective-permute-start(bf16[16,4096]{1,0:T(8,128)(2,1)S(1)} %get-tuple-element.76), channel_id=1, source_target_pairs={{0,4},{1,3},{2,6},{3,1},{4,0},{5,7},{6,2},{7,5},{8,12},{9,11},{10,... | collective-permute-start | bytes 393224 | tf_op jit(solution)/shard_map/ppermute | solution.py:100
  32.9 5.0 %collective-permute-start.18 = (bf16[16,4096]{1,0:T(8,128)(2,1)S(1)}, bf16[16,4096]{1,0:T(8,128)(2,1)S(1)}, u32[]{:S(2)}, u32[]{:S(2)}) collective-permute-start(bf16[16,4096]{1,0:T(8,128)(2,1)S(1)} %get-tuple-element.78), channel_id=1, source_target_pairs={{0,4},{1,3},{2,6},{3,1},{4,0},{5,7},{6,2},{7,5},{8,12},{9,11},{10,... | collective-permute-start | bytes 393224 | tf_op jit(solution)/shard_map/ppermute | solution.py:100
  33.7 9.3 %collective-permute-start.15 = (bf16[16,8192]{1,0:T(8,128)(2,1)S(1)}, bf16[16,8192]{1,0:T(8,128)(2,1)S(1)}, u32[]{:S(2)}, u32[]{:S(2)}) collective-permute-start(bf16[16,8192]{1,0:T(8,128)(2,1)S(1)} %get-tuple-element.73), channel_id=1, source_target_pairs={{0,4},{1,3},{2,6},{3,1},{4,0},{5,7},{6,2},{7,5},{8,12},{9,11},{10,... | collective-permute-start | bytes 786440 | tf_op jit(solution)/shard_map/ppermute | solution.py:100
  36.5 5.0 %collective-permute-start.17 = (bf16[16,4096]{1,0:T(8,128)(2,1)S(1)}, bf16[16,4096]{1,0:T(8,128)(2,1)S(1)}, u32[]{:S(2)}, u32[]{:S(2)}) collective-permute-start(bf16[16,4096]{1,0:T(8,128)(2,1)S(1)} %shard_map.121), channel_id=1, source_target_pairs={{0,2},{1,5},{2,0},{3,7},{4,6},{5,1},{6,4},{7,3},{8,10},{9,13},{10,... | collective-permute-start | bytes 393224 | tf_op jit(solution)/shard_map/ppermute | solution.py:100
  37.9 5.0 %collective-permute-start.19 = (bf16[16,4096]{1,0:T(8,128)(2,1)S(1)}, bf16[16,4096]{1,0:T(8,128)(2,1)S(1)}, u32[]{:S(2)}, u32[]{:S(2)}) collective-permute-start(bf16[16,4096]{1,0:T(8,128)(2,1)S(1)} %shard_map.122), channel_id=1, source_target_pairs={{0,2},{1,5},{2,0},{3,7},{4,6},{5,1},{6,4},{7,3},{8,10},{9,13},{10,... | collective-permute-start | bytes 393224 | tf_op jit(solution)/shard_map/ppermute | solution.py:100
  43.1 6.9 %collective-permute-start.20 = (bf16[4,8192]{1,0:T(4,128)(2,1)S(1)}, bf16[4,8192]{1,0:T(4,128)(2,1)S(1)}, u32[]{:S(2)}, u32[]{:S(2)}) collective-permute-start(bf16[4,8192]{1,0:T(4,128)(2,1)S(1)} %get-tuple-element.82), channel_id=1, source_target_pairs={{0,24},{1,25},{2,26},{3,27},{4,28},{5,29},{6,30},{7,31},{8,16},{9,... | collective-permute-start | bytes 196616 | tf_op jit(solution)/shard_map/ppermute | solution.py:100
  45.3 6.8 %collective-permute-start.21 = (bf16[4,8192]{1,0:T(4,128)(2,1)S(1)}, bf16[4,8192]{1,0:T(4,128)(2,1)S(1)}, u32[]{:S(2)}, u32[]{:S(2)}) collective-permute-start(bf16[4,8192]{1,0:T(4,128)(2,1)S(1)} %get-tuple-element.83), channel_id=1, source_target_pairs={{0,16},{1,17},{2,18},{3,19},{4,20},{5,21},{6,22},{7,23},{8,24},{9,... | collective-permute-start | bytes 196616 | tf_op jit(solution)/shard_map/ppermute | solution.py:100
  45.3 6.8 %collective-permute-start.22 = (bf16[4,8192]{1,0:T(4,128)(2,1)S(1)}, bf16[4,8192]{1,0:T(4,128)(2,1)S(1)}, u32[]{:S(2)}, u32[]{:S(2)}) collective-permute-start(bf16[4,8192]{1,0:T(4,128)(2,1)S(1)} %get-tuple-element.84), channel_id=1, source_target_pairs={{0,8},{1,9},{2,10},{3,11},{4,12},{5,13},{6,14},{7,15},{8,0},{9,1},... | collective-permute-start | bytes 196616 | tf_op jit(solution)/shard_map/ppermute | solution.py:100

commit v13 on v11

--- a/solution.py
+++ b/solution.py
@@ -138,16 +138,19 @@
         copy.wait()
 
 
+LOAD_PARTS = 4
+
+
 def load_body(gate_ref, up_ref, down_ref, pair_ref, down_out_ref, sems):
     ff = gate_ref.shape[1]
-    copy_all(
-        [
-            (gate_ref.at[0], pair_ref.at[pl.ds(0, ff)]),
-            (up_ref.at[0], pair_ref.at[pl.ds(ff, ff)]),
-            (down_ref.at[0], down_out_ref),
-        ],
-        sems,
-    )
+    part = ff // LOAD_PARTS
+    pairs = []
+    for k in range(LOAD_PARTS):
+        here = pl.ds(k * part, part)
+        pairs.append((gate_ref.at[0, here], pair_ref.at[here]))
+        pairs.append((up_ref.at[0, here], pair_ref.at[pl.ds(ff + k * part, part)]))
+        pairs.append((down_ref.at[0, here], down_out_ref.at[here]))
+    copy_all(pairs, sems)
 
 
 def pack_body(x_ref, dy_ref, ids_ref, w_ref, expert_ref, msg_ref, mine_ref):
@@ -317,7 +320,7 @@
         gate_weight,
         up_weight,
         down_weight,
-        scratch=[pltpu.SemaphoreType.DMA((3,))],
+        scratch=[pltpu.SemaphoreType.DMA((3 * LOAD_PARTS,))],
         hbm=(0, 1, 2),
     )
     arrived = [message] + [passed(message, m) for m in near]

time: 53 us -> 53 us (level)
  transfers between devices with their start and end apart: 23 -> 23, of which waited for: 14 -> 14; matrix products, arithmetic and copies ran while one was open for 0% -> 0% of each run, Pallas kernels for 15% -> 16%
where the time goes in v13:
time: 53 us; the launch traced here: 52.8 us
  starting transfers between devices  22.7 us (43%)
  waiting for transfers between devices  17.2 us (32%)
  Pallas kernels  11.8 us (22%)
  between operations  0.85 us (2%)
    ppermute x23, starting transfers between devices, from_xor(): lax.ppermute(value, AXES, [(i, i ^ masks[i % 2]) for i in range(devices)])  22.7 us
    ppermute x23, waiting for transfers between devices, from_xor(): lax.ppermute(value, AXES, [(i, i ^ masks[i % 2]) for i in range(devices)])  17.2 us
    pallas_call x16, Pallas kernels, kernel_call(): pl.pallas_call(body, out_shape=out_shape, in_specs=specs, out_specs=jax.t...  11.8 us
  transfers between devices with their start and end apart: 23, of which 14 were waited for; matrix products, arithmetic and copies ran while one was open for 0% of the time, Pallas kernels for 16%

profile of v13, /device:TPU:0, one launch (start us, length us, event | category | flops | bytes accessed | tf_op | source)
XLA Modules:
  0.0 52.8 jit_solution(3853264919514840278)
XLA Ops:
  0.6 0.9 %shard_map.110 = (bf16[4,8320]{1,0:T(4,128)(2,1)S(1)}, f32[8,128]{1,0:T(8,128)S(1)}) custom-call(bf16[4,4096]{1,0:T(4,128)(2,1)} %x_ref.1, bf16[4,4096]{1,0:T(4,128)(2,1)} %dy_ref.1, s32[2,4]{1,0:T(2,128)} %bitcast.3, bf16[2,4]{1,0:T(2,128)(2,1)} %bitcast.4, s32[1]{0:T(128)} %bitcast.2.expert_ref), custom_call_target="tpu_custom_call" | custom-call | bytes 4194304 | tf_op jit(solution)/shard_map/pallas_call | solution.py:121
  1.5 5.1 %collective-permute-start.2 = (bf16[4,8320]{1,0:T(4,128)(2,1)S(1)}, bf16[4,8320]{1,0:T(4,128)(2,1)S(1)}, u32[]{:S(2)}, u32[]{:S(2)}) collective-permute-start(bf16[4,8320]{1,0:T(4,128)(2,1)S(1)} %get-tuple-element.48), channel_id=1, source_target_pairs={{0,24},{1,25},{2,26},{3,27},{4,28},{5,29},{6,30},{7,31},{8,16},{9,... | collective-permute-start | bytes 199688 | tf_op jit(solution)/shard_map/ppermute | solution.py:100
  7.3 2.4 %shard_map.111 = (bf16[384,4096]{1,0:T(8,128)(2,1)S(1)}, bf16[192,4096]{1,0:T(8,128)(2,1)S(1)}) custom-call(bf16[1,192,4096]{2,1,0:T(8,128)(2,1)} %gate_ref.1, bf16[1,192,4096]{2,1,0:T(8,128)(2,1)} %up_ref.1, bf16[1,192,4096]{2,1,0:T(8,128)(2,1)} %down_ref.1), custom_call_target="tpu_custom_call" | custom-call | bytes 4194304 | tf_op jit(solution)/shard_map/pallas_call | solution.py:121
  9.7 2.6 %collective-permute-done.1 = bf16[4,8320]{1,0:T(4,128)(2,1)S(1)} collective-permute-done((bf16[4,8320]{1,0:T(4,128)(2,1)S(1)}, bf16[4,8320]{1,0:T(4,128)(2,1)S(1)}, u32[]{:S(2)}, u32[]{:S(2)}) %collective-permute-start.1) | collective-permute-done | bytes 66592 | tf_op jit(solution)/shard_map/ppermute | solution.py:100
  12.4 1.6 %collective-permute-start.10 = (bf16[16,4096]{1,0:T(8,128)(2,1)S(1)}, bf16[16,4096]{1,0:T(8,128)(2,1)S(1)}, u32[]{:S(2)}, u32[]{:S(2)}) collective-permute-start(bf16[16,4096]{1,0:T(8,128)(2,1)S(1)} %pad_maximum_fusion.1.refs_0_), channel_id=1, source_target_pairs={{0,4},{1,3},{2,6},{3,1},{4,0},{5,7},{6,2},{7,5},{8,12},{9,11},{10,... | collective-permute-start | bytes 393224 | tf_op jit(solution)/shard_map/ppermute | solution.py:100
  14.1 1.6 %collective-permute-start.4 = (bf16[16,4224]{1,0:T(8,128)(2,1)S(1)}, bf16[16,4224]{1,0:T(8,128)(2,1)S(1)}, u32[]{:S(2)}, u32[]{:S(2)}) collective-permute-start(bf16[16,4224]{1,0:T(8,128)(2,1)S(1)} %pad_maximum_fusion.refs_0_), channel_id=1, source_target_pairs={{0,2},{1,5},{2,0},{3,7},{4,6},{5,1},{6,4},{7,3},{8,10},{9,13},{10,... | collective-permute-start | bytes 405512 | tf_op jit(solution)/shard_map/ppermute | solution.py:100
  16.7 1.8 %collective-permute-done.10.refs_0_ = bf16[16,4096]{1,0:T(8,128)(2,1)S(1)} collective-permute-done((bf16[16,4096]{1,0:T(8,128)(2,1)S(1)}, bf16[16,4096]{1,0:T(8,128)(2,1)S(1)}, u32[]{:S(2)}, u32[]{:S(2)}) %collective-permute-start.10) | collective-permute-done | bytes 131104 | tf_op jit(solution)/shard_map/ppermute | solution.py:100
  18.6 1.1 %collective-permute-start.11 = (bf16[16,4096]{1,0:T(8,128)(2,1)S(1)}, bf16[16,4096]{1,0:T(8,128)(2,1)S(1)}, u32[]{:S(2)}, u32[]{:S(2)}) collective-permute-start(bf16[16,4096]{1,0:T(8,128)(2,1)S(1)} %collective-permute-done.10.refs_0_), channel_id=1, source_target_pairs={{0,2},{1,5},{2,0},{3,7},{4,6},{5,1},{6,4},{7,3},{8,10},{9,13},{10,... | collective-permute-start | bytes 393224 | tf_op jit(solution)/shard_map/ppermute | solution.py:100
  19.7 0.8 %collective-permute-done.4.refs_0_ = bf16[16,4224]{1,0:T(8,128)(2,1)S(1)} collective-permute-done((bf16[16,4224]{1,0:T(8,128)(2,1)S(1)}, bf16[16,4224]{1,0:T(8,128)(2,1)S(1)}, u32[]{:S(2)}, u32[]{:S(2)}) %collective-permute-start.4) | collective-permute-done | bytes 135200 | tf_op jit(solution)/shard_map/ppermute | solution.py:100
  20.5 1.3 %collective-permute-start.5 = (bf16[16,4224]{1,0:T(8,128)(2,1)S(1)}, bf16[16,4224]{1,0:T(8,128)(2,1)S(1)}, u32[]{:S(2)}, u32[]{:S(2)}) collective-permute-start(bf16[16,4224]{1,0:T(8,128)(2,1)S(1)} %collective-permute-done.4.refs_0_), channel_id=1, source_target_pairs={{0,4},{1,3},{2,6},{3,1},{4,0},{5,7},{6,2},{7,5},{8,12},{9,11},{10,... | collective-permute-start | bytes 405512 | tf_op jit(solution)/shard_map/ppermute | solution.py:100
  22.9 1.9 %collective-permute-done.11.refs_1_ = bf16[16,4096]{1,0:T(8,128)(2,1)S(1)} collective-permute-done((bf16[16,4096]{1,0:T(8,128)(2,1)S(1)}, bf16[16,4096]{1,0:T(8,128)(2,1)S(1)}, u32[]{:S(2)}, u32[]{:S(2)}) %collective-permute-start.11) | collective-permute-done | bytes 131104 | tf_op jit(solution)/shard_map/ppermute | solution.py:100
  26.4 1.2 %shard_map.116 = (bf16[128,4096]{1,0:T(8,128)(2,1)S(1)}, f32[128,192]{1,0:T(8,128)S(1)}, f32[128,192]{1,0:T(8,128)S(1)}, f32[128,192]{1,0:T(8,128)S(1)}) custom-call(bf16[32,4096]{1,0:T(8,128)(2,1)S(1)} %shard_map.114.refs_0_, bf16[32,4096]{1,0:T(8,128)(2,1)S(1)} %shard_map.115.refs_1_, bf16[32,4096]{1,0:T(8,128)(2,1)S(1)} %collective-permute-done.7.refs_2_, ...), custom_call_target="tpu_custom_call" | custom-call | flops 402653184 | bytes 4194304 | tf_op jit(solution)/shard_map/pallas_call | solution.py:121
  27.6 1.9 %shard_map.117 = (bf16[128,4096]{1,0:T(8,128)(2,1)S(1)}, bf16[128,192]{1,0:T(8,128)(2,1)S(1)}, bf16[128,384]{1,0:T(8,128)(2,1)S(1)}, f32[64,8192]{1,0:T(8,128)S(...) custom-call(bf16[32,4224]{1,0:T(8,128)(2,1)S(1)} %shard_map.112.refs_0_, ...), custom_call_target="tpu_custom_call" | custom-call | flops 603979776 | bytes 4194304 | tf_op jit(solution)/shard_map/pallas_call | solution.py:121
  29.8 1.4 %collective-permute-done.13.came_ref = bf16[16,8192]{1,0:T(8,128)(2,1)S(1)} collective-permute-done((bf16[16,8192]{1,0:T(8,128)(2,1)S(1)}, bf16[16,8192]{1,0:T(8,128)(2,1)S(1)}, u32[]{:S(2)}, u32[]{:S(2)}) %collective-permute-start.13) | collective-permute-done | bytes 262176 | tf_op jit(solution)/shard_map/ppermute | solution.py:100
  31.4 1.6 %collective-permute-start.16 = (bf16[16,4096]{1,0:T(8,128)(2,1)S(1)}, bf16[16,4096]{1,0:T(8,128)(2,1)S(1)}, u32[]{:S(2)}, u32[]{:S(2)}) collective-permute-start(bf16[16,4096]{1,0:T(8,128)(2,1)S(1)} %get-tuple-element.76), channel_id=1, source_target_pairs={{0,4},{1,3},{2,6},{3,1},{4,0},{5,7},{6,2},{7,5},{8,12},{9,11},{10,... | collective-permute-start | bytes 393224 | tf_op jit(solution)/shard_map/ppermute | solution.py:100
  33.7 1.6 %collective-permute-start.15 = (bf16[16,8192]{1,0:T(8,128)(2,1)S(1)}, bf16[16,8192]{1,0:T(8,128)(2,1)S(1)}, u32[]{:S(2)}, u32[]{:S(2)}) collective-permute-start(bf16[16,8192]{1,0:T(8,128)(2,1)S(1)} %get-tuple-element.73), channel_id=1, source_target_pairs={{0,4},{1,3},{2,6},{3,1},{4,0},{5,7},{6,2},{7,5},{8,12},{9,11},{10,... | collective-permute-start | bytes 786440 | tf_op jit(solution)/shard_map/ppermute | solution.py:100
  35.2 1.2 %collective-permute-done.16.came_ref = bf16[16,4096]{1,0:T(8,128)(2,1)S(1)} collective-permute-done((bf16[16,4096]{1,0:T(8,128)(2,1)S(1)}, bf16[16,4096]{1,0:T(8,128)(2,1)S(1)}, u32[]{:S(2)}, u32[]{:S(2)}) %collective-permute-start.16) | collective-permute-done | bytes 131104 | tf_op jit(solution)/shard_map/ppermute | solution.py:100
  37.0 0.9 %collective-permute-done.18.came_ref = bf16[16,4096]{1,0:T(8,128)(2,1)S(1)} collective-permute-done((bf16[16,4096]{1,0:T(8,128)(2,1)S(1)}, bf16[16,4096]{1,0:T(8,128)(2,1)S(1)}, u32[]{:S(2)}, u32[]{:S(2)}) %collective-permute-start.18) | collective-permute-done | bytes 131104 | tf_op jit(solution)/shard_map/ppermute | solution.py:100
  38.6 2.5 %shard_map.119 = (bf16[1,192,4096]{2,1,0:T(8,128)(2,1)}, bf16[1,192,4096]{2,1,0:T(8,128)(2,1)}) custom-call(bf16[128,4096]{1,0:T(8,128)(2,1)S(1)} %get-tuple-element.68.rows_ref, bf16[128,384]{1,0:T(8,128)(2,1)S(1)} %get-tuple-element.69.acts_ref), custom_call_target="tpu_custom_call" | custom-call | flops 402653184 | bytes 4194304 | tf_op jit(solution)/shard_map/pallas_call | solution.py:121
  41.5 1.5 %collective-permute-done.19.refs_1_ = bf16[16,4096]{1,0:T(8,128)(2,1)S(1)} collective-permute-done((bf16[16,4096]{1,0:T(8,128)(2,1)S(1)}, bf16[16,4096]{1,0:T(8,128)(2,1)S(1)}, u32[]{:S(2)}, u32[]{:S(2)}) %collective-permute-start.19) | collective-permute-done | bytes 131104 | tf_op jit(solution)/shard_map/ppermute | solution.py:100
  43.1 2.2 %collective-permute-start.20 = (bf16[4,8192]{1,0:T(4,128)(2,1)S(1)}, bf16[4,8192]{1,0:T(4,128)(2,1)S(1)}, u32[]{:S(2)}, u32[]{:S(2)}) collective-permute-start(bf16[4,8192]{1,0:T(4,128)(2,1)S(1)} %get-tuple-element.82), channel_id=1, source_target_pairs={{0,24},{1,25},{2,26},{3,27},{4,28},{5,29},{6,30},{7,31},{8,16},{9,... | collective-permute-start | bytes 196616 | tf_op jit(solution)/shard_map/ppermute | solution.py:100
  45.3 2.2 %collective-permute-start.22 = (bf16[4,8192]{1,0:T(4,128)(2,1)S(1)}, bf16[4,8192]{1,0:T(4,128)(2,1)S(1)}, u32[]{:S(2)}, u32[]{:S(2)}) collective-permute-start(bf16[4,8192]{1,0:T(4,128)(2,1)S(1)} %get-tuple-element.84), channel_id=1, source_target_pairs={{0,8},{1,9},{2,10},{3,11},{4,12},{5,13},{6,14},{7,15},{8,0},{9,1},... | collective-permute-start | bytes 196616 | tf_op jit(solution)/shard_map/ppermute | solution.py:100
  47.6 1.7 %shard_map.125 = bf16[1,192,4096]{2,1,0:T(8,128)(2,1)} custom-call(bf16[128,4096]{1,0:T(8,128)(2,1)S(1)} %get-tuple-element.89.rows_ref, bf16[128,192]{1,0:T(8,128)(2,1)S(1)} %get-tuple-element.90.acts_ref), custom_call_target="tpu_custom_call" | custom-call | flops 201326592 | bytes 4194304 | tf_op jit(solution)/shard_map/pallas_call | solution.py:121
  50.0 2.2 %collective-permute-done.21.refs_1_ = bf16[4,8192]{1,0:T(4,128)(2,1)S(1)} collective-permute-done((bf16[4,8192]{1,0:T(4,128)(2,1)S(1)}, bf16[4,8192]{1,0:T(4,128)(2,1)S(1)}, u32[]{:S(2)}, u32[]{:S(2)}) %collective-permute-start.21) | collective-permute-done | bytes 65568 | tf_op jit(solution)/shard_map/ppermute | solution.py:100
  (48 shorter events, 8.8 us)
Async XLA Ops:
  1.5 8.2 %collective-permute-start.2 = (bf16[4,8320]{1,0:T(4,128)(2,1)S(1)}, bf16[4,8320]{1,0:T(4,128)(2,1)S(1)}, u32[]{:S(2)}, u32[]{:S(2)}) collective-permute-start(bf16[4,8320]{1,0:T(4,128)(2,1)S(1)} %get-tuple-element.48), channel_id=1, source_target_pairs={{0,24},{1,25},{2,26},{3,27},{4,28},{5,29},{6,30},{7,31},{8,16},{9,... | collective-permute-start | bytes 199688 | tf_op jit(solution)/shard_map/ppermute | solution.py:100
  6.6 5.7 %collective-permute-start.1 = (bf16[4,8320]{1,0:T(4,128)(2,1)S(1)}, bf16[4,8320]{1,0:T(4,128)(2,1)S(1)}, u32[]{:S(2)}, u32[]{:S(2)}) collective-permute-start(bf16[4,8320]{1,0:T(4,128)(2,1)S(1)} %get-tuple-element.48), channel_id=1, source_target_pairs={{0,16},{1,17},{2,18},{3,19},{4,20},{5,21},{6,22},{7,23},{8,24},{9,... | collective-permute-start | bytes 199688 | tf_op jit(solution)/shard_map/ppermute | solution.py:100
  6.6 5.7 %collective-permute-start = (bf16[4,8320]{1,0:T(4,128)(2,1)S(1)}, bf16[4,8320]{1,0:T(4,128)(2,1)S(1)}, u32[]{:S(2)}, u32[]{:S(2)}) collective-permute-start(bf16[4,8320]{1,0:T(4,128)(2,1)S(1)} %get-tuple-element.48), channel_id=1, source_target_pairs={{0,8},{1,9},{2,10},{3,11},{4,12},{5,13},{6,14},{7,15},{8,0},{9,1},... | collective-permute-start | bytes 199688 | tf_op jit(solution)/shard_map/ppermute | solution.py:100
  12.4 6.2 %collective-permute-start.10 = (bf16[16,4096]{1,0:T(8,128)(2,1)S(1)}, bf16[16,4096]{1,0:T(8,128)(2,1)S(1)}, u32[]{:S(2)}, u32[]{:S(2)}) collective-permute-start(bf16[16,4096]{1,0:T(8,128)(2,1)S(1)} %pad_maximum_fusion.1.refs_0_), channel_id=1, source_target_pairs={{0,4},{1,3},{2,6},{3,1},{4,0},{5,7},{6,2},{7,5},{8,12},{9,11},{10,... | collective-permute-start | bytes 393224 | tf_op jit(solution)/shard_map/ppermute | solution.py:100
  14.1 6.4 %collective-permute-start.4 = (bf16[16,4224]{1,0:T(8,128)(2,1)S(1)}, bf16[16,4224]{1,0:T(8,128)(2,1)S(1)}, u32[]{:S(2)}, u32[]{:S(2)}) collective-permute-start(bf16[16,4224]{1,0:T(8,128)(2,1)S(1)} %pad_maximum_fusion.refs_0_), channel_id=1, source_target_pairs={{0,2},{1,5},{2,0},{3,7},{4,6},{5,1},{6,4},{7,3},{8,10},{9,13},{10,... | collective-permute-start | bytes 405512 | tf_op jit(solution)/shard_map/ppermute | solution.py:100
  15.7 6.5 %collective-permute-start.3 = (bf16[16,4224]{1,0:T(8,128)(2,1)S(1)}, bf16[16,4224]{1,0:T(8,128)(2,1)S(1)}, u32[]{:S(2)}, u32[]{:S(2)}) collective-permute-start(bf16[16,4224]{1,0:T(8,128)(2,1)S(1)} %pad_maximum_fusion.refs_0_), channel_id=1, source_target_pairs={{0,4},{1,3},{2,6},{3,1},{4,0},{5,7},{6,2},{7,5},{8,12},{9,11},{10,... | collective-permute-start | bytes 405512 | tf_op jit(solution)/shard_map/ppermute | solution.py:100
  16.2 6.1 %collective-permute-start.6 = (bf16[16,4096]{1,0:T(8,128)(2,1)S(1)}, bf16[16,4096]{1,0:T(8,128)(2,1)S(1)}, u32[]{:S(2)}, u32[]{:S(2)}) collective-permute-start(bf16[16,4096]{1,0:T(8,128)(2,1)S(1)} %pad_maximum_fusion.1.refs_0_), channel_id=1, source_target_pairs={{0,2},{1,5},{2,0},{3,7},{4,6},{5,1},{6,4},{7,3},{8,10},{9,13},{10,... | collective-permute-start | bytes 393224 | tf_op jit(solution)/shard_map/ppermute | solution.py:100
  18.6 6.2 %collective-permute-start.11 = (bf16[16,4096]{1,0:T(8,128)(2,1)S(1)}, bf16[16,4096]{1,0:T(8,128)(2,1)S(1)}, u32[]{:S(2)}, u32[]{:S(2)}) collective-permute-start(bf16[16,4096]{1,0:T(8,128)(2,1)S(1)} %collective-permute-done.10.refs_0_), channel_id=1, source_target_pairs={{0,2},{1,5},{2,0},{3,7},{4,6},{5,1},{6,4},{7,3},{8,10},{9,13},{10,... | collective-permute-start | bytes 393224 | tf_op jit(solution)/shard_map/ppermute | solution.py:100
  20.5 5.0 %collective-permute-start.5 = (bf16[16,4224]{1,0:T(8,128)(2,1)S(1)}, bf16[16,4224]{1,0:T(8,128)(2,1)S(1)}, u32[]{:S(2)}, u32[]{:S(2)}) collective-permute-start(bf16[16,4224]{1,0:T(8,128)(2,1)S(1)} %collective-permute-done.4.refs_0_), channel_id=1, source_target_pairs={{0,4},{1,3},{2,6},{3,1},{4,0},{5,7},{6,2},{7,5},{8,12},{9,11},{10,... | collective-permute-start | bytes 405512 | tf_op jit(solution)/shard_map/ppermute | solution.py:100
  22.2 3.4 %collective-permute-start.8 = (bf16[32,4224]{1,0:T(8,128)(2,1)S(1)}, bf16[32,4224]{1,0:T(8,128)(2,1)S(1)}, u32[]{:S(2)}, u32[]{:S(2)}) collective-permute-start(bf16[32,4224]{1,0:T(8,128)(2,1)S(1)} %shard_map.112.refs_0_), channel_id=1, source_target_pairs={{0,1},{1,0},{2,3},{3,2},{4,5},{5,4},{6,7},{7,6},{8,9},{9,8},{10,11... | collective-permute-start | bytes 811016 | tf_op jit(solution)/shard_map/ppermute | solution.py:100
  22.4 3.3 %collective-permute-start.7 = (bf16[32,4096]{1,0:T(8,128)(2,1)S(1)}, bf16[32,4096]{1,0:T(8,128)(2,1)S(1)}, u32[]{:S(2)}, u32[]{:S(2)}) collective-permute-start(bf16[32,4096]{1,0:T(8,128)(2,1)S(1)} %shard_map.114.refs_0_), channel_id=1, source_target_pairs={{0,1},{1,0},{2,3},{3,2},{4,5},{5,4},{6,7},{7,6},{8,9},{9,8},{10,11... | collective-permute-start | bytes 786440 | tf_op jit(solution)/shard_map/ppermute | solution.py:100
  24.8 1.6 %collective-permute-start.12 = (bf16[32,4096]{1,0:T(8,128)(2,1)S(1)}, bf16[32,4096]{1,0:T(8,128)(2,1)S(1)}, u32[]{:S(2)}, u32[]{:S(2)}) collective-permute-start(bf16[32,4096]{1,0:T(8,128)(2,1)S(1)} %shard_map.115.refs_1_), channel_id=1, source_target_pairs={{0,1},{1,0},{2,3},{3,2},{4,5},{5,4},{6,7},{7,6},{8,9},{9,8},{10,11... | collective-permute-start | bytes 786440 | tf_op jit(solution)/shard_map/ppermute | solution.py:100
  25.5 2.1 %collective-permute-start.9 = (bf16[32,4224]{1,0:T(8,128)(2,1)S(1)}, bf16[32,4224]{1,0:T(8,128)(2,1)S(1)}, u32[]{:S(2)}, u32[]{:S(2)}) collective-permute-start(bf16[32,4224]{1,0:T(8,128)(2,1)S(1)} %shard_map.113.refs_1_), channel_id=1, source_target_pairs={{0,1},{1,0},{2,3},{3,2},{4,5},{5,4},{6,7},{7,6},{8,9},{9,8},{10,11... | collective-permute-start | bytes 811016 | tf_op jit(solution)/shard_map/ppermute | solution.py:100
  29.6 1.6 %collective-permute-start.13 = (bf16[16,8192]{1,0:T(8,128)(2,1)S(1)}, bf16[16,8192]{1,0:T(8,128)(2,1)S(1)}, u32[]{:S(2)}, u32[]{:S(2)}) collective-permute-start(bf16[16,8192]{1,0:T(8,128)(2,1)S(1)} %get-tuple-element.61), channel_id=1, source_target_pairs={{0,1},{1,0},{2,3},{3,2},{4,5},{5,4},{6,7},{7,6},{8,9},{9,8},{10,11... | collective-permute-start | bytes 786440 | tf_op jit(solution)/shard_map/ppermute | solution.py:100
  31.2 2.3 %collective-permute-start.14 = (bf16[48,8192]{1,0:T(8,128)(2,1)S(1)}, bf16[48,8192]{1,0:T(8,128)(2,1)S(1)}, u32[]{:S(2)}, u32[]{:S(2)}) collective-permute-start(bf16[48,8192]{1,0:T(8,128)(2,1)S(1)} %get-tuple-element.63), channel_id=1, source_target_pairs={{0,1},{1,0},{2,3},{3,2},{4,5},{5,4},{6,7},{7,6},{8,9},{9,8},{10,11... | collective-permute-start | bytes 2359304 | tf_op jit(solution)/shard_map/ppermute | solution.py:100
  31.4 5.0 %collective-permute-start.16 = (bf16[16,4096]{1,0:T(8,128)(2,1)S(1)}, bf16[16,4096]{1,0:T(8,128)(2,1)S(1)}, u32[]{:S(2)}, u32[]{:S(2)}) collective-permute-start(bf16[16,4096]{1,0:T(8,128)(2,1)S(1)} %get-tuple-element.76), channel_id=1, source_target_pairs={{0,4},{1,3},{2,6},{3,1},{4,0},{5,7},{6,2},{7,5},{8,12},{9,11},{10,... | collective-permute-start | bytes 393224 | tf_op jit(solution)/shard_map/ppermute | solution.py:100
  32.9 5.0 %collective-permute-start.18 = (bf16[16,4096]{1,0:T(8,128)(2,1)S(1)}, bf16[16,4096]{1,0:T(8,128)(2,1)S(1)}, u32[]{:S(2)}, u32[]{:S(2)}) collective-permute-start(bf16[16,4096]{1,0:T(8,128)(2,1)S(1)} %get-tuple-element.78), channel_id=1, source_target_pairs={{0,4},{1,3},{2,6},{3,1},{4,0},{5,7},{6,2},{7,5},{8,12},{9,11},{10,... | collective-permute-start | bytes 393224 | tf_op jit(solution)/shard_map/ppermute | solution.py:100
  33.7 9.3 %collective-permute-start.15 = (bf16[16,8192]{1,0:T(8,128)(2,1)S(1)}, bf16[16,8192]{1,0:T(8,128)(2,1)S(1)}, u32[]{:S(2)}, u32[]{:S(2)}) collective-permute-start(bf16[16,8192]{1,0:T(8,128)(2,1)S(1)} %get-tuple-element.73), channel_id=1, source_target_pairs={{0,4},{1,3},{2,6},{3,1},{4,0},{5,7},{6,2},{7,5},{8,12},{9,11},{10,... | collective-permute-start | bytes 786440 | tf_op jit(solution)/shard_map/ppermute | solution.py:100
  36.5 5.0 %collective-permute-start.17 = (bf16[16,4096]{1,0:T(8,128)(2,1)S(1)}, bf16[16,4096]{1,0:T(8,128)(2,1)S(1)}, u32[]{:S(2)}, u32[]{:S(2)}) collective-permute-start(bf16[16,4096]{1,0:T(8,128)(2,1)S(1)} %shard_map.121), channel_id=1, source_target_pairs={{0,2},{1,5},{2,0},{3,7},{4,6},{5,1},{6,4},{7,3},{8,10},{9,13},{10,... | collective-permute-start | bytes 393224 | tf_op jit(solution)/shard_map/ppermute | solution.py:100
  37.9 5.0 %collective-permute-start.19 = (bf16[16,4096]{1,0:T(8,128)(2,1)S(1)}, bf16[16,4096]{1,0:T(8,128)(2,1)S(1)}, u32[]{:S(2)}, u32[]{:S(2)}) collective-permute-start(bf16[16,4096]{1,0:T(8,128)(2,1)S(1)} %shard_map.122), channel_id=1, source_target_pairs={{0,2},{1,5},{2,0},{3,7},{4,6},{5,1},{6,4},{7,3},{8,10},{9,13},{10,... | collective-permute-start | bytes 393224 | tf_op jit(solution)/shard_map/ppermute | solution.py:100
  43.1 6.9 %collective-permute-start.20 = (bf16[4,8192]{1,0:T(4,128)(2,1)S(1)}, bf16[4,8192]{1,0:T(4,128)(2,1)S(1)}, u32[]{:S(2)}, u32[]{:S(2)}) collective-permute-start(bf16[4,8192]{1,0:T(4,128)(2,1)S(1)} %get-tuple-element.82), channel_id=1, source_target_pairs={{0,24},{1,25},{2,26},{3,27},{4,28},{5,29},{6,30},{7,31},{8,16},{9,... | collective-permute-start | bytes 196616 | tf_op jit(solution)/shard_map/ppermute | solution.py:100
  45.3 6.8 %collective-permute-start.21 = (bf16[4,8192]{1,0:T(4,128)(2,1)S(1)}, bf16[4,8192]{1,0:T(4,128)(2,1)S(1)}, u32[]{:S(2)}, u32[]{:S(2)}) collective-permute-start(bf16[4,8192]{1,0:T(4,128)(2,1)S(1)} %get-tuple-element.83), channel_id=1, source_target_pairs={{0,16},{1,17},{2,18},{3,19},{4,20},{5,21},{6,22},{7,23},{8,24},{9,... | collective-permute-start | bytes 196616 | tf_op jit(solution)/shard_map/ppermute | solution.py:100
  45.3 6.8 %collective-permute-start.22 = (bf16[4,8192]{1,0:T(4,128)(2,1)S(1)}, bf16[4,8192]{1,0:T(4,128)(2,1)S(1)}, u32[]{:S(2)}, u32[]{:S(2)}) collective-permute-start(bf16[4,8192]{1,0:T(4,128)(2,1)S(1)} %get-tuple-element.84), channel_id=1, source_target_pairs={{0,8},{1,9},{2,10},{3,11},{4,12},{5,13},{6,14},{7,15},{8,0},{9,1},... | collective-permute-start | bytes 196616 | tf_op jit(solution)/shard_map/ppermute | solution.py:100

commit v14 on v11

--- a/solution.py
+++ b/solution.py
@@ -339,7 +339,9 @@
 
     x_pieces = both_cores((block_x, across_x), (aside_x, corner_x))
     dy_pieces = both_cores((block_dy, aside_dy), (across_dy, corner_dy))
-    x_pieces[2], dy_pieces[2] = lax.optimization_barrier((x_pieces[2], dy_pieces[2]))
+    x_pieces[2], dy_pieces[2], dy_pieces[1] = lax.optimization_barrier(
+        (x_pieces[2], dy_pieces[2], dy_pieces[1])
+    )
     all_x, hidden, gate_part, up_part = kernel_call(
         functools.partial(forward_body, len(x_pieces)),
         (shape(2 * half, width),) + (shape(2 * half, ff, dtype=f32),) * 3,

time: 53 us -> 53 us (level)
  no operation moved by 1% of the time
where the time goes in v14:
time: 53 us; the launch traced here: 52.8 us
  starting transfers between devices  22.7 us (43%)
  waiting for transfers between devices  17.2 us (32%)
  Pallas kernels  11.7 us (22%)
  between operations  0.85 us (2%)
    ppermute x23, starting transfers between devices, from_xor(): lax.ppermute(value, AXES, [(i, i ^ masks[i % 2]) for i in range(devices)])  22.7 us
    ppermute x23, waiting for transfers between devices, from_xor(): lax.ppermute(value, AXES, [(i, i ^ masks[i % 2]) for i in range(devices)])  17.2 us
    pallas_call x16, Pallas kernels, kernel_call(): pl.pallas_call(body, out_shape=out_shape, in_specs=specs, out_specs=jax.t...  11.7 us
  transfers between devices with their start and end apart: 23, of which 14 were waited for; matrix products, arithmetic and copies ran while one was open for 0% of the time, Pallas kernels for 15%

profile of v14, /device:TPU:0, one launch (start us, length us, event | category | flops | bytes accessed | tf_op | source)
XLA Modules:
  0.0 52.8 jit_solution(7959522538409468163)
XLA Ops:
  0.6 0.9 %shard_map.110 = (bf16[4,8320]{1,0:T(4,128)(2,1)S(1)}, f32[8,128]{1,0:T(8,128)S(1)}) custom-call(bf16[4,4096]{1,0:T(4,128)(2,1)} %x_ref.1, bf16[4,4096]{1,0:T(4,128)(2,1)} %dy_ref.1, s32[2,4]{1,0:T(2,128)} %bitcast.3, bf16[2,4]{1,0:T(2,128)(2,1)} %bitcast.4, s32[1]{0:T(128)} %bitcast.2.expert_ref), custom_call_target="tpu_custom_call" | custom-call | bytes 4194304 | tf_op jit(solution)/shard_map/pallas_call | solution.py:121
  1.5 5.1 %collective-permute-start.2 = (bf16[4,8320]{1,0:T(4,128)(2,1)S(1)}, bf16[4,8320]{1,0:T(4,128)(2,1)S(1)}, u32[]{:S(2)}, u32[]{:S(2)}) collective-permute-start(bf16[4,8320]{1,0:T(4,128)(2,1)S(1)} %get-tuple-element.49), channel_id=1, source_target_pairs={{0,24},{1,25},{2,26},{3,27},{4,28},{5,29},{6,30},{7,31},{8,16},{9,... | collective-permute-start | bytes 199688 | tf_op jit(solution)/shard_map/ppermute | solution.py:100
  7.3 2.4 %shard_map.111 = (bf16[384,4096]{1,0:T(8,128)(2,1)S(1)}, bf16[192,4096]{1,0:T(8,128)(2,1)S(1)}) custom-call(bf16[1,192,4096]{2,1,0:T(8,128)(2,1)} %gate_ref.1, bf16[1,192,4096]{2,1,0:T(8,128)(2,1)} %up_ref.1, bf16[1,192,4096]{2,1,0:T(8,128)(2,1)} %down_ref.1), custom_call_target="tpu_custom_call" | custom-call | bytes 4194304 | tf_op jit(solution)/shard_map/pallas_call | solution.py:121
  9.7 2.6 %collective-permute-done.1 = bf16[4,8320]{1,0:T(4,128)(2,1)S(1)} collective-permute-done((bf16[4,8320]{1,0:T(4,128)(2,1)S(1)}, bf16[4,8320]{1,0:T(4,128)(2,1)S(1)}, u32[]{:S(2)}, u32[]{:S(2)}) %collective-permute-start.1) | collective-permute-done | bytes 66592 | tf_op jit(solution)/shard_map/ppermute | solution.py:100
  12.4 1.6 %collective-permute-start.10 = (bf16[16,4096]{1,0:T(8,128)(2,1)S(1)}, bf16[16,4096]{1,0:T(8,128)(2,1)S(1)}, u32[]{:S(2)}, u32[]{:S(2)}) collective-permute-start(bf16[16,4096]{1,0:T(8,128)(2,1)S(1)} %pad_maximum_fusion.1.refs_0_), channel_id=1, source_target_pairs={{0,4},{1,3},{2,6},{3,1},{4,0},{5,7},{6,2},{7,5},{8,12},{9,11},{10,... | collective-permute-start | bytes 393224 | tf_op jit(solution)/shard_map/ppermute | solution.py:100
  14.1 1.6 %collective-permute-start.7 = (bf16[16,4224]{1,0:T(8,128)(2,1)S(1)}, bf16[16,4224]{1,0:T(8,128)(2,1)S(1)}, u32[]{:S(2)}, u32[]{:S(2)}) collective-permute-start(bf16[16,4224]{1,0:T(8,128)(2,1)S(1)} %pad_maximum_fusion.refs_0_), channel_id=1, source_target_pairs={{0,2},{1,5},{2,0},{3,7},{4,6},{5,1},{6,4},{7,3},{8,10},{9,13},{10,... | collective-permute-start | bytes 405512 | tf_op jit(solution)/shard_map/ppermute | solution.py:100
  16.7 1.8 %collective-permute-done.10.refs_0_ = bf16[16,4096]{1,0:T(8,128)(2,1)S(1)} collective-permute-done((bf16[16,4096]{1,0:T(8,128)(2,1)S(1)}, bf16[16,4096]{1,0:T(8,128)(2,1)S(1)}, u32[]{:S(2)}, u32[]{:S(2)}) %collective-permute-start.10) | collective-permute-done | bytes 131104 | tf_op jit(solution)/shard_map/ppermute | solution.py:100
  18.6 1.1 %collective-permute-start.11 = (bf16[16,4096]{1,0:T(8,128)(2,1)S(1)}, bf16[16,4096]{1,0:T(8,128)(2,1)S(1)}, u32[]{:S(2)}, u32[]{:S(2)}) collective-permute-start(bf16[16,4096]{1,0:T(8,128)(2,1)S(1)} %collective-permute-done.10.refs_0_), channel_id=1, source_target_pairs={{0,2},{1,5},{2,0},{3,7},{4,6},{5,1},{6,4},{7,3},{8,10},{9,13},{10,... | collective-permute-start | bytes 393224 | tf_op jit(solution)/shard_map/ppermute | solution.py:100
  19.7 0.8 %collective-permute-done.7.refs_0_ = bf16[16,4224]{1,0:T(8,128)(2,1)S(1)} collective-permute-done((bf16[16,4224]{1,0:T(8,128)(2,1)S(1)}, bf16[16,4224]{1,0:T(8,128)(2,1)S(1)}, u32[]{:S(2)}, u32[]{:S(2)}) %collective-permute-start.7) | collective-permute-done | bytes 135200 | tf_op jit(solution)/shard_map/ppermute | solution.py:100
  20.5 1.3 %collective-permute-start.8 = (bf16[16,4224]{1,0:T(8,128)(2,1)S(1)}, bf16[16,4224]{1,0:T(8,128)(2,1)S(1)}, u32[]{:S(2)}, u32[]{:S(2)}) collective-permute-start(bf16[16,4224]{1,0:T(8,128)(2,1)S(1)} %collective-permute-done.7.refs_0_), channel_id=1, source_target_pairs={{0,4},{1,3},{2,6},{3,1},{4,0},{5,7},{6,2},{7,5},{8,12},{9,11},{10,... | collective-permute-start | bytes 405512 | tf_op jit(solution)/shard_map/ppermute | solution.py:100
  22.9 1.9 %collective-permute-done.11.refs_1_ = bf16[16,4096]{1,0:T(8,128)(2,1)S(1)} collective-permute-done((bf16[16,4096]{1,0:T(8,128)(2,1)S(1)}, bf16[16,4096]{1,0:T(8,128)(2,1)S(1)}, u32[]{:S(2)}, u32[]{:S(2)}) %collective-permute-start.11) | collective-permute-done | bytes 131104 | tf_op jit(solution)/shard_map/ppermute | solution.py:100
  26.4 1.2 %shard_map.116 = (bf16[128,4096]{1,0:T(8,128)(2,1)S(1)}, f32[128,192]{1,0:T(8,128)S(1)}, f32[128,192]{1,0:T(8,128)S(1)}, f32[128,192]{1,0:T(8,128)S(1)}) custom-call(bf16[32,4096]{1,0:T(8,128)(2,1)S(1)} %shard_map.113.refs_0_, bf16[32,4096]{1,0:T(8,128)(2,1)S(1)} %shard_map.115.refs_1_, bf16[32,4096]{1,0:T(8,128)(2,1)S(1)} %collective-permute-done.5.refs_2_, ...), custom_call_target="tpu_custom_call" | custom-call | flops 402653184 | bytes 4194304 | tf_op jit(solution)/shard_map/pallas_call | solution.py:121
  27.6 1.9 %shard_map.117 = (bf16[128,4096]{1,0:T(8,128)(2,1)S(1)}, bf16[128,192]{1,0:T(8,128)(2,1)S(1)}, bf16[128,384]{1,0:T(8,128)(2,1)S(1)}, f32[64,8192]{1,0:T(8,128)S(...) custom-call(bf16[32,4224]{1,0:T(8,128)(2,1)S(1)} %shard_map.112.refs_0_, ...), custom_call_target="tpu_custom_call" | custom-call | flops 603979776 | bytes 4194304 | tf_op jit(solution)/shard_map/pallas_call | solution.py:121
  29.8 1.4 %collective-permute-done.13.came_ref = bf16[16,8192]{1,0:T(8,128)(2,1)S(1)} collective-permute-done((bf16[16,8192]{1,0:T(8,128)(2,1)S(1)}, bf16[16,8192]{1,0:T(8,128)(2,1)S(1)}, u32[]{:S(2)}, u32[]{:S(2)}) %collective-permute-start.13) | collective-permute-done | bytes 262176 | tf_op jit(solution)/shard_map/ppermute | solution.py:100
  31.4 1.6 %collective-permute-start.16 = (bf16[16,4096]{1,0:T(8,128)(2,1)S(1)}, bf16[16,4096]{1,0:T(8,128)(2,1)S(1)}, u32[]{:S(2)}, u32[]{:S(2)}) collective-permute-start(bf16[16,4096]{1,0:T(8,128)(2,1)S(1)} %get-tuple-element.78), channel_id=1, source_target_pairs={{0,4},{1,3},{2,6},{3,1},{4,0},{5,7},{6,2},{7,5},{8,12},{9,11},{10,... | collective-permute-start | bytes 393224 | tf_op jit(solution)/shard_map/ppermute | solution.py:100
  33.7 1.6 %collective-permute-start.15 = (bf16[16,8192]{1,0:T(8,128)(2,1)S(1)}, bf16[16,8192]{1,0:T(8,128)(2,1)S(1)}, u32[]{:S(2)}, u32[]{:S(2)}) collective-permute-start(bf16[16,8192]{1,0:T(8,128)(2,1)S(1)} %get-tuple-element.75), channel_id=1, source_target_pairs={{0,4},{1,3},{2,6},{3,1},{4,0},{5,7},{6,2},{7,5},{8,12},{9,11},{10,... | collective-permute-start | bytes 786440 | tf_op jit(solution)/shard_map/ppermute | solution.py:100
  35.2 1.2 %collective-permute-done.16.came_ref = bf16[16,4096]{1,0:T(8,128)(2,1)S(1)} collective-permute-done((bf16[16,4096]{1,0:T(8,128)(2,1)S(1)}, bf16[16,4096]{1,0:T(8,128)(2,1)S(1)}, u32[]{:S(2)}, u32[]{:S(2)}) %collective-permute-start.16) | collective-permute-done | bytes 131104 | tf_op jit(solution)/shard_map/ppermute | solution.py:100
  37.0 0.9 %collective-permute-done.18.came_ref = bf16[16,4096]{1,0:T(8,128)(2,1)S(1)} collective-permute-done((bf16[16,4096]{1,0:T(8,128)(2,1)S(1)}, bf16[16,4096]{1,0:T(8,128)(2,1)S(1)}, u32[]{:S(2)}, u32[]{:S(2)}) %collective-permute-start.18) | collective-permute-done | bytes 131104 | tf_op jit(solution)/shard_map/ppermute | solution.py:100
  38.6 2.5 %shard_map.119 = (bf16[1,192,4096]{2,1,0:T(8,128)(2,1)}, bf16[1,192,4096]{2,1,0:T(8,128)(2,1)}) custom-call(bf16[128,4096]{1,0:T(8,128)(2,1)S(1)} %get-tuple-element.70.rows_ref, bf16[128,384]{1,0:T(8,128)(2,1)S(1)} %get-tuple-element.71.acts_ref), custom_call_target="tpu_custom_call" | custom-call | flops 402653184 | bytes 4194304 | tf_op jit(solution)/shard_map/pallas_call | solution.py:121
  41.5 1.5 %collective-permute-done.19.refs_1_ = bf16[16,4096]{1,0:T(8,128)(2,1)S(1)} collective-permute-done((bf16[16,4096]{1,0:T(8,128)(2,1)S(1)}, bf16[16,4096]{1,0:T(8,128)(2,1)S(1)}, u32[]{:S(2)}, u32[]{:S(2)}) %collective-permute-start.19) | collective-permute-done | bytes 131104 | tf_op jit(solution)/shard_map/ppermute | solution.py:100
  43.1 2.2 %collective-permute-start.20 = (bf16[4,8192]{1,0:T(4,128)(2,1)S(1)}, bf16[4,8192]{1,0:T(4,128)(2,1)S(1)}, u32[]{:S(2)}, u32[]{:S(2)}) collective-permute-start(bf16[4,8192]{1,0:T(4,128)(2,1)S(1)} %get-tuple-element.84), channel_id=1, source_target_pairs={{0,24},{1,25},{2,26},{3,27},{4,28},{5,29},{6,30},{7,31},{8,16},{9,... | collective-permute-start | bytes 196616 | tf_op jit(solution)/shard_map/ppermute | solution.py:100
  45.3 2.2 %collective-permute-start.22 = (bf16[4,8192]{1,0:T(4,128)(2,1)S(1)}, bf16[4,8192]{1,0:T(4,128)(2,1)S(1)}, u32[]{:S(2)}, u32[]{:S(2)}) collective-permute-start(bf16[4,8192]{1,0:T(4,128)(2,1)S(1)} %get-tuple-element.86), channel_id=1, source_target_pairs={{0,8},{1,9},{2,10},{3,11},{4,12},{5,13},{6,14},{7,15},{8,0},{9,1},... | collective-permute-start | bytes 196616 | tf_op jit(solution)/shard_map/ppermute | solution.py:100
  47.6 1.7 %shard_map.125 = bf16[1,192,4096]{2,1,0:T(8,128)(2,1)} custom-call(bf16[128,4096]{1,0:T(8,128)(2,1)S(1)} %get-tuple-element.91.rows_ref, bf16[128,192]{1,0:T(8,128)(2,1)S(1)} %get-tuple-element.92.acts_ref), custom_call_target="tpu_custom_call" | custom-call | flops 201326592 | bytes 4194304 | tf_op jit(solution)/shard_map/pallas_call | solution.py:121
  50.0 2.2 %collective-permute-done.21.refs_1_ = bf16[4,8192]{1,0:T(4,128)(2,1)S(1)} collective-permute-done((bf16[4,8192]{1,0:T(4,128)(2,1)S(1)}, bf16[4,8192]{1,0:T(4,128)(2,1)S(1)}, u32[]{:S(2)}, u32[]{:S(2)}) %collective-permute-start.21) | collective-permute-done | bytes 65568 | tf_op jit(solution)/shard_map/ppermute | solution.py:100
  (48 shorter events, 8.8 us)
Async XLA Ops:
  1.5 8.2 %collective-permute-start.2 = (bf16[4,8320]{1,0:T(4,128)(2,1)S(1)}, bf16[4,8320]{1,0:T(4,128)(2,1)S(1)}, u32[]{:S(2)}, u32[]{:S(2)}) collective-permute-start(bf16[4,8320]{1,0:T(4,128)(2,1)S(1)} %get-tuple-element.49), channel_id=1, source_target_pairs={{0,24},{1,25},{2,26},{3,27},{4,28},{5,29},{6,30},{7,31},{8,16},{9,... | collective-permute-start | bytes 199688 | tf_op jit(solution)/shard_map/ppermute | solution.py:100
  6.6 5.7 %collective-permute-start.1 = (bf16[4,8320]{1,0:T(4,128)(2,1)S(1)}, bf16[4,8320]{1,0:T(4,128)(2,1)S(1)}, u32[]{:S(2)}, u32[]{:S(2)}) collective-permute-start(bf16[4,8320]{1,0:T(4,128)(2,1)S(1)} %get-tuple-element.49), channel_id=1, source_target_pairs={{0,16},{1,17},{2,18},{3,19},{4,20},{5,21},{6,22},{7,23},{8,24},{9,... | collective-permute-start | bytes 199688 | tf_op jit(solution)/shard_map/ppermute | solution.py:100
  6.6 5.7 %collective-permute-start = (bf16[4,8320]{1,0:T(4,128)(2,1)S(1)}, bf16[4,8320]{1,0:T(4,128)(2,1)S(1)}, u32[]{:S(2)}, u32[]{:S(2)}) collective-permute-start(bf16[4,8320]{1,0:T(4,128)(2,1)S(1)} %get-tuple-element.49), channel_id=1, source_target_pairs={{0,8},{1,9},{2,10},{3,11},{4,12},{5,13},{6,14},{7,15},{8,0},{9,1},... | collective-permute-start | bytes 199688 | tf_op jit(solution)/shard_map/ppermute | solution.py:100
  12.4 6.2 %collective-permute-start.10 = (bf16[16,4096]{1,0:T(8,128)(2,1)S(1)}, bf16[16,4096]{1,0:T(8,128)(2,1)S(1)}, u32[]{:S(2)}, u32[]{:S(2)}) collective-permute-start(bf16[16,4096]{1,0:T(8,128)(2,1)S(1)} %pad_maximum_fusion.1.refs_0_), channel_id=1, source_target_pairs={{0,4},{1,3},{2,6},{3,1},{4,0},{5,7},{6,2},{7,5},{8,12},{9,11},{10,... | collective-permute-start | bytes 393224 | tf_op jit(solution)/shard_map/ppermute | solution.py:100
  14.1 6.4 %collective-permute-start.7 = (bf16[16,4224]{1,0:T(8,128)(2,1)S(1)}, bf16[16,4224]{1,0:T(8,128)(2,1)S(1)}, u32[]{:S(2)}, u32[]{:S(2)}) collective-permute-start(bf16[16,4224]{1,0:T(8,128)(2,1)S(1)} %pad_maximum_fusion.refs_0_), channel_id=1, source_target_pairs={{0,2},{1,5},{2,0},{3,7},{4,6},{5,1},{6,4},{7,3},{8,10},{9,13},{10,... | collective-permute-start | bytes 405512 | tf_op jit(solution)/shard_map/ppermute | solution.py:100
  15.7 6.5 %collective-permute-start.3 = (bf16[16,4224]{1,0:T(8,128)(2,1)S(1)}, bf16[16,4224]{1,0:T(8,128)(2,1)S(1)}, u32[]{:S(2)}, u32[]{:S(2)}) collective-permute-start(bf16[16,4224]{1,0:T(8,128)(2,1)S(1)} %pad_maximum_fusion.refs_0_), channel_id=1, source_target_pairs={{0,4},{1,3},{2,6},{3,1},{4,0},{5,7},{6,2},{7,5},{8,12},{9,11},{10,... | collective-permute-start | bytes 405512 | tf_op jit(solution)/shard_map/ppermute | solution.py:100
  16.2 6.1 %collective-permute-start.4 = (bf16[16,4096]{1,0:T(8,128)(2,1)S(1)}, bf16[16,4096]{1,0:T(8,128)(2,1)S(1)}, u32[]{:S(2)}, u32[]{:S(2)}) collective-permute-start(bf16[16,4096]{1,0:T(8,128)(2,1)S(1)} %pad_maximum_fusion.1.refs_0_), channel_id=1, source_target_pairs={{0,2},{1,5},{2,0},{3,7},{4,6},{5,1},{6,4},{7,3},{8,10},{9,13},{10,... | collective-permute-start | bytes 393224 | tf_op jit(solution)/shard_map/ppermute | solution.py:100
  18.6 6.2 %collective-permute-start.11 = (bf16[16,4096]{1,0:T(8,128)(2,1)S(1)}, bf16[16,4096]{1,0:T(8,128)(2,1)S(1)}, u32[]{:S(2)}, u32[]{:S(2)}) collective-permute-start(bf16[16,4096]{1,0:T(8,128)(2,1)S(1)} %collective-permute-done.10.refs_0_), channel_id=1, source_target_pairs={{0,2},{1,5},{2,0},{3,7},{4,6},{5,1},{6,4},{7,3},{8,10},{9,13},{10,... | collective-permute-start | bytes 393224 | tf_op jit(solution)/shard_map/ppermute | solution.py:100
  20.5 5.0 %collective-permute-start.8 = (bf16[16,4224]{1,0:T(8,128)(2,1)S(1)}, bf16[16,4224]{1,0:T(8,128)(2,1)S(1)}, u32[]{:S(2)}, u32[]{:S(2)}) collective-permute-start(bf16[16,4224]{1,0:T(8,128)(2,1)S(1)} %collective-permute-done.7.refs_0_), channel_id=1, source_target_pairs={{0,4},{1,3},{2,6},{3,1},{4,0},{5,7},{6,2},{7,5},{8,12},{9,11},{10,... | collective-permute-start | bytes 405512 | tf_op jit(solution)/shard_map/ppermute | solution.py:100
  22.2 3.4 %collective-permute-start.6 = (bf16[32,4224]{1,0:T(8,128)(2,1)S(1)}, bf16[32,4224]{1,0:T(8,128)(2,1)S(1)}, u32[]{:S(2)}, u32[]{:S(2)}) collective-permute-start(bf16[32,4224]{1,0:T(8,128)(2,1)S(1)} %shard_map.112.refs_0_), channel_id=1, source_target_pairs={{0,1},{1,0},{2,3},{3,2},{4,5},{5,4},{6,7},{7,6},{8,9},{9,8},{10,11... | collective-permute-start | bytes 811016 | tf_op jit(solution)/shard_map/ppermute | solution.py:100
  22.4 3.3 %collective-permute-start.5 = (bf16[32,4096]{1,0:T(8,128)(2,1)S(1)}, bf16[32,4096]{1,0:T(8,128)(2,1)S(1)}, u32[]{:S(2)}, u32[]{:S(2)}) collective-permute-start(bf16[32,4096]{1,0:T(8,128)(2,1)S(1)} %shard_map.113.refs_0_), channel_id=1, source_target_pairs={{0,1},{1,0},{2,3},{3,2},{4,5},{5,4},{6,7},{7,6},{8,9},{9,8},{10,11... | collective-permute-start | bytes 786440 | tf_op jit(solution)/shard_map/ppermute | solution.py:100
  24.8 1.6 %collective-permute-start.12 = (bf16[32,4096]{1,0:T(8,128)(2,1)S(1)}, bf16[32,4096]{1,0:T(8,128)(2,1)S(1)}, u32[]{:S(2)}, u32[]{:S(2)}) collective-permute-start(bf16[32,4096]{1,0:T(8,128)(2,1)S(1)} %shard_map.115.refs_1_), channel_id=1, source_target_pairs={{0,1},{1,0},{2,3},{3,2},{4,5},{5,4},{6,7},{7,6},{8,9},{9,8},{10,11... | collective-permute-start | bytes 786440 | tf_op jit(solution)/shard_map/ppermute | solution.py:100
  25.5 2.1 %collective-permute-start.9 = (bf16[32,4224]{1,0:T(8,128)(2,1)S(1)}, bf16[32,4224]{1,0:T(8,128)(2,1)S(1)}, u32[]{:S(2)}, u32[]{:S(2)}) collective-permute-start(bf16[32,4224]{1,0:T(8,128)(2,1)S(1)} %shard_map.114.refs_1_), channel_id=1, source_target_pairs={{0,1},{1,0},{2,3},{3,2},{4,5},{5,4},{6,7},{7,6},{8,9},{9,8},{10,11... | collective-permute-start | bytes 811016 | tf_op jit(solution)/shard_map/ppermute | solution.py:100
  29.6 1.6 %collective-permute-start.13 = (bf16[16,8192]{1,0:T(8,128)(2,1)S(1)}, bf16[16,8192]{1,0:T(8,128)(2,1)S(1)}, u32[]{:S(2)}, u32[]{:S(2)}) collective-permute-start(bf16[16,8192]{1,0:T(8,128)(2,1)S(1)} %get-tuple-element.63), channel_id=1, source_target_pairs={{0,1},{1,0},{2,3},{3,2},{4,5},{5,4},{6,7},{7,6},{8,9},{9,8},{10,11... | collective-permute-start | bytes 786440 | tf_op jit(solution)/shard_map/ppermute | solution.py:100
  31.2 2.3 %collective-permute-start.14 = (bf16[48,8192]{1,0:T(8,128)(2,1)S(1)}, bf16[48,8192]{1,0:T(8,128)(2,1)S(1)}, u32[]{:S(2)}, u32[]{:S(2)}) collective-permute-start(bf16[48,8192]{1,0:T(8,128)(2,1)S(1)} %get-tuple-element.65), channel_id=1, source_target_pairs={{0,1},{1,0},{2,3},{3,2},{4,5},{5,4},{6,7},{7,6},{8,9},{9,8},{10,11... | collective-permute-start | bytes 2359304 | tf_op jit(solution)/shard_map/ppermute | solution.py:100
  31.4 5.0 %collective-permute-start.16 = (bf16[16,4096]{1,0:T(8,128)(2,1)S(1)}, bf16[16,4096]{1,0:T(8,128)(2,1)S(1)}, u32[]{:S(2)}, u32[]{:S(2)}) collective-permute-start(bf16[16,4096]{1,0:T(8,128)(2,1)S(1)} %get-tuple-element.78), channel_id=1, source_target_pairs={{0,4},{1,3},{2,6},{3,1},{4,0},{5,7},{6,2},{7,5},{8,12},{9,11},{10,... | collective-permute-start | bytes 393224 | tf_op jit(solution)/shard_map/ppermute | solution.py:100
  32.9 5.0 %collective-permute-start.18 = (bf16[16,4096]{1,0:T(8,128)(2,1)S(1)}, bf16[16,4096]{1,0:T(8,128)(2,1)S(1)}, u32[]{:S(2)}, u32[]{:S(2)}) collective-permute-start(bf16[16,4096]{1,0:T(8,128)(2,1)S(1)} %get-tuple-element.80), channel_id=1, source_target_pairs={{0,4},{1,3},{2,6},{3,1},{4,0},{5,7},{6,2},{7,5},{8,12},{9,11},{10,... | collective-permute-start | bytes 393224 | tf_op jit(solution)/shard_map/ppermute | solution.py:100
  33.7 9.3 %collective-permute-start.15 = (bf16[16,8192]{1,0:T(8,128)(2,1)S(1)}, bf16[16,8192]{1,0:T(8,128)(2,1)S(1)}, u32[]{:S(2)}, u32[]{:S(2)}) collective-permute-start(bf16[16,8192]{1,0:T(8,128)(2,1)S(1)} %get-tuple-element.75), channel_id=1, source_target_pairs={{0,4},{1,3},{2,6},{3,1},{4,0},{5,7},{6,2},{7,5},{8,12},{9,11},{10,... | collective-permute-start | bytes 786440 | tf_op jit(solution)/shard_map/ppermute | solution.py:100
  36.5 5.0 %collective-permute-start.17 = (bf16[16,4096]{1,0:T(8,128)(2,1)S(1)}, bf16[16,4096]{1,0:T(8,128)(2,1)S(1)}, u32[]{:S(2)}, u32[]{:S(2)}) collective-permute-start(bf16[16,4096]{1,0:T(8,128)(2,1)S(1)} %shard_map.121), channel_id=1, source_target_pairs={{0,2},{1,5},{2,0},{3,7},{4,6},{5,1},{6,4},{7,3},{8,10},{9,13},{10,... | collective-permute-start | bytes 393224 | tf_op jit(solution)/shard_map/ppermute | solution.py:100
  37.9 5.0 %collective-permute-start.19 = (bf16[16,4096]{1,0:T(8,128)(2,1)S(1)}, bf16[16,4096]{1,0:T(8,128)(2,1)S(1)}, u32[]{:S(2)}, u32[]{:S(2)}) collective-permute-start(bf16[16,4096]{1,0:T(8,128)(2,1)S(1)} %shard_map.122), channel_id=1, source_target_pairs={{0,2},{1,5},{2,0},{3,7},{4,6},{5,1},{6,4},{7,3},{8,10},{9,13},{10,... | collective-permute-start | bytes 393224 | tf_op jit(solution)/shard_map/ppermute | solution.py:100
  43.1 6.9 %collective-permute-start.20 = (bf16[4,8192]{1,0:T(4,128)(2,1)S(1)}, bf16[4,8192]{1,0:T(4,128)(2,1)S(1)}, u32[]{:S(2)}, u32[]{:S(2)}) collective-permute-start(bf16[4,8192]{1,0:T(4,128)(2,1)S(1)} %get-tuple-element.84), channel_id=1, source_target_pairs={{0,24},{1,25},{2,26},{3,27},{4,28},{5,29},{6,30},{7,31},{8,16},{9,... | collective-permute-start | bytes 196616 | tf_op jit(solution)/shard_map/ppermute | solution.py:100
  45.3 6.8 %collective-permute-start.21 = (bf16[4,8192]{1,0:T(4,128)(2,1)S(1)}, bf16[4,8192]{1,0:T(4,128)(2,1)S(1)}, u32[]{:S(2)}, u32[]{:S(2)}) collective-permute-start(bf16[4,8192]{1,0:T(4,128)(2,1)S(1)} %get-tuple-element.85), channel_id=1, source_target_pairs={{0,16},{1,17},{2,18},{3,19},{4,20},{5,21},{6,22},{7,23},{8,24},{9,... | collective-permute-start | bytes 196616 | tf_op jit(solution)/shard_map/ppermute | solution.py:100
  45.3 6.8 %collective-permute-start.22 = (bf16[4,8192]{1,0:T(4,128)(2,1)S(1)}, bf16[4,8192]{1,0:T(4,128)(2,1)S(1)}, u32[]{:S(2)}, u32[]{:S(2)}) collective-permute-start(bf16[4,8192]{1,0:T(4,128)(2,1)S(1)} %get-tuple-element.86), channel_id=1, source_target_pairs={{0,8},{1,9},{2,10},{3,11},{4,12},{5,13},{6,14},{7,15},{8,0},{9,1},... | collective-permute-start | bytes 196616 | tf_op jit(solution)/shard_map/ppermute | solution.py:100
